TPU v7x, 32 devices: a whole 2x2x4 slice. The times are simulated.
32 devices in a mesh: section: 4 (over x, core), dom: 8 (over z, y).
Axes of the slice: x: 2, y: 2, z: 4, core: 2. Of those that a mesh axis runs over, the one named last changes fastest.
Arguments:
- initial_features: bfloat16 [12288, 384], P('dom'), may hold values from -16 to 16
- layer_weights: bfloat16 [8, 384, 384], P('section'), may hold values from -0.3125 to 0.3125
- adjacency_tiles: bfloat16 [96, 24, 128, 128], P('dom'), may hold values from -0.15625 to 0.15625
- tile_columns: int32 [96, 24], P('dom'), may hold values from 0 to 35, as said below
- send_blocks: int32 [8, 3, 8], P('dom'), may hold values from -1 to 3, as said below
- stale_imports: bfloat16 [8, 8, 16, 128, 384], P('section', 'dom'), may hold values from 0 to 1.5
Outputs:
- final_features: bfloat16 [12288, 384], P('dom', 'section')
Inputs may be any that keep to these rules, and one draw needn't show every extreme that they name: send_blocks[q, h, p] is -1 when q equals p, else -1 or a block index of 0 to 3 within row group h. `tile_columns`: for a tile of partition p's local block r: a value j < 12 names p's own block j with j // 4 <= r // 4; a value 12 + h*8 + q names an import slot with send_blocks[q, h, p] >= 0.
All inputs are finite; a program needn't handle non-finite values.
Results may differ from a plain program's by a relative error of at most 0.011.
Values may be sent and summed in bfloat16 or wider, within the bound.
No kernel may reach another device: no remote copies, remote signals or barrier semaphores. Data moves between devices by JAX's collectives and lax.ppermute only.
A program may use at most 256 MiB of HBM per device.

v0:
```python
import jax
import jax.numpy as jnp
from jax import lax
from jax.sharding import PartitionSpec as P

alpha_mix = 0.1
lambda_decay = 0.5


def shifted(value, axis, steps):
    count = lax.axis_size(axis)
    initial, last = (max(0, -steps), min(count, count - steps))
    return lax.ppermute(value, axis, [(source, source + steps) for source in range(initial, last)])


def gather_rows(table, columns, tile_rows):
    picked = table[columns]
    flat = picked.reshape(picked.shape[0], picked.shape[1] * picked.shape[2], picked.shape[3])
    return jnp.einsum("rim,rmd->rid", tile_rows, flat, preferred_element_type=jnp.float32)


def finish(summed, initial_rows, weight, beta_layer):
    mixed = ((1.0 - alpha_mix) * summed + alpha_mix * initial_rows.astype(jnp.float32)).astype(
        jnp.bfloat16
    )
    product = jnp.einsum("rid,de->rie", mixed, weight, preferred_element_type=jnp.float32)
    return jax.nn.relu(
        (1.0 - beta_layer) * mixed.astype(jnp.float32) + beta_layer * product
    ).astype(jnp.bfloat16)


def per_device(
    initial_features, layer_weights, adjacency_tiles, tile_columns, send_blocks, stale_imports
):
    segment_index = lax.axis_index("section")
    segment_count = lax.axis_size("section")
    part_count = lax.axis_size("dom")
    blocks_dev = adjacency_tiles.shape[0]
    fanout = adjacency_tiles.shape[1]
    block = adjacency_tiles.shape[2]
    width = initial_features.shape[1]
    groups = send_blocks.shape[1]
    group_blocks = blocks_dev // groups
    depth = layer_weights.shape[0]
    tile_rows_all = adjacency_tiles.transpose(0, 2, 1, 3).reshape(blocks_dev, block, fanout * block)
    initial_blocks = initial_features.reshape(blocks_dev, block, width)
    send_row = send_blocks[0]
    block_ids = jnp.arange(group_blocks, dtype=jnp.int32)
    turns = groups + segment_count - 1

    def turn(position, carry):
        inbox, owned, imported, results = carry
        group_index = position - segment_index
        active = (group_index >= 0) & (group_index < groups)
        current = jnp.clip(group_index, 0, groups - 1)
        first_row = current * group_blocks
        initial_rows = lax.dynamic_slice_in_dim(initial_blocks, first_row, group_blocks, 0)
        columns = lax.dynamic_slice_in_dim(tile_columns, first_row, group_blocks, 0)
        tile_rows = lax.dynamic_slice_in_dim(tile_rows_all, first_row, group_blocks, 0)
        features = jnp.where(segment_index == 0, initial_rows, inbox)
        picks = send_row[current]
        selector = (picks[:, None] == block_ids[None, :]).astype(jnp.bfloat16)
        owned_next = []
        imported_next = []
        for sublayer in range(depth):
            weight = layer_weights[sublayer]
            beta_layer = jnp.log(
                lambda_decay / (depth * segment_index + sublayer + 1).astype(jnp.float32) + 1.0
            )
            own_table = owned[sublayer]
            kept_rows = lax.dynamic_slice_in_dim(own_table, first_row, group_blocks, 0)
            own_table = lax.dynamic_update_slice_in_dim(
                own_table, jnp.where(active, features, kept_rows), first_row, 0
            )
            stale_table = imported[sublayer]
            outgoing = jnp.einsum(
                "eb,bid->eid", selector, features, preferred_element_type=jnp.float32
            ).astype(jnp.bfloat16)
            received = lax.all_to_all(outgoing, "dom", split_axis=0, concat_axis=0, tiled=True)
            kept_slots = lax.dynamic_slice_in_dim(stale_table, current * part_count, part_count, 0)
            stale_table = lax.dynamic_update_slice_in_dim(
                stale_table, jnp.where(active, received, kept_slots), current * part_count, 0
            )
            table = jnp.concatenate([own_table, stale_table], 0)
            features = lax.cond(
                active,
                lambda: finish(
                    gather_rows(table, columns, tile_rows), initial_rows, weight, beta_layer
                ),
                lambda: features,
            )
            owned_next.append(own_table)
            imported_next.append(stale_table)
        kept_out = lax.dynamic_slice_in_dim(results, first_row, group_blocks, 0)
        results = lax.dynamic_update_slice_in_dim(
            results, jnp.where(active, features, kept_out), first_row, 0
        )
        inbox = shifted(features, "section", 1)
        return (inbox, jnp.stack(owned_next), jnp.stack(imported_next), results)

    start_carry = (
        jnp.zeros((group_blocks, block, width), jnp.bfloat16),
        jnp.zeros((depth, blocks_dev, block, width), jnp.bfloat16),
        jnp.concatenate(
            [jnp.zeros((depth, part_count, block, width), jnp.bfloat16), stale_imports[:, 0]], 1
        ),
        jnp.zeros((blocks_dev, block, width), jnp.bfloat16),
    )
    final_carry = lax.fori_loop(0, turns, turn, start_carry)
    finished = final_carry[3].reshape(blocks_dev * block, width)
    pieces = lax.all_to_all(finished, "section", split_axis=1, concat_axis=0, tiled=True)
    return pieces[(segment_count - 1) * blocks_dev * block :]


def solution(mesh):
    return jax.shard_map(
        per_device,
        mesh=mesh,
        in_specs=(
            P("dom", None),
            P("section", None, None),
            P("dom", None, None, None),
            P("dom", None),
            P("dom", None, None),
            P("section", "dom", None, None, None),
        ),
        out_specs=P("dom", "section"),
        check_vma=False,
    )
```

profile of v0, /device:TPU:0, one launch (start us, length us, event | category | flops | bytes accessed | tf_op | source)
XLA Modules:
  0.0 654.3 jit_solution(3326671766765669448)
XLA Ops:
  0.7 9.0 %copy_bitcast_fusion = bf16[12,128,3072]{2,1,0:T(8,128)(2,1)} fusion(bf16[12,24,128,128]{3,2,1,0:T(8,128)(2,1)} %param.14), kind=kLoop, calls=%fused_computation.60 | loop fusion | bytes 18874368 | tf_op jit(solution)/shard_map/reshape | solution.py:45
  15.3 590.7 %while.22 = (s32[]{:T(128)}, bf16[4,128,384]{1,2,0:T(8,128)(2,1)}, bf16[2,12,128,384]{3,2,1,0:T(8,128)(2,1)S(1)}, bf16[2,24,128,384]{3,2,1,0:T(8,128)(2,1)}, bf1...) while((s32[]{:T(128)}, bf16[4,128,384]{1,2,0:T(8,128)(2,1)}, ...), condition=%wide.region_5.6_spmd.clone, body=%wide.region_0.5_spmd.clone.sunk | while | flops 2737965568 | bytes 205470944 | solution.py:109
  41.4 9.0 %all-to-all-done = bf16[8,128,384]{2,1,0:T(8,128)(2,1)} async-done(((bf16[8,128,384]{2,1,0:T(8,128)(2,1)}), bf16[8,128,384]{2,1,0:T(8,128)(2,1)}, u32[]{:S(2)}, u32[]{:S(2)}) %all-to-all-start) | async-done | bytes 786464 | tf_op jit(solution)/shard_map/while/body/eval_jaxpr/all_to_all | solution.py:79
  54.8 17.2 %conditional.6 = (bf16[4,128,384]{1,2,0:T(8,128)(2,1)}) conditional(s32[]{:T(128)} %convert_element_type.93, bf16[4,128,384]{1,2,0:T(8,128)(2,1)} %copy-done.6, (f32[]{:T(128)}, s32[4,24]{1,0:T(4,128)S(1)}, bf16[36,128,384]{2,1,0:T(8,128)(2,1)S(1)}, bf16[4,128,3072]{2,1,0:T(8,128)(2,1)}, bf16[4,128,384]{1,2,0:T(8,128)(2,1)}, ...), branch_computations={%region_1.1_spmd, %region_2.2_spmd} | conditional | flops 1361118464 | bytes 36084024 | solution.py:85
  62.8 7.9 %fusion.6 = bf16[4,128,384]{1,2,0:T(8,128)(2,1)S(1)} fusion(bf16[4,3072,384]{2,1,0:T(8,128)(2,1)} %bitcast.104, bf16[4,128,3072]{2,1,0:T(8,128)(2,1)} %get-tuple-element.336, bf16[4,128,384]{1,2,0:T(8,128)(2,1)} %get-tuple-element.337), kind=kOutput, calls=%fused_computation.9 | convolution fusion | flops 1208942592 | bytes 13369344 | tf_op jit(solution)/shard_map/while/body/eval_jaxpr/cond/branch_1_fun/rim,rmd->rid/dot_general | solution.py:19
  96.0 17.2 %conditional.7 = (bf16[4,128,384]{1,2,0:T(8,128)(2,1)}) conditional(s32[]{:T(128)} %convert_element_type.93, bf16[4,128,384]{1,2,0:T(8,128)(2,1)} %get-tuple-element.638, (f32[]{:T(128)}, s32[4,24]{1,0:T(4,128)S(1)}, bf16[36,128,384]{2,1,0:T(8,128)(2,1)S(1)}, bf16[4,128,3072]{2,1,0:T(8,128)(2,1)}, bf16[4,128,384]{1,2,0:T(8,128)(2,1)}, ...), branch_computations={%region_3.3_spmd, %region_4.4_spmd} | conditional | flops 1361118464 | bytes 36084024 | solution.py:85
  104.0 7.9 %fusion.14 = bf16[4,128,384]{1,2,0:T(8,128)(2,1)S(1)} fusion(bf16[4,3072,384]{2,1,0:T(8,128)(2,1)} %bitcast.105, bf16[4,128,3072]{2,1,0:T(8,128)(2,1)} %get-tuple-element.342, bf16[4,128,384]{1,2,0:T(8,128)(2,1)} %get-tuple-element.343), kind=kOutput, calls=%fused_computation.21 | convolution fusion | flops 1208942592 | bytes 13369344 | tf_op jit(solution)/shard_map/while/body/eval_jaxpr/cond/branch_1_fun/rim,rmd->rid/dot_general | solution.py:19
  154.0 17.1 %conditional.6 = (bf16[4,128,384]{1,2,0:T(8,128)(2,1)}) conditional(s32[]{:T(128)} %convert_element_type.93, bf16[4,128,384]{1,2,0:T(8,128)(2,1)} %copy-done.6, (f32[]{:T(128)}, s32[4,24]{1,0:T(4,128)S(1)}, bf16[36,128,384]{2,1,0:T(8,128)(2,1)S(1)}, bf16[4,128,3072]{2,1,0:T(8,128)(2,1)}, bf16[4,128,384]{1,2,0:T(8,128)(2,1)}, ...), branch_computations={%region_1.1_spmd, %region_2.2_spmd} | conditional | flops 1361118464 | bytes 36084024 | solution.py:85
  162.0 7.9 %fusion.6 = bf16[4,128,384]{1,2,0:T(8,128)(2,1)S(1)} fusion(bf16[4,3072,384]{2,1,0:T(8,128)(2,1)} %bitcast.104, bf16[4,128,3072]{2,1,0:T(8,128)(2,1)} %get-tuple-element.336, bf16[4,128,384]{1,2,0:T(8,128)(2,1)} %get-tuple-element.337), kind=kOutput, calls=%fused_computation.9 | convolution fusion | flops 1208942592 | bytes 13369344 | tf_op jit(solution)/shard_map/while/body/eval_jaxpr/cond/branch_1_fun/rim,rmd->rid/dot_general | solution.py:19
  186.5 8.8 %all-to-all-done.1 = bf16[8,128,384]{2,1,0:T(8,128)(2,1)S(1)} async-done(((bf16[8,128,384]{2,1,0:T(8,128)(2,1)}), bf16[8,128,384]{2,1,0:T(8,128)(2,1)S(1)}, u32[]{:S(2)}, u32[]{:S(2)}) %all-to-all-start.1) | async-done | bytes 786464 | tf_op jit(solution)/shard_map/while/body/eval_jaxpr/all_to_all | solution.py:79
  199.7 17.2 %conditional.7 = (bf16[4,128,384]{1,2,0:T(8,128)(2,1)}) conditional(s32[]{:T(128)} %convert_element_type.93, bf16[4,128,384]{1,2,0:T(8,128)(2,1)} %get-tuple-element.638, (f32[]{:T(128)}, s32[4,24]{1,0:T(4,128)S(1)}, bf16[36,128,384]{2,1,0:T(8,128)(2,1)S(1)}, bf16[4,128,3072]{2,1,0:T(8,128)(2,1)}, bf16[4,128,384]{1,2,0:T(8,128)(2,1)}, ...), branch_computations={%region_3.3_spmd, %region_4.4_spmd} | conditional | flops 1361118464 | bytes 36084024 | solution.py:85
  207.7 7.9 %fusion.14 = bf16[4,128,384]{1,2,0:T(8,128)(2,1)S(1)} fusion(bf16[4,3072,384]{2,1,0:T(8,128)(2,1)} %bitcast.105, bf16[4,128,3072]{2,1,0:T(8,128)(2,1)} %get-tuple-element.342, bf16[4,128,384]{1,2,0:T(8,128)(2,1)} %get-tuple-element.343), kind=kOutput, calls=%fused_computation.21 | convolution fusion | flops 1208942592 | bytes 13369344 | tf_op jit(solution)/shard_map/while/body/eval_jaxpr/cond/branch_1_fun/rim,rmd->rid/dot_general | solution.py:19
  261.9 17.1 %conditional.6 = (bf16[4,128,384]{1,2,0:T(8,128)(2,1)}) conditional(s32[]{:T(128)} %convert_element_type.93, bf16[4,128,384]{1,2,0:T(8,128)(2,1)} %copy-done.6, (f32[]{:T(128)}, s32[4,24]{1,0:T(4,128)S(1)}, bf16[36,128,384]{2,1,0:T(8,128)(2,1)S(1)}, bf16[4,128,3072]{2,1,0:T(8,128)(2,1)}, bf16[4,128,384]{1,2,0:T(8,128)(2,1)}, ...), branch_computations={%region_1.1_spmd, %region_2.2_spmd} | conditional | flops 1361118464 | bytes 36084024 | solution.py:85
  269.9 7.9 %fusion.6 = bf16[4,128,384]{1,2,0:T(8,128)(2,1)S(1)} fusion(bf16[4,3072,384]{2,1,0:T(8,128)(2,1)} %bitcast.104, bf16[4,128,3072]{2,1,0:T(8,128)(2,1)} %get-tuple-element.336, bf16[4,128,384]{1,2,0:T(8,128)(2,1)} %get-tuple-element.337), kind=kOutput, calls=%fused_computation.9 | convolution fusion | flops 1208942592 | bytes 13369344 | tf_op jit(solution)/shard_map/while/body/eval_jaxpr/cond/branch_1_fun/rim,rmd->rid/dot_general | solution.py:19
  294.4 11.2 %all-to-all-done.1 = bf16[8,128,384]{2,1,0:T(8,128)(2,1)S(1)} async-done(((bf16[8,128,384]{2,1,0:T(8,128)(2,1)}), bf16[8,128,384]{2,1,0:T(8,128)(2,1)S(1)}, u32[]{:S(2)}, u32[]{:S(2)}) %all-to-all-start.1) | async-done | bytes 786464 | tf_op jit(solution)/shard_map/while/body/eval_jaxpr/all_to_all | solution.py:79
  310.0 17.1 %conditional.7 = (bf16[4,128,384]{1,2,0:T(8,128)(2,1)}) conditional(s32[]{:T(128)} %convert_element_type.93, bf16[4,128,384]{1,2,0:T(8,128)(2,1)} %get-tuple-element.638, (f32[]{:T(128)}, s32[4,24]{1,0:T(4,128)S(1)}, bf16[36,128,384]{2,1,0:T(8,128)(2,1)S(1)}, bf16[4,128,3072]{2,1,0:T(8,128)(2,1)}, bf16[4,128,384]{1,2,0:T(8,128)(2,1)}, ...), branch_computations={%region_3.3_spmd, %region_4.4_spmd} | conditional | flops 1361118464 | bytes 36084024 | solution.py:85
  317.9 7.9 %fusion.14 = bf16[4,128,384]{1,2,0:T(8,128)(2,1)S(1)} fusion(bf16[4,3072,384]{2,1,0:T(8,128)(2,1)} %bitcast.105, bf16[4,128,3072]{2,1,0:T(8,128)(2,1)} %get-tuple-element.342, bf16[4,128,384]{1,2,0:T(8,128)(2,1)} %get-tuple-element.343), kind=kOutput, calls=%fused_computation.21 | convolution fusion | flops 1208942592 | bytes 13369344 | tf_op jit(solution)/shard_map/while/body/eval_jaxpr/cond/branch_1_fun/rim,rmd->rid/dot_general | solution.py:19
  359.9 9.1 %all-to-all-done = bf16[8,128,384]{2,1,0:T(8,128)(2,1)} async-done(((bf16[8,128,384]{2,1,0:T(8,128)(2,1)}), bf16[8,128,384]{2,1,0:T(8,128)(2,1)}, u32[]{:S(2)}, u32[]{:S(2)}) %all-to-all-start) | async-done | bytes 786464 | tf_op jit(solution)/shard_map/while/body/eval_jaxpr/all_to_all | solution.py:79
  396.7 35.5 %collective-permute-start = (bf16[4,128,384]{1,2,0:T(8,128)(2,1)}, bf16[4,128,384]{1,2,0:T(8,128)(2,1)S(1)}, u32[]{:S(2)}, u32[]{:S(2)}) collective-permute-start(bf16[4,128,384]{1,2,0:T(8,128)(2,1)} %get-tuple-element.639), channel_id=1, source_target_pairs={{0,8},{8,16},{16,24},{1,9},{9,17},{17,25},{2,10},{10,18},{18,26},{... | collective-permute-start | bytes 1179656 | tf_op jit(solution)/shard_map/while/body/eval_jaxpr/ppermute | solution.py:13
  463.5 9.4 %all-to-all-done = bf16[8,128,384]{2,1,0:T(8,128)(2,1)} async-done(((bf16[8,128,384]{2,1,0:T(8,128)(2,1)}), bf16[8,128,384]{2,1,0:T(8,128)(2,1)}, u32[]{:S(2)}, u32[]{:S(2)}) %all-to-all-start) | async-done | bytes 786464 | tf_op jit(solution)/shard_map/while/body/eval_jaxpr/all_to_all | solution.py:79
  491.9 11.4 %all-to-all-done.1 = bf16[8,128,384]{2,1,0:T(8,128)(2,1)S(1)} async-done(((bf16[8,128,384]{2,1,0:T(8,128)(2,1)}), bf16[8,128,384]{2,1,0:T(8,128)(2,1)S(1)}, u32[]{:S(2)}, u32[]{:S(2)}) %all-to-all-start.1) | async-done | bytes 786464 | tf_op jit(solution)/shard_map/while/body/eval_jaxpr/all_to_all | solution.py:79
  561.8 9.1 %all-to-all-done.1 = bf16[8,128,384]{2,1,0:T(8,128)(2,1)S(1)} async-done(((bf16[8,128,384]{2,1,0:T(8,128)(2,1)}), bf16[8,128,384]{2,1,0:T(8,128)(2,1)S(1)}, u32[]{:S(2)}, u32[]{:S(2)}) %all-to-all-start.1) | async-done | bytes 786464 | tf_op jit(solution)/shard_map/while/body/eval_jaxpr/all_to_all | solution.py:79
  575.3 22.5 %collective-permute-start = (bf16[4,128,384]{1,2,0:T(8,128)(2,1)}, bf16[4,128,384]{1,2,0:T(8,128)(2,1)S(1)}, u32[]{:S(2)}, u32[]{:S(2)}) collective-permute-start(bf16[4,128,384]{1,2,0:T(8,128)(2,1)} %get-tuple-element.639), channel_id=1, source_target_pairs={{0,8},{8,16},{16,24},{1,9},{9,17},{17,25},{2,10},{10,18},{18,26},{... | collective-permute-start | bytes 1179656 | tf_op jit(solution)/shard_map/while/body/eval_jaxpr/ppermute | solution.py:13
  608.6 45.0 %all_to_all.42 = bf16[1536,4,96]{0,2,1:T(8,128)(2,1)S(1)} all-to-all(bf16[1536,4,96]{0,2,1:T(8,128)(2,1)S(1)} %all_to_all.30), channel_id=1, replica_groups=mesh['section'=4,'dom'=8] {'section'}, dimensions={1} | all-to-all | bytes 2359296 | tf_op jit(solution)/shard_map/all_to_all | solution.py:111
  (438 shorter events, 424.9 us)
Async XLA Ops:
  22.8 27.6 %all-to-all-start = ((bf16[8,128,384]{2,1,0:T(8,128)(2,1)}), bf16[8,128,384]{2,1,0:T(8,128)(2,1)}, u32[]{:S(2)}, u32[]{:S(2)}) async-start(bf16[8,128,384]{2,1,0:T(8,128)(2,1)} %copy.95), calls=%async_computation | async-start | bytes 1572864 | tf_op jit(solution)/shard_map/while/body/eval_jaxpr/all_to_all | solution.py:79
  74.7 10.8 %copy-start = (bf16[12,128,384]{2,1,0:T(8,128)(2,1)S(1)}, bf16[12,128,384]{2,1,0:T(8,128)(2,1)}, u32[]{:S(2)}) copy-start(bf16[12,128,384]{2,1,0:T(8,128)(2,1)} %get-tuple-element.570) | copy-start | bytes 3538948 | tf_op jit(solution)/shard_map/while
  74.7 16.9 %all-to-all-start.1 = ((bf16[8,128,384]{2,1,0:T(8,128)(2,1)}), bf16[8,128,384]{2,1,0:T(8,128)(2,1)S(1)}, u32[]{:S(2)}, u32[]{:S(2)}) async-start(bf16[8,128,384]{2,1,0:T(8,128)(2,1)} %copy.98), calls=%async_computation.1 | async-start | bytes 1572864 | tf_op jit(solution)/shard_map/while/body/eval_jaxpr/all_to_all | solution.py:79
  113.2 8.9 %collective-permute-start = (bf16[4,128,384]{1,2,0:T(8,128)(2,1)}, bf16[4,128,384]{1,2,0:T(8,128)(2,1)S(1)}, u32[]{:S(2)}, u32[]{:S(2)}) collective-permute-start(bf16[4,128,384]{1,2,0:T(8,128)(2,1)} %get-tuple-element.639), channel_id=1, source_target_pairs={{0,8},{8,16},{16,24},{1,9},{9,17},{17,25},{2,10},{10,18},{18,26},{... | collective-permute-start | bytes 1179656 | tf_op jit(solution)/shard_map/while/body/eval_jaxpr/ppermute | solution.py:13
  130.4 19.2 %all-to-all-start = ((bf16[8,128,384]{2,1,0:T(8,128)(2,1)}), bf16[8,128,384]{2,1,0:T(8,128)(2,1)}, u32[]{:S(2)}, u32[]{:S(2)}) async-start(bf16[8,128,384]{2,1,0:T(8,128)(2,1)} %copy.95), calls=%async_computation | async-start | bytes 1572864 | tf_op jit(solution)/shard_map/while/body/eval_jaxpr/all_to_all | solution.py:79
  173.8 10.8 %copy-start = (bf16[12,128,384]{2,1,0:T(8,128)(2,1)S(1)}, bf16[12,128,384]{2,1,0:T(8,128)(2,1)}, u32[]{:S(2)}) copy-start(bf16[12,128,384]{2,1,0:T(8,128)(2,1)} %get-tuple-element.570) | copy-start | bytes 3538948 | tf_op jit(solution)/shard_map/while
  173.8 21.5 %all-to-all-start.1 = ((bf16[8,128,384]{2,1,0:T(8,128)(2,1)}), bf16[8,128,384]{2,1,0:T(8,128)(2,1)S(1)}, u32[]{:S(2)}, u32[]{:S(2)}) async-start(bf16[8,128,384]{2,1,0:T(8,128)(2,1)} %copy.98), calls=%async_computation.1 | async-start | bytes 1572864 | tf_op jit(solution)/shard_map/while/body/eval_jaxpr/all_to_all | solution.py:79
  216.9 8.9 %collective-permute-start = (bf16[4,128,384]{1,2,0:T(8,128)(2,1)}, bf16[4,128,384]{1,2,0:T(8,128)(2,1)S(1)}, u32[]{:S(2)}, u32[]{:S(2)}) collective-permute-start(bf16[4,128,384]{1,2,0:T(8,128)(2,1)} %get-tuple-element.639), channel_id=1, source_target_pairs={{0,8},{8,16},{16,24},{1,9},{9,17},{17,25},{2,10},{10,18},{18,26},{... | collective-permute-start | bytes 1179656 | tf_op jit(solution)/shard_map/while/body/eval_jaxpr/ppermute | solution.py:13
  234.1 23.4 %all-to-all-start = ((bf16[8,128,384]{2,1,0:T(8,128)(2,1)}), bf16[8,128,384]{2,1,0:T(8,128)(2,1)}, u32[]{:S(2)}, u32[]{:S(2)}) async-start(bf16[8,128,384]{2,1,0:T(8,128)(2,1)} %copy.95), calls=%async_computation | async-start | bytes 1572864 | tf_op jit(solution)/shard_map/while/body/eval_jaxpr/all_to_all | solution.py:79
  281.7 10.8 %copy-start = (bf16[12,128,384]{2,1,0:T(8,128)(2,1)S(1)}, bf16[12,128,384]{2,1,0:T(8,128)(2,1)}, u32[]{:S(2)}) copy-start(bf16[12,128,384]{2,1,0:T(8,128)(2,1)} %get-tuple-element.570) | copy-start | bytes 3538948 | tf_op jit(solution)/shard_map/while
  281.7 23.9 %all-to-all-start.1 = ((bf16[8,128,384]{2,1,0:T(8,128)(2,1)}), bf16[8,128,384]{2,1,0:T(8,128)(2,1)S(1)}, u32[]{:S(2)}, u32[]{:S(2)}) async-start(bf16[8,128,384]{2,1,0:T(8,128)(2,1)} %copy.98), calls=%async_computation.1 | async-start | bytes 1572864 | tf_op jit(solution)/shard_map/while/body/eval_jaxpr/all_to_all | solution.py:79
  327.1 8.9 %collective-permute-start = (bf16[4,128,384]{1,2,0:T(8,128)(2,1)}, bf16[4,128,384]{1,2,0:T(8,128)(2,1)S(1)}, u32[]{:S(2)}, u32[]{:S(2)}) collective-permute-start(bf16[4,128,384]{1,2,0:T(8,128)(2,1)} %get-tuple-element.639), channel_id=1, source_target_pairs={{0,8},{8,16},{16,24},{1,9},{9,17},{17,25},{2,10},{10,18},{18,26},{... | collective-permute-start | bytes 1179656 | tf_op jit(solution)/shard_map/while/body/eval_jaxpr/ppermute | solution.py:13
  344.3 24.7 %all-to-all-start = ((bf16[8,128,384]{2,1,0:T(8,128)(2,1)}), bf16[8,128,384]{2,1,0:T(8,128)(2,1)}, u32[]{:S(2)}, u32[]{:S(2)}) async-start(bf16[8,128,384]{2,1,0:T(8,128)(2,1)} %copy.95), calls=%async_computation | async-start | bytes 1572864 | tf_op jit(solution)/shard_map/while/body/eval_jaxpr/all_to_all | solution.py:79
  375.3 10.8 %copy-start = (bf16[12,128,384]{2,1,0:T(8,128)(2,1)S(1)}, bf16[12,128,384]{2,1,0:T(8,128)(2,1)}, u32[]{:S(2)}) copy-start(bf16[12,128,384]{2,1,0:T(8,128)(2,1)} %get-tuple-element.570) | copy-start | bytes 3538948 | tf_op jit(solution)/shard_map/while
  375.3 16.9 %all-to-all-start.1 = ((bf16[8,128,384]{2,1,0:T(8,128)(2,1)}), bf16[8,128,384]{2,1,0:T(8,128)(2,1)S(1)}, u32[]{:S(2)}, u32[]{:S(2)}) async-start(bf16[8,128,384]{2,1,0:T(8,128)(2,1)} %copy.98), calls=%async_computation.1 | async-start | bytes 1572864 | tf_op jit(solution)/shard_map/while/body/eval_jaxpr/all_to_all | solution.py:79
  396.7 43.0 %collective-permute-start = (bf16[4,128,384]{1,2,0:T(8,128)(2,1)}, bf16[4,128,384]{1,2,0:T(8,128)(2,1)S(1)}, u32[]{:S(2)}, u32[]{:S(2)}) collective-permute-start(bf16[4,128,384]{1,2,0:T(8,128)(2,1)} %get-tuple-element.639), channel_id=1, source_target_pairs={{0,8},{8,16},{16,24},{1,9},{9,17},{17,25},{2,10},{10,18},{18,26},{... | collective-permute-start | bytes 1179656 | tf_op jit(solution)/shard_map/while/body/eval_jaxpr/ppermute | solution.py:13
  447.9 24.9 %all-to-all-start = ((bf16[8,128,384]{2,1,0:T(8,128)(2,1)}), bf16[8,128,384]{2,1,0:T(8,128)(2,1)}, u32[]{:S(2)}, u32[]{:S(2)}) async-start(bf16[8,128,384]{2,1,0:T(8,128)(2,1)} %copy.95), calls=%async_computation | async-start | bytes 1572864 | tf_op jit(solution)/shard_map/while/body/eval_jaxpr/all_to_all | solution.py:79
  479.2 10.9 %copy-start = (bf16[12,128,384]{2,1,0:T(8,128)(2,1)S(1)}, bf16[12,128,384]{2,1,0:T(8,128)(2,1)}, u32[]{:S(2)}) copy-start(bf16[12,128,384]{2,1,0:T(8,128)(2,1)} %get-tuple-element.570) | copy-start | bytes 3538948 | tf_op jit(solution)/shard_map/while
  479.2 24.1 %all-to-all-start.1 = ((bf16[8,128,384]{2,1,0:T(8,128)(2,1)}), bf16[8,128,384]{2,1,0:T(8,128)(2,1)S(1)}, u32[]{:S(2)}, u32[]{:S(2)}) async-start(bf16[8,128,384]{2,1,0:T(8,128)(2,1)} %copy.98), calls=%async_computation.1 | async-start | bytes 1572864 | tf_op jit(solution)/shard_map/while/body/eval_jaxpr/all_to_all | solution.py:79
  507.7 8.8 %collective-permute-start = (bf16[4,128,384]{1,2,0:T(8,128)(2,1)}, bf16[4,128,384]{1,2,0:T(8,128)(2,1)S(1)}, u32[]{:S(2)}, u32[]{:S(2)}) collective-permute-start(bf16[4,128,384]{1,2,0:T(8,128)(2,1)} %get-tuple-element.639), channel_id=1, source_target_pairs={{0,8},{8,16},{16,24},{1,9},{9,17},{17,25},{2,10},{10,18},{18,26},{... | collective-permute-start | bytes 1179656 | tf_op jit(solution)/shard_map/while/body/eval_jaxpr/ppermute | solution.py:13
  524.8 17.5 %all-to-all-start = ((bf16[8,128,384]{2,1,0:T(8,128)(2,1)}), bf16[8,128,384]{2,1,0:T(8,128)(2,1)}, u32[]{:S(2)}, u32[]{:S(2)}) async-start(bf16[8,128,384]{2,1,0:T(8,128)(2,1)} %copy.95), calls=%async_computation | async-start | bytes 1572864 | tf_op jit(solution)/shard_map/while/body/eval_jaxpr/all_to_all | solution.py:79
  548.6 11.2 %copy-start = (bf16[12,128,384]{2,1,0:T(8,128)(2,1)S(1)}, bf16[12,128,384]{2,1,0:T(8,128)(2,1)}, u32[]{:S(2)}) copy-start(bf16[12,128,384]{2,1,0:T(8,128)(2,1)} %get-tuple-element.570) | copy-start | bytes 3538948 | tf_op jit(solution)/shard_map/while
  548.6 22.2 %all-to-all-start.1 = ((bf16[8,128,384]{2,1,0:T(8,128)(2,1)}), bf16[8,128,384]{2,1,0:T(8,128)(2,1)S(1)}, u32[]{:S(2)}, u32[]{:S(2)}) async-start(bf16[8,128,384]{2,1,0:T(8,128)(2,1)} %copy.98), calls=%async_computation.1 | async-start | bytes 1572864 | tf_op jit(solution)/shard_map/while/body/eval_jaxpr/all_to_all | solution.py:79
  575.3 30.0 %collective-permute-start = (bf16[4,128,384]{1,2,0:T(8,128)(2,1)}, bf16[4,128,384]{1,2,0:T(8,128)(2,1)S(1)}, u32[]{:S(2)}, u32[]{:S(2)}) collective-permute-start(bf16[4,128,384]{1,2,0:T(8,128)(2,1)} %get-tuple-element.639), channel_id=1, source_target_pairs={{0,8},{8,16},{16,24},{1,9},{9,17},{17,25},{2,10},{10,18},{18,26},{... | collective-permute-start | bytes 1179656 | tf_op jit(solution)/shard_map/while/body/eval_jaxpr/ppermute | solution.py:13
  (85 other events, 398.7 us)
where the time goes:
time: 658 us; the launch traced here: 654 us
  local copies, waits for them, and re-layouts  234 us (36%)
  starting transfers between devices  114 us (17%)
  other arithmetic  110 us (17%)
  waiting for transfers between devices  89.9 us (14%)
  matrix products  60 us (9%)
  blocking collectives  45 us (7%)
    all_to_all x12, waiting for transfers between devices, turn(): lax.all_to_all(outgoing, 'dom', split_axis=0, concat_axis=0, tiled=True)  89.9 us
    ppermute x6, starting transfers between devices, shifted(): lax.ppermute(value, axis, [(source, source + steps) for source in range(i...  63.3 us
    all_to_all x12, starting transfers between devices, turn(): lax.all_to_all(outgoing, 'dom', split_axis=0, concat_axis=0, tiled=True)  51 us
    dot_general x6, matrix products, gather_rows(): jnp.einsum('rim,rmd->rid', tile_rows, flat, preferred_element_type=jnp.fl...  47.6 us
    gather x6, local copies, waits for them, and re-layouts, gather_rows(): picked = table[columns]  47.2 us
    all_to_all x1, blocking collectives, per_device(): lax.all_to_all(finished, 'section', split_axis=1, concat_axis=0, tiled=True)  45 us
    another operation x12, other arithmetic, turn(): return (inbox, jnp.stack(owned_next), jnp.stack(imported_next), results)  42.3 us
    slice x6, local copies, waits for them, and re-layouts, turn(): stale_table = imported[sublayer]  39.1 us
  transfers between devices with their start and end apart: 18, of which 12 were waited for; matrix products, arithmetic and copies ran while one was open for 25% of the time, Pallas kernels for 0%

commit v1 on v0

v1 whole, which is shorter than its diff:
```python
import functools
import math

import jax
import jax.numpy as jnp
from jax import lax
from jax.experimental import pallas as pl
from jax.experimental.pallas import tpu as pltpu
from jax.sharding import PartitionSpec as P

alpha_mix = 0.1
lambda_decay = 0.5
vmem_bytes = 48 * 1024 * 1024


def group_streams(groups):
    return [list(range(groups))]


def params():
    return pltpu.CompilerParams(vmem_limit_bytes=vmem_bytes)


def whole(shape):
    return pl.BlockSpec(shape, lambda i, *prefetched: (0,) * len(shape))


def pick_outgoing(picks, blocks_ref, outgoing_ref, stream, group_blocks, part_count):
    for local, group in enumerate(stream):

        def pick(dest, carry):
            chosen = jnp.maximum(picks[group * part_count + dest], 0)
            outgoing_ref[dest, local] = blocks_ref[local * group_blocks + chosen]
            return carry

        lax.fori_loop(0, part_count, pick, 0)


def prologue_kernel(streams, group_blocks, part_count, info, picks, rows_ref, *refs):
    own_refs = refs[: len(streams)]
    outgoing_refs = refs[len(streams) : 2 * len(streams)]
    turned = refs[-1]
    block = own_refs[0].shape[2]
    part_width = own_refs[0].shape[1]
    first = pl.multiple_of(info[0] * part_width, part_width)
    for stream, own_ref, outgoing_ref in zip(streams, own_refs, outgoing_refs):
        for local in range(len(stream) * group_blocks):
            row = (stream[0] * group_blocks + local) * block
            turned[local % 2] = rows_ref[row : row + block, :].T
            own_ref[local] = turned[local % 2, pl.ds(first, part_width), :]
        pick_outgoing(picks, own_ref, outgoing_ref, stream, group_blocks, part_count)


def prologue(initial_features, section, picks, streams, group_blocks, block, part_width, part_count):
    rows, width = initial_features.shape
    own_shapes = [(len(s) * group_blocks, part_width, block) for s in streams]
    out_shapes = [(part_count, len(s), part_width, block) for s in streams]
    return pl.pallas_call(
        functools.partial(prologue_kernel, streams, group_blocks, part_count),
        grid_spec=pltpu.PrefetchScalarGridSpec(
            num_scalar_prefetch=2,
            grid=(1,),
            in_specs=[whole((rows, width))],
            out_specs=[whole(s) for s in own_shapes + out_shapes],
            scratch_shapes=[pltpu.VMEM((2, width, block), jnp.bfloat16)],
        ),
        out_shape=[jax.ShapeDtypeStruct(s, jnp.bfloat16) for s in own_shapes + out_shapes],
        compiler_params=params(),
        name="prologue",
    )(section, picks, initial_features)


def turn_kernel(in_ref, out_ref):
    count = in_ref.shape[0]
    parts, part_width = out_ref.shape[0], out_ref.shape[2]
    for item in range(count):
        turned = in_ref[item].T
        for part in range(parts):
            out_ref[part, item] = turned[part * part_width : (part + 1) * part_width, :]


def turn_blocks(blocks, parts):
    count, block, width = blocks.shape
    step = 4 if count % 4 == 0 else 1
    part_width = width // parts
    return pl.pallas_call(
        turn_kernel,
        grid=(count // step,),
        in_specs=[pl.BlockSpec((step, block, width), lambda i: (i, 0, 0))],
        out_specs=pl.BlockSpec((parts, step, part_width, block), lambda i: (0, i, 0, 0)),
        out_shape=jax.ShapeDtypeStruct((parts, count, part_width, block), jnp.bfloat16),
        compiler_params=params(),
        name="turn",
    )(blocks)


def aggregate_kernel(plan, columns, initial_ref, tiles_ref, *refs):
    stream, group_blocks, fanout, sources, layer_slot = plan
    source_refs = refs[: len(sources)]
    mixed_ref, table, tiles, table_sem, tiles_sem = refs[len(sources) :]
    rows = len(stream) * group_blocks
    first_row = stream[0] * group_blocks

    def tile_copy(row):
        return pltpu.make_async_copy(tiles_ref.at[first_row + row], tiles.at[row], tiles_sem.at[row])

    copies = []
    for index, (kind, target, detail) in enumerate(sources):
        ref = source_refs[index]
        if kind == "own":
            source = ref
        elif kind == "import":
            source = ref.at[:, detail]
        else:
            source = ref.at[layer_slot]
        count = source.shape[0]
        copies.append(
            pltpu.make_async_copy(source, table.at[pl.ds(target, count)], table_sem.at[index])
        )
    for copy in copies:
        copy.start()
    for row in range(rows):
        tile_copy(row).start()
    for copy in copies:
        copy.wait()

    def one_row(row, carry):
        tile_copy(row).wait()
        base = (first_row + row) * fanout
        total = None
        for tile in range(0, fanout, 2):
            span = range(tile, min(tile + 2, fanout))
            left = jnp.concatenate([table[columns[base + t]] for t in span], 1)
            right = jnp.concatenate([tiles[row, t] for t in span], 1)
            term = lax.dot_general(
                left, right, (((1,), (1,)), ((), ())), preferred_element_type=jnp.float32
            )
            total = term if total is None else total + term
        mixed_ref[row] = (
            (1.0 - alpha_mix) * total + alpha_mix * initial_ref[row].astype(jnp.float32)
        ).astype(jnp.bfloat16)
        return carry

    lax.fori_loop(0, rows, one_row, 0)


def aggregate(columns, initial_blocks, tiles, own, imports, stale, layer_slot, stream, streams, group_blocks, part_count):
    rows, part_width, block = initial_blocks.shape
    blocks_dev, fanout = tiles.shape[:2]
    groups = blocks_dev // group_blocks
    sources, operands = [], []
    for other, own_blocks, imported in zip(streams, own, imports):
        if other[0] > stream[-1]:
            continue
        sources.append(("own", other[0] * group_blocks, None))
        operands.append(own_blocks)
        for local, group in enumerate(other):
            sources.append(("import", blocks_dev + group * part_count, local))
            operands.append(imported)
    if groups > 1 and stream[0] < groups - 1:
        sources.append(("stale", blocks_dev + groups * part_count, None))
        operands.append(stale)
    table_size = blocks_dev + (2 * groups - 1) * part_count
    plan = (stream, group_blocks, fanout, sources, layer_slot)
    flops = 2 * rows * fanout * block * block * part_width
    return pl.pallas_call(
        functools.partial(aggregate_kernel, plan),
        grid_spec=pltpu.PrefetchScalarGridSpec(
            num_scalar_prefetch=1,
            grid=(1,),
            in_specs=[whole(initial_blocks.shape)]
            + [pl.BlockSpec(memory_space=pl.ANY)] * (1 + len(operands)),
            out_specs=whole((rows, part_width, block)),
            scratch_shapes=[
                pltpu.VMEM((table_size, part_width, block), jnp.bfloat16),
                pltpu.VMEM((rows, fanout, block, block), jnp.bfloat16),
                pltpu.SemaphoreType.DMA((len(sources),)),
                pltpu.SemaphoreType.DMA((rows,)),
            ],
        ),
        out_shape=jax.ShapeDtypeStruct((rows, part_width, block), jnp.bfloat16),
        cost_estimate=pl.CostEstimate(
            flops=flops, bytes_accessed=rows * fanout * block * block * 2, transcendentals=0
        ),
        compiler_params=params(),
        name="aggregate",
    )(columns, initial_blocks, tiles, *operands)


def finish_kernel(plan, picks, mixed_ref, gathered_ref, weight_ref, *refs):
    beta_layer, stream, group_blocks, part_count, last = plan
    rows, part_width, block = mixed_ref.shape
    parts = gathered_ref.shape[0]
    weight = weight_ref[0]
    for row in range(0, rows, 2):
        span = range(row, min(row + 2, rows))
        right = jnp.concatenate(
            [jnp.concatenate([gathered_ref[p, r] for p in range(parts)], 0) for r in span], 1
        )
        product = jnp.dot(weight, right, preferred_element_type=jnp.float32)
        for place, r in enumerate(span):
            value = (1.0 - beta_layer) * mixed_ref[r].astype(jnp.float32) + beta_layer * product[
                :, place * block : (place + 1) * block
            ]
            value = jnp.maximum(value, 0.0).astype(jnp.bfloat16)
            if last:
                refs[0][r * block : (r + 1) * block, :] = value.T
            else:
                refs[0][r] = value
    if not last:
        pick_outgoing(picks, refs[0], refs[1], stream, group_blocks, part_count)


def finish(picks, mixed, gathered, weights, layer, stream, group_blocks, part_count, last):
    rows, part_width, block = mixed.shape
    width = weights.shape[2]
    beta_layer = math.log(lambda_decay / (layer + 1) + 1.0)
    plan = (beta_layer, stream, group_blocks, part_count, last)
    if last:
        shapes = [(rows * block, part_width)]
    else:
        shapes = [(rows, part_width, block), (part_count, len(stream), part_width, block)]
    return pl.pallas_call(
        functools.partial(finish_kernel, plan),
        grid_spec=pltpu.PrefetchScalarGridSpec(
            num_scalar_prefetch=1,
            grid=(1,),
            in_specs=[
                whole(mixed.shape),
                whole(gathered.shape),
                pl.BlockSpec((1, part_width, width), lambda i, *prefetched: (layer, 0, 0)),
            ],
            out_specs=[whole(s) for s in shapes],
        ),
        out_shape=[jax.ShapeDtypeStruct(s, jnp.bfloat16) for s in shapes],
        cost_estimate=pl.CostEstimate(
            flops=2 * rows * block * width * part_width,
            bytes_accessed=rows * block * width * 2,
            transcendentals=0,
        ),
        compiler_params=params(),
        name="finish",
    )(picks, mixed, gathered, weights)


def per_device(
    initial_features, layer_weights, adjacency_tiles, tile_columns, send_blocks, stale_imports
):
    section_count = lax.axis_size("section")
    part_count = lax.axis_size("dom")
    blocks_dev, fanout, block = adjacency_tiles.shape[:3]
    width = initial_features.shape[1]
    part_width = width // section_count
    groups = send_blocks.shape[1]
    group_blocks = blocks_dev // groups
    depth = layer_weights.shape[0]
    layers = depth * section_count
    streams = group_streams(groups)
    section = lax.axis_index("section").astype(jnp.int32).reshape(1)
    picks = send_blocks.reshape(-1)

    row_group = (jnp.arange(blocks_dev, dtype=jnp.int32) // group_blocks)[:, None]
    slot_group = (tile_columns - blocks_dev) // part_count
    is_stale = (tile_columns >= blocks_dev) & (slot_group > row_group)
    columns = jnp.where(
        is_stale, tile_columns + (groups - 1) * part_count, tile_columns
    ).reshape(-1)

    started = prologue(
        initial_features, section, picks, streams, group_blocks, block, part_width, part_count
    )
    own = started[: len(streams)]
    outgoing = started[len(streams) :]
    initial_blocks = own

    def exchange(value):
        return lax.all_to_all(value, "dom", split_axis=0, concat_axis=0, tiled=True)

    imports = [exchange(value) for value in outgoing]
    stale = [
        lax.all_to_all(
            turn_blocks(stale_imports[sub, 0], section_count),
            "section",
            split_axis=0,
            concat_axis=0,
            tiled=True,
        )
        for sub in range(depth)
    ]
    weights = lax.all_to_all(
        layer_weights.transpose(0, 2, 1).reshape(depth, section_count, part_width, width),
        "section",
        split_axis=1,
        concat_axis=0,
        tiled=True,
    ).reshape(layers, part_width, width)

    pieces = []
    for layer in range(layers):
        last = layer == layers - 1
        own_next, imports_next = [], []
        for index, stream in enumerate(streams):
            mixed = aggregate(
                columns,
                initial_blocks[index],
                adjacency_tiles,
                own,
                imports,
                stale[layer % depth],
                layer // depth,
                stream,
                streams,
                group_blocks,
                part_count,
            )
            gathered = lax.all_gather(mixed, "section", axis=0, tiled=False)
            result = finish(
                picks, mixed, gathered, weights, layer, stream, group_blocks, part_count, last
            )
            if last:
                pieces.append(result[0])
            else:
                own_next.append(result[0])
                imports_next.append(exchange(result[1]))
        own, imports = own_next, imports_next
    return jnp.concatenate(pieces, 0) if len(pieces) > 1 else pieces[0]


def solution(mesh):
    return jax.shard_map(
        per_device,
        mesh=mesh,
        in_specs=(
            P("dom", None),
            P("section", None, None),
            P("dom", None, None, None),
            P("dom", None),
            P("dom", None, None),
            P("section", "dom", None, None, None),
        ),
        out_specs=P("dom", "section"),
        check_vma=False,
    )
```

time: 658 us -> 463 us (0.70)
  local copies, waits for them, and re-layouts: 234 us -> 21 us
  other arithmetic: 110 us -> 0.78 us
  blocking collectives: 45 us -> 152 us
  starting transfers between devices: 114 us -> 19 us
  Pallas kernels: 0 us -> 89.7 us
  waiting for transfers between devices: 89.9 us -> 165 us
  matrix products: 60 us -> 0 us
  between operations: 0.2 us -> 13.8 us
    all_to_all x1 -> x7, blocking collectives: 45 us -> 152 us  [exchange(): return lax.all_to_all(value, 'dom', split_axis=0, concat_axis=0, tiled=True)]
    all_gather x0 -> x8, waiting for transfers between devices: none -> 105 us  [per_device(): gathered = lax.all_gather(mixed, 'section', axis=0, tiled=False)]
    pallas_call x0 -> x19, Pallas kernels: none -> 89.7 us  [the longest x8 69.7 us: aggregate(): pl.pallas_call(functools.partial(aggregate_kernel, plan), grid_spec=pltpu...]
    dynamic_slice x48 -> x0, local copies, waits for them, and re-layouts: 72.5 us -> none  [the longest x18 25.5 us: turn(): kept_rows = lax.dynamic_slice_in_dim(own_table, first_row, group_blocks, 0)]
    ppermute x6 -> x0, starting transfers between devices: 63.3 us -> none  [shifted(): lax.ppermute(value, axis, [(source, source + steps) for source in range(i...]
    dot_general x24 -> x0, matrix products: 60 us -> none  [the longest x6 47.6 us: gather_rows(): jnp.einsum('rim,rmd->rid', tile_rows, flat, preferred_element_type=jnp.fl...]
    slice x13 -> x0, local copies, waits for them, and re-layouts: 52.7 us -> none  [the longest x6 39.1 us: turn(): stale_table = imported[sublayer]]
    gather x6 -> x0, local copies, waits for them, and re-layouts: 47.2 us -> none  [gather_rows(): picked = table[columns]]
  transfers between devices with their start and end apart: 18 -> 12, of which waited for: 12 -> 11; matrix products, arithmetic and copies ran while one was open for 25% -> 1% of each run, Pallas kernels for 0% -> 1%
where the time goes in v1:
time: 463 us; the launch traced here: 462 us
  waiting for transfers between devices  165 us (36%)
  blocking collectives  152 us (33%)
  Pallas kernels  89.7 us (19%)
  local copies, waits for them, and re-layouts  21 us (5%)
  starting transfers between devices  19 us (4%)
  between operations  13.8 us (3%)
    all_to_all x7, blocking collectives, exchange(): return lax.all_to_all(value, 'dom', split_axis=0, concat_axis=0, tiled=True)  152 us
    all_gather x8, waiting for transfers between devices, per_device(): gathered = lax.all_gather(mixed, 'section', axis=0, tiled=False)  105 us
    pallas_call x8, Pallas kernels, aggregate(): pl.pallas_call(functools.partial(aggregate_kernel, plan), grid_spec=pltpu...  69.7 us
    all_to_all x2, waiting for transfers between devices, per_device(): lax.all_to_all(turn_blocks(stale_imports[sub, 0], section_count), 'sectio...  36.5 us
    pallas_call x8, Pallas kernels, finish(): pl.pallas_call(functools.partial(finish_kernel, plan), grid_spec=pltpu.Pr...  16.5 us
    unnamed x29, local copies, waits for them, and re-layouts  15.4 us
    all_to_all x1, waiting for transfers between devices, per_device(): lax.all_to_all(layer_weights.transpose(0, 2, 1).reshape(depth, section_co...  12.5 us
    all_to_all x1, waiting for transfers between devices, exchange(): return lax.all_to_all(value, 'dom', split_axis=0, concat_axis=0, tiled=True)  10.4 us
  transfers between devices with their start and end apart: 12, of which 11 were waited for; matrix products, arithmetic and copies ran while one was open for 1% of the time, Pallas kernels for 1%

profile of v1, /device:TPU:0, one launch (start us, length us, event | category | flops | bytes accessed | tf_op | source)
XLA Modules:
  0.0 461.8 jit_solution(2286170546603262726)
XLA Ops:
  23.3 10.4 %all-to-all-done.refs_1_.refs_2_.refs_3_ = bf16[8,3,96,128]{3,2,1,0:T(8,128)(2,1)S(1)} async-done(((bf16[8,3,96,128]{3,2,1,0:T(8,128)(2,1)}), bf16[8,3,96,128]{3,2,1,0:T(8,128)(2,1)S(1)}, u32[]{:S(2)}, u32[]{:S(2)}) %all-to-all-start) | async-done | bytes 589856 | tf_op jit(solution)/shard_map/all_to_all | solution.py:277
  37.5 19.8 %all-to-all-done.1.refs_4_ = bf16[4,16,96,128]{3,2,1,0:T(8,128)(2,1)S(1)} async-done(((bf16[4,16,96,128]{3,2,1,0:T(8,128)(2,1)}), bf16[4,16,96,128]{3,2,1,0:T(8,128)(2,1)S(1)}, u32[]{:S(2)}, u32[]{:S(2)}) %all-to-all-start.1) | async-done | bytes 1572896 | tf_op jit(solution)/shard_map/all_to_all | solution.py:281
  57.3 7.6 %aggregate.8.mixed_ref = bf16[12,96,128]{2,1,0:T(8,128)(2,1)} custom-call(s32[288]{0:T(512)S(1)} %reshape.30.columns, bf16[12,96,128]{2,1,0:T(8,128)(2,1)S(1)} %get-tuple-element.21.initial_ref.refs_0_, bf16[12,24,128,128]{3,2,1,0:T(8,128)(2,1)} %tiles_ref.15, bf16[12,96,128]{2,1,0:T(8,128)(2,1)S(1)} %get-tuple-element.21.initial_ref.refs_0_, ...), custom_call_target="tpu_custom_call" | custom-call | flops 905969664 | bytes 9437184 | tf_op jit(solution)/shard_map/aggregate/pallas_call | solution.py:166
  73.0 12.5 %all-to-all-done.2 = bf16[2,4,96,384]{3,2,0,1:T(8,128)(2,1)S(1)} async-done(((bf16[2,4,96,384]{3,2,0,1:T(8,128)(2,1)}), bf16[2,4,96,384]{3,2,0,1:T(8,128)(2,1)S(1)}, u32[]{:S(2)}, u32[]{:S(2)}) %all-to-all-start.2) | async-done | bytes 589856 | tf_op jit(solution)/shard_map/all_to_all | solution.py:290
  93.3 16.7 %all-to-all-done.4.refs_4_ = bf16[4,16,96,128]{3,2,1,0:T(8,128)(2,1)} async-done(((bf16[4,16,96,128]{3,2,1,0:T(8,128)(2,1)}), bf16[4,16,96,128]{3,2,1,0:T(8,128)(2,1)}, u32[]{:S(2)}, u32[]{:S(2)}) %all-to-all-start.4) | async-done | bytes 1572896 | tf_op jit(solution)/shard_map/all_to_all | solution.py:281
  110.0 19.0 %all_to_all.65.refs_1_.refs_2_.refs_3_ = bf16[8,3,96,128]{3,2,1,0:T(8,128)(2,1)S(1)} all-to-all(bf16[8,3,96,128]{3,2,1,0:T(8,128)(2,1)S(1)} %get-tuple-element.24), channel_id=1, replica_groups=mesh['section'=4,'dom'=8] {'dom'}, dimensions={0} | all-to-all | bytes 1179648 | tf_op jit(solution)/shard_map/all_to_all | solution.py:277
  129.1 9.8 %aggregate.9.mixed_ref = bf16[12,96,128]{2,1,0:T(8,128)(2,1)} custom-call(s32[288]{0:T(512)S(1)} %reshape.30.columns, bf16[12,96,128]{2,1,0:T(8,128)(2,1)S(1)} %get-tuple-element.21.initial_ref.refs_0_, bf16[12,24,128,128]{3,2,1,0:T(8,128)(2,1)} %tiles_ref.15, bf16[12,96,128]{2,1,0:T(8,128)(2,1)S(1)} %get-tuple-element.23.refs_0_, ...), custom_call_target="tpu_custom_call" | custom-call | flops 905969664 | bytes 9437184 | tf_op jit(solution)/shard_map/aggregate/pallas_call | solution.py:166
  139.0 15.1 %all-gather.19.cloned.1.call-done = bf16[48,96,128]{2,1,0:T(8,128)(2,1)} async-done(((bf16[12,96,128]{2,1,0:T(8,128)(2,1)}), bf16[48,96,128]{2,1,0:T(8,128)(2,1)}) %all-gather.19.cloned.1.call-update) | async-done | bytes 1179664 | tf_op jit(solution)/shard_map/all_gather | solution.py:316
  157.4 22.2 %all_to_all.66.refs_1_.refs_2_.refs_3_ = bf16[8,3,96,128]{3,2,1,0:T(8,128)(2,1)S(1)} all-to-all(bf16[8,3,96,128]{3,2,1,0:T(8,128)(2,1)S(1)} %get-tuple-element.26), channel_id=1, replica_groups=mesh['section'=4,'dom'=8] {'dom'}, dimensions={0} | all-to-all | bytes 1179648 | tf_op jit(solution)/shard_map/all_to_all | solution.py:277
  187.3 15.1 %all-gather.21.cloned.1.call-done = bf16[48,96,128]{2,1,0:T(8,128)(2,1)} async-done(((bf16[12,96,128]{2,1,0:T(8,128)(2,1)}), bf16[48,96,128]{2,1,0:T(8,128)(2,1)}) %all-gather.21.cloned.1.call-update) | async-done | bytes 1179664 | tf_op jit(solution)/shard_map/all_gather | solution.py:316
  205.7 22.2 %all_to_all.67.refs_1_.refs_2_.refs_3_ = bf16[8,3,96,128]{3,2,1,0:T(8,128)(2,1)S(1)} all-to-all(bf16[8,3,96,128]{3,2,1,0:T(8,128)(2,1)S(1)} %get-tuple-element.28), channel_id=1, replica_groups=mesh['section'=4,'dom'=8] {'dom'}, dimensions={0} | all-to-all | bytes 1179648 | tf_op jit(solution)/shard_map/all_to_all | solution.py:277
  228.0 9.8 %aggregate.11.mixed_ref = bf16[12,96,128]{2,1,0:T(8,128)(2,1)} custom-call(s32[288]{0:T(512)S(1)} %reshape.30.columns, bf16[12,96,128]{2,1,0:T(8,128)(2,1)S(1)} %get-tuple-element.21.initial_ref.refs_0_, bf16[12,24,128,128]{3,2,1,0:T(8,128)(2,1)} %tiles_ref.15, bf16[12,96,128]{2,1,0:T(8,128)(2,1)S(1)} %get-tuple-element.27.refs_0_, ...), custom_call_target="tpu_custom_call" | custom-call | flops 905969664 | bytes 9437184 | tf_op jit(solution)/shard_map/aggregate/pallas_call | solution.py:166
  237.9 15.1 %all-gather.23.cloned.1.call-done = bf16[48,96,128]{2,1,0:T(8,128)(2,1)} async-done(((bf16[12,96,128]{2,1,0:T(8,128)(2,1)}), bf16[48,96,128]{2,1,0:T(8,128)(2,1)}) %all-gather.23.cloned.1.call-update) | async-done | bytes 1179664 | tf_op jit(solution)/shard_map/all_gather | solution.py:316
  256.3 22.2 %all_to_all.68.refs_1_.refs_2_.refs_3_ = bf16[8,3,96,128]{3,2,1,0:T(8,128)(2,1)S(1)} all-to-all(bf16[8,3,96,128]{3,2,1,0:T(8,128)(2,1)S(1)} %get-tuple-element.30), channel_id=1, replica_groups=mesh['section'=4,'dom'=8] {'dom'}, dimensions={0} | all-to-all | bytes 1179648 | tf_op jit(solution)/shard_map/all_to_all | solution.py:277
  278.6 7.6 %aggregate.12.mixed_ref = bf16[12,96,128]{2,1,0:T(8,128)(2,1)} custom-call(s32[288]{0:T(512)S(1)} %reshape.30.columns, bf16[12,96,128]{2,1,0:T(8,128)(2,1)S(1)} %get-tuple-element.21.initial_ref.refs_0_, bf16[12,24,128,128]{3,2,1,0:T(8,128)(2,1)} %tiles_ref.15, bf16[12,96,128]{2,1,0:T(8,128)(2,1)S(1)} %get-tuple-element.29.refs_0_, ...), custom_call_target="tpu_custom_call" | custom-call | flops 905969664 | bytes 9437184 | tf_op jit(solution)/shard_map/aggregate/pallas_call | solution.py:166
  286.3 15.1 %all-gather.25.cloned.1.call-done = bf16[48,96,128]{2,1,0:T(8,128)(2,1)} async-done(((bf16[12,96,128]{2,1,0:T(8,128)(2,1)}), bf16[48,96,128]{2,1,0:T(8,128)(2,1)}) %all-gather.25.cloned.1.call-update) | async-done | bytes 1179664 | tf_op jit(solution)/shard_map/all_gather | solution.py:316
  304.7 22.2 %all_to_all.69.refs_1_.refs_2_.refs_3_ = bf16[8,3,96,128]{3,2,1,0:T(8,128)(2,1)S(1)} all-to-all(bf16[8,3,96,128]{3,2,1,0:T(8,128)(2,1)S(1)} %get-tuple-element.32), channel_id=1, replica_groups=mesh['section'=4,'dom'=8] {'dom'}, dimensions={0} | all-to-all | bytes 1179648 | tf_op jit(solution)/shard_map/all_to_all | solution.py:277
  326.9 9.8 %aggregate.13.mixed_ref = bf16[12,96,128]{2,1,0:T(8,128)(2,1)} custom-call(s32[288]{0:T(512)S(1)} %reshape.30.columns, bf16[12,96,128]{2,1,0:T(8,128)(2,1)S(1)} %get-tuple-element.21.initial_ref.refs_0_, bf16[12,24,128,128]{3,2,1,0:T(8,128)(2,1)} %tiles_ref.15, bf16[12,96,128]{2,1,0:T(8,128)(2,1)S(1)} %get-tuple-element.31.refs_0_, ...), custom_call_target="tpu_custom_call" | custom-call | flops 905969664 | bytes 9437184 | tf_op jit(solution)/shard_map/aggregate/pallas_call | solution.py:166
  336.8 15.1 %all-gather.27.cloned.1.call-done = bf16[48,96,128]{2,1,0:T(8,128)(2,1)} async-done(((bf16[12,96,128]{2,1,0:T(8,128)(2,1)}), bf16[48,96,128]{2,1,0:T(8,128)(2,1)}) %all-gather.27.cloned.1.call-update) | async-done | bytes 1179664 | tf_op jit(solution)/shard_map/all_gather | solution.py:316
  355.2 22.2 %all_to_all.70.refs_1_.refs_2_.refs_3_ = bf16[8,3,96,128]{3,2,1,0:T(8,128)(2,1)S(1)} all-to-all(bf16[8,3,96,128]{3,2,1,0:T(8,128)(2,1)S(1)} %get-tuple-element.34), channel_id=1, replica_groups=mesh['section'=4,'dom'=8] {'dom'}, dimensions={0} | all-to-all | bytes 1179648 | tf_op jit(solution)/shard_map/all_to_all | solution.py:277
  385.2 15.1 %all-gather.29.cloned.1.call-done = bf16[48,96,128]{2,1,0:T(8,128)(2,1)} async-done(((bf16[12,96,128]{2,1,0:T(8,128)(2,1)}), bf16[48,96,128]{2,1,0:T(8,128)(2,1)}) %all-gather.29.cloned.1.call-update) | async-done | bytes 1179664 | tf_op jit(solution)/shard_map/all_gather | solution.py:316
  403.6 22.2 %all_to_all.71.refs_1_.refs_2_.refs_3_ = bf16[8,3,96,128]{3,2,1,0:T(8,128)(2,1)S(1)} all-to-all(bf16[8,3,96,128]{3,2,1,0:T(8,128)(2,1)S(1)} %get-tuple-element.36), channel_id=1, replica_groups=mesh['section'=4,'dom'=8] {'dom'}, dimensions={0} | all-to-all | bytes 1179648 | tf_op jit(solution)/shard_map/all_to_all | solution.py:277
  425.8 9.8 %aggregate.15.mixed_ref = bf16[12,96,128]{2,1,0:T(8,128)(2,1)} custom-call(s32[288]{0:T(512)S(1)} %reshape.30.columns, bf16[12,96,128]{2,1,0:T(8,128)(2,1)S(1)} %get-tuple-element.21.initial_ref.refs_0_, bf16[12,24,128,128]{3,2,1,0:T(8,128)(2,1)} %tiles_ref.15, bf16[12,96,128]{2,1,0:T(8,128)(2,1)S(1)} %get-tuple-element.35.refs_0_, ...), custom_call_target="tpu_custom_call" | custom-call | flops 905969664 | bytes 9437184 | tf_op jit(solution)/shard_map/aggregate/pallas_call | solution.py:166
  435.7 15.1 %all-gather.31.cloned.1.call-done = bf16[48,96,128]{2,1,0:T(8,128)(2,1)} async-done(((bf16[12,96,128]{2,1,0:T(8,128)(2,1)}), bf16[48,96,128]{2,1,0:T(8,128)(2,1)}) %all-gather.31.cloned.1.call-update) | async-done | bytes 1179664 | tf_op jit(solution)/shard_map/all_gather | solution.py:316
  (71 shorter events, 76.1 us)
Async XLA Ops:
  7.3 1.3 copy-start.10
  10.5 23.2 %all-to-all-start = ((bf16[8,3,96,128]{3,2,1,0:T(8,128)(2,1)}), bf16[8,3,96,128]{3,2,1,0:T(8,128)(2,1)S(1)}, u32[]{:S(2)}, u32[]{:S(2)}) async-start(bf16[8,3,96,128]{3,2,1,0:T(8,128)(2,1)} %get-tuple-element.22), calls=%async_computation | async-start | bytes 1179648 | tf_op jit(solution)/shard_map/all_to_all | solution.py:277
  23.3 14.1 %copy-start.13 = (s32[12,24]{1,0:T(8,128)S(1)}, s32[12,24]{1,0:T(8,128)}, u32[]{:S(2)}) copy-start(s32[12,24]{1,0:T(8,128)} %param.9) | copy-start | bytes 3460
  33.7 23.6 %all-to-all-start.1 = ((bf16[4,16,96,128]{3,2,1,0:T(8,128)(2,1)}), bf16[4,16,96,128]{3,2,1,0:T(8,128)(2,1)S(1)}, u32[]{:S(2)}, u32[]{:S(2)}) async-start(bf16[4,16,96,128]{3,2,1,0:T(8,128)(2,1)} %copy-done.1), calls=%async_computation.1 | async-start | bytes 3145728 | tf_op jit(solution)/shard_map/all_to_all | solution.py:281
  37.3 52.7 %all-gather.17.cloned.1.call-start = ((), (), s32[]{:S(2)}) async-start(), calls=%async_computation.11 | async-start | bytes 1474560 | tf_op jit(solution)/shard_map/all_gather | solution.py:316
  57.3 7.6 %copy-start.12 = (bf16[2,384,384]{2,1,0:T(8,128)(2,1)S(1)}, bf16[2,384,384]{2,1,0:T(8,128)(2,1)}, u32[]{:S(2)}) copy-start(bf16[2,384,384]{2,1,0:T(8,128)(2,1)} %param.7) | copy-start | bytes 1769476
  66.2 19.3 %all-to-all-start.2 = ((bf16[2,4,96,384]{3,2,0,1:T(8,128)(2,1)}), bf16[2,4,96,384]{3,2,0,1:T(8,128)(2,1)S(1)}, u32[]{:S(2)}, u32[]{:S(2)}) async-start(bf16[2,4,96,384]{3,2,0,1:T(8,128)(2,1)} %copy.13), calls=%async_computation.2 | async-start | bytes 1179648 | tf_op jit(solution)/shard_map/all_to_all | solution.py:290
  69.7 1.4 copy-start.2
  85.5 24.5 %all-to-all-start.4 = ((bf16[4,16,96,128]{3,2,1,0:T(8,128)(2,1)}), bf16[4,16,96,128]{3,2,1,0:T(8,128)(2,1)}, u32[]{:S(2)}, u32[]{:S(2)}) async-start(bf16[4,16,96,128]{3,2,1,0:T(8,128)(2,1)} %copy-done), calls=%async_computation.4 | async-start | bytes 3145728 | tf_op jit(solution)/shard_map/all_to_all | solution.py:281
  89.9 64.1 %all-gather.19.cloned.1.call-start = ((), (), s32[]{:S(2)}) async-start(), calls=%async_computation.12 | async-start | bytes 1474560 | tf_op jit(solution)/shard_map/all_gather | solution.py:316
  90.0 1.3 copy-start.3
  138.9 63.5 %all-gather.21.cloned.1.call-start = ((), (), s32[]{:S(2)}) async-start(), calls=%async_computation.13 | async-start | bytes 1474560 | tf_op jit(solution)/shard_map/all_gather | solution.py:316
  154.0 1.3 copy-start.4
  187.3 65.7 %all-gather.23.cloned.1.call-start = ((), (), s32[]{:S(2)}) async-start(), calls=%async_computation.14 | async-start | bytes 1474560 | tf_op jit(solution)/shard_map/all_gather | solution.py:316
  202.4 1.3 copy-start.5
  237.8 63.5 %all-gather.25.cloned.1.call-start = ((), (), s32[]{:S(2)}) async-start(), calls=%async_computation.15 | async-start | bytes 1474560 | tf_op jit(solution)/shard_map/all_gather | solution.py:316
  253.0 1.3 copy-start.6
  286.2 65.7 %all-gather.27.cloned.1.call-start = ((), (), s32[]{:S(2)}) async-start(), calls=%async_computation.16 | async-start | bytes 1474560 | tf_op jit(solution)/shard_map/all_gather | solution.py:316
  301.3 1.3 copy-start.7
  336.8 63.5 %all-gather.29.cloned.1.call-start = ((), (), s32[]{:S(2)}) async-start(), calls=%async_computation.17 | async-start | bytes 1474560 | tf_op jit(solution)/shard_map/all_gather | solution.py:316
  351.9 1.3 copy-start.8
  385.1 65.7 %all-gather.31.cloned.1.call-start = ((), (), s32[]{:S(2)}) async-start(), calls=%async_computation.18 | async-start | bytes 1474560 | tf_op jit(solution)/shard_map/all_gather | solution.py:316
  400.2 1.3 copy-start.9
  450.8 1.3 copy-start.11
  (2 other events, 2.3 us)
Sparse Core Ops, SparseCore 0:
  65.1 21.8 all-gather.16
  139.0 14.9 all-gather.18
  187.4 14.9 all-gather.20
  238.0 14.9 all-gather.22
  286.3 14.9 all-gather.24
  336.9 14.9 all-gather.26
  385.2 14.9 all-gather.28
  435.8 14.9 all-gather.30

commit v2 on v1

--- a/solution.py
+++ b/solution.py
@@ -14,7 +14,7 @@
 
 
 def group_streams(groups):
-    return [list(range(groups))]
+    return [[group] for group in range(groups)]
 
 
 def params():
@@ -189,13 +189,24 @@
 
 def finish_kernel(plan, picks, mixed_ref, gathered_ref, weight_ref, *refs):
     beta_layer, stream, group_blocks, part_count, last = plan
+    *refs, held, held_sem = refs
     rows, part_width, block = mixed_ref.shape
     parts = gathered_ref.shape[0]
+    spans = [(row, min(row + 2, rows)) for row in range(0, rows, 2)]
+    copies = [
+        pltpu.make_async_copy(
+            gathered_ref.at[:, low:high], held.at[:, low:high], held_sem.at[index]
+        )
+        for index, (low, high) in enumerate(spans)
+    ]
+    for copy in copies:
+        copy.start()
     weight = weight_ref[0]
-    for row in range(0, rows, 2):
-        span = range(row, min(row + 2, rows))
+    for copy, (low, high) in zip(copies, spans):
+        copy.wait()
+        span = range(low, high)
         right = jnp.concatenate(
-            [jnp.concatenate([gathered_ref[p, r] for p in range(parts)], 0) for r in span], 1
+            [jnp.concatenate([held[p, r] for p in range(parts)], 0) for r in span], 1
         )
         product = jnp.dot(weight, right, preferred_element_type=jnp.float32)
         for place, r in enumerate(span):
@@ -227,10 +238,14 @@
             grid=(1,),
             in_specs=[
                 whole(mixed.shape),
-                whole(gathered.shape),
+                pl.BlockSpec(memory_space=pl.ANY),
                 pl.BlockSpec((1, part_width, width), lambda i, *prefetched: (layer, 0, 0)),
             ],
             out_specs=[whole(s) for s in shapes],
+            scratch_shapes=[
+                pltpu.VMEM(gathered.shape, jnp.bfloat16),
+                pltpu.SemaphoreType.DMA(((rows + 1) // 2,)),
+            ],
         ),
         out_shape=[jax.ShapeDtypeStruct(s, jnp.bfloat16) for s in shapes],
         cost_estimate=pl.CostEstimate(

time: 463 us -> 543 us (1.17)
  waiting for transfers between devices: 165 us -> 26.5 us
  starting transfers between devices: 19 us -> 132 us
  Pallas kernels: 89.7 us -> 139 us
  blocking collectives: 152 us -> 191 us
  local copies, waits for them, and re-layouts: 21 us -> 48.5 us
  between operations: 13.8 us -> 1.01 us
    all_gather x0 -> x24, blocking collectives: none -> 166 us  [per_device(): gathered = lax.all_gather(mixed, 'section', axis=0, tiled=False)]
    all_to_all x7 -> x2, blocking collectives: 152 us -> 25.7 us  [exchange(): return lax.all_to_all(value, 'dom', split_axis=0, concat_axis=0, tiled=True)]
    all_to_all x1 -> x22, starting transfers between devices: 7.28 us -> 121 us  [exchange(): return lax.all_to_all(value, 'dom', split_axis=0, concat_axis=0, tiled=True)]
    all_gather x8 -> x0, waiting for transfers between devices: 105 us -> none  [per_device(): gathered = lax.all_gather(mixed, 'section', axis=0, tiled=False)]
    pallas_call x8 -> x24, Pallas kernels: 69.7 us -> 101 us  [aggregate(): pl.pallas_call(functools.partial(aggregate_kernel, plan), grid_spec=pltpu...]
    unnamed x29 -> x127, local copies, waits for them, and re-layouts: 15.4 us -> 43 us
    all_to_all x2, waiting for transfers between devices: 36.5 us -> 16.7 us  [per_device(): lax.all_to_all(turn_blocks(stale_imports[sub, 0], section_count), 'sectio...]
    pallas_call x8 -> x24, Pallas kernels: 16.5 us -> 34.8 us  [finish(): pl.pallas_call(functools.partial(finish_kernel, plan), grid_spec=pltpu.Pr...]
  transfers between devices with their start and end apart: 12 -> 25, of which waited for: 11 -> 3; matrix products, arithmetic and copies ran while one was open for 1% -> 1% of each run, Pallas kernels for 1% -> 24%
where the time goes in v2:
time: 543 us; the launch traced here: 540 us
  blocking collectives  191 us (35%)
  Pallas kernels  139 us (26%)
  starting transfers between devices  132 us (24%)
  local copies, waits for them, and re-layouts  48.5 us (9%)
  waiting for transfers between devices  26.5 us (5%)
    all_gather x24, blocking collectives, per_device(): gathered = lax.all_gather(mixed, 'section', axis=0, tiled=False)  166 us
    all_to_all x22, starting transfers between devices, exchange(): return lax.all_to_all(value, 'dom', split_axis=0, concat_axis=0, tiled=True)  121 us
    pallas_call x24, Pallas kernels, aggregate(): pl.pallas_call(functools.partial(aggregate_kernel, plan), grid_spec=pltpu...  101 us
    unnamed x127, local copies, waits for them, and re-layouts  43 us
    pallas_call x24, Pallas kernels, finish(): pl.pallas_call(functools.partial(finish_kernel, plan), grid_spec=pltpu.Pr...  34.8 us
    all_to_all x2, blocking collectives, exchange(): return lax.all_to_all(value, 'dom', split_axis=0, concat_axis=0, tiled=True)  25.7 us
    all_to_all x2, waiting for transfers between devices, per_device(): lax.all_to_all(turn_blocks(stale_imports[sub, 0], section_count), 'sectio...  16.7 us
  transfers between devices with their start and end apart: 25, of which 3 were waited for; matrix products, arithmetic and copies ran while one was open for 1% of the time, Pallas kernels for 24%

profile of v2, /device:TPU:0, one launch (start us, length us, event | category | flops | bytes accessed | tf_op | source)
XLA Modules:
  0.0 539.6 jit_solution(11619552841470167675)
XLA Ops:
  4.0 15.0 %all_to_all.145.refs_1_ = bf16[8,1,96,128]{3,2,1,0:T(8,128)(2,1)S(1)} all-to-all(bf16[8,1,96,128]{3,2,1,0:T(8,128)(2,1)S(1)} %get-tuple-element.54), channel_id=1, replica_groups=mesh['section'=4,'dom'=8] {'dom'}, dimensions={0} | all-to-all | bytes 393216 | tf_op jit(solution)/shard_map/all_to_all | solution.py:292
  19.0 10.7 %all_to_all.146.refs_3_ = bf16[8,1,96,128]{3,2,1,0:T(8,128)(2,1)S(1)} all-to-all(bf16[8,1,96,128]{3,2,1,0:T(8,128)(2,1)S(1)} %get-tuple-element.70), channel_id=1, replica_groups=mesh['section'=4,'dom'=8] {'dom'}, dimensions={0} | all-to-all | bytes 393216 | tf_op jit(solution)/shard_map/all_to_all | solution.py:292
  34.3 6.5 %all-to-all-done.19.refs_5_ = bf16[8,1,96,128]{3,2,1,0:T(8,128)(2,1)S(1)} async-done(((bf16[8,1,96,128]{3,2,1,0:T(8,128)(2,1)}), bf16[8,1,96,128]{3,2,1,0:T(8,128)(2,1)S(1)}, u32[]{:S(2)}, u32[]{:S(2)}) %all-to-all-start.19) | async-done | bytes 196640 | tf_op jit(solution)/shard_map/all_to_all | solution.py:292
  49.0 7.8 %all-gather.16 = bf16[16,96,128]{2,1,0:T(8,128)(2,1)S(1)} all-gather(bf16[4,96,128]{2,1,0:T(8,128)(2,1)S(1)} %aggregate.40.mixed_ref), channel_id=18, replica_groups=mesh['section'=4,'dom'=8] {'section'}, dimensions={0}, use_global_device_ids=true | all-gather | bytes 491520 | tf_op jit(solution)/shard_map/all_gather | solution.py:331
  78.9 16.7 %all-to-all-done.1.refs_2_.refs_4_ = bf16[4,16,96,128]{3,2,1,0:T(8,128)(2,1)S(1)} async-done(((bf16[4,16,96,128]{3,2,1,0:T(8,128)(2,1)}), bf16[4,16,96,128]{3,2,1,0:T(8,128)(2,1)S(1)}, u32[]{:S(2)}, u32[]{:S(2)}) %all-to-all-start.1) | async-done | bytes 1572896 | tf_op jit(solution)/shard_map/all_to_all | solution.py:296
  105.7 17.7 %all-gather = bf16[16,96,128]{2,1,0:T(8,128)(2,1)S(1)} all-gather(bf16[4,96,128]{2,1,0:T(8,128)(2,1)S(1)} %aggregate.24.mixed_ref), channel_id=2, replica_groups=mesh['section'=4,'dom'=8] {'section'}, dimensions={0}, use_global_device_ids=true | all-gather | bytes 491520 | tf_op jit(solution)/shard_map/all_gather | solution.py:331
  134.4 6.6 %all-gather.8 = bf16[16,96,128]{2,1,0:T(8,128)(2,1)S(1)} all-gather(bf16[4,96,128]{2,1,0:T(8,128)(2,1)S(1)} %aggregate.32.mixed_ref), channel_id=10, replica_groups=mesh['section'=4,'dom'=8] {'section'}, dimensions={0}, use_global_device_ids=true | all-gather | bytes 491520 | tf_op jit(solution)/shard_map/all_gather | solution.py:331
  170.7 6.3 %all-gather.9 = bf16[16,96,128]{2,1,0:T(8,128)(2,1)S(1)} all-gather(bf16[4,96,128]{2,1,0:T(8,128)(2,1)S(1)} %aggregate.33.mixed_ref), channel_id=11, replica_groups=mesh['section'=4,'dom'=8] {'section'}, dimensions={0}, use_global_device_ids=true | all-gather | bytes 491520 | tf_op jit(solution)/shard_map/all_gather | solution.py:331
  211.2 6.3 %all-gather.2 = bf16[16,96,128]{2,1,0:T(8,128)(2,1)S(1)} all-gather(bf16[4,96,128]{2,1,0:T(8,128)(2,1)S(1)} %aggregate.26.mixed_ref), channel_id=4, replica_groups=mesh['section'=4,'dom'=8] {'section'}, dimensions={0}, use_global_device_ids=true | all-gather | bytes 491520 | tf_op jit(solution)/shard_map/all_gather | solution.py:331
  230.9 6.3 %all-gather.10 = bf16[16,96,128]{2,1,0:T(8,128)(2,1)S(1)} all-gather(bf16[4,96,128]{2,1,0:T(8,128)(2,1)S(1)} %aggregate.34.mixed_ref), channel_id=12, replica_groups=mesh['section'=4,'dom'=8] {'section'}, dimensions={0}, use_global_device_ids=true | all-gather | bytes 491520 | tf_op jit(solution)/shard_map/all_gather | solution.py:331
  251.9 6.3 %all-gather.18 = bf16[16,96,128]{2,1,0:T(8,128)(2,1)S(1)} all-gather(bf16[4,96,128]{2,1,0:T(8,128)(2,1)S(1)} %aggregate.42.mixed_ref), channel_id=20, replica_groups=mesh['section'=4,'dom'=8] {'section'}, dimensions={0}, use_global_device_ids=true | all-gather | bytes 491520 | tf_op jit(solution)/shard_map/all_gather | solution.py:331
  269.8 6.4 %all-gather.3 = bf16[16,96,128]{2,1,0:T(8,128)(2,1)S(1)} all-gather(bf16[4,96,128]{2,1,0:T(8,128)(2,1)S(1)} %aggregate.27.mixed_ref), channel_id=5, replica_groups=mesh['section'=4,'dom'=8] {'section'}, dimensions={0}, use_global_device_ids=true | all-gather | bytes 491520 | tf_op jit(solution)/shard_map/all_gather | solution.py:331
  288.9 6.5 %all-gather.11 = bf16[16,96,128]{2,1,0:T(8,128)(2,1)S(1)} all-gather(bf16[4,96,128]{2,1,0:T(8,128)(2,1)S(1)} %aggregate.35.mixed_ref), channel_id=13, replica_groups=mesh['section'=4,'dom'=8] {'section'}, dimensions={0}, use_global_device_ids=true | all-gather | bytes 491520 | tf_op jit(solution)/shard_map/all_gather | solution.py:331
  310.1 6.3 %all-gather.19 = bf16[16,96,128]{2,1,0:T(8,128)(2,1)S(1)} all-gather(bf16[4,96,128]{2,1,0:T(8,128)(2,1)S(1)} %aggregate.43.mixed_ref), channel_id=21, replica_groups=mesh['section'=4,'dom'=8] {'section'}, dimensions={0}, use_global_device_ids=true | all-gather | bytes 491520 | tf_op jit(solution)/shard_map/all_gather | solution.py:331
  329.4 6.4 %all-gather.4 = bf16[16,96,128]{2,1,0:T(8,128)(2,1)S(1)} all-gather(bf16[4,96,128]{2,1,0:T(8,128)(2,1)S(1)} %aggregate.28.mixed_ref), channel_id=6, replica_groups=mesh['section'=4,'dom'=8] {'section'}, dimensions={0}, use_global_device_ids=true | all-gather | bytes 491520 | tf_op jit(solution)/shard_map/all_gather | solution.py:331
  349.3 6.3 %all-gather.12 = bf16[16,96,128]{2,1,0:T(8,128)(2,1)S(1)} all-gather(bf16[4,96,128]{2,1,0:T(8,128)(2,1)S(1)} %aggregate.36.mixed_ref), channel_id=14, replica_groups=mesh['section'=4,'dom'=8] {'section'}, dimensions={0}, use_global_device_ids=true | all-gather | bytes 491520 | tf_op jit(solution)/shard_map/all_gather | solution.py:331
  370.2 6.3 %all-gather.20 = bf16[16,96,128]{2,1,0:T(8,128)(2,1)S(1)} all-gather(bf16[4,96,128]{2,1,0:T(8,128)(2,1)S(1)} %aggregate.44.mixed_ref), channel_id=22, replica_groups=mesh['section'=4,'dom'=8] {'section'}, dimensions={0}, use_global_device_ids=true | all-gather | bytes 491520 | tf_op jit(solution)/shard_map/all_gather | solution.py:331
  388.2 6.4 %all-gather.5 = bf16[16,96,128]{2,1,0:T(8,128)(2,1)S(1)} all-gather(bf16[4,96,128]{2,1,0:T(8,128)(2,1)S(1)} %aggregate.29.mixed_ref), channel_id=7, replica_groups=mesh['section'=4,'dom'=8] {'section'}, dimensions={0}, use_global_device_ids=true | all-gather | bytes 491520 | tf_op jit(solution)/shard_map/all_gather | solution.py:331
  447.8 6.3 %all-gather.6 = bf16[16,96,128]{2,1,0:T(8,128)(2,1)S(1)} all-gather(bf16[4,96,128]{2,1,0:T(8,128)(2,1)S(1)} %aggregate.30.mixed_ref), channel_id=8, replica_groups=mesh['section'=4,'dom'=8] {'section'}, dimensions={0}, use_global_device_ids=true | all-gather | bytes 491520 | tf_op jit(solution)/shard_map/all_gather | solution.py:331
  467.5 6.3 %all-gather.14 = bf16[16,96,128]{2,1,0:T(8,128)(2,1)S(1)} all-gather(bf16[4,96,128]{2,1,0:T(8,128)(2,1)S(1)} %aggregate.38.mixed_ref), channel_id=16, replica_groups=mesh['section'=4,'dom'=8] {'section'}, dimensions={0}, use_global_device_ids=true | all-gather | bytes 491520 | tf_op jit(solution)/shard_map/all_gather | solution.py:331
  488.5 6.3 %all-gather.22 = bf16[16,96,128]{2,1,0:T(8,128)(2,1)S(1)} all-gather(bf16[4,96,128]{2,1,0:T(8,128)(2,1)S(1)} %aggregate.46.mixed_ref), channel_id=24, replica_groups=mesh['section'=4,'dom'=8] {'section'}, dimensions={0}, use_global_device_ids=true | all-gather | bytes 491520 | tf_op jit(solution)/shard_map/all_gather | solution.py:331
  506.4 6.4 %all-gather.7 = bf16[16,96,128]{2,1,0:T(8,128)(2,1)S(1)} all-gather(bf16[4,96,128]{2,1,0:T(8,128)(2,1)S(1)} %aggregate.31.mixed_ref), channel_id=9, replica_groups=mesh['section'=4,'dom'=8] {'section'}, dimensions={0}, use_global_device_ids=true | all-gather | bytes 491520 | tf_op jit(solution)/shard_map/all_gather | solution.py:331
  518.4 6.7 %all-gather.15 = bf16[16,96,128]{2,1,0:T(8,128)(2,1)S(1)} all-gather(bf16[4,96,128]{2,1,0:T(8,128)(2,1)S(1)} %aggregate.39.mixed_ref), channel_id=17, replica_groups=mesh['section'=4,'dom'=8] {'section'}, dimensions={0}, use_global_device_ids=true | all-gather | bytes 491520 | tf_op jit(solution)/shard_map/all_gather | solution.py:331
  530.8 6.6 %all-gather.23 = bf16[16,96,128]{2,1,0:T(8,128)(2,1)S(1)} all-gather(bf16[4,96,128]{2,1,0:T(8,128)(2,1)S(1)} %aggregate.47.mixed_ref), channel_id=25, replica_groups=mesh['section'=4,'dom'=8] {'section'}, dimensions={0}, use_global_device_ids=true | all-gather | bytes 491520 | tf_op jit(solution)/shard_map/all_gather | solution.py:331
  (239 shorter events, 349.1 us)
Async XLA Ops:
  40.8 16.0 %all-to-all-start.2 = ((bf16[2,4,96,384]{3,2,0,1:T(8,128)(2,1)}), bf16[2,4,96,384]{3,2,0,1:T(8,128)(2,1)S(1)}, u32[]{:S(2)}, u32[]{:S(2)}) async-start(bf16[2,4,96,384]{3,2,0,1:T(8,128)(2,1)} %copy.13), calls=%async_computation.2 | async-start | bytes 1179648 | tf_op jit(solution)/shard_map/all_to_all | solution.py:305
  59.3 12.1 %all-to-all-start.20 = ((bf16[8,1,96,128]{3,2,1,0:T(8,128)(2,1)}), bf16[8,1,96,128]{3,2,1,0:T(8,128)(2,1)S(1)}, u32[]{:S(2)}, u32[]{:S(2)}) async-start(bf16[8,1,96,128]{3,2,1,0:T(8,128)(2,1)} %get-tuple-element.88), calls=%async_computation.20 | async-start | bytes 393216 | tf_op jit(solution)/shard_map/all_to_all | solution.py:292
  72.0 23.6 %all-to-all-start.1 = ((bf16[4,16,96,128]{3,2,1,0:T(8,128)(2,1)}), bf16[4,16,96,128]{3,2,1,0:T(8,128)(2,1)S(1)}, u32[]{:S(2)}, u32[]{:S(2)}) async-start(bf16[4,16,96,128]{3,2,1,0:T(8,128)(2,1)} %copy-done.10), calls=%async_computation.1 | async-start | bytes 3145728 | tf_op jit(solution)/shard_map/all_to_all | solution.py:296
  96.8 28.4 %all-to-all-start.4 = ((bf16[4,16,96,128]{3,2,1,0:T(8,128)(2,1)}), bf16[4,16,96,128]{3,2,1,0:T(8,128)(2,1)S(1)}, u32[]{:S(2)}, u32[]{:S(2)}) async-start(bf16[4,16,96,128]{3,2,1,0:T(8,128)(2,1)} %copy-done.9), calls=%async_computation.4 | async-start | bytes 3145728 | tf_op jit(solution)/shard_map/all_to_all | solution.py:296
  125.2 17.5 %all-to-all-start.3 = ((bf16[8,1,96,128]{3,2,1,0:T(8,128)(2,1)}), bf16[8,1,96,128]{3,2,1,0:T(8,128)(2,1)S(1)}, u32[]{:S(2)}, u32[]{:S(2)}) async-start(bf16[8,1,96,128]{3,2,1,0:T(8,128)(2,1)} %get-tuple-element.56), calls=%async_computation.3 | async-start | bytes 393216 | tf_op jit(solution)/shard_map/all_to_all | solution.py:292
  142.8 17.7 %all-to-all-start.12 = ((bf16[8,1,96,128]{3,2,1,0:T(8,128)(2,1)}), bf16[8,1,96,128]{3,2,1,0:T(8,128)(2,1)S(1)}, u32[]{:S(2)}, u32[]{:S(2)}) async-start(bf16[8,1,96,128]{3,2,1,0:T(8,128)(2,1)} %get-tuple-element.72), calls=%async_computation.12 | async-start | bytes 393216 | tf_op jit(solution)/shard_map/all_to_all | solution.py:292
  160.5 18.3 %all-to-all-start.5 = ((bf16[8,1,96,128]{3,2,1,0:T(8,128)(2,1)}), bf16[8,1,96,128]{3,2,1,0:T(8,128)(2,1)S(1)}, u32[]{:S(2)}, u32[]{:S(2)}) async-start(bf16[8,1,96,128]{3,2,1,0:T(8,128)(2,1)} %copy-done.43), calls=%async_computation.5 | async-start | bytes 393216 | tf_op jit(solution)/shard_map/all_to_all | solution.py:292
  178.8 21.2 %all-to-all-start.13 = ((bf16[8,1,96,128]{3,2,1,0:T(8,128)(2,1)}), bf16[8,1,96,128]{3,2,1,0:T(8,128)(2,1)S(1)}, u32[]{:S(2)}, u32[]{:S(2)}) async-start(bf16[8,1,96,128]{3,2,1,0:T(8,128)(2,1)} %copy-done.36), calls=%async_computation.13 | async-start | bytes 393216 | tf_op jit(solution)/shard_map/all_to_all | solution.py:292
  200.0 19.3 %all-to-all-start.21 = ((bf16[8,1,96,128]{3,2,1,0:T(8,128)(2,1)}), bf16[8,1,96,128]{3,2,1,0:T(8,128)(2,1)S(1)}, u32[]{:S(2)}, u32[]{:S(2)}) async-start(bf16[8,1,96,128]{3,2,1,0:T(8,128)(2,1)} %get-tuple-element.90), calls=%async_computation.21 | async-start | bytes 393216 | tf_op jit(solution)/shard_map/all_to_all | solution.py:292
  219.4 20.3 %all-to-all-start.6 = ((bf16[8,1,96,128]{3,2,1,0:T(8,128)(2,1)}), bf16[8,1,96,128]{3,2,1,0:T(8,128)(2,1)S(1)}, u32[]{:S(2)}, u32[]{:S(2)}) async-start(bf16[8,1,96,128]{3,2,1,0:T(8,128)(2,1)} %copy-done.44), calls=%async_computation.6 | async-start | bytes 393216 | tf_op jit(solution)/shard_map/all_to_all | solution.py:292
  239.7 20.3 %all-to-all-start.14 = ((bf16[8,1,96,128]{3,2,1,0:T(8,128)(2,1)}), bf16[8,1,96,128]{3,2,1,0:T(8,128)(2,1)S(1)}, u32[]{:S(2)}, u32[]{:S(2)}) async-start(bf16[8,1,96,128]{3,2,1,0:T(8,128)(2,1)} %copy-done.37), calls=%async_computation.14 | async-start | bytes 393216 | tf_op jit(solution)/shard_map/all_to_all | solution.py:292
  260.0 18.1 %all-to-all-start.22 = ((bf16[8,1,96,128]{3,2,1,0:T(8,128)(2,1)}), bf16[8,1,96,128]{3,2,1,0:T(8,128)(2,1)S(1)}, u32[]{:S(2)}, u32[]{:S(2)}) async-start(bf16[8,1,96,128]{3,2,1,0:T(8,128)(2,1)} %get-tuple-element.92), calls=%async_computation.22 | async-start | bytes 393216 | tf_op jit(solution)/shard_map/all_to_all | solution.py:292
  278.8 19.1 %all-to-all-start.7 = ((bf16[8,1,96,128]{3,2,1,0:T(8,128)(2,1)}), bf16[8,1,96,128]{3,2,1,0:T(8,128)(2,1)S(1)}, u32[]{:S(2)}, u32[]{:S(2)}) async-start(bf16[8,1,96,128]{3,2,1,0:T(8,128)(2,1)} %get-tuple-element.62), calls=%async_computation.7 | async-start | bytes 393216 | tf_op jit(solution)/shard_map/all_to_all | solution.py:292
  297.9 20.3 %all-to-all-start.15 = ((bf16[8,1,96,128]{3,2,1,0:T(8,128)(2,1)}), bf16[8,1,96,128]{3,2,1,0:T(8,128)(2,1)S(1)}, u32[]{:S(2)}, u32[]{:S(2)}) async-start(bf16[8,1,96,128]{3,2,1,0:T(8,128)(2,1)} %copy-done.38), calls=%async_computation.15 | async-start | bytes 393216 | tf_op jit(solution)/shard_map/all_to_all | solution.py:292
  318.2 19.5 %all-to-all-start.23 = ((bf16[8,1,96,128]{3,2,1,0:T(8,128)(2,1)}), bf16[8,1,96,128]{3,2,1,0:T(8,128)(2,1)S(1)}, u32[]{:S(2)}, u32[]{:S(2)}) async-start(bf16[8,1,96,128]{3,2,1,0:T(8,128)(2,1)} %get-tuple-element.94), calls=%async_computation.23 | async-start | bytes 393216 | tf_op jit(solution)/shard_map/all_to_all | solution.py:292
  337.7 20.4 %all-to-all-start.8 = ((bf16[8,1,96,128]{3,2,1,0:T(8,128)(2,1)}), bf16[8,1,96,128]{3,2,1,0:T(8,128)(2,1)S(1)}, u32[]{:S(2)}, u32[]{:S(2)}) async-start(bf16[8,1,96,128]{3,2,1,0:T(8,128)(2,1)} %copy-done.45), calls=%async_computation.8 | async-start | bytes 393216 | tf_op jit(solution)/shard_map/all_to_all | solution.py:292
  358.1 20.3 %all-to-all-start.16 = ((bf16[8,1,96,128]{3,2,1,0:T(8,128)(2,1)}), bf16[8,1,96,128]{3,2,1,0:T(8,128)(2,1)S(1)}, u32[]{:S(2)}, u32[]{:S(2)}) async-start(bf16[8,1,96,128]{3,2,1,0:T(8,128)(2,1)} %copy-done.39), calls=%async_computation.16 | async-start | bytes 393216 | tf_op jit(solution)/shard_map/all_to_all | solution.py:292
  378.4 18.1 %all-to-all-start.24 = ((bf16[8,1,96,128]{3,2,1,0:T(8,128)(2,1)}), bf16[8,1,96,128]{3,2,1,0:T(8,128)(2,1)S(1)}, u32[]{:S(2)}, u32[]{:S(2)}) async-start(bf16[8,1,96,128]{3,2,1,0:T(8,128)(2,1)} %get-tuple-element.96), calls=%async_computation.24 | async-start | bytes 393216 | tf_op jit(solution)/shard_map/all_to_all | solution.py:292
  397.1 18.3 %all-to-all-start.9 = ((bf16[8,1,96,128]{3,2,1,0:T(8,128)(2,1)}), bf16[8,1,96,128]{3,2,1,0:T(8,128)(2,1)S(1)}, u32[]{:S(2)}, u32[]{:S(2)}) async-start(bf16[8,1,96,128]{3,2,1,0:T(8,128)(2,1)} %copy-done.46), calls=%async_computation.9 | async-start | bytes 393216 | tf_op jit(solution)/shard_map/all_to_all | solution.py:292
  415.4 21.2 %all-to-all-start.17 = ((bf16[8,1,96,128]{3,2,1,0:T(8,128)(2,1)}), bf16[8,1,96,128]{3,2,1,0:T(8,128)(2,1)S(1)}, u32[]{:S(2)}, u32[]{:S(2)}) async-start(bf16[8,1,96,128]{3,2,1,0:T(8,128)(2,1)} %copy-done.40), calls=%async_computation.17 | async-start | bytes 393216 | tf_op jit(solution)/shard_map/all_to_all | solution.py:292
  436.6 19.3 %all-to-all-start.25 = ((bf16[8,1,96,128]{3,2,1,0:T(8,128)(2,1)}), bf16[8,1,96,128]{3,2,1,0:T(8,128)(2,1)S(1)}, u32[]{:S(2)}, u32[]{:S(2)}) async-start(bf16[8,1,96,128]{3,2,1,0:T(8,128)(2,1)} %get-tuple-element.98), calls=%async_computation.25 | async-start | bytes 393216 | tf_op jit(solution)/shard_map/all_to_all | solution.py:292
  456.0 20.3 %all-to-all-start.10 = ((bf16[8,1,96,128]{3,2,1,0:T(8,128)(2,1)}), bf16[8,1,96,128]{3,2,1,0:T(8,128)(2,1)S(1)}, u32[]{:S(2)}, u32[]{:S(2)}) async-start(bf16[8,1,96,128]{3,2,1,0:T(8,128)(2,1)} %copy-done.42), calls=%async_computation.10 | async-start | bytes 393216 | tf_op jit(solution)/shard_map/all_to_all | solution.py:292
  476.3 20.3 %all-to-all-start.18 = ((bf16[8,1,96,128]{3,2,1,0:T(8,128)(2,1)}), bf16[8,1,96,128]{3,2,1,0:T(8,128)(2,1)S(1)}, u32[]{:S(2)}, u32[]{:S(2)}) async-start(bf16[8,1,96,128]{3,2,1,0:T(8,128)(2,1)} %copy-done.41), calls=%async_computation.18 | async-start | bytes 393216 | tf_op jit(solution)/shard_map/all_to_all | solution.py:292
  496.7 29.7 %all-to-all-start.26 = ((bf16[8,1,96,128]{3,2,1,0:T(8,128)(2,1)}), bf16[8,1,96,128]{3,2,1,0:T(8,128)(2,1)S(1)}, u32[]{:S(2)}, u32[]{:S(2)}) async-start(bf16[8,1,96,128]{3,2,1,0:T(8,128)(2,1)} %get-tuple-element.100), calls=%async_computation.26 | async-start | bytes 393216 | tf_op jit(solution)/shard_map/all_to_all | solution.py:292
  (64 other events, 250.5 us)

commit v3 on v0

v3 whole, which is shorter than its diff:
```python
import functools
import math

import jax
import jax.numpy as jnp
from jax import lax
from jax.experimental import pallas as pl
from jax.experimental.pallas import tpu as pltpu
from jax.sharding import PartitionSpec as P

alpha_mix = 0.1
lambda_decay = 0.5
vmem_bytes = 24 * 1024 * 1024
anywhere = pl.BlockSpec(memory_space=pl.ANY)


def unit_of(tick, section, sections):
    group = (tick - section) % sections
    return group, tick - group


def start_when(condition, copy):
    pl.when(condition)(lambda: copy.start())


def wait_when(condition, copy):
    pl.when(condition)(lambda: copy.wait())


def tick_kernel(plan, info, columns, picks, *refs):
    tick, sections, parts, groups, depth, layers, history, moved_keys, sends, is_last = plan
    initial_ref, tiles_ref, stale_ref, weights_ref = refs[:4]
    refs = list(refs[4:])
    arrived = [[refs.pop(0) for _ in range(parts)] for _ in range(history)]
    moved = {key: (refs.pop(0), refs.pop(0)) for key in moved_keys}
    out_refs = [refs.pop(0) for _ in range(parts)] if sends else []
    final_refs = [refs.pop(0) for _ in range(sections)] if is_last else []
    table, tiles, stored_weight, initial, made, table_sem, tile_sem, other_sem, out_sem = refs
    fanout, block = tiles_ref.shape[1:3]
    blocks_dev = tiles_ref.shape[0]
    group_blocks = blocks_dev // groups
    width = initial_ref.shape[1]

    section, part = info[0], info[1]
    group = lax.rem(tick - section + 4 * sections, sections)
    layer = tick - group
    first_row = group * group_blocks
    computing = (group < groups) & (layer >= 0) & (layer < layers)
    passing = (group < groups) & (layer == -1)
    home = lax.div(jnp.maximum(layer, 0), depth)
    sub = lax.rem(jnp.maximum(layer, 0), depth)
    turn = lax.div(jnp.maximum(layer, 0), sections)

    first_initial = pl.multiple_of(first_row * block, block)
    initial_copy = pltpu.make_async_copy(
        initial_ref.at[pl.ds(first_initial, group_blocks * block)], initial, other_sem.at[0]
    )

    if history > 0:
        copies = []
        for back in range(history):
            known = computing & (group >= back)
            source_group = jnp.maximum(group - back, 0)
            sem = lambda index: table_sem.at[back * parts + index]
            copies.append(
                (
                    known,
                    pltpu.make_async_copy(
                        arrived[back][0],
                        table.at[pl.ds(source_group * group_blocks, group_blocks)],
                        sem(0),
                    ),
                )
            )
            for distance in range(1, parts):
                origin = lax.rem(part - distance + parts, parts)
                copies.append(
                    (
                        known,
                        pltpu.make_async_copy(
                            arrived[back][distance],
                            table.at[blocks_dev + source_group * parts + origin],
                            sem(distance),
                        ),
                    )
                )
        here = section == home
        sources = [(here, stale_ref.at[sub, 0], weights_ref.at[sub])]
        for (moved_turn, moved_sub), (moved_stale, moved_weight) in moved.items():
            chosen = jnp.logical_not(here) & (turn == moved_turn) & (sub == moved_sub)
            sources.append((chosen, moved_stale, moved_weight))
        for chosen, stale_source, weight_source in sources:
            for later in range(1, groups):
                copies.append(
                    (
                        computing & chosen & (group < later),
                        pltpu.make_async_copy(
                            stale_source.at[(later - 1) * parts : later * parts],
                            table.at[pl.ds(blocks_dev + later * parts, parts)],
                            other_sem.at[1 + later],
                        ),
                    )
                )
            copies.append(
                (
                    computing & chosen,
                    pltpu.make_async_copy(weight_source, stored_weight, other_sem.at[1]),
                )
            )

        def tile_copy(row):
            return pltpu.make_async_copy(
                tiles_ref.at[first_row + row], tiles.at[row], tile_sem.at[row]
            )

        for condition, copy in copies:
            start_when(condition, copy)

        @pl.when(computing)
        def _():
            for row in range(group_blocks):
                tile_copy(row).start()
            initial_copy.start()

        for condition, copy in copies:
            wait_when(condition, copy)

        @pl.when(computing)
        def _():
            initial_copy.wait()
            beta_layer = jnp.float32(0.0)
            for known_layer in range(max(tick - groups + 1, 0), min(tick, layers - 1) + 1):
                beta_layer = jnp.where(
                    layer == known_layer,
                    jnp.float32(math.log(lambda_decay / (known_layer + 1) + 1.0)),
                    beta_layer,
                )
            mixed_rows = []
            for row in range(group_blocks):
                tile_copy(row).wait()
                base = (first_row + row) * fanout
                total = None
                for tile in range(0, fanout, 2):
                    span = range(tile, min(tile + 2, fanout))
                    left = jnp.concatenate([tiles[row, t] for t in span], 1)
                    right = jnp.concatenate([table[columns[base + t]] for t in span], 0)
                    term = jnp.dot(left, right, preferred_element_type=jnp.float32)
                    total = term if total is None else total + term
                start = initial[row * block : (row + 1) * block].astype(jnp.float32)
                mixed = ((1.0 - alpha_mix) * total + alpha_mix * start).astype(jnp.bfloat16)
                product = jnp.dot(mixed, stored_weight[...], preferred_element_type=jnp.float32)
                value = (1.0 - beta_layer) * mixed.astype(jnp.float32) + beta_layer * product
                made[row] = jnp.maximum(value, 0.0).astype(jnp.bfloat16)

    if tick < groups - 1:

        @pl.when(passing)
        def _():
            initial_copy.start()
            initial_copy.wait()
            for row in range(group_blocks):
                made[row] = initial[row * block : (row + 1) * block]

    if sends:
        sending = passing | (computing & (layer < layers - 1))

        @pl.when(sending)
        def _():
            out_copies = [pltpu.make_async_copy(made, out_refs[0], out_sem.at[0])]
            for distance in range(1, parts):
                dest = lax.rem(part + distance, parts)
                chosen = jnp.maximum(picks[group * parts + dest], 0)
                out_copies.append(
                    pltpu.make_async_copy(
                        made.at[chosen], out_refs[distance], out_sem.at[distance]
                    )
                )
            for copy in out_copies:
                copy.start()
            for copy in out_copies:
                copy.wait()

    if is_last:

        @pl.when(computing & (layer == layers - 1))
        def _():
            piece = width // sections
            for index, final_ref in enumerate(final_refs):
                for row in range(group_blocks):
                    final_ref[row * block : (row + 1) * block, :] = made[row][
                        :, index * piece : (index + 1) * piece
                    ]


def run_tick(tick, scalars, arrays, arrived, moved, sizes):
    sections, parts, groups, depth, layers = sizes
    initial_features, tiles = arrays[:2]
    width = initial_features.shape[1]
    blocks_dev, fanout, block = tiles.shape[:3]
    group_blocks = blocks_dev // groups
    sends = tick < layers + groups - 2
    is_last = tick >= layers - 1
    units = [unit_of(tick, s, sections) for s in range(sections)]
    units = [(g, l) for g, l in units if g < groups and 0 <= l < layers]
    moved_keys = sorted(
        {(l // sections, l % depth) for g, l in units if l // depth != l % sections}
    )
    plan = (
        tick, sections, parts, groups, depth, layers, len(arrived), moved_keys, sends, is_last,
    )
    operands = list(arrays)
    for back in arrived:
        operands += back
    for key in moved_keys:
        operands += list(moved[key])
    out_shape, out_specs = [], []
    if sends:
        shapes = [(group_blocks, block, width)] + [(block, width)] * (parts - 1)
        out_shape += [jax.ShapeDtypeStruct(s, jnp.bfloat16) for s in shapes]
        out_specs += [anywhere] * parts
    if is_last:
        shape = (group_blocks * block, width // sections)
        out_shape += [jax.ShapeDtypeStruct(shape, jnp.bfloat16)] * sections
        out_specs += [pl.BlockSpec(shape, lambda i, *prefetched: (0, 0))] * sections
    work = group_blocks if units else 0
    results = pl.pallas_call(
        functools.partial(tick_kernel, plan),
        grid_spec=pltpu.PrefetchScalarGridSpec(
            num_scalar_prefetch=3,
            grid=(1,),
            in_specs=[anywhere] * len(operands),
            out_specs=out_specs,
            scratch_shapes=[
                pltpu.VMEM((blocks_dev + groups * parts, block, width), jnp.bfloat16),
                pltpu.VMEM((group_blocks, fanout, block, block), jnp.bfloat16),
                pltpu.VMEM((width, width), jnp.bfloat16),
                pltpu.VMEM((group_blocks * block, width), jnp.bfloat16),
                pltpu.VMEM((group_blocks, block, width), jnp.bfloat16),
                pltpu.SemaphoreType.DMA((groups * parts,)),
                pltpu.SemaphoreType.DMA((group_blocks,)),
                pltpu.SemaphoreType.DMA((groups + 1,)),
                pltpu.SemaphoreType.DMA((parts,)),
            ],
        ),
        out_shape=out_shape,
        cost_estimate=pl.CostEstimate(
            flops=2 * work * block * width * (fanout * block + width) + 1,
            bytes_accessed=work * fanout * block * (block + width) * 2 + 1,
            transcendentals=0,
        ),
        compiler_params=pltpu.CompilerParams(vmem_limit_bytes=vmem_bytes),
        name="tick",
    )(*scalars, *operands)
    return (results[:parts] if sends else []), (results[-sections:] if is_last else [])


def per_device(
    initial_features, layer_weights, adjacency_tiles, tile_columns, send_blocks, stale_imports
):
    sections = lax.axis_size("section")
    parts = lax.axis_size("dom")
    groups = send_blocks.shape[1]
    depth = layer_weights.shape[0]
    layers = depth * sections
    section = lax.axis_index("section").astype(jnp.int32)
    part = lax.axis_index("dom").astype(jnp.int32)
    scalars = (jnp.stack([section, part]), tile_columns.reshape(-1), send_blocks.reshape(-1))
    arrays = (initial_features, adjacency_tiles, stale_imports, layer_weights)
    sizes = (sections, parts, groups, depth, layers)

    def move(value, pairs, distance):
        routes = [
            (a * parts + q, b * parts + (q + distance) % parts) for a, b in pairs for q in range(parts)
        ]
        return lax.ppermute(value, ("section", "dom"), routes)

    routes = {}
    for layer in range(layers):
        if layer // depth != layer % sections:
            key = (layer // sections, layer % depth)
            routes.setdefault(key, []).append((layer // depth, layer % sections))
    moved = {
        key: (move(stale_imports[key[1], 0], pairs, 0), move(layer_weights[key[1]], pairs, 0))
        for key, pairs in sorted(routes.items())
    }

    arrived = []
    pieces = []
    for tick in range(-1, layers + groups - 1):
        outgoing, final = run_tick(tick, scalars, arrays, arrived, moved, sizes)
        senders = []
        for s in range(sections):
            group, layer = unit_of(tick, s, sections)
            if group < groups and -1 <= layer < layers - 1:
                senders.append((s, (s + 1) % sections))
        if outgoing:
            received = [move(value, senders, distance) for distance, value in enumerate(outgoing)]
            arrived = [received] + arrived[: groups - 1]
        if final:
            last = (layers - 1) % sections
            piece = final[last]
            for s in range(sections):
                if s != last:
                    piece = jnp.where(section == s, move(final[s], [(last, s)], 0), piece)
            pieces.append(piece)
    return jnp.concatenate(pieces, 0)


def solution(mesh):
    return jax.shard_map(
        per_device,
        mesh=mesh,
        in_specs=(
            P("dom", None),
            P("section", None, None),
            P("dom", None, None, None),
            P("dom", None),
            P("dom", None, None),
            P("section", "dom", None, None, None),
        ),
        out_specs=P("dom", "section"),
        check_vma=False,
    )
```

time: 658 us -> 597 us (0.907)
  starting transfers between devices: 114 us -> 436 us
  local copies, waits for them, and re-layouts: 234 us -> 35.4 us
  other arithmetic: 110 us -> 1.18 us
  matrix products: 60 us -> 0 us
  Pallas kernels: 0 us -> 56.2 us
  blocking collectives: 45 us -> 0 us
  waiting for transfers between devices: 89.9 us -> 55.8 us
    ppermute x6 -> x97, starting transfers between devices: 63.3 us -> 436 us  [move(): return lax.ppermute(value, ('section', 'dom'), routes)]
    all_to_all x12 -> x0, waiting for transfers between devices: 89.9 us -> none  [turn(): lax.all_to_all(outgoing, 'dom', split_axis=0, concat_axis=0, tiled=True)]
    dynamic_slice x48 -> x0, local copies, waits for them, and re-layouts: 72.5 us -> none  [the longest x18 25.5 us: turn(): kept_rows = lax.dynamic_slice_in_dim(own_table, first_row, group_blocks, 0)]
    dot_general x24 -> x0, matrix products: 60 us -> none  [the longest x6 47.6 us: gather_rows(): jnp.einsum('rim,rmd->rid', tile_rows, flat, preferred_element_type=jnp.fl...]
    pallas_call x0 -> x11, Pallas kernels: none -> 56.2 us  [run_tick(): pl.pallas_call(functools.partial(tick_kernel, plan), grid_spec=pltpu.Pref...]
    ppermute x6 -> x97, waiting for transfers between devices: 0.02 us -> 55.8 us  [move(): return lax.ppermute(value, ('section', 'dom'), routes)]
    slice x13 -> x0, local copies, waits for them, and re-layouts: 52.7 us -> none  [the longest x6 39.1 us: turn(): stale_table = imported[sublayer]]
    all_to_all x12 -> x0, starting transfers between devices: 51 us -> none  [turn(): lax.all_to_all(outgoing, 'dom', split_axis=0, concat_axis=0, tiled=True)]
  transfers between devices with their start and end apart: 18 -> 97, of which waited for: 12 -> 17; matrix products, arithmetic and copies ran while one was open for 25% -> 0% of each run, Pallas kernels for 0% -> 6%
where the time goes in v3:
time: 597 us; the launch traced here: 587 us
  starting transfers between devices  436 us (73%)
  Pallas kernels  56.2 us (9%)
  waiting for transfers between devices  55.8 us (9%)
  local copies, waits for them, and re-layouts  35.4 us (6%)
    ppermute x97, starting transfers between devices, move(): return lax.ppermute(value, ('section', 'dom'), routes)  436 us
    pallas_call x11, Pallas kernels, run_tick(): pl.pallas_call(functools.partial(tick_kernel, plan), grid_spec=pltpu.Pref...  56.2 us
    ppermute x97, waiting for transfers between devices, move(): return lax.ppermute(value, ('section', 'dom'), routes)  55.8 us
    unnamed x102, local copies, waits for them, and re-layouts  30.1 us
  transfers between devices with their start and end apart: 97, of which 17 were waited for; matrix products, arithmetic and copies ran while one was open for 0% of the time, Pallas kernels for 6%

profile of v3, /device:TPU:0, one launch (start us, length us, event | category | flops | bytes accessed | tf_op | source)
XLA Modules:
  0.0 587.0 jit_solution(5425710923768048392)
XLA Ops:
  4.2 9.5 %collective-permute-start.16 = (bf16[16,128,384]{2,1,0:T(8,128)(2,1)}, bf16[16,128,384]{2,1,0:T(8,128)(2,1)}, u32[]{:S(2)}, u32[]{:S(2)}) collective-permute-start(bf16[16,128,384]{2,1,0:T(8,128)(2,1)} %get-tuple-element.190), channel_id=1, source_target_pairs={{0,8},{1,9},{2,10},{3,11},{4,12},{5,13},{6,14},{7,15},{8,24},{9,25... | collective-permute-start | bytes 4718600 | tf_op jit(solution)/shard_map/ppermute | solution.py:275
  54.0 7.4 %collective-permute-start.17 = (bf16[384,384]{1,0:T(8,128)(2,1)S(1)}, bf16[384,384]{1,0:T(8,128)(2,1)S(1)}, u32[]{:S(2)}, u32[]{:S(2)}) collective-permute-start(bf16[384,384]{1,0:T(8,128)(2,1)S(1)} %get-tuple-element.192), channel_id=1, source_target_pairs={{0,8},{1,9},{2,10},{3,11},{4,12},{5,13},{6,14},{7,15},{8,24},{9,25... | collective-permute-start | bytes 884744 | tf_op jit(solution)/shard_map/ppermute | solution.py:275
  61.5 7.0 %tick.12 = (bf16[4,128,384]{2,1,0:T(8,128)(2,1)S(1)}, bf16[128,384]{1,0:T(8,128)(2,1)S(1)}, bf16[128,384]{1,0:T(8,128)(2,1)S(1)}, bf16[128,384]{1,0:T(8,128)(2,1...) custom-call(s32[2]{0:T(128)S(1)} %pad_add_fusion.info, ...), custom_call_target="tpu_custom_call" | custom-call | flops 1358954496 | bytes 12582913 | tf_op jit(solution)/shard_map/tick/pallas_call | solution.py:226
  121.5 7.6 %collective-permute-start.15 = (bf16[128,384]{1,0:T(8,128)(2,1)S(1)}, bf16[128,384]{1,0:T(8,128)(2,1)S(1)}, u32[]{:S(2)}, u32[]{:S(2)}) collective-permute-start(bf16[128,384]{1,0:T(8,128)(2,1)S(1)} %get-tuple-element.112), channel_id=1, source_target_pairs={{0,15},{1,8},{2,9},{3,10},{4,11},{5,12},{6,13},{7,14},{24,7},{25,0... | collective-permute-start | bytes 294920 | tf_op jit(solution)/shard_map/ppermute | solution.py:275
  135.8 8.3 %tick.13 = (bf16[4,128,384]{2,1,0:T(8,128)(2,1)S(1)}, bf16[128,384]{1,0:T(8,128)(2,1)S(1)}, bf16[128,384]{1,0:T(8,128)(2,1)S(1)}, bf16[128,384]{1,0:T(8,128)(2,1...) custom-call(s32[2]{0:T(128)S(1)} %pad_add_fusion.info, ...), custom_call_target="tpu_custom_call" | custom-call | flops 1358954496 | bytes 12582913 | tf_op jit(solution)/shard_map/tick/pallas_call | solution.py:226
  177.4 9.7 %tick.14 = (bf16[4,128,384]{2,1,0:T(8,128)(2,1)S(1)}, bf16[128,384]{1,0:T(8,128)(2,1)S(1)}, bf16[128,384]{1,0:T(8,128)(2,1)S(1)}, bf16[128,384]{1,0:T(8,128)(2,1...) custom-call(s32[2]{0:T(128)S(1)} %pad_add_fusion.info, ...), custom_call_target="tpu_custom_call" | custom-call | flops 1358954496 | bytes 12582913 | tf_op jit(solution)/shard_map/tick/pallas_call | solution.py:226
  194.6 7.4 %collective-permute-start.32 = (bf16[128,384]{1,0:T(8,128)(2,1)S(1)}, bf16[128,384]{1,0:T(8,128)(2,1)S(1)}, u32[]{:S(2)}, u32[]{:S(2)}) collective-permute-start(bf16[128,384]{1,0:T(8,128)(2,1)S(1)} %get-tuple-element.125), channel_id=1, source_target_pairs={{0,12},{1,13},{2,14},{3,15},{4,8},{5,9},{6,10},{7,11},{8,20},{9,21... | collective-permute-start | bytes 294920 | tf_op jit(solution)/shard_map/ppermute | solution.py:275
  214.1 8.1 %collective-permute-start.45 = (bf16[384,384]{1,0:T(8,128)(2,1)S(1)}, bf16[384,384]{1,0:T(8,128)(2,1)S(1)}, u32[]{:S(2)}, u32[]{:S(2)}) collective-permute-start(bf16[384,384]{1,0:T(8,128)(2,1)S(1)} %get-tuple-element.191), channel_id=1, source_target_pairs={{16,0},{17,1},{18,2},{19,3},{20,4},{21,5},{22,6},{23,7},{24,16},{2... | collective-permute-start | bytes 884744 | tf_op jit(solution)/shard_map/ppermute | solution.py:275
  223.4 15.1 %collective-permute-start.36 = (bf16[4,128,384]{2,1,0:T(8,128)(2,1)S(1)}, bf16[4,128,384]{2,1,0:T(8,128)(2,1)S(1)}, u32[]{:S(2)}, u32[]{:S(2)}) collective-permute-start(bf16[4,128,384]{2,1,0:T(8,128)(2,1)S(1)} %get-tuple-element.129), channel_id=1, source_target_pairs={{8,16},{9,17},{10,18},{11,19},{12,20},{13,21},{14,22},{15,23},{16,... | collective-permute-start | bytes 1179656 | tf_op jit(solution)/shard_map/ppermute | solution.py:275
  293.2 7.1 %tick.16 = (bf16[4,128,384]{2,1,0:T(8,128)(2,1)S(1)}, bf16[128,384]{1,0:T(8,128)(2,1)S(1)}, bf16[128,384]{1,0:T(8,128)(2,1)S(1)}, bf16[128,384]{1,0:T(8,128)(2,1...) custom-call(s32[2]{0:T(128)S(1)} %pad_add_fusion.info, ...), custom_call_target="tpu_custom_call" | custom-call | flops 1358954496 | bytes 12582913 | tf_op jit(solution)/shard_map/tick/pallas_call | solution.py:226
  300.3 7.5 %collective-permute-start.46 = (bf16[4,128,384]{2,1,0:T(8,128)(2,1)S(1)}, bf16[4,128,384]{2,1,0:T(8,128)(2,1)S(1)}, u32[]{:S(2)}, u32[]{:S(2)}) collective-permute-start(bf16[4,128,384]{2,1,0:T(8,128)(2,1)S(1)} %get-tuple-element.137), channel_id=1, source_target_pairs={{0,8},{1,9},{2,10},{3,11},{4,12},{5,13},{6,14},{7,15},{16,24},{17,... | collective-permute-start | bytes 1179656 | tf_op jit(solution)/shard_map/ppermute | solution.py:275
  307.8 7.0 %collective-permute-start.47 = (bf16[128,384]{1,0:T(8,128)(2,1)S(1)}, bf16[128,384]{1,0:T(8,128)(2,1)S(1)}, u32[]{:S(2)}, u32[]{:S(2)}) collective-permute-start(bf16[128,384]{1,0:T(8,128)(2,1)S(1)} %get-tuple-element.138), channel_id=1, source_target_pairs={{0,9},{1,10},{2,11},{3,12},{4,13},{5,14},{6,15},{7,8},{16,25},{17,... | collective-permute-start | bytes 294920 | tf_op jit(solution)/shard_map/ppermute | solution.py:275
  314.8 7.0 %collective-permute-start.48 = (bf16[128,384]{1,0:T(8,128)(2,1)S(1)}, bf16[128,384]{1,0:T(8,128)(2,1)S(1)}, u32[]{:S(2)}, u32[]{:S(2)}) collective-permute-start(bf16[128,384]{1,0:T(8,128)(2,1)S(1)} %get-tuple-element.139), channel_id=1, source_target_pairs={{0,10},{1,11},{2,12},{3,13},{4,14},{5,15},{6,8},{7,9},{16,26},{17,... | collective-permute-start | bytes 294920 | tf_op jit(solution)/shard_map/ppermute | solution.py:275
  321.9 7.0 %collective-permute-start.49 = (bf16[128,384]{1,0:T(8,128)(2,1)S(1)}, bf16[128,384]{1,0:T(8,128)(2,1)S(1)}, u32[]{:S(2)}, u32[]{:S(2)}) collective-permute-start(bf16[128,384]{1,0:T(8,128)(2,1)S(1)} %get-tuple-element.140), channel_id=1, source_target_pairs={{0,11},{1,12},{2,13},{3,14},{4,15},{5,8},{6,9},{7,10},{16,27},{17,... | collective-permute-start | bytes 294920 | tf_op jit(solution)/shard_map/ppermute | solution.py:275
  328.9 7.0 %collective-permute-start.50 = (bf16[128,384]{1,0:T(8,128)(2,1)S(1)}, bf16[128,384]{1,0:T(8,128)(2,1)S(1)}, u32[]{:S(2)}, u32[]{:S(2)}) collective-permute-start(bf16[128,384]{1,0:T(8,128)(2,1)S(1)} %get-tuple-element.141), channel_id=1, source_target_pairs={{0,12},{1,13},{2,14},{3,15},{4,8},{5,9},{6,10},{7,11},{16,28},{17,... | collective-permute-start | bytes 294920 | tf_op jit(solution)/shard_map/ppermute | solution.py:275
  335.9 7.0 %collective-permute-start.51 = (bf16[128,384]{1,0:T(8,128)(2,1)S(1)}, bf16[128,384]{1,0:T(8,128)(2,1)S(1)}, u32[]{:S(2)}, u32[]{:S(2)}) collective-permute-start(bf16[128,384]{1,0:T(8,128)(2,1)S(1)} %get-tuple-element.142), channel_id=1, source_target_pairs={{0,13},{1,14},{2,15},{3,8},{4,9},{5,10},{6,11},{7,12},{16,29},{17,... | collective-permute-start | bytes 294920 | tf_op jit(solution)/shard_map/ppermute | solution.py:275
  342.9 7.0 %collective-permute-start.52 = (bf16[128,384]{1,0:T(8,128)(2,1)S(1)}, bf16[128,384]{1,0:T(8,128)(2,1)S(1)}, u32[]{:S(2)}, u32[]{:S(2)}) collective-permute-start(bf16[128,384]{1,0:T(8,128)(2,1)S(1)} %get-tuple-element.143), channel_id=1, source_target_pairs={{0,14},{1,15},{2,8},{3,9},{4,10},{5,11},{6,12},{7,13},{16,30},{17,... | collective-permute-start | bytes 294920 | tf_op jit(solution)/shard_map/ppermute | solution.py:275
  350.0 7.0 %collective-permute-start.53 = (bf16[128,384]{1,0:T(8,128)(2,1)S(1)}, bf16[128,384]{1,0:T(8,128)(2,1)S(1)}, u32[]{:S(2)}, u32[]{:S(2)}) collective-permute-start(bf16[128,384]{1,0:T(8,128)(2,1)S(1)} %get-tuple-element.144), channel_id=1, source_target_pairs={{0,15},{1,8},{2,9},{3,10},{4,11},{5,12},{6,13},{7,14},{16,31},{17,... | collective-permute-start | bytes 294920 | tf_op jit(solution)/shard_map/ppermute | solution.py:275
  361.9 8.6 %tick.17 = (bf16[4,128,384]{2,1,0:T(8,128)(2,1)S(1)}, bf16[128,384]{1,0:T(8,128)(2,1)S(1)}, bf16[128,384]{1,0:T(8,128)(2,1)S(1)}, bf16[128,384]{1,0:T(8,128)(2,1...) custom-call(s32[2]{0:T(128)S(1)} %pad_add_fusion.info, ...), custom_call_target="tpu_custom_call" | custom-call | flops 1358954496 | bytes 12582913 | tf_op jit(solution)/shard_map/tick/pallas_call | solution.py:226
  395.8 9.6 %tick.18 = (bf16[4,128,384]{2,1,0:T(8,128)(2,1)S(1)}, bf16[128,384]{1,0:T(8,128)(2,1)S(1)}, bf16[128,384]{1,0:T(8,128)(2,1)S(1)}, bf16[128,384]{1,0:T(8,128)(2,1...) custom-call(s32[2]{0:T(128)S(1)} %pad_add_fusion.info, ...), custom_call_target="tpu_custom_call" | custom-call | flops 1358954496 | bytes 12582913 | tf_op jit(solution)/shard_map/tick/pallas_call | solution.py:226
  430.0 18.1 %collective-permute-start.75 = (bf16[4,128,384]{2,1,0:T(8,128)(2,1)S(1)}, bf16[4,128,384]{2,1,0:T(8,128)(2,1)S(1)}, u32[]{:S(2)}, u32[]{:S(2)}) collective-permute-start(bf16[4,128,384]{2,1,0:T(8,128)(2,1)S(1)} %get-tuple-element.165), channel_id=1, source_target_pairs={{8,16},{9,17},{10,18},{11,19},{12,20},{13,21},{14,22},{15,23},{16,... | collective-permute-start | bytes 1179656 | tf_op jit(solution)/shard_map/ppermute | solution.py:275
  469.1 7.3 %collective-permute-start.79 = (bf16[128,384]{1,0:T(8,128)(2,1)S(1)}, bf16[128,384]{1,0:T(8,128)(2,1)S(1)}, u32[]{:S(2)}, u32[]{:S(2)}) collective-permute-start(bf16[128,384]{1,0:T(8,128)(2,1)S(1)} %get-tuple-element.169), channel_id=1, source_target_pairs={{8,20},{9,21},{10,22},{11,23},{12,16},{13,17},{14,18},{15,19},{16,... | collective-permute-start | bytes 294920 | tf_op jit(solution)/shard_map/ppermute | solution.py:275
  511.4 9.6 %collective-permute-done.74 = bf16[512,96]{1,0:T(8,128)(2,1)} collective-permute-done((bf16[512,96]{1,0:T(8,128)(2,1)}, bf16[512,96]{1,0:T(8,128)(2,1)}, u32[]{:S(2)}, u32[]{:S(2)}) %collective-permute-start.74) | collective-permute-done | bytes 98336 | tf_op jit(solution)/shard_map/ppermute | solution.py:275
  547.9 24.6 %collective-permute-start.94 = (bf16[512,96]{1,0:T(8,128)(2,1)S(1)}, bf16[512,96]{1,0:T(8,128)(2,1)S(1)}, u32[]{:S(2)}, u32[]{:S(2)}) collective-permute-start(bf16[512,96]{1,0:T(8,128)(2,1)S(1)} %get-tuple-element.185), channel_id=1, source_target_pairs={{24,16},{25,17},{26,18},{27,19},{28,20},{29,21},{30,22},{31,23}} | collective-permute-start | bytes 294920 | tf_op jit(solution)/shard_map/ppermute | solution.py:275
  (294 shorter events, 363.4 us)
Async XLA Ops:
  4.2 131.6 %collective-permute-start.16 = (bf16[16,128,384]{2,1,0:T(8,128)(2,1)}, bf16[16,128,384]{2,1,0:T(8,128)(2,1)}, u32[]{:S(2)}, u32[]{:S(2)}) collective-permute-start(bf16[16,128,384]{2,1,0:T(8,128)(2,1)} %get-tuple-element.190), channel_id=1, source_target_pairs={{0,8},{1,9},{2,10},{3,11},{4,12},{5,13},{6,14},{7,15},{8,24},{9,25... | collective-permute-start | bytes 4718600 | tf_op jit(solution)/shard_map/ppermute | solution.py:275
  13.7 136.7 %collective-permute-start.26 = (bf16[16,128,384]{2,1,0:T(8,128)(2,1)}, bf16[16,128,384]{2,1,0:T(8,128)(2,1)}, u32[]{:S(2)}, u32[]{:S(2)}) collective-permute-start(bf16[16,128,384]{2,1,0:T(8,128)(2,1)} %get-tuple-element.189), channel_id=1, source_target_pairs={{8,16},{9,17},{10,18},{11,19},{12,20},{13,21},{14,22},{15,23}} | collective-permute-start | bytes 4718600 | tf_op jit(solution)/shard_map/ppermute | solution.py:275
  88.2 47.6 %collective-permute-start.8 = (bf16[4,128,384]{2,1,0:T(8,128)(2,1)S(1)}, bf16[4,128,384]{2,1,0:T(8,128)(2,1)S(1)}, u32[]{:S(2)}, u32[]{:S(2)}) collective-permute-start(bf16[4,128,384]{2,1,0:T(8,128)(2,1)S(1)} %get-tuple-element.105), channel_id=1, source_target_pairs={{0,8},{1,9},{2,10},{3,11},{4,12},{5,13},{6,14},{7,15},{24,0},{25,1... | collective-permute-start | bytes 1179656 | tf_op jit(solution)/shard_map/ppermute | solution.py:275
  115.3 137.3 %collective-permute-start.44 = (bf16[16,128,384]{2,1,0:T(8,128)(2,1)}, bf16[16,128,384]{2,1,0:T(8,128)(2,1)S(1)}, u32[]{:S(2)}, u32[]{:S(2)}) collective-permute-start(bf16[16,128,384]{2,1,0:T(8,128)(2,1)} %get-tuple-element.189), channel_id=1, source_target_pairs={{16,0},{17,1},{18,2},{19,3},{20,4},{21,5},{22,6},{23,7},{24,16},{2... | collective-permute-start | bytes 4718600 | tf_op jit(solution)/shard_map/ppermute | solution.py:275
  144.1 33.3 %collective-permute-start.18 = (bf16[4,128,384]{2,1,0:T(8,128)(2,1)S(1)}, bf16[4,128,384]{2,1,0:T(8,128)(2,1)S(1)}, u32[]{:S(2)}, u32[]{:S(2)}) collective-permute-start(bf16[4,128,384]{2,1,0:T(8,128)(2,1)S(1)} %get-tuple-element.113), channel_id=1, source_target_pairs={{0,8},{1,9},{2,10},{3,11},{4,12},{5,13},{6,14},{7,15},{8,16},{9,17... | collective-permute-start | bytes 1179656 | tf_op jit(solution)/shard_map/ppermute | solution.py:275
  161.3 167.6 %collective-permute-start.54 = (bf16[16,128,384]{2,1,0:T(8,128)(2,1)}, bf16[16,128,384]{2,1,0:T(8,128)(2,1)S(1)}, u32[]{:S(2)}, u32[]{:S(2)}) collective-permute-start(bf16[16,128,384]{2,1,0:T(8,128)(2,1)} %get-tuple-element.190), channel_id=1, source_target_pairs={{16,8},{17,9},{18,10},{19,11},{20,12},{21,13},{22,14},{23,15}} | collective-permute-start | bytes 4718600 | tf_op jit(solution)/shard_map/ppermute | solution.py:275
  189.8 32.5 %collective-permute-start.28 = (bf16[4,128,384]{2,1,0:T(8,128)(2,1)S(1)}, bf16[4,128,384]{2,1,0:T(8,128)(2,1)S(1)}, u32[]{:S(2)}, u32[]{:S(2)}) collective-permute-start(bf16[4,128,384]{2,1,0:T(8,128)(2,1)S(1)} %get-tuple-element.121), channel_id=1, source_target_pairs={{0,8},{1,9},{2,10},{3,11},{4,12},{5,13},{6,14},{7,15},{8,16},{9,17... | collective-permute-start | bytes 1179656 | tf_op jit(solution)/shard_map/ppermute | solution.py:275
  214.1 31.5 %collective-permute-start.45 = (bf16[384,384]{1,0:T(8,128)(2,1)S(1)}, bf16[384,384]{1,0:T(8,128)(2,1)S(1)}, u32[]{:S(2)}, u32[]{:S(2)}) collective-permute-start(bf16[384,384]{1,0:T(8,128)(2,1)S(1)} %get-tuple-element.191), channel_id=1, source_target_pairs={{16,0},{17,1},{18,2},{19,3},{20,4},{21,5},{22,6},{23,7},{24,16},{2... | collective-permute-start | bytes 884744 | tf_op jit(solution)/shard_map/ppermute | solution.py:275
  223.4 69.8 %collective-permute-start.36 = (bf16[4,128,384]{2,1,0:T(8,128)(2,1)S(1)}, bf16[4,128,384]{2,1,0:T(8,128)(2,1)S(1)}, u32[]{:S(2)}, u32[]{:S(2)}) collective-permute-start(bf16[4,128,384]{2,1,0:T(8,128)(2,1)S(1)} %get-tuple-element.129), channel_id=1, source_target_pairs={{8,16},{9,17},{10,18},{11,19},{12,20},{13,21},{14,22},{15,23},{16,... | collective-permute-start | bytes 1179656 | tf_op jit(solution)/shard_map/ppermute | solution.py:275
  287.8 34.1 %collective-permute-start.55 = (bf16[384,384]{1,0:T(8,128)(2,1)S(1)}, bf16[384,384]{1,0:T(8,128)(2,1)S(1)}, u32[]{:S(2)}, u32[]{:S(2)}) collective-permute-start(bf16[384,384]{1,0:T(8,128)(2,1)S(1)} %get-tuple-element.192), channel_id=1, source_target_pairs={{16,8},{17,9},{18,10},{19,11},{20,12},{21,13},{22,14},{23,15}} | collective-permute-start | bytes 884744 | tf_op jit(solution)/shard_map/ppermute | solution.py:275
  300.3 61.6 %collective-permute-start.46 = (bf16[4,128,384]{2,1,0:T(8,128)(2,1)S(1)}, bf16[4,128,384]{2,1,0:T(8,128)(2,1)S(1)}, u32[]{:S(2)}, u32[]{:S(2)}) collective-permute-start(bf16[4,128,384]{2,1,0:T(8,128)(2,1)S(1)} %get-tuple-element.137), channel_id=1, source_target_pairs={{0,8},{1,9},{2,10},{3,11},{4,12},{5,13},{6,14},{7,15},{16,24},{17,... | collective-permute-start | bytes 1179656 | tf_op jit(solution)/shard_map/ppermute | solution.py:275
  307.8 28.1 %collective-permute-start.47 = (bf16[128,384]{1,0:T(8,128)(2,1)S(1)}, bf16[128,384]{1,0:T(8,128)(2,1)S(1)}, u32[]{:S(2)}, u32[]{:S(2)}) collective-permute-start(bf16[128,384]{1,0:T(8,128)(2,1)S(1)} %get-tuple-element.138), channel_id=1, source_target_pairs={{0,9},{1,10},{2,11},{3,12},{4,13},{5,14},{6,15},{7,8},{16,25},{17,... | collective-permute-start | bytes 294920 | tf_op jit(solution)/shard_map/ppermute | solution.py:275
  314.8 28.1 %collective-permute-start.48 = (bf16[128,384]{1,0:T(8,128)(2,1)S(1)}, bf16[128,384]{1,0:T(8,128)(2,1)S(1)}, u32[]{:S(2)}, u32[]{:S(2)}) collective-permute-start(bf16[128,384]{1,0:T(8,128)(2,1)S(1)} %get-tuple-element.139), channel_id=1, source_target_pairs={{0,10},{1,11},{2,12},{3,13},{4,14},{5,15},{6,8},{7,9},{16,26},{17,... | collective-permute-start | bytes 294920 | tf_op jit(solution)/shard_map/ppermute | solution.py:275
  321.9 28.1 %collective-permute-start.49 = (bf16[128,384]{1,0:T(8,128)(2,1)S(1)}, bf16[128,384]{1,0:T(8,128)(2,1)S(1)}, u32[]{:S(2)}, u32[]{:S(2)}) collective-permute-start(bf16[128,384]{1,0:T(8,128)(2,1)S(1)} %get-tuple-element.140), channel_id=1, source_target_pairs={{0,11},{1,12},{2,13},{3,14},{4,15},{5,8},{6,9},{7,10},{16,27},{17,... | collective-permute-start | bytes 294920 | tf_op jit(solution)/shard_map/ppermute | solution.py:275
  328.9 28.1 %collective-permute-start.50 = (bf16[128,384]{1,0:T(8,128)(2,1)S(1)}, bf16[128,384]{1,0:T(8,128)(2,1)S(1)}, u32[]{:S(2)}, u32[]{:S(2)}) collective-permute-start(bf16[128,384]{1,0:T(8,128)(2,1)S(1)} %get-tuple-element.141), channel_id=1, source_target_pairs={{0,12},{1,13},{2,14},{3,15},{4,8},{5,9},{6,10},{7,11},{16,28},{17,... | collective-permute-start | bytes 294920 | tf_op jit(solution)/shard_map/ppermute | solution.py:275
  430.0 69.0 %collective-permute-start.75 = (bf16[4,128,384]{2,1,0:T(8,128)(2,1)S(1)}, bf16[4,128,384]{2,1,0:T(8,128)(2,1)S(1)}, u32[]{:S(2)}, u32[]{:S(2)}) collective-permute-start(bf16[4,128,384]{2,1,0:T(8,128)(2,1)S(1)} %get-tuple-element.165), channel_id=1, source_target_pairs={{8,16},{9,17},{10,18},{11,19},{12,20},{13,21},{14,22},{15,23},{16,... | collective-permute-start | bytes 1179656 | tf_op jit(solution)/shard_map/ppermute | solution.py:275
  448.1 28.3 %collective-permute-start.76 = (bf16[128,384]{1,0:T(8,128)(2,1)S(1)}, bf16[128,384]{1,0:T(8,128)(2,1)S(1)}, u32[]{:S(2)}, u32[]{:S(2)}) collective-permute-start(bf16[128,384]{1,0:T(8,128)(2,1)S(1)} %get-tuple-element.166), channel_id=1, source_target_pairs={{8,17},{9,18},{10,19},{11,20},{12,21},{13,22},{14,23},{15,16},{16,... | collective-permute-start | bytes 294920 | tf_op jit(solution)/shard_map/ppermute | solution.py:275
  455.1 28.3 %collective-permute-start.77 = (bf16[128,384]{1,0:T(8,128)(2,1)S(1)}, bf16[128,384]{1,0:T(8,128)(2,1)S(1)}, u32[]{:S(2)}, u32[]{:S(2)}) collective-permute-start(bf16[128,384]{1,0:T(8,128)(2,1)S(1)} %get-tuple-element.167), channel_id=1, source_target_pairs={{8,18},{9,19},{10,20},{11,21},{12,22},{13,23},{14,16},{15,17},{16,... | collective-permute-start | bytes 294920 | tf_op jit(solution)/shard_map/ppermute | solution.py:275
  462.1 28.4 %collective-permute-start.78 = (bf16[128,384]{1,0:T(8,128)(2,1)S(1)}, bf16[128,384]{1,0:T(8,128)(2,1)S(1)}, u32[]{:S(2)}, u32[]{:S(2)}) collective-permute-start(bf16[128,384]{1,0:T(8,128)(2,1)S(1)} %get-tuple-element.168), channel_id=1, source_target_pairs={{8,19},{9,20},{10,21},{11,22},{12,23},{13,16},{14,17},{15,18},{16,... | collective-permute-start | bytes 294920 | tf_op jit(solution)/shard_map/ppermute | solution.py:275
  469.1 28.4 %collective-permute-start.79 = (bf16[128,384]{1,0:T(8,128)(2,1)S(1)}, bf16[128,384]{1,0:T(8,128)(2,1)S(1)}, u32[]{:S(2)}, u32[]{:S(2)}) collective-permute-start(bf16[128,384]{1,0:T(8,128)(2,1)S(1)} %get-tuple-element.169), channel_id=1, source_target_pairs={{8,20},{9,21},{10,22},{11,23},{12,16},{13,17},{14,18},{15,19},{16,... | collective-permute-start | bytes 294920 | tf_op jit(solution)/shard_map/ppermute | solution.py:275
  524.6 54.6 %collective-permute-start.83 = (bf16[512,96]{1,0:T(8,128)(2,1)}, bf16[512,96]{1,0:T(8,128)(2,1)S(1)}, u32[]{:S(2)}, u32[]{:S(2)}) collective-permute-start(bf16[512,96]{1,0:T(8,128)(2,1)} %copy-done.42), channel_id=1, source_target_pairs={{24,16},{25,17},{26,18},{27,19},{28,20},{29,21},{30,22},{31,23}} | collective-permute-start | bytes 294920 | tf_op jit(solution)/shard_map/ppermute | solution.py:275
  525.3 55.2 %collective-permute-start.84 = (bf16[512,96]{1,0:T(8,128)(2,1)}, bf16[512,96]{1,0:T(8,128)(2,1)S(1)}, u32[]{:S(2)}, u32[]{:S(2)}) collective-permute-start(bf16[512,96]{1,0:T(8,128)(2,1)} %copy-done.41), channel_id=1, source_target_pairs={{24,8},{25,9},{26,10},{27,11},{28,12},{29,13},{30,14},{31,15}} | collective-permute-start | bytes 294920 | tf_op jit(solution)/shard_map/ppermute | solution.py:275
  526.0 54.5 %collective-permute-start.85 = (bf16[512,96]{1,0:T(8,128)(2,1)}, bf16[512,96]{1,0:T(8,128)(2,1)S(1)}, u32[]{:S(2)}, u32[]{:S(2)}) collective-permute-start(bf16[512,96]{1,0:T(8,128)(2,1)} %copy-done.40), channel_id=1, source_target_pairs={{24,0},{25,1},{26,2},{27,3},{28,4},{29,5},{30,6},{31,7}} | collective-permute-start | bytes 294920 | tf_op jit(solution)/shard_map/ppermute | solution.py:275
  547.9 32.7 %collective-permute-start.94 = (bf16[512,96]{1,0:T(8,128)(2,1)S(1)}, bf16[512,96]{1,0:T(8,128)(2,1)S(1)}, u32[]{:S(2)}, u32[]{:S(2)}) collective-permute-start(bf16[512,96]{1,0:T(8,128)(2,1)S(1)} %get-tuple-element.185), channel_id=1, source_target_pairs={{24,16},{25,17},{26,18},{27,19},{28,20},{29,21},{30,22},{31,23}} | collective-permute-start | bytes 294920 | tf_op jit(solution)/shard_map/ppermute | solution.py:275
  (124 other events, 1688.6 us)

commit v4 on v3

--- a/solution.py
+++ b/solution.py
@@ -139,13 +139,9 @@
             for row in range(group_blocks):
                 tile_copy(row).wait()
                 base = (first_row + row) * fanout
-                total = None
-                for tile in range(0, fanout, 2):
-                    span = range(tile, min(tile + 2, fanout))
-                    left = jnp.concatenate([tiles[row, t] for t in span], 1)
-                    right = jnp.concatenate([table[columns[base + t]] for t in span], 0)
-                    term = jnp.dot(left, right, preferred_element_type=jnp.float32)
-                    total = term if total is None else total + term
+                left = jnp.concatenate([tiles[row, t] for t in range(fanout)], 1)
+                right = jnp.concatenate([table[columns[base + t]] for t in range(fanout)], 0)
+                total = jnp.dot(left, right, preferred_element_type=jnp.float32)
                 start = initial[row * block : (row + 1) * block].astype(jnp.float32)
                 mixed = ((1.0 - alpha_mix) * total + alpha_mix * start).astype(jnp.bfloat16)
                 product = jnp.dot(mixed, stored_weight[...], preferred_element_type=jnp.float32)
@@ -272,6 +268,13 @@
         routes = [
             (a * parts + q, b * parts + (q + distance) % parts) for a, b in pairs for q in range(parts)
         ]
+        idle_from = [s for s in range(sections) if s not in [a for a, b in pairs]]
+        idle_to = [s for s in range(sections) if s not in [b for a, b in pairs]]
+        both = [s for s in idle_from if s in idle_to]
+        fill = [(s, s) for s in both] + list(
+            zip([s for s in idle_from if s not in both], [s for s in idle_to if s not in both])
+        )
+        routes += [(a * parts + q, b * parts + q) for a, b in fill for q in range(parts)]
         return lax.ppermute(value, ("section", "dom"), routes)
 
     routes = {}

time: 597 us -> 558 us (0.935)
  starting transfers between devices: 436 us -> 411 us
  waiting for transfers between devices: 55.8 us -> 41.9 us
    ppermute x97, starting transfers between devices: 436 us -> 411 us  [move(): return lax.ppermute(value, ('section', 'dom'), routes)]
    ppermute x97, waiting for transfers between devices: 55.8 us -> 41.9 us  [move(): return lax.ppermute(value, ('section', 'dom'), routes)]
  transfers between devices with their start and end apart: 97 -> 97, of which waited for: 17 -> 14; matrix products, arithmetic and copies ran while one was open for 0% -> 0% of each run, Pallas kernels for 6% -> 7%
where the time goes in v4:
time: 558 us; the launch traced here: 548 us
  starting transfers between devices  411 us (74%)
  Pallas kernels  56.4 us (10%)
  waiting for transfers between devices  41.9 us (8%)
  local copies, waits for them, and re-layouts  35.4 us (6%)
    ppermute x97, starting transfers between devices, move(): return lax.ppermute(value, ('section', 'dom'), routes)  411 us
    pallas_call x11, Pallas kernels, run_tick(): pl.pallas_call(functools.partial(tick_kernel, plan), grid_spec=pltpu.Pref...  56.4 us
    ppermute x97, waiting for transfers between devices, move(): return lax.ppermute(value, ('section', 'dom'), routes)  41.9 us
    unnamed x102, local copies, waits for them, and re-layouts  30.1 us
  transfers between devices with their start and end apart: 97, of which 14 were waited for; matrix products, arithmetic and copies ran while one was open for 0% of the time, Pallas kernels for 7%

profile of v4, /device:TPU:0, one launch (start us, length us, event | category | flops | bytes accessed | tf_op | source)
XLA Modules:
  0.0 547.5 jit_solution(7597026974566007953)
XLA Ops:
  4.2 8.3 %collective-permute-start.16 = (bf16[16,128,384]{2,1,0:T(8,128)(2,1)}, bf16[16,128,384]{2,1,0:T(8,128)(2,1)}, u32[]{:S(2)}, u32[]{:S(2)}) collective-permute-start(bf16[16,128,384]{2,1,0:T(8,128)(2,1)} %get-tuple-element.190), channel_id=1, source_target_pairs={{0,8},{1,9},{2,10},{3,11},{4,12},{5,13},{6,14},{7,15},{8,24},{9,25... | collective-permute-start | bytes 4718600 | tf_op jit(solution)/shard_map/ppermute | solution.py:278
  12.5 13.3 %collective-permute-start.26 = (bf16[16,128,384]{2,1,0:T(8,128)(2,1)}, bf16[16,128,384]{2,1,0:T(8,128)(2,1)}, u32[]{:S(2)}, u32[]{:S(2)}) collective-permute-start(bf16[16,128,384]{2,1,0:T(8,128)(2,1)} %get-tuple-element.189), channel_id=1, source_target_pairs={{8,16},{9,17},{10,18},{11,19},{12,20},{13,21},{14,22},{15,23},{0,0... | collective-permute-start | bytes 4718600 | tf_op jit(solution)/shard_map/ppermute | solution.py:278
  33.1 8.1 %collective-permute-start.1 = (bf16[128,384]{1,0:T(8,128)(2,1)S(1)}, bf16[128,384]{1,0:T(8,128)(2,1)S(1)}, u32[]{:S(2)}, u32[]{:S(2)}) collective-permute-start(bf16[128,384]{1,0:T(8,128)(2,1)S(1)} %get-tuple-element.98), channel_id=1, source_target_pairs={{24,1},{25,2},{26,3},{27,4},{28,5},{29,6},{30,7},{31,0},{8,8},{9,9... | collective-permute-start | bytes 294920 | tf_op jit(solution)/shard_map/ppermute | solution.py:278
  41.2 6.8 %collective-permute-start.2 = (bf16[128,384]{1,0:T(8,128)(2,1)S(1)}, bf16[128,384]{1,0:T(8,128)(2,1)S(1)}, u32[]{:S(2)}, u32[]{:S(2)}) collective-permute-start(bf16[128,384]{1,0:T(8,128)(2,1)S(1)} %get-tuple-element.99), channel_id=1, source_target_pairs={{24,2},{25,3},{26,4},{27,5},{28,6},{29,7},{30,0},{31,1},{8,8},{9,9... | collective-permute-start | bytes 294920 | tf_op jit(solution)/shard_map/ppermute | solution.py:278
  48.0 6.8 %collective-permute-start.3 = (bf16[128,384]{1,0:T(8,128)(2,1)S(1)}, bf16[128,384]{1,0:T(8,128)(2,1)S(1)}, u32[]{:S(2)}, u32[]{:S(2)}) collective-permute-start(bf16[128,384]{1,0:T(8,128)(2,1)S(1)} %get-tuple-element.100), channel_id=1, source_target_pairs={{24,3},{25,4},{26,5},{27,6},{28,7},{29,0},{30,1},{31,2},{8,8},{9,9... | collective-permute-start | bytes 294920 | tf_op jit(solution)/shard_map/ppermute | solution.py:278
  61.5 6.8 %collective-permute-start.5 = (bf16[128,384]{1,0:T(8,128)(2,1)S(1)}, bf16[128,384]{1,0:T(8,128)(2,1)S(1)}, u32[]{:S(2)}, u32[]{:S(2)}) collective-permute-start(bf16[128,384]{1,0:T(8,128)(2,1)S(1)} %get-tuple-element.102), channel_id=1, source_target_pairs={{24,5},{25,6},{26,7},{27,0},{28,1},{29,2},{30,3},{31,4},{8,8},{9,9... | collective-permute-start | bytes 294920 | tf_op jit(solution)/shard_map/ppermute | solution.py:278
  77.6 6.8 %collective-permute-start.7 = (bf16[128,384]{1,0:T(8,128)(2,1)S(1)}, bf16[128,384]{1,0:T(8,128)(2,1)S(1)}, u32[]{:S(2)}, u32[]{:S(2)}) collective-permute-start(bf16[128,384]{1,0:T(8,128)(2,1)S(1)} %get-tuple-element.104), channel_id=1, source_target_pairs={{24,7},{25,0},{26,1},{27,2},{28,3},{29,4},{30,5},{31,6},{8,8},{9,9... | collective-permute-start | bytes 294920 | tf_op jit(solution)/shard_map/ppermute | solution.py:278
  89.2 7.0 %tick.12 = (bf16[4,128,384]{2,1,0:T(8,128)(2,1)S(1)}, bf16[128,384]{1,0:T(8,128)(2,1)S(1)}, bf16[128,384]{1,0:T(8,128)(2,1)S(1)}, bf16[128,384]{1,0:T(8,128)(2,1...) custom-call(s32[2]{0:T(128)S(1)} %pad_add_fusion.info, ...), custom_call_target="tpu_custom_call" | custom-call | flops 1358954496 | bytes 12582913 | tf_op jit(solution)/shard_map/tick/pallas_call | solution.py:222
  116.8 6.9 %collective-permute-start.12 = (bf16[128,384]{1,0:T(8,128)(2,1)S(1)}, bf16[128,384]{1,0:T(8,128)(2,1)S(1)}, u32[]{:S(2)}, u32[]{:S(2)}) collective-permute-start(bf16[128,384]{1,0:T(8,128)(2,1)S(1)} %get-tuple-element.109), channel_id=1, source_target_pairs={{0,12},{1,13},{2,14},{3,15},{4,8},{5,9},{6,10},{7,11},{24,4},{25,5... | collective-permute-start | bytes 294920 | tf_op jit(solution)/shard_map/ppermute | solution.py:278
  123.8 6.8 %collective-permute-start.13 = (bf16[128,384]{1,0:T(8,128)(2,1)S(1)}, bf16[128,384]{1,0:T(8,128)(2,1)S(1)}, u32[]{:S(2)}, u32[]{:S(2)}) collective-permute-start(bf16[128,384]{1,0:T(8,128)(2,1)S(1)} %get-tuple-element.110), channel_id=1, source_target_pairs={{0,13},{1,14},{2,15},{3,8},{4,9},{5,10},{6,11},{7,12},{24,5},{25,6... | collective-permute-start | bytes 294920 | tf_op jit(solution)/shard_map/ppermute | solution.py:278
  144.1 7.0 %collective-permute-start.15 = (bf16[128,384]{1,0:T(8,128)(2,1)S(1)}, bf16[128,384]{1,0:T(8,128)(2,1)S(1)}, u32[]{:S(2)}, u32[]{:S(2)}) collective-permute-start(bf16[128,384]{1,0:T(8,128)(2,1)S(1)} %get-tuple-element.112), channel_id=1, source_target_pairs={{0,15},{1,8},{2,9},{3,10},{4,11},{5,12},{6,13},{7,14},{24,7},{25,0... | collective-permute-start | bytes 294920 | tf_op jit(solution)/shard_map/ppermute | solution.py:278
  157.8 8.3 %tick.13 = (bf16[4,128,384]{2,1,0:T(8,128)(2,1)S(1)}, bf16[128,384]{1,0:T(8,128)(2,1)S(1)}, bf16[128,384]{1,0:T(8,128)(2,1)S(1)}, bf16[128,384]{1,0:T(8,128)(2,1...) custom-call(s32[2]{0:T(128)S(1)} %pad_add_fusion.info, ...), custom_call_target="tpu_custom_call" | custom-call | flops 1358954496 | bytes 12582913 | tf_op jit(solution)/shard_map/tick/pallas_call | solution.py:222
  192.4 9.7 %tick.14 = (bf16[4,128,384]{2,1,0:T(8,128)(2,1)S(1)}, bf16[128,384]{1,0:T(8,128)(2,1)S(1)}, bf16[128,384]{1,0:T(8,128)(2,1)S(1)}, bf16[128,384]{1,0:T(8,128)(2,1...) custom-call(s32[2]{0:T(128)S(1)} %pad_add_fusion.info, ...), custom_call_target="tpu_custom_call" | custom-call | flops 1358954496 | bytes 12582913 | tf_op jit(solution)/shard_map/tick/pallas_call | solution.py:222
  202.1 9.5 %collective-permute-start.29 = (bf16[128,384]{1,0:T(8,128)(2,1)S(1)}, bf16[128,384]{1,0:T(8,128)(2,1)S(1)}, u32[]{:S(2)}, u32[]{:S(2)}) collective-permute-start(bf16[128,384]{1,0:T(8,128)(2,1)S(1)} %get-tuple-element.122), channel_id=1, source_target_pairs={{0,9},{1,10},{2,11},{3,12},{4,13},{5,14},{6,15},{7,8},{8,17},{9,18... | collective-permute-start | bytes 294920 | tf_op jit(solution)/shard_map/ppermute | solution.py:278
  234.0 8.6 %collective-permute-start.45 = (bf16[384,384]{1,0:T(8,128)(2,1)S(1)}, bf16[384,384]{1,0:T(8,128)(2,1)S(1)}, u32[]{:S(2)}, u32[]{:S(2)}) collective-permute-start(bf16[384,384]{1,0:T(8,128)(2,1)S(1)} %get-tuple-element.191), channel_id=1, source_target_pairs={{16,0},{17,1},{18,2},{19,3},{20,4},{21,5},{22,6},{23,7},{24,16},{2... | collective-permute-start | bytes 884744 | tf_op jit(solution)/shard_map/ppermute | solution.py:278
  243.8 8.2 %collective-permute-start.36 = (bf16[4,128,384]{2,1,0:T(8,128)(2,1)S(1)}, bf16[4,128,384]{2,1,0:T(8,128)(2,1)S(1)}, u32[]{:S(2)}, u32[]{:S(2)}) collective-permute-start(bf16[4,128,384]{2,1,0:T(8,128)(2,1)S(1)} %get-tuple-element.129), channel_id=1, source_target_pairs={{8,16},{9,17},{10,18},{11,19},{12,20},{13,21},{14,22},{15,23},{16,... | collective-permute-start | bytes 1179656 | tf_op jit(solution)/shard_map/ppermute | solution.py:278
  296.8 7.0 %tick.16 = (bf16[4,128,384]{2,1,0:T(8,128)(2,1)S(1)}, bf16[128,384]{1,0:T(8,128)(2,1)S(1)}, bf16[128,384]{1,0:T(8,128)(2,1)S(1)}, bf16[128,384]{1,0:T(8,128)(2,1...) custom-call(s32[2]{0:T(128)S(1)} %pad_add_fusion.info, ...), custom_call_target="tpu_custom_call" | custom-call | flops 1358954496 | bytes 12582913 | tf_op jit(solution)/shard_map/tick/pallas_call | solution.py:222
  349.7 8.5 %tick.17 = (bf16[4,128,384]{2,1,0:T(8,128)(2,1)S(1)}, bf16[128,384]{1,0:T(8,128)(2,1)S(1)}, bf16[128,384]{1,0:T(8,128)(2,1)S(1)}, bf16[128,384]{1,0:T(8,128)(2,1...) custom-call(s32[2]{0:T(128)S(1)} %pad_add_fusion.info, ...), custom_call_target="tpu_custom_call" | custom-call | flops 1358954496 | bytes 12582913 | tf_op jit(solution)/shard_map/tick/pallas_call | solution.py:222
  377.2 9.5 %tick.18 = (bf16[4,128,384]{2,1,0:T(8,128)(2,1)S(1)}, bf16[128,384]{1,0:T(8,128)(2,1)S(1)}, bf16[128,384]{1,0:T(8,128)(2,1)S(1)}, bf16[128,384]{1,0:T(8,128)(2,1...) custom-call(s32[2]{0:T(128)S(1)} %pad_add_fusion.info, ...), custom_call_target="tpu_custom_call" | custom-call | flops 1358954496 | bytes 12582913 | tf_op jit(solution)/shard_map/tick/pallas_call | solution.py:222
  413.8 36.3 %collective-permute-start.82 = (bf16[128,384]{1,0:T(8,128)(2,1)S(1)}, bf16[128,384]{1,0:T(8,128)(2,1)S(1)}, u32[]{:S(2)}, u32[]{:S(2)}) collective-permute-start(bf16[128,384]{1,0:T(8,128)(2,1)S(1)} %get-tuple-element.172), channel_id=1, source_target_pairs={{8,23},{9,16},{10,17},{11,18},{12,19},{13,20},{14,21},{15,22},{16,... | collective-permute-start | bytes 294920 | tf_op jit(solution)/shard_map/ppermute | solution.py:278
  461.2 12.1 %collective-permute-start.74 = (bf16[512,96]{1,0:T(8,128)(2,1)}, bf16[512,96]{1,0:T(8,128)(2,1)}, u32[]{:S(2)}, u32[]{:S(2)}) collective-permute-start(bf16[512,96]{1,0:T(8,128)(2,1)} %get-tuple-element.163), channel_id=1, source_target_pairs={{24,0},{25,1},{26,2},{27,3},{28,4},{29,5},{30,6},{31,7},{8,8},{9,9... | collective-permute-start | bytes 294920 | tf_op jit(solution)/shard_map/ppermute | solution.py:278
  490.7 11.7 %collective-permute-start.85 = (bf16[512,96]{1,0:T(8,128)(2,1)}, bf16[512,96]{1,0:T(8,128)(2,1)S(1)}, u32[]{:S(2)}, u32[]{:S(2)}) collective-permute-start(bf16[512,96]{1,0:T(8,128)(2,1)} %copy-done.40), channel_id=1, source_target_pairs={{24,0},{25,1},{26,2},{27,3},{28,4},{29,5},{30,6},{31,7},{8,8},{9,9... | collective-permute-start | bytes 294920 | tf_op jit(solution)/shard_map/ppermute | solution.py:278
  523.7 10.7 %collective-permute-start.95 = (bf16[512,96]{1,0:T(8,128)(2,1)S(1)}, bf16[512,96]{1,0:T(8,128)(2,1)S(1)}, u32[]{:S(2)}, u32[]{:S(2)}) collective-permute-start(bf16[512,96]{1,0:T(8,128)(2,1)S(1)} %get-tuple-element.186), channel_id=1, source_target_pairs={{24,8},{25,9},{26,10},{27,11},{28,12},{29,13},{30,14},{31,15},{0,0... | collective-permute-start | bytes 294920 | tf_op jit(solution)/shard_map/ppermute | solution.py:278
  534.4 7.4 %collective-permute-start.96 = (bf16[512,96]{1,0:T(8,128)(2,1)S(1)}, bf16[512,96]{1,0:T(8,128)(2,1)S(1)}, u32[]{:S(2)}, u32[]{:S(2)}) collective-permute-start(bf16[512,96]{1,0:T(8,128)(2,1)S(1)} %get-tuple-element.187), channel_id=1, source_target_pairs={{24,0},{25,1},{26,2},{27,3},{28,4},{29,5},{30,6},{31,7},{8,8},{9,9... | collective-permute-start | bytes 294920 | tf_op jit(solution)/shard_map/ppermute | solution.py:278
  (294 shorter events, 313.6 us)
Async XLA Ops:
  4.2 153.6 %collective-permute-start.16 = (bf16[16,128,384]{2,1,0:T(8,128)(2,1)}, bf16[16,128,384]{2,1,0:T(8,128)(2,1)}, u32[]{:S(2)}, u32[]{:S(2)}) collective-permute-start(bf16[16,128,384]{2,1,0:T(8,128)(2,1)} %get-tuple-element.190), channel_id=1, source_target_pairs={{0,8},{1,9},{2,10},{3,11},{4,12},{5,13},{6,14},{7,15},{8,24},{9,25... | collective-permute-start | bytes 4718600 | tf_op jit(solution)/shard_map/ppermute | solution.py:278
  12.5 157.2 %collective-permute-start.26 = (bf16[16,128,384]{2,1,0:T(8,128)(2,1)}, bf16[16,128,384]{2,1,0:T(8,128)(2,1)}, u32[]{:S(2)}, u32[]{:S(2)}) collective-permute-start(bf16[16,128,384]{2,1,0:T(8,128)(2,1)} %get-tuple-element.189), channel_id=1, source_target_pairs={{8,16},{9,17},{10,18},{11,19},{12,20},{13,21},{14,22},{15,23},{0,0... | collective-permute-start | bytes 4718600 | tf_op jit(solution)/shard_map/ppermute | solution.py:278
  84.4 23.3 %collective-permute-start.17 = (bf16[384,384]{1,0:T(8,128)(2,1)S(1)}, bf16[384,384]{1,0:T(8,128)(2,1)S(1)}, u32[]{:S(2)}, u32[]{:S(2)}) collective-permute-start(bf16[384,384]{1,0:T(8,128)(2,1)S(1)} %get-tuple-element.192), channel_id=1, source_target_pairs={{0,8},{1,9},{2,10},{3,11},{4,12},{5,13},{6,14},{7,15},{8,24},{9,25... | collective-permute-start | bytes 884744 | tf_op jit(solution)/shard_map/ppermute | solution.py:278
  114.5 43.2 %collective-permute-start.8 = (bf16[4,128,384]{2,1,0:T(8,128)(2,1)S(1)}, bf16[4,128,384]{2,1,0:T(8,128)(2,1)S(1)}, u32[]{:S(2)}, u32[]{:S(2)}) collective-permute-start(bf16[4,128,384]{2,1,0:T(8,128)(2,1)S(1)} %get-tuple-element.105), channel_id=1, source_target_pairs={{0,8},{1,9},{2,10},{3,11},{4,12},{5,13},{6,14},{7,15},{24,0},{25,1... | collective-permute-start | bytes 1179656 | tf_op jit(solution)/shard_map/ppermute | solution.py:278
  137.3 126.0 %collective-permute-start.44 = (bf16[16,128,384]{2,1,0:T(8,128)(2,1)}, bf16[16,128,384]{2,1,0:T(8,128)(2,1)S(1)}, u32[]{:S(2)}, u32[]{:S(2)}) collective-permute-start(bf16[16,128,384]{2,1,0:T(8,128)(2,1)} %get-tuple-element.189), channel_id=1, source_target_pairs={{16,0},{17,1},{18,2},{19,3},{20,4},{21,5},{22,6},{23,7},{24,16},{2... | collective-permute-start | bytes 4718600 | tf_op jit(solution)/shard_map/ppermute | solution.py:278
  166.1 26.4 %collective-permute-start.18 = (bf16[4,128,384]{2,1,0:T(8,128)(2,1)S(1)}, bf16[4,128,384]{2,1,0:T(8,128)(2,1)S(1)}, u32[]{:S(2)}, u32[]{:S(2)}) collective-permute-start(bf16[4,128,384]{2,1,0:T(8,128)(2,1)S(1)} %get-tuple-element.113), channel_id=1, source_target_pairs={{0,8},{1,9},{2,10},{3,11},{4,12},{5,13},{6,14},{7,15},{8,16},{9,17... | collective-permute-start | bytes 1179656 | tf_op jit(solution)/shard_map/ppermute | solution.py:278
  179.1 142.7 %collective-permute-start.54 = (bf16[16,128,384]{2,1,0:T(8,128)(2,1)}, bf16[16,128,384]{2,1,0:T(8,128)(2,1)S(1)}, u32[]{:S(2)}, u32[]{:S(2)}) collective-permute-start(bf16[16,128,384]{2,1,0:T(8,128)(2,1)} %get-tuple-element.190), channel_id=1, source_target_pairs={{16,8},{17,9},{18,10},{19,11},{20,12},{21,13},{22,14},{23,15},{0,0... | collective-permute-start | bytes 4718600 | tf_op jit(solution)/shard_map/ppermute | solution.py:278
  211.6 31.0 %collective-permute-start.28 = (bf16[4,128,384]{2,1,0:T(8,128)(2,1)S(1)}, bf16[4,128,384]{2,1,0:T(8,128)(2,1)S(1)}, u32[]{:S(2)}, u32[]{:S(2)}) collective-permute-start(bf16[4,128,384]{2,1,0:T(8,128)(2,1)S(1)} %get-tuple-element.121), channel_id=1, source_target_pairs={{0,8},{1,9},{2,10},{3,11},{4,12},{5,13},{6,14},{7,15},{8,16},{9,17... | collective-permute-start | bytes 1179656 | tf_op jit(solution)/shard_map/ppermute | solution.py:278
  234.0 23.5 %collective-permute-start.45 = (bf16[384,384]{1,0:T(8,128)(2,1)S(1)}, bf16[384,384]{1,0:T(8,128)(2,1)S(1)}, u32[]{:S(2)}, u32[]{:S(2)}) collective-permute-start(bf16[384,384]{1,0:T(8,128)(2,1)S(1)} %get-tuple-element.191), channel_id=1, source_target_pairs={{16,0},{17,1},{18,2},{19,3},{20,4},{21,5},{22,6},{23,7},{24,16},{2... | collective-permute-start | bytes 884744 | tf_op jit(solution)/shard_map/ppermute | solution.py:278
  243.8 53.0 %collective-permute-start.36 = (bf16[4,128,384]{2,1,0:T(8,128)(2,1)S(1)}, bf16[4,128,384]{2,1,0:T(8,128)(2,1)S(1)}, u32[]{:S(2)}, u32[]{:S(2)}) collective-permute-start(bf16[4,128,384]{2,1,0:T(8,128)(2,1)S(1)} %get-tuple-element.129), channel_id=1, source_target_pairs={{8,16},{9,17},{10,18},{11,19},{12,20},{13,21},{14,22},{15,23},{16,... | collective-permute-start | bytes 1179656 | tf_op jit(solution)/shard_map/ppermute | solution.py:278
  291.9 24.2 %collective-permute-start.55 = (bf16[384,384]{1,0:T(8,128)(2,1)S(1)}, bf16[384,384]{1,0:T(8,128)(2,1)S(1)}, u32[]{:S(2)}, u32[]{:S(2)}) collective-permute-start(bf16[384,384]{1,0:T(8,128)(2,1)S(1)} %get-tuple-element.192), channel_id=1, source_target_pairs={{16,8},{17,9},{18,10},{19,11},{20,12},{21,13},{22,14},{23,15},{0,0... | collective-permute-start | bytes 884744 | tf_op jit(solution)/shard_map/ppermute | solution.py:278
  303.8 45.9 %collective-permute-start.46 = (bf16[4,128,384]{2,1,0:T(8,128)(2,1)S(1)}, bf16[4,128,384]{2,1,0:T(8,128)(2,1)S(1)}, u32[]{:S(2)}, u32[]{:S(2)}) collective-permute-start(bf16[4,128,384]{2,1,0:T(8,128)(2,1)S(1)} %get-tuple-element.137), channel_id=1, source_target_pairs={{0,8},{1,9},{2,10},{3,11},{4,12},{5,13},{6,14},{7,15},{16,24},{17,... | collective-permute-start | bytes 1179656 | tf_op jit(solution)/shard_map/ppermute | solution.py:278
  303.9 23.7 %collective-permute-start.47 = (bf16[128,384]{1,0:T(8,128)(2,1)S(1)}, bf16[128,384]{1,0:T(8,128)(2,1)S(1)}, u32[]{:S(2)}, u32[]{:S(2)}) collective-permute-start(bf16[128,384]{1,0:T(8,128)(2,1)S(1)} %get-tuple-element.138), channel_id=1, source_target_pairs={{0,9},{1,10},{2,11},{3,12},{4,13},{5,14},{6,15},{7,8},{16,25},{17,... | collective-permute-start | bytes 294920 | tf_op jit(solution)/shard_map/ppermute | solution.py:278
  409.0 42.6 %collective-permute-start.75 = (bf16[4,128,384]{2,1,0:T(8,128)(2,1)S(1)}, bf16[4,128,384]{2,1,0:T(8,128)(2,1)S(1)}, u32[]{:S(2)}, u32[]{:S(2)}) collective-permute-start(bf16[4,128,384]{2,1,0:T(8,128)(2,1)S(1)} %get-tuple-element.165), channel_id=1, source_target_pairs={{8,16},{9,17},{10,18},{11,19},{12,20},{13,21},{14,22},{15,23},{16,... | collective-permute-start | bytes 1179656 | tf_op jit(solution)/shard_map/ppermute | solution.py:278
  411.7 38.4 %collective-permute-start.79 = (bf16[128,384]{1,0:T(8,128)(2,1)S(1)}, bf16[128,384]{1,0:T(8,128)(2,1)S(1)}, u32[]{:S(2)}, u32[]{:S(2)}) collective-permute-start(bf16[128,384]{1,0:T(8,128)(2,1)S(1)} %get-tuple-element.169), channel_id=1, source_target_pairs={{8,20},{9,21},{10,22},{11,23},{12,16},{13,17},{14,18},{15,19},{16,... | collective-permute-start | bytes 294920 | tf_op jit(solution)/shard_map/ppermute | solution.py:278
  412.4 38.4 %collective-permute-start.80 = (bf16[128,384]{1,0:T(8,128)(2,1)S(1)}, bf16[128,384]{1,0:T(8,128)(2,1)S(1)}, u32[]{:S(2)}, u32[]{:S(2)}) collective-permute-start(bf16[128,384]{1,0:T(8,128)(2,1)S(1)} %get-tuple-element.170), channel_id=1, source_target_pairs={{8,21},{9,22},{10,23},{11,16},{12,17},{13,18},{14,19},{15,20},{16,... | collective-permute-start | bytes 294920 | tf_op jit(solution)/shard_map/ppermute | solution.py:278
  413.1 38.4 %collective-permute-start.81 = (bf16[128,384]{1,0:T(8,128)(2,1)S(1)}, bf16[128,384]{1,0:T(8,128)(2,1)S(1)}, u32[]{:S(2)}, u32[]{:S(2)}) collective-permute-start(bf16[128,384]{1,0:T(8,128)(2,1)S(1)} %get-tuple-element.171), channel_id=1, source_target_pairs={{8,22},{9,23},{10,16},{11,17},{12,18},{13,19},{14,20},{15,21},{16,... | collective-permute-start | bytes 294920 | tf_op jit(solution)/shard_map/ppermute | solution.py:278
  413.8 37.7 %collective-permute-start.82 = (bf16[128,384]{1,0:T(8,128)(2,1)S(1)}, bf16[128,384]{1,0:T(8,128)(2,1)S(1)}, u32[]{:S(2)}, u32[]{:S(2)}) collective-permute-start(bf16[128,384]{1,0:T(8,128)(2,1)S(1)} %get-tuple-element.172), channel_id=1, source_target_pairs={{8,23},{9,16},{10,17},{11,18},{12,19},{13,20},{14,21},{15,22},{16,... | collective-permute-start | bytes 294920 | tf_op jit(solution)/shard_map/ppermute | solution.py:278
  450.2 25.3 %collective-permute-start.72 = (bf16[512,96]{1,0:T(8,128)(2,1)S(1)}, bf16[512,96]{1,0:T(8,128)(2,1)S(1)}, u32[]{:S(2)}, u32[]{:S(2)}) collective-permute-start(bf16[512,96]{1,0:T(8,128)(2,1)S(1)} %get-tuple-element.161), channel_id=1, source_target_pairs={{24,16},{25,17},{26,18},{27,19},{28,20},{29,21},{30,22},{31,23},{0... | collective-permute-start | bytes 294920 | tf_op jit(solution)/shard_map/ppermute | solution.py:278
  450.9 26.8 %collective-permute-start.73 = (bf16[512,96]{1,0:T(8,128)(2,1)S(1)}, bf16[512,96]{1,0:T(8,128)(2,1)S(1)}, u32[]{:S(2)}, u32[]{:S(2)}) collective-permute-start(bf16[512,96]{1,0:T(8,128)(2,1)S(1)} %get-tuple-element.162), channel_id=1, source_target_pairs={{24,8},{25,9},{26,10},{27,11},{28,12},{29,13},{30,14},{31,15},{0,0... | collective-permute-start | bytes 294920 | tf_op jit(solution)/shard_map/ppermute | solution.py:278
  456.8 45.7 %collective-permute-start.86 = (bf16[4,128,384]{2,1,0:T(8,128)(2,1)}, bf16[4,128,384]{2,1,0:T(8,128)(2,1)}, u32[]{:S(2)}, u32[]{:S(2)}) collective-permute-start(bf16[4,128,384]{2,1,0:T(8,128)(2,1)} %get-tuple-element.177), channel_id=1, source_target_pairs={{16,24},{17,25},{18,26},{19,27},{20,28},{21,29},{22,30},{23,31},{0... | collective-permute-start | bytes 1179656 | tf_op jit(solution)/shard_map/ppermute | solution.py:278
  487.6 46.8 %collective-permute-start.83 = (bf16[512,96]{1,0:T(8,128)(2,1)}, bf16[512,96]{1,0:T(8,128)(2,1)S(1)}, u32[]{:S(2)}, u32[]{:S(2)}) collective-permute-start(bf16[512,96]{1,0:T(8,128)(2,1)} %copy-done.42), channel_id=1, source_target_pairs={{24,16},{25,17},{26,18},{27,19},{28,20},{29,21},{30,22},{31,23},{0... | collective-permute-start | bytes 294920 | tf_op jit(solution)/shard_map/ppermute | solution.py:278
  489.1 52.7 %collective-permute-start.84 = (bf16[512,96]{1,0:T(8,128)(2,1)}, bf16[512,96]{1,0:T(8,128)(2,1)S(1)}, u32[]{:S(2)}, u32[]{:S(2)}) collective-permute-start(bf16[512,96]{1,0:T(8,128)(2,1)} %copy-done.41), channel_id=1, source_target_pairs={{24,8},{25,9},{26,10},{27,11},{28,12},{29,13},{30,14},{31,15},{0,0... | collective-permute-start | bytes 294920 | tf_op jit(solution)/shard_map/ppermute | solution.py:278
  490.7 51.1 %collective-permute-start.85 = (bf16[512,96]{1,0:T(8,128)(2,1)}, bf16[512,96]{1,0:T(8,128)(2,1)S(1)}, u32[]{:S(2)}, u32[]{:S(2)}) collective-permute-start(bf16[512,96]{1,0:T(8,128)(2,1)} %copy-done.40), channel_id=1, source_target_pairs={{24,0},{25,1},{26,2},{27,3},{28,4},{29,5},{30,6},{31,7},{8,8},{9,9... | collective-permute-start | bytes 294920 | tf_op jit(solution)/shard_map/ppermute | solution.py:278
  (124 other events, 1532.2 us)

commit v5 on v2

--- a/solution.py
+++ b/solution.py
@@ -10,11 +10,11 @@
 
 alpha_mix = 0.1
 lambda_decay = 0.5
-vmem_bytes = 48 * 1024 * 1024
+vmem_bytes = 20 * 1024 * 1024
 
 
 def group_streams(groups):
-    return [[group] for group in range(groups)]
+    return [list(range(groups - 1)), [groups - 1]]
 
 
 def params():

time: 543 us -> 505 us (0.930)
  starting transfers between devices: 132 us -> 48.8 us
  blocking collectives: 191 us -> 260 us
  Pallas kernels: 139 us -> 96.4 us
  local copies, waits for them, and re-layouts: 48.5 us -> 73.2 us
    all_to_all x2 -> x6, blocking collectives: 25.7 us -> 109 us  [exchange(): return lax.all_to_all(value, 'dom', split_axis=0, concat_axis=0, tiled=True)]
    all_to_all x22 -> x10, starting transfers between devices: 121 us -> 40.9 us  [exchange(): return lax.all_to_all(value, 'dom', split_axis=0, concat_axis=0, tiled=True)]
    pallas_call x24 -> x16, Pallas kernels: 101 us -> 64.4 us  [aggregate(): pl.pallas_call(functools.partial(aggregate_kernel, plan), grid_spec=pltpu...]
    all_gather x24 -> x16, blocking collectives: 166 us -> 138 us  [per_device(): gathered = lax.all_gather(mixed, 'section', axis=0, tiled=False)]
    unnamed x127 -> x57, local copies, waits for them, and re-layouts: 43 us -> 68.6 us
    all_to_all x2, waiting for transfers between devices: 16.7 us -> 0.01 us  [per_device(): lax.all_to_all(turn_blocks(stale_imports[sub, 0], section_count), 'sectio...]
    all_to_all x22 -> x10, waiting for transfers between devices: 9.75 us -> 22.8 us  [exchange(): return lax.all_to_all(value, 'dom', split_axis=0, concat_axis=0, tiled=True)]
    all_to_all x0 -> x1, blocking collectives: none -> 12.1 us  [per_device(): lax.all_to_all(layer_weights.transpose(0, 2, 1).reshape(depth, section_co...]
  transfers between devices with their start and end apart: 25 -> 12, of which waited for: 3 -> 3; matrix products, arithmetic and copies ran while one was open for 1% -> 1% of each run, Pallas kernels for 24% -> 12%
where the time goes in v5:
time: 505 us; the launch traced here: 502 us
  blocking collectives  260 us (51%)
  Pallas kernels  96.4 us (19%)
  local copies, waits for them, and re-layouts  73.2 us (14%)
  starting transfers between devices  48.8 us (10%)
  waiting for transfers between devices  22.8 us (5%)
    all_gather x16, blocking collectives, per_device(): gathered = lax.all_gather(mixed, 'section', axis=0, tiled=False)  138 us
    all_to_all x6, blocking collectives, exchange(): return lax.all_to_all(value, 'dom', split_axis=0, concat_axis=0, tiled=True)  109 us
    unnamed x57, local copies, waits for them, and re-layouts  68.6 us
    pallas_call x16, Pallas kernels, aggregate(): pl.pallas_call(functools.partial(aggregate_kernel, plan), grid_spec=pltpu...  64.4 us
    all_to_all x10, starting transfers between devices, exchange(): return lax.all_to_all(value, 'dom', split_axis=0, concat_axis=0, tiled=True)  40.9 us
    pallas_call x16, Pallas kernels, finish(): pl.pallas_call(functools.partial(finish_kernel, plan), grid_spec=pltpu.Pr...  28.5 us
    all_to_all x10, waiting for transfers between devices, exchange(): return lax.all_to_all(value, 'dom', split_axis=0, concat_axis=0, tiled=True)  22.8 us
    all_to_all x1, blocking collectives, per_device(): lax.all_to_all(layer_weights.transpose(0, 2, 1).reshape(depth, section_co...  12.1 us
  transfers between devices with their start and end apart: 12, of which 3 were waited for; matrix products, arithmetic and copies ran while one was open for 1% of the time, Pallas kernels for 12%

profile of v5, /device:TPU:0, one launch (start us, length us, event | category | flops | bytes accessed | tf_op | source)
XLA Modules:
  0.0 502.2 jit_solution(14624644351267164077)
XLA Ops:
  4.0 7.3 %all-to-all-start.11 = ((bf16[8,1,96,128]{3,2,1,0:T(8,128)(2,1)}), bf16[8,1,96,128]{3,2,1,0:T(8,128)(2,1)S(1)}, u32[]{:S(2)}, u32[]{:S(2)}) async-start(bf16[8,1,96,128]{3,2,1,0:T(8,128)(2,1)} %get-tuple-element.54), calls=%async_computation.11 | async-start | bytes 393216 | tf_op jit(solution)/shard_map/all_to_all | solution.py:292
  11.7 7.5 %all-to-all-done.11.refs_4_ = bf16[8,1,96,128]{3,2,1,0:T(8,128)(2,1)S(1)} async-done(((bf16[8,1,96,128]{3,2,1,0:T(8,128)(2,1)}), bf16[8,1,96,128]{3,2,1,0:T(8,128)(2,1)S(1)}, u32[]{:S(2)}, u32[]{:S(2)}) %all-to-all-start.11) | async-done | bytes 196640 | tf_op jit(solution)/shard_map/all_to_all | solution.py:292
  19.3 12.1 %all_to_all.105 = bf16[2,4,96,384]{3,2,0,1:T(8,128)(2,1)S(1)} all-to-all(bf16[2,4,96,384]{3,2,0,1:T(8,128)(2,1)S(1)} %copy.13), channel_id=1, replica_groups=mesh['section'=4,'dom'=8] {'section'}, dimensions={1} | all-to-all | bytes 1179648 | tf_op jit(solution)/shard_map/all_to_all | solution.py:305
  40.2 6.4 %all-to-all-done.refs_1_.refs_2_ = bf16[8,2,96,128]{3,2,1,0:T(8,128)(2,1)S(1)} async-done(((bf16[8,2,96,128]{3,2,1,0:T(8,128)(2,1)}), bf16[8,2,96,128]{3,2,1,0:T(8,128)(2,1)S(1)}, u32[]{:S(2)}, u32[]{:S(2)}) %all-to-all-start) | async-done | bytes 393248 | tf_op jit(solution)/shard_map/all_to_all | solution.py:292
  57.2 16.0 %all-gather.8 = bf16[16,96,128]{2,1,0:T(8,128)(2,1)S(1)} all-gather(bf16[4,96,128]{2,1,0:T(8,128)(2,1)S(1)} %aggregate.24.mixed_ref), channel_id=10, replica_groups=mesh['section'=4,'dom'=8] {'section'}, dimensions={0}, use_global_device_ids=true | all-gather | bytes 491520 | tf_op jit(solution)/shard_map/all_gather | solution.py:331
  87.1 8.5 %all-gather = bf16[32,96,128]{2,1,0:T(8,128)(2,1)S(1)} all-gather(bf16[8,96,128]{2,1,0:T(8,128)(2,1)S(1)} %aggregate.16.mixed_ref), channel_id=2, replica_groups=mesh['section'=4,'dom'=8] {'section'}, dimensions={0}, use_global_device_ids=true | all-gather | bytes 983040 | tf_op jit(solution)/shard_map/all_gather | solution.py:331
  107.1 8.9 %all-to-all-done.3.refs_1_.refs_2_ = bf16[8,2,96,128]{3,2,1,0:T(8,128)(2,1)S(1)} async-done(((bf16[8,2,96,128]{3,2,1,0:T(8,128)(2,1)}), bf16[8,2,96,128]{3,2,1,0:T(8,128)(2,1)S(1)}, u32[]{:S(2)}, u32[]{:S(2)}) %all-to-all-start.3) | async-done | bytes 393248 | tf_op jit(solution)/shard_map/all_to_all | solution.py:292
  127.2 16.2 %all-gather.9 = bf16[16,96,128]{2,1,0:T(8,128)(2,1)S(1)} all-gather(bf16[4,96,128]{2,1,0:T(8,128)(2,1)S(1)} %aggregate.25.mixed_ref), channel_id=11, replica_groups=mesh['section'=4,'dom'=8] {'section'}, dimensions={0}, use_global_device_ids=true | all-gather | bytes 491520 | tf_op jit(solution)/shard_map/all_gather | solution.py:331
  157.7 8.5 %all-gather.1 = bf16[32,96,128]{2,1,0:T(8,128)(2,1)S(1)} all-gather(bf16[8,96,128]{2,1,0:T(8,128)(2,1)S(1)} %aggregate.17.mixed_ref), channel_id=3, replica_groups=mesh['section'=4,'dom'=8] {'section'}, dimensions={0}, use_global_device_ids=true | all-gather | bytes 983040 | tf_op jit(solution)/shard_map/all_gather | solution.py:331
  168.7 18.2 %all_to_all.106.refs_1_.refs_2_ = bf16[8,2,96,128]{3,2,1,0:T(8,128)(2,1)S(1)} all-to-all(bf16[8,2,96,128]{3,2,1,0:T(8,128)(2,1)} %copy-done.21), channel_id=1, replica_groups=mesh['section'=4,'dom'=8] {'dom'}, dimensions={0} | all-to-all | bytes 786432 | tf_op jit(solution)/shard_map/all_to_all | solution.py:292
  193.8 6.1 %all-gather.10 = bf16[16,96,128]{2,1,0:T(8,128)(2,1)S(1)} all-gather(bf16[4,96,128]{2,1,0:T(8,128)(2,1)S(1)} %aggregate.26.mixed_ref), channel_id=12, replica_groups=mesh['section'=4,'dom'=8] {'section'}, dimensions={0}, use_global_device_ids=true | all-gather | bytes 491520 | tf_op jit(solution)/shard_map/all_gather | solution.py:331
  213.6 8.7 %all-gather.2 = bf16[32,96,128]{2,1,0:T(8,128)(2,1)S(1)} all-gather(bf16[8,96,128]{2,1,0:T(8,128)(2,1)S(1)} %aggregate.18.mixed_ref), channel_id=4, replica_groups=mesh['section'=4,'dom'=8] {'section'}, dimensions={0}, use_global_device_ids=true | all-gather | bytes 983040 | tf_op jit(solution)/shard_map/all_gather | solution.py:331
  224.9 18.2 %all_to_all.107.refs_1_.refs_2_ = bf16[8,2,96,128]{3,2,1,0:T(8,128)(2,1)S(1)} all-to-all(bf16[8,2,96,128]{3,2,1,0:T(8,128)(2,1)} %copy-done.22), channel_id=1, replica_groups=mesh['section'=4,'dom'=8] {'dom'}, dimensions={0} | all-to-all | bytes 786432 | tf_op jit(solution)/shard_map/all_to_all | solution.py:292
  249.9 6.1 %all-gather.11 = bf16[16,96,128]{2,1,0:T(8,128)(2,1)S(1)} all-gather(bf16[4,96,128]{2,1,0:T(8,128)(2,1)S(1)} %aggregate.27.mixed_ref), channel_id=13, replica_groups=mesh['section'=4,'dom'=8] {'section'}, dimensions={0}, use_global_device_ids=true | all-gather | bytes 491520 | tf_op jit(solution)/shard_map/all_gather | solution.py:331
  270.1 8.7 %all-gather.3 = bf16[32,96,128]{2,1,0:T(8,128)(2,1)S(1)} all-gather(bf16[8,96,128]{2,1,0:T(8,128)(2,1)S(1)} %aggregate.19.mixed_ref), channel_id=5, replica_groups=mesh['section'=4,'dom'=8] {'section'}, dimensions={0}, use_global_device_ids=true | all-gather | bytes 983040 | tf_op jit(solution)/shard_map/all_gather | solution.py:331
  281.4 18.2 %all_to_all.108.refs_1_.refs_2_ = bf16[8,2,96,128]{3,2,1,0:T(8,128)(2,1)S(1)} all-to-all(bf16[8,2,96,128]{3,2,1,0:T(8,128)(2,1)} %copy-done.23), channel_id=1, replica_groups=mesh['section'=4,'dom'=8] {'dom'}, dimensions={0} | all-to-all | bytes 786432 | tf_op jit(solution)/shard_map/all_to_all | solution.py:292
  326.4 8.7 %all-gather.4 = bf16[32,96,128]{2,1,0:T(8,128)(2,1)S(1)} all-gather(bf16[8,96,128]{2,1,0:T(8,128)(2,1)S(1)} %aggregate.20.mixed_ref), channel_id=6, replica_groups=mesh['section'=4,'dom'=8] {'section'}, dimensions={0}, use_global_device_ids=true | all-gather | bytes 983040 | tf_op jit(solution)/shard_map/all_gather | solution.py:331
  337.7 18.2 %all_to_all.109.refs_1_.refs_2_ = bf16[8,2,96,128]{3,2,1,0:T(8,128)(2,1)S(1)} all-to-all(bf16[8,2,96,128]{3,2,1,0:T(8,128)(2,1)} %copy-done.24), channel_id=1, replica_groups=mesh['section'=4,'dom'=8] {'dom'}, dimensions={0} | all-to-all | bytes 786432 | tf_op jit(solution)/shard_map/all_to_all | solution.py:292
  382.9 8.7 %all-gather.5 = bf16[32,96,128]{2,1,0:T(8,128)(2,1)S(1)} all-gather(bf16[8,96,128]{2,1,0:T(8,128)(2,1)S(1)} %aggregate.21.mixed_ref), channel_id=7, replica_groups=mesh['section'=4,'dom'=8] {'section'}, dimensions={0}, use_global_device_ids=true | all-gather | bytes 983040 | tf_op jit(solution)/shard_map/all_gather | solution.py:331
  394.2 18.2 %all_to_all.110.refs_1_.refs_2_ = bf16[8,2,96,128]{3,2,1,0:T(8,128)(2,1)S(1)} all-to-all(bf16[8,2,96,128]{3,2,1,0:T(8,128)(2,1)} %copy-done.25), channel_id=1, replica_groups=mesh['section'=4,'dom'=8] {'dom'}, dimensions={0} | all-to-all | bytes 786432 | tf_op jit(solution)/shard_map/all_to_all | solution.py:292
  439.1 8.7 %all-gather.6 = bf16[32,96,128]{2,1,0:T(8,128)(2,1)S(1)} all-gather(bf16[8,96,128]{2,1,0:T(8,128)(2,1)S(1)} %aggregate.22.mixed_ref), channel_id=8, replica_groups=mesh['section'=4,'dom'=8] {'section'}, dimensions={0}, use_global_device_ids=true | all-gather | bytes 983040 | tf_op jit(solution)/shard_map/all_gather | solution.py:331
  449.6 18.0 %all_to_all.111.refs_1_.refs_2_ = bf16[8,2,96,128]{3,2,1,0:T(8,128)(2,1)S(1)} all-to-all(bf16[8,2,96,128]{3,2,1,0:T(8,128)(2,1)S(1)} %get-tuple-element.52), channel_id=1, replica_groups=mesh['section'=4,'dom'=8] {'dom'}, dimensions={0} | all-to-all | bytes 786432 | tf_op jit(solution)/shard_map/all_to_all | solution.py:292
  474.4 6.1 %all-gather.15 = bf16[16,96,128]{2,1,0:T(8,128)(2,1)S(1)} all-gather(bf16[4,96,128]{2,1,0:T(8,128)(2,1)S(1)} %aggregate.31.mixed_ref), channel_id=17, replica_groups=mesh['section'=4,'dom'=8] {'section'}, dimensions={0}, use_global_device_ids=true | all-gather | bytes 491520 | tf_op jit(solution)/shard_map/all_gather | solution.py:331
  490.6 8.7 %all-gather.7 = bf16[32,96,128]{2,1,0:T(8,128)(2,1)S(1)} all-gather(bf16[8,96,128]{2,1,0:T(8,128)(2,1)S(1)} %aggregate.23.mixed_ref), channel_id=9, replica_groups=mesh['section'=4,'dom'=8] {'section'}, dimensions={0}, use_global_device_ids=true | all-gather | bytes 983040 | tf_op jit(solution)/shard_map/all_gather | solution.py:331
  (124 shorter events, 230.4 us)
Async XLA Ops:
  2.1 9.3 %copy-start.26 = (bf16[2,384,384]{2,1,0:T(8,128)(2,1)S(1)}, bf16[2,384,384]{2,1,0:T(8,128)(2,1)}, u32[]{:S(2)}) copy-start(bf16[2,384,384]{2,1,0:T(8,128)(2,1)} %param.7) | copy-start | bytes 1769476
  4.0 15.2 %all-to-all-start.11 = ((bf16[8,1,96,128]{3,2,1,0:T(8,128)(2,1)}), bf16[8,1,96,128]{3,2,1,0:T(8,128)(2,1)S(1)}, u32[]{:S(2)}, u32[]{:S(2)}) async-start(bf16[8,1,96,128]{3,2,1,0:T(8,128)(2,1)} %get-tuple-element.54), calls=%async_computation.11 | async-start | bytes 393216 | tf_op jit(solution)/shard_map/all_to_all | solution.py:292
  31.4 15.3 %all-to-all-start = ((bf16[8,2,96,128]{3,2,1,0:T(8,128)(2,1)}), bf16[8,2,96,128]{3,2,1,0:T(8,128)(2,1)S(1)}, u32[]{:S(2)}, u32[]{:S(2)}) async-start(bf16[8,2,96,128]{3,2,1,0:T(8,128)(2,1)} %get-tuple-element.38), calls=%async_computation | async-start | bytes 786432 | tf_op jit(solution)/shard_map/all_to_all | solution.py:292
  40.2 10.0 %copy-start.27 = (s32[12,24]{1,0:T(8,128)S(1)}, s32[12,24]{1,0:T(8,128)}, u32[]{:S(2)}) copy-start(s32[12,24]{1,0:T(8,128)} %param.9) | copy-start | bytes 3460
  46.6 28.4 %all-to-all-start.1 = ((bf16[4,16,96,128]{3,2,1,0:T(8,128)(2,1)}), bf16[4,16,96,128]{3,2,1,0:T(8,128)(2,1)S(1)}, u32[]{:S(2)}, u32[]{:S(2)}) async-start(bf16[4,16,96,128]{3,2,1,0:T(8,128)(2,1)} %copy-done.16), calls=%async_computation.1 | async-start | bytes 3145728 | tf_op jit(solution)/shard_map/all_to_all | solution.py:296
  50.4 3.7 copy-start
  75.1 23.1 %all-to-all-start.12 = ((bf16[8,1,96,128]{3,2,1,0:T(8,128)(2,1)}), bf16[8,1,96,128]{3,2,1,0:T(8,128)(2,1)S(1)}, u32[]{:S(2)}, u32[]{:S(2)}) async-start(bf16[8,1,96,128]{3,2,1,0:T(8,128)(2,1)} %get-tuple-element.56), calls=%async_computation.12 | async-start | bytes 393216 | tf_op jit(solution)/shard_map/all_to_all | solution.py:292
  98.2 17.8 %all-to-all-start.3 = ((bf16[8,2,96,128]{3,2,1,0:T(8,128)(2,1)}), bf16[8,2,96,128]{3,2,1,0:T(8,128)(2,1)S(1)}, u32[]{:S(2)}, u32[]{:S(2)}) async-start(bf16[8,2,96,128]{3,2,1,0:T(8,128)(2,1)} %copy-done.20), calls=%async_computation.3 | async-start | bytes 786432 | tf_op jit(solution)/shard_map/all_to_all | solution.py:292
  116.0 29.2 %all-to-all-start.4 = ((bf16[4,16,96,128]{3,2,1,0:T(8,128)(2,1)}), bf16[4,16,96,128]{3,2,1,0:T(8,128)(2,1)}, u32[]{:S(2)}, u32[]{:S(2)}) async-start(bf16[4,16,96,128]{3,2,1,0:T(8,128)(2,1)} %copy-done.17), calls=%async_computation.4 | async-start | bytes 3145728 | tf_op jit(solution)/shard_map/all_to_all | solution.py:296
  120.4 3.7 copy-start.2
  145.2 23.5 %all-to-all-start.13 = ((bf16[8,1,96,128]{3,2,1,0:T(8,128)(2,1)}), bf16[8,1,96,128]{3,2,1,0:T(8,128)(2,1)S(1)}, u32[]{:S(2)}, u32[]{:S(2)}) async-start(bf16[8,1,96,128]{3,2,1,0:T(8,128)(2,1)} %get-tuple-element.58), calls=%async_computation.13 | async-start | bytes 393216 | tf_op jit(solution)/shard_map/all_to_all | solution.py:292
  186.9 3.7 copy-start.4
  201.7 23.1 %all-to-all-start.14 = ((bf16[8,1,96,128]{3,2,1,0:T(8,128)(2,1)}), bf16[8,1,96,128]{3,2,1,0:T(8,128)(2,1)S(1)}, u32[]{:S(2)}, u32[]{:S(2)}) async-start(bf16[8,1,96,128]{3,2,1,0:T(8,128)(2,1)} %get-tuple-element.60), calls=%async_computation.14 | async-start | bytes 393216 | tf_op jit(solution)/shard_map/all_to_all | solution.py:292
  205.2 3.7 copy-start.5
  243.1 3.7 copy-start.6
  257.9 23.5 %all-to-all-start.15 = ((bf16[8,1,96,128]{3,2,1,0:T(8,128)(2,1)}), bf16[8,1,96,128]{3,2,1,0:T(8,128)(2,1)S(1)}, u32[]{:S(2)}, u32[]{:S(2)}) async-start(bf16[8,1,96,128]{3,2,1,0:T(8,128)(2,1)} %get-tuple-element.62), calls=%async_computation.15 | async-start | bytes 393216 | tf_op jit(solution)/shard_map/all_to_all | solution.py:292
  261.3 3.7 copy-start.7
  314.4 23.3 %all-to-all-start.16 = ((bf16[8,1,96,128]{3,2,1,0:T(8,128)(2,1)}), bf16[8,1,96,128]{3,2,1,0:T(8,128)(2,1)S(1)}, u32[]{:S(2)}, u32[]{:S(2)}) async-start(bf16[8,1,96,128]{3,2,1,0:T(8,128)(2,1)} %get-tuple-element.64), calls=%async_computation.16 | async-start | bytes 393216 | tf_op jit(solution)/shard_map/all_to_all | solution.py:292
  318.0 3.7 copy-start.9
  370.7 23.5 %all-to-all-start.17 = ((bf16[8,1,96,128]{3,2,1,0:T(8,128)(2,1)}), bf16[8,1,96,128]{3,2,1,0:T(8,128)(2,1)S(1)}, u32[]{:S(2)}, u32[]{:S(2)}) async-start(bf16[8,1,96,128]{3,2,1,0:T(8,128)(2,1)} %get-tuple-element.66), calls=%async_computation.17 | async-start | bytes 393216 | tf_op jit(solution)/shard_map/all_to_all | solution.py:292
  374.1 3.7 copy-start.11
  427.2 22.3 %all-to-all-start.18 = ((bf16[8,1,96,128]{3,2,1,0:T(8,128)(2,1)}), bf16[8,1,96,128]{3,2,1,0:T(8,128)(2,1)S(1)}, u32[]{:S(2)}, u32[]{:S(2)}) async-start(bf16[8,1,96,128]{3,2,1,0:T(8,128)(2,1)} %get-tuple-element.68), calls=%async_computation.18 | async-start | bytes 393216 | tf_op jit(solution)/shard_map/all_to_all | solution.py:292
  430.6 3.7 copy-start.13
  481.8 3.7 copy-start.15
  (16 other events, 31.5 us)

commit v6 on v5

--- a/solution.py
+++ b/solution.py
@@ -10,7 +10,7 @@
 
 alpha_mix = 0.1
 lambda_decay = 0.5
-vmem_bytes = 20 * 1024 * 1024
+vmem_bytes = 48 * 1024 * 1024
 
 
 def group_streams(groups):
@@ -97,7 +97,7 @@
 def aggregate_kernel(plan, columns, initial_ref, tiles_ref, *refs):
     stream, group_blocks, fanout, sources, layer_slot = plan
     source_refs = refs[: len(sources)]
-    mixed_ref, table, tiles, table_sem, tiles_sem = refs[len(sources) :]
+    mixed_ref, table, tiles, table_sem, tiles_sem = refs[-5:]
     rows = len(stream) * group_blocks
     first_row = stream[0] * group_blocks
 
@@ -144,7 +144,7 @@
     lax.fori_loop(0, rows, one_row, 0)
 
 
-def aggregate(columns, initial_blocks, tiles, own, imports, stale, layer_slot, stream, streams, group_blocks, part_count):
+def aggregate(columns, initial_blocks, tiles, own, imports, stale, layer_slot, stream, streams, group_blocks, part_count, after):
     rows, part_width, block = initial_blocks.shape
     blocks_dev, fanout = tiles.shape[:2]
     groups = blocks_dev // group_blocks
@@ -160,6 +160,7 @@
     if groups > 1 and stream[0] < groups - 1:
         sources.append(("stale", blocks_dev + groups * part_count, None))
         operands.append(stale)
+    operands += after
     table_size = blocks_dev + (2 * groups - 1) * part_count
     plan = (stream, group_blocks, fanout, sources, layer_slot)
     flops = 2 * rows * fanout * block * block * part_width
@@ -311,6 +312,7 @@
     ).reshape(layers, part_width, width)
 
     pieces = []
+    after = []
     for layer in range(layers):
         last = layer == layers - 1
         own_next, imports_next = [], []
@@ -327,6 +329,7 @@
                 streams,
                 group_blocks,
                 part_count,
+                after,
             )
             gathered = lax.all_gather(mixed, "section", axis=0, tiled=False)
             result = finish(
@@ -335,6 +338,7 @@
             if last:
                 pieces.append(result[0])
             else:
+                after = [result[1]]
                 own_next.append(result[0])
                 imports_next.append(exchange(result[1]))
         own, imports = own_next, imports_next

time: 505 us -> 435 us (0.86)
  blocking collectives: 260 us -> 171 us
  local copies, waits for them, and re-layouts: 73.2 us -> 30.9 us
  starting transfers between devices: 48.8 us -> 85.9 us
  Pallas kernels: 96.4 us -> 112 us
  waiting for transfers between devices: 22.8 us -> 30.6 us
    all_to_all x6 -> x2, blocking collectives: 109 us -> 28.8 us  [exchange(): return lax.all_to_all(value, 'dom', split_axis=0, concat_axis=0, tiled=True)]
    unnamed x57 -> x77, local copies, waits for them, and re-layouts: 68.6 us -> 26.2 us
    all_to_all x10 -> x14, starting transfers between devices: 40.9 us -> 78 us  [exchange(): return lax.all_to_all(value, 'dom', split_axis=0, concat_axis=0, tiled=True)]
    pallas_call x16, Pallas kernels: 64.4 us -> 81.2 us  [aggregate(): pl.pallas_call(functools.partial(aggregate_kernel, plan), grid_spec=pltpu...]
    all_to_all x2, waiting for transfers between devices: 0.01 us -> 16.7 us  [per_device(): lax.all_to_all(turn_blocks(stale_imports[sub, 0], section_count), 'sectio...]
    all_to_all x10 -> x14, waiting for transfers between devices: 22.8 us -> 13.9 us  [exchange(): return lax.all_to_all(value, 'dom', split_axis=0, concat_axis=0, tiled=True)]
    all_gather x16, blocking collectives: 138 us -> 131 us  [per_device(): gathered = lax.all_gather(mixed, 'section', axis=0, tiled=False)]
  transfers between devices with their start and end apart: 12 -> 16, of which waited for: 3 -> 3; matrix products, arithmetic and copies ran while one was open for 1% -> 1% of each run, Pallas kernels for 12% -> 21%
where the time goes in v6:
time: 435 us; the launch traced here: 433 us
  blocking collectives  171 us (39%)
  Pallas kernels  112 us (26%)
  starting transfers between devices  85.9 us (20%)
  local copies, waits for them, and re-layouts  30.9 us (7%)
  waiting for transfers between devices  30.6 us (7%)
    all_gather x16, blocking collectives, per_device(): gathered = lax.all_gather(mixed, 'section', axis=0, tiled=False)  131 us
    pallas_call x16, Pallas kernels, aggregate(): pl.pallas_call(functools.partial(aggregate_kernel, plan), grid_spec=pltpu...  81.2 us
    all_to_all x14, starting transfers between devices, exchange(): return lax.all_to_all(value, 'dom', split_axis=0, concat_axis=0, tiled=True)  78 us
    all_to_all x2, blocking collectives, exchange(): return lax.all_to_all(value, 'dom', split_axis=0, concat_axis=0, tiled=True)  28.8 us
    pallas_call x16, Pallas kernels, finish(): pl.pallas_call(functools.partial(finish_kernel, plan), grid_spec=pltpu.Pr...  27.8 us
    unnamed x77, local copies, waits for them, and re-layouts  26.2 us
    all_to_all x2, waiting for transfers between devices, per_device(): lax.all_to_all(turn_blocks(stale_imports[sub, 0], section_count), 'sectio...  16.7 us
    all_to_all x14, waiting for transfers between devices, exchange(): return lax.all_to_all(value, 'dom', split_axis=0, concat_axis=0, tiled=True)  13.9 us
  transfers between devices with their start and end apart: 16, of which 3 were waited for; matrix products, arithmetic and copies ran while one was open for 1% of the time, Pallas kernels for 21%

profile of v6, /device:TPU:0, one launch (start us, length us, event | category | flops | bytes accessed | tf_op | source)
XLA Modules:
  0.0 432.8 jit_solution(17881325070204351513)
XLA Ops:
  4.0 7.3 %all-to-all-start.5 = ((bf16[8,1,96,128]{3,2,1,0:T(8,128)(2,1)}), bf16[8,1,96,128]{3,2,1,0:T(8,128)(2,1)S(1)}, u32[]{:S(2)}, u32[]{:S(2)}) async-start(bf16[8,1,96,128]{3,2,1,0:T(8,128)(2,1)} %get-tuple-element.42), calls=%async_computation.5 | async-start | bytes 393216 | tf_op jit(solution)/shard_map/all_to_all | solution.py:293
  11.7 7.6 %all-to-all-done.5.refs_4_ = bf16[8,1,96,128]{3,2,1,0:T(8,128)(2,1)S(1)} async-done(((bf16[8,1,96,128]{3,2,1,0:T(8,128)(2,1)}), bf16[8,1,96,128]{3,2,1,0:T(8,128)(2,1)S(1)}, u32[]{:S(2)}, u32[]{:S(2)}) %all-to-all-start.5) | async-done | bytes 196640 | tf_op jit(solution)/shard_map/all_to_all | solution.py:293
  19.3 12.1 %all_to_all.105 = bf16[2,4,96,384]{3,2,0,1:T(8,128)(2,1)S(1)} all-to-all(bf16[2,4,96,384]{3,2,0,1:T(8,128)(2,1)S(1)} %copy.13), channel_id=1, replica_groups=mesh['section'=4,'dom'=8] {'section'}, dimensions={1} | all-to-all | bytes 1179648 | tf_op jit(solution)/shard_map/all_to_all | solution.py:306
  53.5 16.7 %all-to-all-done.1.refs_3_ = bf16[4,16,96,128]{3,2,1,0:T(8,128)(2,1)S(1)} async-done(((bf16[4,16,96,128]{3,2,1,0:T(8,128)(2,1)}), bf16[4,16,96,128]{3,2,1,0:T(8,128)(2,1)S(1)}, u32[]{:S(2)}, u32[]{:S(2)}) %all-to-all-start.1) | async-done | bytes 1572896 | tf_op jit(solution)/shard_map/all_to_all | solution.py:297
  80.3 19.5 %all-gather = bf16[32,96,128]{2,1,0:T(8,128)(2,1)S(1)} all-gather(bf16[8,96,128]{2,1,0:T(8,128)(2,1)S(1)} %aggregate.16.mixed_ref), channel_id=2, replica_groups=mesh['section'=4,'dom'=8] {'section'}, dimensions={0}, use_global_device_ids=true | all-gather | bytes 983040 | tf_op jit(solution)/shard_map/all_gather | solution.py:334
  111.7 6.6 %all-gather.1 = bf16[16,96,128]{2,1,0:T(8,128)(2,1)S(1)} all-gather(bf16[4,96,128]{2,1,0:T(8,128)(2,1)S(1)} %aggregate.17.mixed_ref), channel_id=3, replica_groups=mesh['section'=4,'dom'=8] {'section'}, dimensions={0}, use_global_device_ids=true | all-gather | bytes 491520 | tf_op jit(solution)/shard_map/all_gather | solution.py:334
  125.8 6.8 %aggregate.18.mixed_ref = bf16[8,96,128]{2,1,0:T(8,128)(2,1)S(1)} custom-call(s32[288]{0:T(512)S(1)} %reshape.30.columns, bf16[8,96,128]{2,1,0:T(8,128)(2,1)S(1)} %get-tuple-element.37.initial_ref.refs_0_, bf16[12,24,128,128]{3,2,1,0:T(8,128)(2,1)} %tiles_ref.31, bf16[8,96,128]{2,1,0:T(8,128)(2,1)S(1)} %copy-done.29, ...), custom_call_target="tpu_custom_call" | custom-call | flops 603979776 | bytes 6291456 | tf_op jit(solution)/shard_map/aggregate/pallas_call | solution.py:167
  132.6 8.4 %all-gather.2 = bf16[32,96,128]{2,1,0:T(8,128)(2,1)S(1)} all-gather(bf16[8,96,128]{2,1,0:T(8,128)(2,1)S(1)} %aggregate.18.mixed_ref), channel_id=4, replica_groups=mesh['section'=4,'dom'=8] {'section'}, dimensions={0}, use_global_device_ids=true | all-gather | bytes 983040 | tf_op jit(solution)/shard_map/all_gather | solution.py:334
  156.0 6.4 %all-gather.3 = bf16[16,96,128]{2,1,0:T(8,128)(2,1)S(1)} all-gather(bf16[4,96,128]{2,1,0:T(8,128)(2,1)S(1)} %aggregate.19.mixed_ref), channel_id=5, replica_groups=mesh['section'=4,'dom'=8] {'section'}, dimensions={0}, use_global_device_ids=true | all-gather | bytes 491520 | tf_op jit(solution)/shard_map/all_gather | solution.py:334
  175.6 8.4 %all-gather.4 = bf16[32,96,128]{2,1,0:T(8,128)(2,1)S(1)} all-gather(bf16[8,96,128]{2,1,0:T(8,128)(2,1)S(1)} %aggregate.20.mixed_ref), channel_id=6, replica_groups=mesh['section'=4,'dom'=8] {'section'}, dimensions={0}, use_global_device_ids=true | all-gather | bytes 983040 | tf_op jit(solution)/shard_map/all_gather | solution.py:334
  199.0 6.4 %all-gather.5 = bf16[16,96,128]{2,1,0:T(8,128)(2,1)S(1)} all-gather(bf16[4,96,128]{2,1,0:T(8,128)(2,1)S(1)} %aggregate.21.mixed_ref), channel_id=7, replica_groups=mesh['section'=4,'dom'=8] {'section'}, dimensions={0}, use_global_device_ids=true | all-gather | bytes 491520 | tf_op jit(solution)/shard_map/all_gather | solution.py:334
  213.2 6.8 %aggregate.22.mixed_ref = bf16[8,96,128]{2,1,0:T(8,128)(2,1)S(1)} custom-call(s32[288]{0:T(512)S(1)} %reshape.30.columns, bf16[8,96,128]{2,1,0:T(8,128)(2,1)S(1)} %get-tuple-element.37.initial_ref.refs_0_, bf16[12,24,128,128]{3,2,1,0:T(8,128)(2,1)} %tiles_ref.31, bf16[8,96,128]{2,1,0:T(8,128)(2,1)S(1)} %copy-done.20, ...), custom_call_target="tpu_custom_call" | custom-call | flops 603979776 | bytes 6291456 | tf_op jit(solution)/shard_map/aggregate/pallas_call | solution.py:167
  219.9 8.4 %all-gather.6 = bf16[32,96,128]{2,1,0:T(8,128)(2,1)S(1)} all-gather(bf16[8,96,128]{2,1,0:T(8,128)(2,1)S(1)} %aggregate.22.mixed_ref), channel_id=8, replica_groups=mesh['section'=4,'dom'=8] {'section'}, dimensions={0}, use_global_device_ids=true | all-gather | bytes 983040 | tf_op jit(solution)/shard_map/all_gather | solution.py:334
  243.3 6.4 %all-gather.7 = bf16[16,96,128]{2,1,0:T(8,128)(2,1)S(1)} all-gather(bf16[4,96,128]{2,1,0:T(8,128)(2,1)S(1)} %aggregate.23.mixed_ref), channel_id=9, replica_groups=mesh['section'=4,'dom'=8] {'section'}, dimensions={0}, use_global_device_ids=true | all-gather | bytes 491520 | tf_op jit(solution)/shard_map/all_gather | solution.py:334
  262.9 8.4 %all-gather.8 = bf16[32,96,128]{2,1,0:T(8,128)(2,1)S(1)} all-gather(bf16[8,96,128]{2,1,0:T(8,128)(2,1)S(1)} %aggregate.24.mixed_ref), channel_id=10, replica_groups=mesh['section'=4,'dom'=8] {'section'}, dimensions={0}, use_global_device_ids=true | all-gather | bytes 983040 | tf_op jit(solution)/shard_map/all_gather | solution.py:334
  286.3 6.6 %all-gather.9 = bf16[16,96,128]{2,1,0:T(8,128)(2,1)S(1)} all-gather(bf16[4,96,128]{2,1,0:T(8,128)(2,1)S(1)} %aggregate.25.mixed_ref), channel_id=11, replica_groups=mesh['section'=4,'dom'=8] {'section'}, dimensions={0}, use_global_device_ids=true | all-gather | bytes 491520 | tf_op jit(solution)/shard_map/all_gather | solution.py:334
  300.6 6.8 %aggregate.26.mixed_ref = bf16[8,96,128]{2,1,0:T(8,128)(2,1)S(1)} custom-call(s32[288]{0:T(512)S(1)} %reshape.30.columns, bf16[8,96,128]{2,1,0:T(8,128)(2,1)S(1)} %get-tuple-element.37.initial_ref.refs_0_, bf16[12,24,128,128]{3,2,1,0:T(8,128)(2,1)} %tiles_ref.31, bf16[8,96,128]{2,1,0:T(8,128)(2,1)S(1)} %copy-done.26, ...), custom_call_target="tpu_custom_call" | custom-call | flops 603979776 | bytes 6291456 | tf_op jit(solution)/shard_map/aggregate/pallas_call | solution.py:167
  307.4 8.4 %all-gather.10 = bf16[32,96,128]{2,1,0:T(8,128)(2,1)S(1)} all-gather(bf16[8,96,128]{2,1,0:T(8,128)(2,1)S(1)} %aggregate.26.mixed_ref), channel_id=12, replica_groups=mesh['section'=4,'dom'=8] {'section'}, dimensions={0}, use_global_device_ids=true | all-gather | bytes 983040 | tf_op jit(solution)/shard_map/all_gather | solution.py:334
  350.5 8.4 %all-gather.12 = bf16[32,96,128]{2,1,0:T(8,128)(2,1)S(1)} all-gather(bf16[8,96,128]{2,1,0:T(8,128)(2,1)S(1)} %aggregate.28.mixed_ref), channel_id=14, replica_groups=mesh['section'=4,'dom'=8] {'section'}, dimensions={0}, use_global_device_ids=true | all-gather | bytes 983040 | tf_op jit(solution)/shard_map/all_gather | solution.py:334
  366.3 6.7 %all-gather.13 = bf16[16,96,128]{2,1,0:T(8,128)(2,1)S(1)} all-gather(bf16[4,96,128]{2,1,0:T(8,128)(2,1)S(1)} %aggregate.29.mixed_ref), channel_id=15, replica_groups=mesh['section'=4,'dom'=8] {'section'}, dimensions={0}, use_global_device_ids=true | all-gather | bytes 491520 | tf_op jit(solution)/shard_map/all_gather | solution.py:334
  374.2 14.0 %all_to_all.106.refs_4_ = bf16[8,1,96,128]{3,2,1,0:T(8,128)(2,1)S(1)} all-to-all(bf16[8,1,96,128]{3,2,1,0:T(8,128)(2,1)S(1)} %get-tuple-element.67.refs_4_.refs_5_), channel_id=1, replica_groups=mesh['section'=4,'dom'=8] {'dom'}, dimensions={0} | all-to-all | bytes 393216 | tf_op jit(solution)/shard_map/all_to_all | solution.py:293
  388.2 14.8 %all_to_all.107.refs_1_.refs_2_ = bf16[8,2,96,128]{3,2,1,0:T(8,128)(2,1)S(1)} all-to-all(bf16[8,2,96,128]{3,2,1,0:T(8,128)(2,1)S(1)} %get-tuple-element.65.refs_5_), channel_id=1, replica_groups=mesh['section'=4,'dom'=8] {'dom'}, dimensions={0} | all-to-all | bytes 786432 | tf_op jit(solution)/shard_map/all_to_all | solution.py:293
  414.4 6.8 %aggregate.30.mixed_ref = bf16[8,96,128]{2,1,0:T(8,128)(2,1)S(1)} custom-call(s32[288]{0:T(512)S(1)} %reshape.30.columns, bf16[8,96,128]{2,1,0:T(8,128)(2,1)S(1)} %get-tuple-element.37.initial_ref.refs_0_, bf16[12,24,128,128]{3,2,1,0:T(8,128)(2,1)} %tiles_ref.31, bf16[8,96,128]{2,1,0:T(8,128)(2,1)S(1)} %copy-done.35, ...), custom_call_target="tpu_custom_call" | custom-call | flops 603979776 | bytes 6291456 | tf_op jit(solution)/shard_map/aggregate/pallas_call | solution.py:167
  421.2 8.7 %all-gather.14 = bf16[32,96,128]{2,1,0:T(8,128)(2,1)S(1)} all-gather(bf16[8,96,128]{2,1,0:T(8,128)(2,1)S(1)} %aggregate.30.mixed_ref), channel_id=16, replica_groups=mesh['section'=4,'dom'=8] {'section'}, dimensions={0}, use_global_device_ids=true | all-gather | bytes 983040 | tf_op jit(solution)/shard_map/all_gather | solution.py:334
  (148 shorter events, 214.6 us)
Async XLA Ops:
  4.0 15.2 %all-to-all-start.5 = ((bf16[8,1,96,128]{3,2,1,0:T(8,128)(2,1)}), bf16[8,1,96,128]{3,2,1,0:T(8,128)(2,1)S(1)}, u32[]{:S(2)}, u32[]{:S(2)}) async-start(bf16[8,1,96,128]{3,2,1,0:T(8,128)(2,1)} %get-tuple-element.42), calls=%async_computation.5 | async-start | bytes 393216 | tf_op jit(solution)/shard_map/all_to_all | solution.py:293
  31.4 15.3 %all-to-all-start = ((bf16[8,2,96,128]{3,2,1,0:T(8,128)(2,1)}), bf16[8,2,96,128]{3,2,1,0:T(8,128)(2,1)S(1)}, u32[]{:S(2)}, u32[]{:S(2)}) async-start(bf16[8,2,96,128]{3,2,1,0:T(8,128)(2,1)} %get-tuple-element.38), calls=%async_computation | async-start | bytes 786432 | tf_op jit(solution)/shard_map/all_to_all | solution.py:293
  46.6 23.6 %all-to-all-start.1 = ((bf16[4,16,96,128]{3,2,1,0:T(8,128)(2,1)}), bf16[4,16,96,128]{3,2,1,0:T(8,128)(2,1)S(1)}, u32[]{:S(2)}, u32[]{:S(2)}) async-start(bf16[4,16,96,128]{3,2,1,0:T(8,128)(2,1)} %copy-done.1), calls=%async_computation.1 | async-start | bytes 3145728 | tf_op jit(solution)/shard_map/all_to_all | solution.py:297
  53.5 21.1 %copy-start.37 = (s32[12,24]{1,0:T(8,128)S(1)}, s32[12,24]{1,0:T(8,128)}, u32[]{:S(2)}) copy-start(s32[12,24]{1,0:T(8,128)} %param.9) | copy-start | bytes 3460
  70.2 32.7 %all-to-all-start.4 = ((bf16[4,16,96,128]{3,2,1,0:T(8,128)(2,1)}), bf16[4,16,96,128]{3,2,1,0:T(8,128)(2,1)}, u32[]{:S(2)}, u32[]{:S(2)}) async-start(bf16[4,16,96,128]{3,2,1,0:T(8,128)(2,1)} %copy-done), calls=%async_computation.4 | async-start | bytes 3145728 | tf_op jit(solution)/shard_map/all_to_all | solution.py:297
  103.0 17.1 %all-to-all-start.3 = ((bf16[8,2,96,128]{3,2,1,0:T(8,128)(2,1)}), bf16[8,2,96,128]{3,2,1,0:T(8,128)(2,1)S(1)}, u32[]{:S(2)}, u32[]{:S(2)}) async-start(bf16[8,2,96,128]{3,2,1,0:T(8,128)(2,1)} %copy-done.13), calls=%async_computation.3 | async-start | bytes 786432 | tf_op jit(solution)/shard_map/all_to_all | solution.py:293
  111.7 14.2 %copy-start.29 = (bf16[8,96,128]{2,1,0:T(8,128)(2,1)S(1)}, bf16[8,96,128]{2,1,0:T(8,128)(2,1)}, u32[]{:S(2)}) copy-start(bf16[8,96,128]{2,1,0:T(8,128)(2,1)} %copy-done.28) | copy-start | bytes 589828
  120.1 24.2 %all-to-all-start.7 = ((bf16[8,1,96,128]{3,2,1,0:T(8,128)(2,1)}), bf16[8,1,96,128]{3,2,1,0:T(8,128)(2,1)S(1)}, u32[]{:S(2)}, u32[]{:S(2)}) async-start(bf16[8,1,96,128]{3,2,1,0:T(8,128)(2,1)} %get-tuple-element.43.refs_4_), calls=%async_computation.7 | async-start | bytes 393216 | tf_op jit(solution)/shard_map/all_to_all | solution.py:293
  144.3 20.0 %all-to-all-start.6 = ((bf16[8,2,96,128]{3,2,1,0:T(8,128)(2,1)}), bf16[8,2,96,128]{3,2,1,0:T(8,128)(2,1)S(1)}, u32[]{:S(2)}, u32[]{:S(2)}) async-start(bf16[8,2,96,128]{3,2,1,0:T(8,128)(2,1)} %copy-done.3), calls=%async_computation.6 | async-start | bytes 786432 | tf_op jit(solution)/shard_map/all_to_all | solution.py:293
  156.0 14.2 %copy-start.17 = (bf16[8,96,128]{2,1,0:T(8,128)(2,1)S(1)}, bf16[8,96,128]{2,1,0:T(8,128)(2,1)}, u32[]{:S(2)}) copy-start(bf16[8,96,128]{2,1,0:T(8,128)(2,1)} %copy-done.16) | copy-start | bytes 589828
  164.3 23.0 %all-to-all-start.9 = ((bf16[8,1,96,128]{3,2,1,0:T(8,128)(2,1)}), bf16[8,1,96,128]{3,2,1,0:T(8,128)(2,1)S(1)}, u32[]{:S(2)}, u32[]{:S(2)}) async-start(bf16[8,1,96,128]{3,2,1,0:T(8,128)(2,1)} %get-tuple-element.47.refs_4_), calls=%async_computation.9 | async-start | bytes 393216 | tf_op jit(solution)/shard_map/all_to_all | solution.py:293
  187.3 20.0 %all-to-all-start.8 = ((bf16[8,2,96,128]{3,2,1,0:T(8,128)(2,1)}), bf16[8,2,96,128]{3,2,1,0:T(8,128)(2,1)S(1)}, u32[]{:S(2)}, u32[]{:S(2)}) async-start(bf16[8,2,96,128]{3,2,1,0:T(8,128)(2,1)} %copy-done.5), calls=%async_computation.8 | async-start | bytes 786432 | tf_op jit(solution)/shard_map/all_to_all | solution.py:293
  199.0 14.2 %copy-start.20 = (bf16[8,96,128]{2,1,0:T(8,128)(2,1)S(1)}, bf16[8,96,128]{2,1,0:T(8,128)(2,1)}, u32[]{:S(2)}) copy-start(bf16[8,96,128]{2,1,0:T(8,128)(2,1)} %copy-done.19) | copy-start | bytes 589828
  207.3 24.3 %all-to-all-start.11 = ((bf16[8,1,96,128]{3,2,1,0:T(8,128)(2,1)}), bf16[8,1,96,128]{3,2,1,0:T(8,128)(2,1)S(1)}, u32[]{:S(2)}, u32[]{:S(2)}) async-start(bf16[8,1,96,128]{3,2,1,0:T(8,128)(2,1)} %get-tuple-element.51.refs_4_), calls=%async_computation.11 | async-start | bytes 393216 | tf_op jit(solution)/shard_map/all_to_all | solution.py:293
  231.6 20.0 %all-to-all-start.10 = ((bf16[8,2,96,128]{3,2,1,0:T(8,128)(2,1)}), bf16[8,2,96,128]{3,2,1,0:T(8,128)(2,1)S(1)}, u32[]{:S(2)}, u32[]{:S(2)}) async-start(bf16[8,2,96,128]{3,2,1,0:T(8,128)(2,1)} %copy-done.7), calls=%async_computation.10 | async-start | bytes 786432 | tf_op jit(solution)/shard_map/all_to_all | solution.py:293
  243.3 14.2 %copy-start.23 = (bf16[8,96,128]{2,1,0:T(8,128)(2,1)S(1)}, bf16[8,96,128]{2,1,0:T(8,128)(2,1)}, u32[]{:S(2)}) copy-start(bf16[8,96,128]{2,1,0:T(8,128)(2,1)} %copy-done.22) | copy-start | bytes 589828
  251.6 23.0 %all-to-all-start.13 = ((bf16[8,1,96,128]{3,2,1,0:T(8,128)(2,1)}), bf16[8,1,96,128]{3,2,1,0:T(8,128)(2,1)S(1)}, u32[]{:S(2)}, u32[]{:S(2)}) async-start(bf16[8,1,96,128]{3,2,1,0:T(8,128)(2,1)} %get-tuple-element.55.refs_4_), calls=%async_computation.13 | async-start | bytes 393216 | tf_op jit(solution)/shard_map/all_to_all | solution.py:293
  274.6 20.2 %all-to-all-start.12 = ((bf16[8,2,96,128]{3,2,1,0:T(8,128)(2,1)}), bf16[8,2,96,128]{3,2,1,0:T(8,128)(2,1)S(1)}, u32[]{:S(2)}, u32[]{:S(2)}) async-start(bf16[8,2,96,128]{3,2,1,0:T(8,128)(2,1)} %copy-done.9), calls=%async_computation.12 | async-start | bytes 786432 | tf_op jit(solution)/shard_map/all_to_all | solution.py:293
  286.3 14.3 %copy-start.26 = (bf16[8,96,128]{2,1,0:T(8,128)(2,1)S(1)}, bf16[8,96,128]{2,1,0:T(8,128)(2,1)}, u32[]{:S(2)}) copy-start(bf16[8,96,128]{2,1,0:T(8,128)(2,1)} %copy-done.25) | copy-start | bytes 589828
  294.8 24.3 %all-to-all-start.15 = ((bf16[8,1,96,128]{3,2,1,0:T(8,128)(2,1)}), bf16[8,1,96,128]{3,2,1,0:T(8,128)(2,1)S(1)}, u32[]{:S(2)}, u32[]{:S(2)}) async-start(bf16[8,1,96,128]{3,2,1,0:T(8,128)(2,1)} %get-tuple-element.59.refs_4_), calls=%async_computation.15 | async-start | bytes 393216 | tf_op jit(solution)/shard_map/all_to_all | solution.py:293
  319.1 20.0 %all-to-all-start.14 = ((bf16[8,2,96,128]{3,2,1,0:T(8,128)(2,1)}), bf16[8,2,96,128]{3,2,1,0:T(8,128)(2,1)S(1)}, u32[]{:S(2)}, u32[]{:S(2)}) async-start(bf16[8,2,96,128]{3,2,1,0:T(8,128)(2,1)} %copy-done.11), calls=%async_computation.14 | async-start | bytes 786432 | tf_op jit(solution)/shard_map/all_to_all | solution.py:293
  330.8 14.2 %copy-start.32 = (bf16[8,96,128]{2,1,0:T(8,128)(2,1)S(1)}, bf16[8,96,128]{2,1,0:T(8,128)(2,1)}, u32[]{:S(2)}) copy-start(bf16[8,96,128]{2,1,0:T(8,128)(2,1)} %copy-done.31) | copy-start | bytes 589828
  339.1 22.2 %all-to-all-start.17 = ((bf16[8,1,96,128]{3,2,1,0:T(8,128)(2,1)}), bf16[8,1,96,128]{3,2,1,0:T(8,128)(2,1)S(1)}, u32[]{:S(2)}, u32[]{:S(2)}) async-start(bf16[8,1,96,128]{3,2,1,0:T(8,128)(2,1)} %get-tuple-element.63.refs_4_), calls=%async_computation.17 | async-start | bytes 393216 | tf_op jit(solution)/shard_map/all_to_all | solution.py:293
  366.3 36.7 %copy-start.35 = (bf16[8,96,128]{2,1,0:T(8,128)(2,1)S(1)}, bf16[8,96,128]{2,1,0:T(8,128)(2,1)}, u32[]{:S(2)}) copy-start(bf16[8,96,128]{2,1,0:T(8,128)(2,1)} %copy-done.34) | copy-start | bytes 589828
  (30 other events, 35.3 us)

commit v7 on v1

--- a/solution.py
+++ b/solution.py
@@ -14,11 +14,31 @@
 
 
 def group_streams(groups):
-    return [list(range(groups))]
+    return [list(range(groups - 1)), [groups - 1]]
 
 
 def params():
     return pltpu.CompilerParams(vmem_limit_bytes=vmem_bytes)
+
+
+def in_hbm(shape):
+    return pltpu.HBM(shape, jnp.bfloat16)
+
+
+def start_all(copies):
+    for condition, copy in copies:
+        if condition is None:
+            copy.start()
+        else:
+            pl.when(condition)(copy.start)
+
+
+def wait_all(copies):
+    for condition, copy in copies:
+        if condition is None:
+            copy.wait()
+        else:
+            pl.when(condition)(copy.wait)
 
 
 def whole(shape):
@@ -70,62 +90,77 @@
     )(section, picks, initial_features)
 
 
-def turn_kernel(in_ref, out_ref):
-    count = in_ref.shape[0]
-    parts, part_width = out_ref.shape[0], out_ref.shape[2]
+def turn_kernel(info, in_ref, *refs):
+    *out_refs, turned = refs
+    count = in_ref.shape[-3]
+    sections, part_width = len(out_refs), out_refs[0].shape[1]
     for item in range(count):
-        turned = in_ref[item].T
-        for part in range(parts):
-            out_ref[part, item] = turned[part * part_width : (part + 1) * part_width, :]
-
-
-def turn_blocks(blocks, parts):
-    count, block, width = blocks.shape
-    step = 4 if count % 4 == 0 else 1
-    part_width = width // parts
+        turned[item % 2] = in_ref[0, item].T if len(in_ref.shape) == 4 else in_ref[0, 0, item].T
+        for distance, out_ref in enumerate(out_refs):
+            owner = lax.rem(info[0] + distance, sections)
+            first = pl.multiple_of(owner * part_width, part_width)
+            out_ref[item] = turned[item % 2, pl.ds(first, part_width), :]
+
+
+def turn_blocks(section, blocks, lead, sections):
+    count, rows, width = blocks.shape[-3:]
+    step = 8 if count % 8 == 0 else count
+    part_width = width // sections
+    block_shape = (1,) * (len(blocks.shape) - 3) + (step, rows, width)
+    out_spec = pl.BlockSpec((step, part_width, rows), lambda i, *prefetched: (i, 0, 0))
     return pl.pallas_call(
         turn_kernel,
-        grid=(count // step,),
-        in_specs=[pl.BlockSpec((step, block, width), lambda i: (i, 0, 0))],
-        out_specs=pl.BlockSpec((parts, step, part_width, block), lambda i: (0, i, 0, 0)),
-        out_shape=jax.ShapeDtypeStruct((parts, count, part_width, block), jnp.bfloat16),
+        grid_spec=pltpu.PrefetchScalarGridSpec(
+            num_scalar_prefetch=1,
+            grid=(count // step,),
+            in_specs=[pl.BlockSpec(block_shape, lambda i, *prefetched: lead + (i, 0, 0))],
+            out_specs=[out_spec] * sections,
+            scratch_shapes=[pltpu.VMEM((2, width, rows), jnp.bfloat16)],
+        ),
+        out_shape=[in_hbm((count, part_width, rows))] * sections,
         compiler_params=params(),
         name="turn",
-    )(blocks)
-
-
-def aggregate_kernel(plan, columns, initial_ref, tiles_ref, *refs):
-    stream, group_blocks, fanout, sources, layer_slot = plan
+    )(section, blocks)
+
+
+def aggregate_kernel(plan, columns, info, initial_ref, tiles_ref, *refs):
+    stream, group_blocks, fanout, sources, home, sections = plan
     source_refs = refs[: len(sources)]
-    mixed_ref, table, tiles, table_sem, tiles_sem = refs[len(sources) :]
+    mixed_ref, table, tiles, initial, table_sem, tiles_sem, initial_sem = refs[-7:]
     rows = len(stream) * group_blocks
     first_row = stream[0] * group_blocks
 
     def tile_copy(row):
         return pltpu.make_async_copy(tiles_ref.at[first_row + row], tiles.at[row], tiles_sem.at[row])
 
+    initial_copy = pltpu.make_async_copy(initial_ref, initial, initial_sem)
     copies = []
     for index, (kind, target, detail) in enumerate(sources):
         ref = source_refs[index]
-        if kind == "own":
-            source = ref
-        elif kind == "import":
-            source = ref.at[:, detail]
-        else:
-            source = ref.at[layer_slot]
-        count = source.shape[0]
+        source = ref.at[:, detail] if kind == "import" else ref
+        condition = None
+        if kind == "stale":
+            condition = lax.rem(info[0] - home + 2 * sections, sections) == detail
         copies.append(
-            pltpu.make_async_copy(source, table.at[pl.ds(target, count)], table_sem.at[index])
+            (
+                condition,
+                pltpu.make_async_copy(
+                    source, table.at[pl.ds(target, source.shape[0])], table_sem.at[index]
+                ),
+            )
         )
-    for copy in copies:
-        copy.start()
+    start_all(copies)
+    for row in range(min(2, rows)):
+        tile_copy(row).start()
+    initial_copy.start()
+    wait_all(copies)
+
     for row in range(rows):
-        tile_copy(row).start()
-    for copy in copies:
-        copy.wait()
-
-    def one_row(row, carry):
         tile_copy(row).wait()
+        if row + 2 < rows:
+            tile_copy(row + 2).start()
+        if row == 0:
+            initial_copy.wait()
         base = (first_row + row) * fanout
         total = None
         for tile in range(0, fanout, 2):
@@ -137,14 +172,11 @@
             )
             total = term if total is None else total + term
         mixed_ref[row] = (
-            (1.0 - alpha_mix) * total + alpha_mix * initial_ref[row].astype(jnp.float32)
+            (1.0 - alpha_mix) * total + alpha_mix * initial[row].astype(jnp.float32)
         ).astype(jnp.bfloat16)
-        return carry
-
-    lax.fori_loop(0, rows, one_row, 0)
-
-
-def aggregate(columns, initial_blocks, tiles, own, imports, stale, layer_slot, stream, streams, group_blocks, part_count):
+
+
+def aggregate(columns, section, initial_blocks, tiles, own, imports, stale, home, stream, streams, group_blocks, part_count, after):
     rows, part_width, block = initial_blocks.shape
     blocks_dev, fanout = tiles.shape[:2]
     groups = blocks_dev // group_blocks
@@ -158,24 +190,27 @@
             sources.append(("import", blocks_dev + group * part_count, local))
             operands.append(imported)
     if groups > 1 and stream[0] < groups - 1:
-        sources.append(("stale", blocks_dev + groups * part_count, None))
-        operands.append(stale)
+        for distance, stale_blocks in enumerate(stale):
+            sources.append(("stale", blocks_dev + groups * part_count, distance))
+            operands.append(stale_blocks)
+    operands += after
     table_size = blocks_dev + (2 * groups - 1) * part_count
-    plan = (stream, group_blocks, fanout, sources, layer_slot)
+    plan = (stream, group_blocks, fanout, sources, home, len(stale))
     flops = 2 * rows * fanout * block * block * part_width
     return pl.pallas_call(
         functools.partial(aggregate_kernel, plan),
         grid_spec=pltpu.PrefetchScalarGridSpec(
-            num_scalar_prefetch=1,
+            num_scalar_prefetch=2,
             grid=(1,),
-            in_specs=[whole(initial_blocks.shape)]
-            + [pl.BlockSpec(memory_space=pl.ANY)] * (1 + len(operands)),
+            in_specs=[pl.BlockSpec(memory_space=pl.ANY)] * (2 + len(operands)),
             out_specs=whole((rows, part_width, block)),
             scratch_shapes=[
                 pltpu.VMEM((table_size, part_width, block), jnp.bfloat16),
                 pltpu.VMEM((rows, fanout, block, block), jnp.bfloat16),
+                pltpu.VMEM(initial_blocks.shape, jnp.bfloat16),
                 pltpu.SemaphoreType.DMA((len(sources),)),
                 pltpu.SemaphoreType.DMA((rows,)),
+                pltpu.SemaphoreType.DMA,
             ],
         ),
         out_shape=jax.ShapeDtypeStruct((rows, part_width, block), jnp.bfloat16),
@@ -184,20 +219,31 @@
         ),
         compiler_params=params(),
         name="aggregate",
-    )(columns, initial_blocks, tiles, *operands)
-
-
-def finish_kernel(plan, picks, mixed_ref, gathered_ref, weight_ref, *refs):
-    beta_layer, stream, group_blocks, part_count, last = plan
+    )(columns, section, initial_blocks, tiles, *operands)
+
+
+def finish_kernel(plan, picks, info, mixed_ref, gathered_ref, *refs):
+    beta_layer, stream, group_blocks, part_count, sub, home, last = plan
     rows, part_width, block = mixed_ref.shape
     parts = gathered_ref.shape[0]
-    weight = weight_ref[0]
+    weight_refs = refs[:parts]
+    weight, weight_sem = refs[-2:]
+    refs = refs[parts:-2]
+    copies = [
+        (
+            lax.rem(info[0] - home + 2 * parts, parts) == distance,
+            pltpu.make_async_copy(weight_ref.at[sub], weight, weight_sem.at[distance]),
+        )
+        for distance, weight_ref in enumerate(weight_refs)
+    ]
+    start_all(copies)
+    wait_all(copies)
     for row in range(0, rows, 2):
         span = range(row, min(row + 2, rows))
         right = jnp.concatenate(
             [jnp.concatenate([gathered_ref[p, r] for p in range(parts)], 0) for r in span], 1
         )
-        product = jnp.dot(weight, right, preferred_element_type=jnp.float32)
+        product = jnp.dot(weight[...], right, preferred_element_type=jnp.float32)
         for place, r in enumerate(span):
             value = (1.0 - beta_layer) * mixed_ref[r].astype(jnp.float32) + beta_layer * product[
                 :, place * block : (place + 1) * block
@@ -209,30 +255,41 @@
                 refs[0][r] = value
     if not last:
         pick_outgoing(picks, refs[0], refs[1], stream, group_blocks, part_count)
-
-
-def finish(picks, mixed, gathered, weights, layer, stream, group_blocks, part_count, last):
+        refs[2][...] = jnp.zeros_like(refs[2])
+
+
+def finish(picks, section, mixed, gathered, weights, layer, depth, stream, group_blocks, part_count, last):
     rows, part_width, block = mixed.shape
-    width = weights.shape[2]
+    width = weights[0].shape[2]
     beta_layer = math.log(lambda_decay / (layer + 1) + 1.0)
-    plan = (beta_layer, stream, group_blocks, part_count, last)
+    plan = (
+        beta_layer, stream, group_blocks, part_count, layer % depth, layer // depth, last,
+    )
     if last:
         shapes = [(rows * block, part_width)]
+        out_shape = [jax.ShapeDtypeStruct(shapes[0], jnp.bfloat16)]
     else:
-        shapes = [(rows, part_width, block), (part_count, len(stream), part_width, block)]
+        outgoing = (part_count, len(stream), part_width, block)
+        shapes = [(rows, part_width, block), outgoing, (16, 128)]
+        out_shape = [
+            in_hbm(shapes[0]),
+            jax.ShapeDtypeStruct(outgoing, jnp.bfloat16),
+            jax.ShapeDtypeStruct((16, 128), jnp.bfloat16),
+        ]
     return pl.pallas_call(
         functools.partial(finish_kernel, plan),
         grid_spec=pltpu.PrefetchScalarGridSpec(
-            num_scalar_prefetch=1,
+            num_scalar_prefetch=2,
             grid=(1,),
-            in_specs=[
-                whole(mixed.shape),
-                whole(gathered.shape),
-                pl.BlockSpec((1, part_width, width), lambda i, *prefetched: (layer, 0, 0)),
+            in_specs=[whole(mixed.shape), whole(gathered.shape)]
+            + [pl.BlockSpec(memory_space=pl.ANY)] * len(weights),
+            out_specs=[whole(s) for s in shapes],
+            scratch_shapes=[
+                pltpu.VMEM((part_width, width), jnp.bfloat16),
+                pltpu.SemaphoreType.DMA((len(weights),)),
             ],
-            out_specs=[whole(s) for s in shapes],
-        ),
-        out_shape=[jax.ShapeDtypeStruct(s, jnp.bfloat16) for s in shapes],
+        ),
+        out_shape=out_shape,
         cost_estimate=pl.CostEstimate(
             flops=2 * rows * block * width * part_width,
             bytes_accessed=rows * block * width * 2,
@@ -240,7 +297,7 @@
         ),
         compiler_params=params(),
         name="finish",
-    )(picks, mixed, gathered, weights)
+    )(picks, section, mixed, gathered, *weights)
 
 
 def per_device(
@@ -276,32 +333,31 @@
     def exchange(value):
         return lax.all_to_all(value, "dom", split_axis=0, concat_axis=0, tiled=True)
 
+    def spread(pieces):
+        ring = range(section_count)
+        return [pieces[0]] + [
+            lax.ppermute(
+                pieces[distance], "section", [(s, (s + distance) % section_count) for s in ring]
+            )
+            for distance in range(1, section_count)
+        ]
+
     imports = [exchange(value) for value in outgoing]
     stale = [
-        lax.all_to_all(
-            turn_blocks(stale_imports[sub, 0], section_count),
-            "section",
-            split_axis=0,
-            concat_axis=0,
-            tiled=True,
-        )
+        spread(turn_blocks(section, stale_imports, (sub, 0), section_count))
         for sub in range(depth)
     ]
-    weights = lax.all_to_all(
-        layer_weights.transpose(0, 2, 1).reshape(depth, section_count, part_width, width),
-        "section",
-        split_axis=1,
-        concat_axis=0,
-        tiled=True,
-    ).reshape(layers, part_width, width)
+    weights = spread(turn_blocks(section, layer_weights[None], (0,), section_count))
 
     pieces = []
+    after = []
     for layer in range(layers):
         last = layer == layers - 1
         own_next, imports_next = [], []
         for index, stream in enumerate(streams):
             mixed = aggregate(
                 columns,
+                section,
                 initial_blocks[index],
                 adjacency_tiles,
                 own,
@@ -312,14 +368,17 @@
                 streams,
                 group_blocks,
                 part_count,
+                after,
             )
             gathered = lax.all_gather(mixed, "section", axis=0, tiled=False)
             result = finish(
-                picks, mixed, gathered, weights, layer, stream, group_blocks, part_count, last
+                picks, section, mixed, gathered, weights, layer, depth, stream, group_blocks,
+                part_count, last,
             )
             if last:
                 pieces.append(result[0])
             else:
+                after = [result[2]]
                 own_next.append(result[0])
                 imports_next.append(exchange(result[1]))
         own, imports = own_next, imports_next

time: 463 us -> 424 us (0.916)
  waiting for transfers between devices: 165 us -> 8.95 us
  starting transfers between devices: 19 us -> 88.8 us
  Pallas kernels: 89.7 us -> 128 us
  local copies, waits for them, and re-layouts: 21 us -> 34.7 us
  between operations: 13.8 us -> 0.65 us
  blocking collectives: 152 us -> 159 us
    all_gather x0 -> x16, blocking collectives: none -> 130 us  [per_device(): gathered = lax.all_gather(mixed, 'section', axis=0, tiled=False)]
    all_to_all x7 -> x2, blocking collectives: 152 us -> 28.8 us  [exchange(): return lax.all_to_all(value, 'dom', split_axis=0, concat_axis=0, tiled=True)]
    all_gather x8 -> x0, waiting for transfers between devices: 105 us -> none  [per_device(): gathered = lax.all_gather(mixed, 'section', axis=0, tiled=False)]
    all_to_all x1 -> x14, starting transfers between devices: 7.28 us -> 83.2 us  [exchange(): return lax.all_to_all(value, 'dom', split_axis=0, concat_axis=0, tiled=True)]
    all_to_all x3 -> x0, waiting for transfers between devices: 49 us -> none  [the longest x2 36.5 us: per_device(): lax.all_to_all(turn_blocks(stale_imports[sub, 0], section_count), 'sectio...]
    pallas_call x8 -> x16, Pallas kernels: 69.7 us -> 94.7 us  [aggregate(): pl.pallas_call(functools.partial(aggregate_kernel, plan), grid_spec=pltpu...]
    unnamed x29 -> x100, local copies, waits for them, and re-layouts: 15.4 us -> 33.6 us
    all_to_all x3 -> x0, starting transfers between devices: 11.4 us -> none  [the longest x2 7.92 us: per_device(): lax.all_to_all(turn_blocks(stale_imports[sub, 0], section_count), 'sectio...]
  transfers between devices with their start and end apart: 12 -> 23, of which waited for: 11 -> 2; matrix products, arithmetic and copies ran while one was open for 1% -> 0% of each run, Pallas kernels for 1% -> 25%
where the time goes in v7:
time: 424 us; the launch traced here: 420 us
  blocking collectives  159 us (38%)
  Pallas kernels  128 us (30%)
  starting transfers between devices  88.8 us (21%)
  local copies, waits for them, and re-layouts  34.7 us (8%)
  waiting for transfers between devices  8.95 us (2%)
    all_gather x16, blocking collectives, per_device(): gathered = lax.all_gather(mixed, 'section', axis=0, tiled=False)  130 us
    pallas_call x16, Pallas kernels, aggregate(): pl.pallas_call(functools.partial(aggregate_kernel, plan), grid_spec=pltpu...  94.7 us
    all_to_all x14, starting transfers between devices, exchange(): return lax.all_to_all(value, 'dom', split_axis=0, concat_axis=0, tiled=True)  83.2 us
    unnamed x100, local copies, waits for them, and re-layouts  33.6 us
    all_to_all x2, blocking collectives, exchange(): return lax.all_to_all(value, 'dom', split_axis=0, concat_axis=0, tiled=True)  28.8 us
    pallas_call x16, Pallas kernels, finish(): pl.pallas_call(functools.partial(finish_kernel, plan), grid_spec=pltpu.Pr...  26.6 us
    ppermute x9, waiting for transfers between devices, spread(): lax.ppermute(pieces[distance], 'section', [(s, (s + distance) % section_c...  8.91 us
  transfers between devices with their start and end apart: 23, of which 2 were waited for; matrix products, arithmetic and copies ran while one was open for 0% of the time, Pallas kernels for 25%

profile of v7, /device:TPU:0, one launch (start us, length us, event | category | flops | bytes accessed | tf_op | source)
XLA Modules:
  0.0 420.5 jit_solution(18412057474749760677)
XLA Ops:
  4.0 7.3 %all-to-all-start = ((bf16[8,2,96,128]{3,2,1,0:T(8,128)(2,1)}), bf16[8,2,96,128]{3,2,1,0:T(8,128)(2,1)S(1)}, u32[]{:S(2)}, u32[]{:S(2)}) async-start(bf16[8,2,96,128]{3,2,1,0:T(8,128)(2,1)} %get-tuple-element.64), calls=%async_computation | async-start | bytes 786432 | tf_op jit(solution)/shard_map/all_to_all | solution.py:334
  35.9 7.0 %aggregate.16.mixed_ref = bf16[8,96,128]{2,1,0:T(8,128)(2,1)S(1)} custom-call(s32[288]{0:T(512)S(1)} %reshape.24.columns, s32[1]{0:T(128)} %bitcast.info, bf16[8,96,128]{2,1,0:T(8,128)(2,1)S(1)} %get-tuple-element.63.initial_ref.refs_0_, bf16[12,24,128,128]{3,2,1,0:T(8,128)(2,1)} %tiles_ref.31, ...), custom_call_target="tpu_custom_call" | custom-call | flops 603979776 | bytes 6291456 | tf_op jit(solution)/shard_map/aggregate/pallas_call | solution.py:200
  42.9 9.4 %all-gather = bf16[32,96,128]{2,1,0:T(8,128)(2,1)S(1)} all-gather(bf16[8,96,128]{2,1,0:T(8,128)(2,1)S(1)} %aggregate.16.mixed_ref), channel_id=2, replica_groups=mesh['section'=4,'dom'=8] {'section'}, dimensions={0}, use_global_device_ids=true | all-gather | bytes 983040 | tf_op jit(solution)/shard_map/all_gather | solution.py:373
  70.9 16.2 %all-gather.1 = bf16[16,96,128]{2,1,0:T(8,128)(2,1)S(1)} all-gather(bf16[4,96,128]{2,1,0:T(8,128)(2,1)S(1)} %aggregate.17.mixed_ref), channel_id=3, replica_groups=mesh['section'=4,'dom'=8] {'section'}, dimensions={0}, use_global_device_ids=true | all-gather | bytes 491520 | tf_op jit(solution)/shard_map/all_gather | solution.py:373
  95.7 7.0 %aggregate.18.mixed_ref = bf16[8,96,128]{2,1,0:T(8,128)(2,1)S(1)} custom-call(s32[288]{0:T(512)S(1)} %reshape.24.columns, s32[1]{0:T(128)} %bitcast.info, bf16[8,96,128]{2,1,0:T(8,128)(2,1)S(1)} %get-tuple-element.63.initial_ref.refs_0_, bf16[12,24,128,128]{3,2,1,0:T(8,128)(2,1)} %tiles_ref.31, bf16[8,96,128]{2,1,0:T(8,128)(2,1)S(1)} %copy-done.21, ...), custom_call_target="tpu_custom_call" | custom-call | flops 603979776 | bytes 6291456 | tf_op jit(solution)/shard_map/aggregate/pallas_call | solution.py:200
  102.8 8.6 %all-gather.2 = bf16[32,96,128]{2,1,0:T(8,128)(2,1)S(1)} all-gather(bf16[8,96,128]{2,1,0:T(8,128)(2,1)S(1)} %aggregate.18.mixed_ref), channel_id=4, replica_groups=mesh['section'=4,'dom'=8] {'section'}, dimensions={0}, use_global_device_ids=true | all-gather | bytes 983040 | tf_op jit(solution)/shard_map/all_gather | solution.py:373
  144.1 7.2 %aggregate.20.mixed_ref = bf16[8,96,128]{2,1,0:T(8,128)(2,1)S(1)} custom-call(s32[288]{0:T(512)S(1)} %reshape.24.columns, s32[1]{0:T(128)} %bitcast.info, bf16[8,96,128]{2,1,0:T(8,128)(2,1)S(1)} %get-tuple-element.63.initial_ref.refs_0_, bf16[12,24,128,128]{3,2,1,0:T(8,128)(2,1)} %tiles_ref.31, bf16[8,96,128]{2,1,0:T(8,128)(2,1)S(1)} %copy-done.23, ...), custom_call_target="tpu_custom_call" | custom-call | flops 603979776 | bytes 6291456 | tf_op jit(solution)/shard_map/aggregate/pallas_call | solution.py:200
  151.3 8.6 %all-gather.4 = bf16[32,96,128]{2,1,0:T(8,128)(2,1)S(1)} all-gather(bf16[8,96,128]{2,1,0:T(8,128)(2,1)S(1)} %aggregate.20.mixed_ref), channel_id=6, replica_groups=mesh['section'=4,'dom'=8] {'section'}, dimensions={0}, use_global_device_ids=true | all-gather | bytes 983040 | tf_op jit(solution)/shard_map/all_gather | solution.py:373
  173.8 6.3 %all-gather.5 = bf16[16,96,128]{2,1,0:T(8,128)(2,1)S(1)} all-gather(bf16[4,96,128]{2,1,0:T(8,128)(2,1)S(1)} %aggregate.21.mixed_ref), channel_id=7, replica_groups=mesh['section'=4,'dom'=8] {'section'}, dimensions={0}, use_global_device_ids=true | all-gather | bytes 491520 | tf_op jit(solution)/shard_map/all_gather | solution.py:373
  188.6 7.0 %aggregate.22.mixed_ref = bf16[8,96,128]{2,1,0:T(8,128)(2,1)S(1)} custom-call(s32[288]{0:T(512)S(1)} %reshape.24.columns, s32[1]{0:T(128)} %bitcast.info, bf16[8,96,128]{2,1,0:T(8,128)(2,1)S(1)} %get-tuple-element.63.initial_ref.refs_0_, bf16[12,24,128,128]{3,2,1,0:T(8,128)(2,1)} %tiles_ref.31, bf16[8,96,128]{2,1,0:T(8,128)(2,1)S(1)} %copy-done.25, ...), custom_call_target="tpu_custom_call" | custom-call | flops 603979776 | bytes 6291456 | tf_op jit(solution)/shard_map/aggregate/pallas_call | solution.py:200
  195.7 8.6 %all-gather.6 = bf16[32,96,128]{2,1,0:T(8,128)(2,1)S(1)} all-gather(bf16[8,96,128]{2,1,0:T(8,128)(2,1)S(1)} %aggregate.22.mixed_ref), channel_id=8, replica_groups=mesh['section'=4,'dom'=8] {'section'}, dimensions={0}, use_global_device_ids=true | all-gather | bytes 983040 | tf_op jit(solution)/shard_map/all_gather | solution.py:373
  218.2 6.3 %all-gather.7 = bf16[16,96,128]{2,1,0:T(8,128)(2,1)S(1)} all-gather(bf16[4,96,128]{2,1,0:T(8,128)(2,1)S(1)} %aggregate.23.mixed_ref), channel_id=9, replica_groups=mesh['section'=4,'dom'=8] {'section'}, dimensions={0}, use_global_device_ids=true | all-gather | bytes 491520 | tf_op jit(solution)/shard_map/all_gather | solution.py:373
  237.0 7.0 %aggregate.24.mixed_ref = bf16[8,96,128]{2,1,0:T(8,128)(2,1)S(1)} custom-call(s32[288]{0:T(512)S(1)} %reshape.24.columns, s32[1]{0:T(128)} %bitcast.info, bf16[8,96,128]{2,1,0:T(8,128)(2,1)S(1)} %get-tuple-element.63.initial_ref.refs_0_, bf16[12,24,128,128]{3,2,1,0:T(8,128)(2,1)} %tiles_ref.31, bf16[8,96,128]{2,1,0:T(8,128)(2,1)S(1)} %copy-done.27, ...), custom_call_target="tpu_custom_call" | custom-call | flops 603979776 | bytes 6291456 | tf_op jit(solution)/shard_map/aggregate/pallas_call | solution.py:200
  244.1 8.6 %all-gather.8 = bf16[32,96,128]{2,1,0:T(8,128)(2,1)S(1)} all-gather(bf16[8,96,128]{2,1,0:T(8,128)(2,1)S(1)} %aggregate.24.mixed_ref), channel_id=10, replica_groups=mesh['section'=4,'dom'=8] {'section'}, dimensions={0}, use_global_device_ids=true | all-gather | bytes 983040 | tf_op jit(solution)/shard_map/all_gather | solution.py:373
  266.6 6.3 %all-gather.9 = bf16[16,96,128]{2,1,0:T(8,128)(2,1)S(1)} all-gather(bf16[4,96,128]{2,1,0:T(8,128)(2,1)S(1)} %aggregate.25.mixed_ref), channel_id=11, replica_groups=mesh['section'=4,'dom'=8] {'section'}, dimensions={0}, use_global_device_ids=true | all-gather | bytes 491520 | tf_op jit(solution)/shard_map/all_gather | solution.py:373
  281.4 7.2 %aggregate.26.mixed_ref = bf16[8,96,128]{2,1,0:T(8,128)(2,1)S(1)} custom-call(s32[288]{0:T(512)S(1)} %reshape.24.columns, s32[1]{0:T(128)} %bitcast.info, bf16[8,96,128]{2,1,0:T(8,128)(2,1)S(1)} %get-tuple-element.63.initial_ref.refs_0_, bf16[12,24,128,128]{3,2,1,0:T(8,128)(2,1)} %tiles_ref.31, bf16[8,96,128]{2,1,0:T(8,128)(2,1)S(1)} %copy-done.29, ...), custom_call_target="tpu_custom_call" | custom-call | flops 603979776 | bytes 6291456 | tf_op jit(solution)/shard_map/aggregate/pallas_call | solution.py:200
  288.6 8.6 %all-gather.10 = bf16[32,96,128]{2,1,0:T(8,128)(2,1)S(1)} all-gather(bf16[8,96,128]{2,1,0:T(8,128)(2,1)S(1)} %aggregate.26.mixed_ref), channel_id=12, replica_groups=mesh['section'=4,'dom'=8] {'section'}, dimensions={0}, use_global_device_ids=true | all-gather | bytes 983040 | tf_op jit(solution)/shard_map/all_gather | solution.py:373
  330.0 7.0 %aggregate.28.mixed_ref = bf16[8,96,128]{2,1,0:T(8,128)(2,1)S(1)} custom-call(s32[288]{0:T(512)S(1)} %reshape.24.columns, s32[1]{0:T(128)} %bitcast.info, bf16[8,96,128]{2,1,0:T(8,128)(2,1)S(1)} %get-tuple-element.63.initial_ref.refs_0_, bf16[12,24,128,128]{3,2,1,0:T(8,128)(2,1)} %tiles_ref.31, bf16[8,96,128]{2,1,0:T(8,128)(2,1)S(1)} %copy-done.31, ...), custom_call_target="tpu_custom_call" | custom-call | flops 603979776 | bytes 6291456 | tf_op jit(solution)/shard_map/aggregate/pallas_call | solution.py:200
  337.0 8.4 %all-gather.12 = bf16[32,96,128]{2,1,0:T(8,128)(2,1)S(1)} all-gather(bf16[8,96,128]{2,1,0:T(8,128)(2,1)S(1)} %aggregate.28.mixed_ref), channel_id=14, replica_groups=mesh['section'=4,'dom'=8] {'section'}, dimensions={0}, use_global_device_ids=true | all-gather | bytes 983040 | tf_op jit(solution)/shard_map/all_gather | solution.py:373
  352.9 6.6 %all-gather.13 = bf16[16,96,128]{2,1,0:T(8,128)(2,1)S(1)} all-gather(bf16[4,96,128]{2,1,0:T(8,128)(2,1)S(1)} %aggregate.29.mixed_ref), channel_id=15, replica_groups=mesh['section'=4,'dom'=8] {'section'}, dimensions={0}, use_global_device_ids=true | all-gather | bytes 491520 | tf_op jit(solution)/shard_map/all_gather | solution.py:373
  361.1 14.0 %all_to_all.80.refs_4_ = bf16[8,1,96,128]{3,2,1,0:T(8,128)(2,1)S(1)} all-to-all(bf16[8,1,96,128]{3,2,1,0:T(8,128)(2,1)S(1)} %get-tuple-element.120), channel_id=1, replica_groups=mesh['section'=4,'dom'=8] {'dom'}, dimensions={0} | all-to-all | bytes 393216 | tf_op jit(solution)/shard_map/all_to_all | solution.py:334
  375.1 14.8 %all_to_all.81.refs_1_.refs_2_ = bf16[8,2,96,128]{3,2,1,0:T(8,128)(2,1)S(1)} all-to-all(bf16[8,2,96,128]{3,2,1,0:T(8,128)(2,1)S(1)} %copy-done.41), channel_id=1, replica_groups=mesh['section'=4,'dom'=8] {'dom'}, dimensions={0} | all-to-all | bytes 786432 | tf_op jit(solution)/shard_map/all_to_all | solution.py:334
  401.7 7.0 %aggregate.30.mixed_ref = bf16[8,96,128]{2,1,0:T(8,128)(2,1)S(1)} custom-call(s32[288]{0:T(512)S(1)} %reshape.24.columns, s32[1]{0:T(128)} %bitcast.info, bf16[8,96,128]{2,1,0:T(8,128)(2,1)S(1)} %get-tuple-element.63.initial_ref.refs_0_, bf16[12,24,128,128]{3,2,1,0:T(8,128)(2,1)} %tiles_ref.31, bf16[8,96,128]{2,1,0:T(8,128)(2,1)S(1)} %copy-done.33, ...), custom_call_target="tpu_custom_call" | custom-call | flops 603979776 | bytes 6291456 | tf_op jit(solution)/shard_map/aggregate/pallas_call | solution.py:200
  408.7 8.7 %all-gather.14 = bf16[32,96,128]{2,1,0:T(8,128)(2,1)S(1)} all-gather(bf16[8,96,128]{2,1,0:T(8,128)(2,1)S(1)} %aggregate.30.mixed_ref), channel_id=16, replica_groups=mesh['section'=4,'dom'=8] {'section'}, dimensions={0}, use_global_device_ids=true | all-gather | bytes 983040 | tf_op jit(solution)/shard_map/all_gather | solution.py:373
  (183 shorter events, 216.1 us)
Async XLA Ops:
  4.0 22.0 %all-to-all-start = ((bf16[8,2,96,128]{3,2,1,0:T(8,128)(2,1)}), bf16[8,2,96,128]{3,2,1,0:T(8,128)(2,1)S(1)}, u32[]{:S(2)}, u32[]{:S(2)}) async-start(bf16[8,2,96,128]{3,2,1,0:T(8,128)(2,1)} %get-tuple-element.64), calls=%async_computation | async-start | bytes 786432 | tf_op jit(solution)/shard_map/all_to_all | solution.py:334
  15.0 11.1 %collective-permute-start = (bf16[16,96,128]{2,1,0:T(8,128)(2,1)}, bf16[16,96,128]{2,1,0:T(8,128)(2,1)S(1)}, u32[]{:S(2)}, u32[]{:S(2)}) collective-permute-start(bf16[16,96,128]{2,1,0:T(8,128)(2,1)} %get-tuple-element.66), channel_id=1, source_target_pairs={{0,8},{8,16},{16,24},{24,0},{1,9},{9,17},{17,25},{25,1},{2,10},{10... | collective-permute-start | bytes 1179656 | tf_op jit(solution)/shard_map/ppermute | solution.py:339
  15.0 17.1 %collective-permute-start.1 = (bf16[16,96,128]{2,1,0:T(8,128)(2,1)}, bf16[16,96,128]{2,1,0:T(8,128)(2,1)S(1)}, u32[]{:S(2)}, u32[]{:S(2)}) collective-permute-start(bf16[16,96,128]{2,1,0:T(8,128)(2,1)} %get-tuple-element.67), channel_id=1, source_target_pairs={{0,16},{8,24},{16,0},{24,8},{1,17},{9,25},{17,1},{25,9},{2,18},{10... | collective-permute-start | bytes 1179656 | tf_op jit(solution)/shard_map/ppermute | solution.py:339
  16.5 18.2 %collective-permute-start.2 = (bf16[16,96,128]{2,1,0:T(8,128)(2,1)}, bf16[16,96,128]{2,1,0:T(8,128)(2,1)S(1)}, u32[]{:S(2)}, u32[]{:S(2)}) collective-permute-start(bf16[16,96,128]{2,1,0:T(8,128)(2,1)} %get-tuple-element.68), channel_id=1, source_target_pairs={{0,24},{8,0},{16,8},{24,16},{1,25},{9,1},{17,9},{25,17},{2,26},{10... | collective-permute-start | bytes 1179656 | tf_op jit(solution)/shard_map/ppermute | solution.py:339
  19.1 33.2 %collective-permute-start.3 = (bf16[2,96,384]{2,1,0:T(8,128)(2,1)}, bf16[2,96,384]{2,1,0:T(8,128)(2,1)S(1)}, u32[]{:S(2)}, u32[]{:S(2)}) collective-permute-start(bf16[2,96,384]{2,1,0:T(8,128)(2,1)} %get-tuple-element.70), channel_id=1, source_target_pairs={{0,8},{8,16},{16,24},{24,0},{1,9},{9,17},{17,25},{25,1},{2,10},{10... | collective-permute-start | bytes 442376 | tf_op jit(solution)/shard_map/ppermute | solution.py:339
  19.1 33.2 %collective-permute-start.4 = (bf16[2,96,384]{2,1,0:T(8,128)(2,1)}, bf16[2,96,384]{2,1,0:T(8,128)(2,1)S(1)}, u32[]{:S(2)}, u32[]{:S(2)}) collective-permute-start(bf16[2,96,384]{2,1,0:T(8,128)(2,1)} %get-tuple-element.71), channel_id=1, source_target_pairs={{0,16},{8,24},{16,0},{24,8},{1,17},{9,25},{17,1},{25,9},{2,18},{10... | collective-permute-start | bytes 442376 | tf_op jit(solution)/shard_map/ppermute | solution.py:339
  26.1 26.2 %collective-permute-start.5 = (bf16[2,96,384]{2,1,0:T(8,128)(2,1)}, bf16[2,96,384]{2,1,0:T(8,128)(2,1)S(1)}, u32[]{:S(2)}, u32[]{:S(2)}) collective-permute-start(bf16[2,96,384]{2,1,0:T(8,128)(2,1)} %get-tuple-element.72), channel_id=1, source_target_pairs={{0,24},{8,0},{16,8},{24,16},{1,25},{9,1},{17,9},{25,17},{2,26},{10... | collective-permute-start | bytes 442376 | tf_op jit(solution)/shard_map/ppermute | solution.py:339
  26.1 28.2 %all-to-all-start.2 = ((bf16[8,1,96,128]{3,2,1,0:T(8,128)(2,1)}), bf16[8,1,96,128]{3,2,1,0:T(8,128)(2,1)S(1)}, u32[]{:S(2)}, u32[]{:S(2)}) async-start(bf16[8,1,96,128]{3,2,1,0:T(8,128)(2,1)} %get-tuple-element.80), calls=%async_computation.2 | async-start | bytes 393216 | tf_op jit(solution)/shard_map/all_to_all | solution.py:334
  54.3 34.4 %all-to-all-start.1 = ((bf16[8,2,96,128]{3,2,1,0:T(8,128)(2,1)}), bf16[8,2,96,128]{3,2,1,0:T(8,128)(2,1)S(1)}, u32[]{:S(2)}, u32[]{:S(2)}) async-start(bf16[8,2,96,128]{3,2,1,0:T(8,128)(2,1)} %get-tuple-element.74), calls=%async_computation.1 | async-start | bytes 786432 | tf_op jit(solution)/shard_map/all_to_all | solution.py:334
  64.0 30.7 %collective-permute-start.6 = (bf16[16,96,128]{2,1,0:T(8,128)(2,1)}, bf16[16,96,128]{2,1,0:T(8,128)(2,1)S(1)}, u32[]{:S(2)}, u32[]{:S(2)}) collective-permute-start(bf16[16,96,128]{2,1,0:T(8,128)(2,1)} %get-tuple-element.76), channel_id=1, source_target_pairs={{0,8},{8,16},{16,24},{24,0},{1,9},{9,17},{17,25},{25,1},{2,10},{10... | collective-permute-start | bytes 1179656 | tf_op jit(solution)/shard_map/ppermute | solution.py:339
  64.1 30.7 %collective-permute-start.7 = (bf16[16,96,128]{2,1,0:T(8,128)(2,1)}, bf16[16,96,128]{2,1,0:T(8,128)(2,1)S(1)}, u32[]{:S(2)}, u32[]{:S(2)}) collective-permute-start(bf16[16,96,128]{2,1,0:T(8,128)(2,1)} %get-tuple-element.77), channel_id=1, source_target_pairs={{0,16},{8,24},{16,0},{24,8},{1,17},{9,25},{17,1},{25,9},{2,18},{10... | collective-permute-start | bytes 1179656 | tf_op jit(solution)/shard_map/ppermute | solution.py:339
  64.7 30.1 %collective-permute-start.8 = (bf16[16,96,128]{2,1,0:T(8,128)(2,1)}, bf16[16,96,128]{2,1,0:T(8,128)(2,1)S(1)}, u32[]{:S(2)}, u32[]{:S(2)}) collective-permute-start(bf16[16,96,128]{2,1,0:T(8,128)(2,1)} %get-tuple-element.78), channel_id=1, source_target_pairs={{0,24},{8,0},{16,8},{24,16},{1,25},{9,1},{17,9},{25,17},{2,26},{10... | collective-permute-start | bytes 1179656 | tf_op jit(solution)/shard_map/ppermute | solution.py:339
  88.7 25.1 %all-to-all-start.4 = ((bf16[8,1,96,128]{3,2,1,0:T(8,128)(2,1)}), bf16[8,1,96,128]{3,2,1,0:T(8,128)(2,1)S(1)}, u32[]{:S(2)}, u32[]{:S(2)}) async-start(bf16[8,1,96,128]{3,2,1,0:T(8,128)(2,1)} %get-tuple-element.86), calls=%async_computation.4 | async-start | bytes 393216 | tf_op jit(solution)/shard_map/all_to_all | solution.py:334
  113.9 19.4 %all-to-all-start.3 = ((bf16[8,2,96,128]{3,2,1,0:T(8,128)(2,1)}), bf16[8,2,96,128]{3,2,1,0:T(8,128)(2,1)S(1)}, u32[]{:S(2)}, u32[]{:S(2)}) async-start(bf16[8,2,96,128]{3,2,1,0:T(8,128)(2,1)} %copy-done.35), calls=%async_computation.3 | async-start | bytes 786432 | tf_op jit(solution)/shard_map/all_to_all | solution.py:334
  133.3 29.1 %all-to-all-start.6 = ((bf16[8,1,96,128]{3,2,1,0:T(8,128)(2,1)}), bf16[8,1,96,128]{3,2,1,0:T(8,128)(2,1)S(1)}, u32[]{:S(2)}, u32[]{:S(2)}) async-start(bf16[8,1,96,128]{3,2,1,0:T(8,128)(2,1)} %get-tuple-element.92), calls=%async_computation.6 | async-start | bytes 393216 | tf_op jit(solution)/shard_map/all_to_all | solution.py:334
  162.4 19.4 %all-to-all-start.5 = ((bf16[8,2,96,128]{3,2,1,0:T(8,128)(2,1)}), bf16[8,2,96,128]{3,2,1,0:T(8,128)(2,1)S(1)}, u32[]{:S(2)}, u32[]{:S(2)}) async-start(bf16[8,2,96,128]{3,2,1,0:T(8,128)(2,1)} %copy-done.36), calls=%async_computation.5 | async-start | bytes 786432 | tf_op jit(solution)/shard_map/all_to_all | solution.py:334
  181.8 24.9 %all-to-all-start.8 = ((bf16[8,1,96,128]{3,2,1,0:T(8,128)(2,1)}), bf16[8,1,96,128]{3,2,1,0:T(8,128)(2,1)S(1)}, u32[]{:S(2)}, u32[]{:S(2)}) async-start(bf16[8,1,96,128]{3,2,1,0:T(8,128)(2,1)} %get-tuple-element.98), calls=%async_computation.8 | async-start | bytes 393216 | tf_op jit(solution)/shard_map/all_to_all | solution.py:334
  206.8 19.4 %all-to-all-start.7 = ((bf16[8,2,96,128]{3,2,1,0:T(8,128)(2,1)}), bf16[8,2,96,128]{3,2,1,0:T(8,128)(2,1)S(1)}, u32[]{:S(2)}, u32[]{:S(2)}) async-start(bf16[8,2,96,128]{3,2,1,0:T(8,128)(2,1)} %copy-done.37), calls=%async_computation.7 | async-start | bytes 786432 | tf_op jit(solution)/shard_map/all_to_all | solution.py:334
  226.2 28.9 %all-to-all-start.10 = ((bf16[8,1,96,128]{3,2,1,0:T(8,128)(2,1)}), bf16[8,1,96,128]{3,2,1,0:T(8,128)(2,1)S(1)}, u32[]{:S(2)}, u32[]{:S(2)}) async-start(bf16[8,1,96,128]{3,2,1,0:T(8,128)(2,1)} %get-tuple-element.104), calls=%async_computation.10 | async-start | bytes 393216 | tf_op jit(solution)/shard_map/all_to_all | solution.py:334
  255.2 19.4 %all-to-all-start.9 = ((bf16[8,2,96,128]{3,2,1,0:T(8,128)(2,1)}), bf16[8,2,96,128]{3,2,1,0:T(8,128)(2,1)S(1)}, u32[]{:S(2)}, u32[]{:S(2)}) async-start(bf16[8,2,96,128]{3,2,1,0:T(8,128)(2,1)} %copy-done.38), calls=%async_computation.9 | async-start | bytes 786432 | tf_op jit(solution)/shard_map/all_to_all | solution.py:334
  274.6 25.2 %all-to-all-start.12 = ((bf16[8,1,96,128]{3,2,1,0:T(8,128)(2,1)}), bf16[8,1,96,128]{3,2,1,0:T(8,128)(2,1)S(1)}, u32[]{:S(2)}, u32[]{:S(2)}) async-start(bf16[8,1,96,128]{3,2,1,0:T(8,128)(2,1)} %get-tuple-element.110), calls=%async_computation.12 | async-start | bytes 393216 | tf_op jit(solution)/shard_map/all_to_all | solution.py:334
  299.8 19.4 %all-to-all-start.11 = ((bf16[8,2,96,128]{3,2,1,0:T(8,128)(2,1)}), bf16[8,2,96,128]{3,2,1,0:T(8,128)(2,1)S(1)}, u32[]{:S(2)}, u32[]{:S(2)}) async-start(bf16[8,2,96,128]{3,2,1,0:T(8,128)(2,1)} %copy-done.39), calls=%async_computation.11 | async-start | bytes 786432 | tf_op jit(solution)/shard_map/all_to_all | solution.py:334
  319.2 28.9 %all-to-all-start.14 = ((bf16[8,1,96,128]{3,2,1,0:T(8,128)(2,1)}), bf16[8,1,96,128]{3,2,1,0:T(8,128)(2,1)S(1)}, u32[]{:S(2)}, u32[]{:S(2)}) async-start(bf16[8,1,96,128]{3,2,1,0:T(8,128)(2,1)} %get-tuple-element.116), calls=%async_computation.14 | async-start | bytes 393216 | tf_op jit(solution)/shard_map/all_to_all | solution.py:334
  348.1 41.8 %copy-start.33 = (bf16[8,96,128]{2,1,0:T(8,128)(2,1)S(1)}, bf16[8,96,128]{2,1,0:T(8,128)(2,1)}, u32[]{:S(2)}) copy-start(bf16[8,96,128]{2,1,0:T(8,128)(2,1)} %get-tuple-element.113.refs_0_) | copy-start | bytes 589828
  (49 other events, 297.6 us)

commit v8 on v7

--- a/solution.py
+++ b/solution.py
@@ -25,6 +25,14 @@
     return pltpu.HBM(shape, jnp.bfloat16)
 
 
+hbm = pl.BlockSpec(memory_space=pltpu.HBM)
+anywhere = pl.BlockSpec(memory_space=pl.ANY)
+
+
+def pinned(value):
+    return pltpu.with_memory_space_constraint(value, pltpu.HBM)
+
+
 def start_all(copies):
     for condition, copy in copies:
         if condition is None:
@@ -56,7 +64,7 @@
         lax.fori_loop(0, part_count, pick, 0)
 
 
-def prologue_kernel(streams, group_blocks, part_count, info, picks, rows_ref, *refs):
+def prologue_kernel(streams, group_blocks, part_count, info, picks, rows_ref, unused, *refs):
     own_refs = refs[: len(streams)]
     outgoing_refs = refs[len(streams) : 2 * len(streams)]
     turned = refs[-1]
@@ -71,7 +79,7 @@
         pick_outgoing(picks, own_ref, outgoing_ref, stream, group_blocks, part_count)
 
 
-def prologue(initial_features, section, picks, streams, group_blocks, block, part_width, part_count):
+def prologue(initial_features, section, picks, after, streams, group_blocks, block, part_width, part_count):
     rows, width = initial_features.shape
     own_shapes = [(len(s) * group_blocks, part_width, block) for s in streams]
     out_shapes = [(part_count, len(s), part_width, block) for s in streams]
@@ -80,14 +88,15 @@
         grid_spec=pltpu.PrefetchScalarGridSpec(
             num_scalar_prefetch=2,
             grid=(1,),
-            in_specs=[whole((rows, width))],
+            in_specs=[whole((rows, width)), hbm],
             out_specs=[whole(s) for s in own_shapes + out_shapes],
             scratch_shapes=[pltpu.VMEM((2, width, block), jnp.bfloat16)],
         ),
-        out_shape=[jax.ShapeDtypeStruct(s, jnp.bfloat16) for s in own_shapes + out_shapes],
+        out_shape=[in_hbm(s) for s in own_shapes]
+        + [jax.ShapeDtypeStruct(s, jnp.bfloat16) for s in out_shapes],
         compiler_params=params(),
         name="prologue",
-    )(section, picks, initial_features)
+    )(section, picks, pinned(initial_features), pinned(after))
 
 
 def turn_kernel(info, in_ref, *refs):
@@ -120,7 +129,7 @@
         out_shape=[in_hbm((count, part_width, rows))] * sections,
         compiler_params=params(),
         name="turn",
-    )(section, blocks)
+    )(section, pinned(blocks))
 
 
 def aggregate_kernel(plan, columns, info, initial_ref, tiles_ref, *refs):
@@ -150,17 +159,14 @@
             )
         )
     start_all(copies)
-    for row in range(min(2, rows)):
+    initial_copy.start()
+    for row in range(rows):
         tile_copy(row).start()
-    initial_copy.start()
     wait_all(copies)
-
-    for row in range(rows):
+    initial_copy.wait()
+
+    def one_row(row, carry):
         tile_copy(row).wait()
-        if row + 2 < rows:
-            tile_copy(row + 2).start()
-        if row == 0:
-            initial_copy.wait()
         base = (first_row + row) * fanout
         total = None
         for tile in range(0, fanout, 2):
@@ -174,26 +180,33 @@
         mixed_ref[row] = (
             (1.0 - alpha_mix) * total + alpha_mix * initial[row].astype(jnp.float32)
         ).astype(jnp.bfloat16)
+        return carry
+
+    lax.fori_loop(0, rows, one_row, 0)
 
 
 def aggregate(columns, section, initial_blocks, tiles, own, imports, stale, home, stream, streams, group_blocks, part_count, after):
     rows, part_width, block = initial_blocks.shape
     blocks_dev, fanout = tiles.shape[:2]
     groups = blocks_dev // group_blocks
-    sources, operands = [], []
+    sources, operands, specs = [], [], []
     for other, own_blocks, imported in zip(streams, own, imports):
         if other[0] > stream[-1]:
             continue
         sources.append(("own", other[0] * group_blocks, None))
-        operands.append(own_blocks)
+        operands.append(pinned(own_blocks))
+        specs.append(hbm)
         for local, group in enumerate(other):
             sources.append(("import", blocks_dev + group * part_count, local))
             operands.append(imported)
+            specs.append(anywhere)
     if groups > 1 and stream[0] < groups - 1:
         for distance, stale_blocks in enumerate(stale):
             sources.append(("stale", blocks_dev + groups * part_count, distance))
-            operands.append(stale_blocks)
+            operands.append(pinned(stale_blocks))
+            specs.append(hbm)
     operands += after
+    specs += [anywhere] * len(after)
     table_size = blocks_dev + (2 * groups - 1) * part_count
     plan = (stream, group_blocks, fanout, sources, home, len(stale))
     flops = 2 * rows * fanout * block * block * part_width
@@ -202,7 +215,7 @@
         grid_spec=pltpu.PrefetchScalarGridSpec(
             num_scalar_prefetch=2,
             grid=(1,),
-            in_specs=[pl.BlockSpec(memory_space=pl.ANY)] * (2 + len(operands)),
+            in_specs=[hbm, hbm] + specs,
             out_specs=whole((rows, part_width, block)),
             scratch_shapes=[
                 pltpu.VMEM((table_size, part_width, block), jnp.bfloat16),
@@ -219,7 +232,7 @@
         ),
         compiler_params=params(),
         name="aggregate",
-    )(columns, section, initial_blocks, tiles, *operands)
+    )(columns, section, pinned(initial_blocks), pinned(tiles), *operands)
 
 
 def finish_kernel(plan, picks, info, mixed_ref, gathered_ref, *refs):
@@ -282,7 +295,7 @@
             num_scalar_prefetch=2,
             grid=(1,),
             in_specs=[whole(mixed.shape), whole(gathered.shape)]
-            + [pl.BlockSpec(memory_space=pl.ANY)] * len(weights),
+            + [hbm] * len(weights),
             out_specs=[whole(s) for s in shapes],
             scratch_shapes=[
                 pltpu.VMEM((part_width, width), jnp.bfloat16),
@@ -297,7 +310,7 @@
         ),
         compiler_params=params(),
         name="finish",
-    )(picks, section, mixed, gathered, *weights)
+    )(picks, section, mixed, gathered, *[pinned(w) for w in weights])
 
 
 def per_device(
@@ -323,8 +336,11 @@
         is_stale, tile_columns + (groups - 1) * part_count, tile_columns
     ).reshape(-1)
 
+    turned = [
+        turn_blocks(section, stale_imports, (sub, 0), section_count) for sub in range(depth)
+    ]
     started = prologue(
-        initial_features, section, picks, streams, group_blocks, block, part_width, part_count
+        initial_features, section, picks, turned[0][0], streams, group_blocks, block, part_width, part_count
     )
     own = started[: len(streams)]
     outgoing = started[len(streams) :]
@@ -343,10 +359,7 @@
         ]
 
     imports = [exchange(value) for value in outgoing]
-    stale = [
-        spread(turn_blocks(section, stale_imports, (sub, 0), section_count))
-        for sub in range(depth)
-    ]
+    stale = [spread(pieces) for pieces in turned]
     weights = spread(turn_blocks(section, layer_weights[None], (0,), section_count))
 
     pieces = []

time: 424 us -> 401 us (0.946)
  local copies, waits for them, and re-layouts: 34.7 us -> 3.54 us
  Pallas kernels: 128 us -> 138 us
    unnamed x100 -> x20, local copies, waits for them, and re-layouts: 33.6 us -> 2.48 us
    pallas_call x16, Pallas kernels: 26.6 us -> 39.7 us  [finish(): pl.pallas_call(functools.partial(finish_kernel, plan), grid_spec=pltpu.Pr...]
    pallas_call x16, Pallas kernels: 94.7 us -> 87 us  [aggregate(): pl.pallas_call(functools.partial(aggregate_kernel, plan), grid_spec=pltpu...]
  transfers between devices with their start and end apart: 23 -> 23, of which waited for: 2 -> 3; matrix products, arithmetic and copies ran while one was open for 0% -> 0% of each run, Pallas kernels for 25% -> 28%
where the time goes in v8:
time: 401 us; the launch traced here: 398 us
  blocking collectives  158 us (39%)
  Pallas kernels  138 us (34%)
  starting transfers between devices  88.1 us (22%)
  waiting for transfers between devices  8.54 us (2%)
    all_gather x16, blocking collectives, per_device(): gathered = lax.all_gather(mixed, 'section', axis=0, tiled=False)  130 us
    pallas_call x16, Pallas kernels, aggregate(): pl.pallas_call(functools.partial(aggregate_kernel, plan), grid_spec=pltpu...  87 us
    all_to_all x14, starting transfers between devices, exchange(): return lax.all_to_all(value, 'dom', split_axis=0, concat_axis=0, tiled=True)  82.5 us
    pallas_call x16, Pallas kernels, finish(): pl.pallas_call(functools.partial(finish_kernel, plan), grid_spec=pltpu.Pr...  39.7 us
    all_to_all x2, blocking collectives, exchange(): return lax.all_to_all(value, 'dom', split_axis=0, concat_axis=0, tiled=True)  28.8 us
    pallas_call x3, Pallas kernels, turn_blocks(): pl.pallas_call(turn_kernel, grid_spec=pltpu.PrefetchScalarGridSpec(num_sc...  8.04 us
  transfers between devices with their start and end apart: 23, of which 3 were waited for; matrix products, arithmetic and copies ran while one was open for 0% of the time, Pallas kernels for 28%

profile of v8, /device:TPU:0, one launch (start us, length us, event | category | flops | bytes accessed | tf_op | source)
XLA Modules:
  0.0 397.9 jit_solution(8784544554690490226)
XLA Ops:
  7.1 7.3 %all-to-all-start = ((bf16[8,2,96,128]{3,2,1,0:T(8,128)(2,1)}), bf16[8,2,96,128]{3,2,1,0:T(8,128)(2,1)S(1)}, u32[]{:S(2)}, u32[]{:S(2)}) async-start(bf16[8,2,96,128]{3,2,1,0:T(8,128)(2,1)} %get-tuple-element.65), calls=%async_computation | async-start | bytes 786432 | tf_op jit(solution)/shard_map/all_to_all | solution.py:350
  34.9 6.8 %aggregate.16.mixed_ref = bf16[8,96,128]{2,1,0:T(8,128)(2,1)S(1)} custom-call(s32[288]{0:T(512)S(1)} %reshape.24.columns, s32[1]{0:T(128)} %bitcast.info, bf16[8,96,128]{2,1,0:T(8,128)(2,1)} %get-tuple-element.64.initial_ref.refs_0_, bf16[12,24,128,128]{3,2,1,0:T(8,128)(2,1)} %tiles_ref.31, bf16[8,96,128]{2,1,0:T(8,128)(2,1)} %get-tuple-element.64.initial_ref.refs_0_, ...), custom_call_target="tpu_custom_call" | custom-call | flops 603979776 | bytes 6291456 | tf_op jit(solution)/shard_map/aggregate/pallas_call | solution.py:213
  41.7 9.4 %all-gather = bf16[32,96,128]{2,1,0:T(8,128)(2,1)S(1)} all-gather(bf16[8,96,128]{2,1,0:T(8,128)(2,1)S(1)} %aggregate.16.mixed_ref), channel_id=2, replica_groups=mesh['section'=4,'dom'=8] {'section'}, dimensions={0}, use_global_device_ids=true | all-gather | bytes 983040 | tf_op jit(solution)/shard_map/all_gather | solution.py:386
  69.8 16.6 %all-gather.1 = bf16[16,96,128]{2,1,0:T(8,128)(2,1)S(1)} all-gather(bf16[4,96,128]{2,1,0:T(8,128)(2,1)S(1)} %aggregate.17.mixed_ref), channel_id=3, replica_groups=mesh['section'=4,'dom'=8] {'section'}, dimensions={0}, use_global_device_ids=true | all-gather | bytes 491520 | tf_op jit(solution)/shard_map/all_gather | solution.py:386
  96.0 6.6 %aggregate.18.mixed_ref = bf16[8,96,128]{2,1,0:T(8,128)(2,1)S(1)} custom-call(s32[288]{0:T(512)S(1)} %reshape.24.columns, s32[1]{0:T(128)} %bitcast.info, bf16[8,96,128]{2,1,0:T(8,128)(2,1)} %get-tuple-element.64.initial_ref.refs_0_, bf16[12,24,128,128]{3,2,1,0:T(8,128)(2,1)} %tiles_ref.31, bf16[8,96,128]{2,1,0:T(8,128)(2,1)} %get-tuple-element.73.refs_0_, ...), custom_call_target="tpu_custom_call" | custom-call | flops 603979776 | bytes 6291456 | tf_op jit(solution)/shard_map/aggregate/pallas_call | solution.py:213
  102.6 8.4 %all-gather.2 = bf16[32,96,128]{2,1,0:T(8,128)(2,1)S(1)} all-gather(bf16[8,96,128]{2,1,0:T(8,128)(2,1)S(1)} %aggregate.18.mixed_ref), channel_id=4, replica_groups=mesh['section'=4,'dom'=8] {'section'}, dimensions={0}, use_global_device_ids=true | all-gather | bytes 983040 | tf_op jit(solution)/shard_map/all_gather | solution.py:386
  123.7 6.3 %all-gather.3 = bf16[16,96,128]{2,1,0:T(8,128)(2,1)S(1)} all-gather(bf16[4,96,128]{2,1,0:T(8,128)(2,1)S(1)} %aggregate.19.mixed_ref), channel_id=5, replica_groups=mesh['section'=4,'dom'=8] {'section'}, dimensions={0}, use_global_device_ids=true | all-gather | bytes 491520 | tf_op jit(solution)/shard_map/all_gather | solution.py:386
  138.4 6.6 %aggregate.20.mixed_ref = bf16[8,96,128]{2,1,0:T(8,128)(2,1)S(1)} custom-call(s32[288]{0:T(512)S(1)} %reshape.24.columns, s32[1]{0:T(128)} %bitcast.info, bf16[8,96,128]{2,1,0:T(8,128)(2,1)} %get-tuple-element.64.initial_ref.refs_0_, bf16[12,24,128,128]{3,2,1,0:T(8,128)(2,1)} %tiles_ref.31, bf16[8,96,128]{2,1,0:T(8,128)(2,1)} %get-tuple-element.83.refs_0_, ...), custom_call_target="tpu_custom_call" | custom-call | flops 603979776 | bytes 6291456 | tf_op jit(solution)/shard_map/aggregate/pallas_call | solution.py:213
  145.0 8.4 %all-gather.4 = bf16[32,96,128]{2,1,0:T(8,128)(2,1)S(1)} all-gather(bf16[8,96,128]{2,1,0:T(8,128)(2,1)S(1)} %aggregate.20.mixed_ref), channel_id=6, replica_groups=mesh['section'=4,'dom'=8] {'section'}, dimensions={0}, use_global_device_ids=true | all-gather | bytes 983040 | tf_op jit(solution)/shard_map/all_gather | solution.py:386
  180.8 6.6 %aggregate.22.mixed_ref = bf16[8,96,128]{2,1,0:T(8,128)(2,1)S(1)} custom-call(s32[288]{0:T(512)S(1)} %reshape.24.columns, s32[1]{0:T(128)} %bitcast.info, bf16[8,96,128]{2,1,0:T(8,128)(2,1)} %get-tuple-element.64.initial_ref.refs_0_, bf16[12,24,128,128]{3,2,1,0:T(8,128)(2,1)} %tiles_ref.31, bf16[8,96,128]{2,1,0:T(8,128)(2,1)} %get-tuple-element.89.refs_0_, ...), custom_call_target="tpu_custom_call" | custom-call | flops 603979776 | bytes 6291456 | tf_op jit(solution)/shard_map/aggregate/pallas_call | solution.py:213
  187.4 8.4 %all-gather.6 = bf16[32,96,128]{2,1,0:T(8,128)(2,1)S(1)} all-gather(bf16[8,96,128]{2,1,0:T(8,128)(2,1)S(1)} %aggregate.22.mixed_ref), channel_id=8, replica_groups=mesh['section'=4,'dom'=8] {'section'}, dimensions={0}, use_global_device_ids=true | all-gather | bytes 983040 | tf_op jit(solution)/shard_map/all_gather | solution.py:386
  223.2 6.6 %aggregate.24.mixed_ref = bf16[8,96,128]{2,1,0:T(8,128)(2,1)S(1)} custom-call(s32[288]{0:T(512)S(1)} %reshape.24.columns, s32[1]{0:T(128)} %bitcast.info, bf16[8,96,128]{2,1,0:T(8,128)(2,1)} %get-tuple-element.64.initial_ref.refs_0_, bf16[12,24,128,128]{3,2,1,0:T(8,128)(2,1)} %tiles_ref.31, bf16[8,96,128]{2,1,0:T(8,128)(2,1)} %get-tuple-element.95.refs_0_, ...), custom_call_target="tpu_custom_call" | custom-call | flops 603979776 | bytes 6291456 | tf_op jit(solution)/shard_map/aggregate/pallas_call | solution.py:213
  229.8 8.4 %all-gather.8 = bf16[32,96,128]{2,1,0:T(8,128)(2,1)S(1)} all-gather(bf16[8,96,128]{2,1,0:T(8,128)(2,1)S(1)} %aggregate.24.mixed_ref), channel_id=10, replica_groups=mesh['section'=4,'dom'=8] {'section'}, dimensions={0}, use_global_device_ids=true | all-gather | bytes 983040 | tf_op jit(solution)/shard_map/all_gather | solution.py:386
  251.0 6.3 %all-gather.9 = bf16[16,96,128]{2,1,0:T(8,128)(2,1)S(1)} all-gather(bf16[4,96,128]{2,1,0:T(8,128)(2,1)S(1)} %aggregate.25.mixed_ref), channel_id=11, replica_groups=mesh['section'=4,'dom'=8] {'section'}, dimensions={0}, use_global_device_ids=true | all-gather | bytes 491520 | tf_op jit(solution)/shard_map/all_gather | solution.py:386
  265.6 6.6 %aggregate.26.mixed_ref = bf16[8,96,128]{2,1,0:T(8,128)(2,1)S(1)} custom-call(s32[288]{0:T(512)S(1)} %reshape.24.columns, s32[1]{0:T(128)} %bitcast.info, bf16[8,96,128]{2,1,0:T(8,128)(2,1)} %get-tuple-element.64.initial_ref.refs_0_, bf16[12,24,128,128]{3,2,1,0:T(8,128)(2,1)} %tiles_ref.31, bf16[8,96,128]{2,1,0:T(8,128)(2,1)} %get-tuple-element.101.refs_0_, ...), custom_call_target="tpu_custom_call" | custom-call | flops 603979776 | bytes 6291456 | tf_op jit(solution)/shard_map/aggregate/pallas_call | solution.py:213
  272.2 8.4 %all-gather.10 = bf16[32,96,128]{2,1,0:T(8,128)(2,1)S(1)} all-gather(bf16[8,96,128]{2,1,0:T(8,128)(2,1)S(1)} %aggregate.26.mixed_ref), channel_id=12, replica_groups=mesh['section'=4,'dom'=8] {'section'}, dimensions={0}, use_global_device_ids=true | all-gather | bytes 983040 | tf_op jit(solution)/shard_map/all_gather | solution.py:386
  293.4 6.3 %all-gather.11 = bf16[16,96,128]{2,1,0:T(8,128)(2,1)S(1)} all-gather(bf16[4,96,128]{2,1,0:T(8,128)(2,1)S(1)} %aggregate.27.mixed_ref), channel_id=13, replica_groups=mesh['section'=4,'dom'=8] {'section'}, dimensions={0}, use_global_device_ids=true | all-gather | bytes 491520 | tf_op jit(solution)/shard_map/all_gather | solution.py:386
  308.0 6.7 %aggregate.28.mixed_ref = bf16[8,96,128]{2,1,0:T(8,128)(2,1)S(1)} custom-call(s32[288]{0:T(512)S(1)} %reshape.24.columns, s32[1]{0:T(128)} %bitcast.info, bf16[8,96,128]{2,1,0:T(8,128)(2,1)} %get-tuple-element.64.initial_ref.refs_0_, bf16[12,24,128,128]{3,2,1,0:T(8,128)(2,1)} %tiles_ref.31, bf16[8,96,128]{2,1,0:T(8,128)(2,1)} %get-tuple-element.107.refs_0_, ...), custom_call_target="tpu_custom_call" | custom-call | flops 603979776 | bytes 6291456 | tf_op jit(solution)/shard_map/aggregate/pallas_call | solution.py:213
  314.7 8.4 %all-gather.12 = bf16[32,96,128]{2,1,0:T(8,128)(2,1)S(1)} all-gather(bf16[8,96,128]{2,1,0:T(8,128)(2,1)S(1)} %aggregate.28.mixed_ref), channel_id=14, replica_groups=mesh['section'=4,'dom'=8] {'section'}, dimensions={0}, use_global_device_ids=true | all-gather | bytes 983040 | tf_op jit(solution)/shard_map/all_gather | solution.py:386
  329.9 6.6 %all-gather.13 = bf16[16,96,128]{2,1,0:T(8,128)(2,1)S(1)} all-gather(bf16[4,96,128]{2,1,0:T(8,128)(2,1)S(1)} %aggregate.29.mixed_ref), channel_id=15, replica_groups=mesh['section'=4,'dom'=8] {'section'}, dimensions={0}, use_global_device_ids=true | all-gather | bytes 491520 | tf_op jit(solution)/shard_map/all_gather | solution.py:386
  338.9 14.0 %all_to_all.80.refs_4_ = bf16[8,1,96,128]{3,2,1,0:T(8,128)(2,1)S(1)} all-to-all(bf16[8,1,96,128]{3,2,1,0:T(8,128)(2,1)S(1)} %get-tuple-element.120), channel_id=1, replica_groups=mesh['section'=4,'dom'=8] {'dom'}, dimensions={0} | all-to-all | bytes 393216 | tf_op jit(solution)/shard_map/all_to_all | solution.py:350
  352.8 14.8 %all_to_all.81.refs_1_.refs_2_ = bf16[8,2,96,128]{3,2,1,0:T(8,128)(2,1)S(1)} all-to-all(bf16[8,2,96,128]{3,2,1,0:T(8,128)(2,1)S(1)} %get-tuple-element.114), channel_id=1, replica_groups=mesh['section'=4,'dom'=8] {'dom'}, dimensions={0} | all-to-all | bytes 786432 | tf_op jit(solution)/shard_map/all_to_all | solution.py:350
  378.0 6.6 %aggregate.30.mixed_ref = bf16[8,96,128]{2,1,0:T(8,128)(2,1)S(1)} custom-call(s32[288]{0:T(512)S(1)} %reshape.24.columns, s32[1]{0:T(128)} %bitcast.info, bf16[8,96,128]{2,1,0:T(8,128)(2,1)} %get-tuple-element.64.initial_ref.refs_0_, bf16[12,24,128,128]{3,2,1,0:T(8,128)(2,1)} %tiles_ref.31, bf16[8,96,128]{2,1,0:T(8,128)(2,1)} %get-tuple-element.113.refs_0_, ...), custom_call_target="tpu_custom_call" | custom-call | flops 603979776 | bytes 6291456 | tf_op jit(solution)/shard_map/aggregate/pallas_call | solution.py:213
  384.6 8.7 %all-gather.14 = bf16[32,96,128]{2,1,0:T(8,128)(2,1)S(1)} all-gather(bf16[8,96,128]{2,1,0:T(8,128)(2,1)S(1)} %aggregate.30.mixed_ref), channel_id=16, replica_groups=mesh['section'=4,'dom'=8] {'section'}, dimensions={0}, use_global_device_ids=true | all-gather | bytes 983040 | tf_op jit(solution)/shard_map/all_gather | solution.py:386
  (103 shorter events, 197.3 us)
Async XLA Ops:
  0.0 20.1 %copy-start.9 = (s32[12,24]{1,0:T(8,128)S(1)}, s32[12,24]{1,0:T(8,128)}, u32[]{:S(2)}) copy-start(s32[12,24]{1,0:T(8,128)} %param.9) | copy-start | bytes 3460
  7.1 19.0 %all-to-all-start = ((bf16[8,2,96,128]{3,2,1,0:T(8,128)(2,1)}), bf16[8,2,96,128]{3,2,1,0:T(8,128)(2,1)S(1)}, u32[]{:S(2)}, u32[]{:S(2)}) async-start(bf16[8,2,96,128]{3,2,1,0:T(8,128)(2,1)} %get-tuple-element.65), calls=%async_computation | async-start | bytes 786432 | tf_op jit(solution)/shard_map/all_to_all | solution.py:350
  14.4 11.0 %collective-permute-start = (bf16[16,96,128]{2,1,0:T(8,128)(2,1)}, bf16[16,96,128]{2,1,0:T(8,128)(2,1)S(1)}, u32[]{:S(2)}, u32[]{:S(2)}) collective-permute-start(bf16[16,96,128]{2,1,0:T(8,128)(2,1)} %get-tuple-element.66), channel_id=1, source_target_pairs={{0,8},{8,16},{16,24},{24,0},{1,9},{9,17},{17,25},{25,1},{2,10},{10... | collective-permute-start | bytes 1179656 | tf_op jit(solution)/shard_map/ppermute | solution.py:355
  14.4 17.1 %collective-permute-start.1 = (bf16[16,96,128]{2,1,0:T(8,128)(2,1)}, bf16[16,96,128]{2,1,0:T(8,128)(2,1)S(1)}, u32[]{:S(2)}, u32[]{:S(2)}) collective-permute-start(bf16[16,96,128]{2,1,0:T(8,128)(2,1)} %get-tuple-element.67), channel_id=1, source_target_pairs={{0,16},{8,24},{16,0},{24,8},{1,17},{9,25},{17,1},{25,9},{2,18},{10... | collective-permute-start | bytes 1179656 | tf_op jit(solution)/shard_map/ppermute | solution.py:355
  15.9 18.2 %collective-permute-start.2 = (bf16[16,96,128]{2,1,0:T(8,128)(2,1)}, bf16[16,96,128]{2,1,0:T(8,128)(2,1)S(1)}, u32[]{:S(2)}, u32[]{:S(2)}) collective-permute-start(bf16[16,96,128]{2,1,0:T(8,128)(2,1)} %get-tuple-element.68), channel_id=1, source_target_pairs={{0,24},{8,0},{16,8},{24,16},{1,25},{9,1},{17,9},{25,17},{2,26},{10... | collective-permute-start | bytes 1179656 | tf_op jit(solution)/shard_map/ppermute | solution.py:355
  19.5 31.5 %collective-permute-start.3 = (bf16[2,96,384]{2,1,0:T(8,128)(2,1)}, bf16[2,96,384]{2,1,0:T(8,128)(2,1)S(1)}, u32[]{:S(2)}, u32[]{:S(2)}) collective-permute-start(bf16[2,96,384]{2,1,0:T(8,128)(2,1)} %get-tuple-element.70), channel_id=1, source_target_pairs={{0,8},{8,16},{16,24},{24,0},{1,9},{9,17},{17,25},{25,1},{2,10},{10... | collective-permute-start | bytes 442376 | tf_op jit(solution)/shard_map/ppermute | solution.py:355
  19.5 31.5 %collective-permute-start.4 = (bf16[2,96,384]{2,1,0:T(8,128)(2,1)}, bf16[2,96,384]{2,1,0:T(8,128)(2,1)S(1)}, u32[]{:S(2)}, u32[]{:S(2)}) collective-permute-start(bf16[2,96,384]{2,1,0:T(8,128)(2,1)} %get-tuple-element.71), channel_id=1, source_target_pairs={{0,16},{8,24},{16,0},{24,8},{1,17},{9,25},{17,1},{25,9},{2,18},{10... | collective-permute-start | bytes 442376 | tf_op jit(solution)/shard_map/ppermute | solution.py:355
  25.4 25.6 %collective-permute-start.5 = (bf16[2,96,384]{2,1,0:T(8,128)(2,1)}, bf16[2,96,384]{2,1,0:T(8,128)(2,1)S(1)}, u32[]{:S(2)}, u32[]{:S(2)}) collective-permute-start(bf16[2,96,384]{2,1,0:T(8,128)(2,1)} %get-tuple-element.72), channel_id=1, source_target_pairs={{0,24},{8,0},{16,8},{24,16},{1,25},{9,1},{17,9},{25,17},{2,26},{10... | collective-permute-start | bytes 442376 | tf_op jit(solution)/shard_map/ppermute | solution.py:355
  26.1 28.5 %all-to-all-start.2 = ((bf16[8,1,96,128]{3,2,1,0:T(8,128)(2,1)}), bf16[8,1,96,128]{3,2,1,0:T(8,128)(2,1)S(1)}, u32[]{:S(2)}, u32[]{:S(2)}) async-start(bf16[8,1,96,128]{3,2,1,0:T(8,128)(2,1)} %get-tuple-element.80), calls=%async_computation.2 | async-start | bytes 393216 | tf_op jit(solution)/shard_map/all_to_all | solution.py:350
  54.6 34.4 %all-to-all-start.1 = ((bf16[8,2,96,128]{3,2,1,0:T(8,128)(2,1)}), bf16[8,2,96,128]{3,2,1,0:T(8,128)(2,1)S(1)}, u32[]{:S(2)}, u32[]{:S(2)}) async-start(bf16[8,2,96,128]{3,2,1,0:T(8,128)(2,1)} %get-tuple-element.74), calls=%async_computation.1 | async-start | bytes 786432 | tf_op jit(solution)/shard_map/all_to_all | solution.py:350
  63.5 31.5 %collective-permute-start.6 = (bf16[16,96,128]{2,1,0:T(8,128)(2,1)}, bf16[16,96,128]{2,1,0:T(8,128)(2,1)S(1)}, u32[]{:S(2)}, u32[]{:S(2)}) collective-permute-start(bf16[16,96,128]{2,1,0:T(8,128)(2,1)} %get-tuple-element.76), channel_id=1, source_target_pairs={{0,8},{8,16},{16,24},{24,0},{1,9},{9,17},{17,25},{25,1},{2,10},{10... | collective-permute-start | bytes 1179656 | tf_op jit(solution)/shard_map/ppermute | solution.py:355
  63.5 31.4 %collective-permute-start.7 = (bf16[16,96,128]{2,1,0:T(8,128)(2,1)}, bf16[16,96,128]{2,1,0:T(8,128)(2,1)S(1)}, u32[]{:S(2)}, u32[]{:S(2)}) collective-permute-start(bf16[16,96,128]{2,1,0:T(8,128)(2,1)} %get-tuple-element.77), channel_id=1, source_target_pairs={{0,16},{8,24},{16,0},{24,8},{1,17},{9,25},{17,1},{25,9},{2,18},{10... | collective-permute-start | bytes 1179656 | tf_op jit(solution)/shard_map/ppermute | solution.py:355
  64.1 30.9 %collective-permute-start.8 = (bf16[16,96,128]{2,1,0:T(8,128)(2,1)}, bf16[16,96,128]{2,1,0:T(8,128)(2,1)S(1)}, u32[]{:S(2)}, u32[]{:S(2)}) collective-permute-start(bf16[16,96,128]{2,1,0:T(8,128)(2,1)} %get-tuple-element.78), channel_id=1, source_target_pairs={{0,24},{8,0},{16,8},{24,16},{1,25},{9,1},{17,9},{25,17},{2,26},{10... | collective-permute-start | bytes 1179656 | tf_op jit(solution)/shard_map/ppermute | solution.py:355
  88.9 24.8 %all-to-all-start.4 = ((bf16[8,1,96,128]{3,2,1,0:T(8,128)(2,1)}), bf16[8,1,96,128]{3,2,1,0:T(8,128)(2,1)S(1)}, u32[]{:S(2)}, u32[]{:S(2)}) async-start(bf16[8,1,96,128]{3,2,1,0:T(8,128)(2,1)} %get-tuple-element.86), calls=%async_computation.4 | async-start | bytes 393216 | tf_op jit(solution)/shard_map/all_to_all | solution.py:350
  113.8 18.7 %all-to-all-start.3 = ((bf16[8,2,96,128]{3,2,1,0:T(8,128)(2,1)}), bf16[8,2,96,128]{3,2,1,0:T(8,128)(2,1)S(1)}, u32[]{:S(2)}, u32[]{:S(2)}) async-start(bf16[8,2,96,128]{3,2,1,0:T(8,128)(2,1)} %get-tuple-element.84), calls=%async_computation.3 | async-start | bytes 786432 | tf_op jit(solution)/shard_map/all_to_all | solution.py:350
  132.5 23.7 %all-to-all-start.6 = ((bf16[8,1,96,128]{3,2,1,0:T(8,128)(2,1)}), bf16[8,1,96,128]{3,2,1,0:T(8,128)(2,1)S(1)}, u32[]{:S(2)}, u32[]{:S(2)}) async-start(bf16[8,1,96,128]{3,2,1,0:T(8,128)(2,1)} %get-tuple-element.92), calls=%async_computation.6 | async-start | bytes 393216 | tf_op jit(solution)/shard_map/all_to_all | solution.py:350
  156.2 18.7 %all-to-all-start.5 = ((bf16[8,2,96,128]{3,2,1,0:T(8,128)(2,1)}), bf16[8,2,96,128]{3,2,1,0:T(8,128)(2,1)S(1)}, u32[]{:S(2)}, u32[]{:S(2)}) async-start(bf16[8,2,96,128]{3,2,1,0:T(8,128)(2,1)} %get-tuple-element.90), calls=%async_computation.5 | async-start | bytes 786432 | tf_op jit(solution)/shard_map/all_to_all | solution.py:350
  174.9 23.7 %all-to-all-start.8 = ((bf16[8,1,96,128]{3,2,1,0:T(8,128)(2,1)}), bf16[8,1,96,128]{3,2,1,0:T(8,128)(2,1)S(1)}, u32[]{:S(2)}, u32[]{:S(2)}) async-start(bf16[8,1,96,128]{3,2,1,0:T(8,128)(2,1)} %get-tuple-element.98), calls=%async_computation.8 | async-start | bytes 393216 | tf_op jit(solution)/shard_map/all_to_all | solution.py:350
  198.6 18.7 %all-to-all-start.7 = ((bf16[8,2,96,128]{3,2,1,0:T(8,128)(2,1)}), bf16[8,2,96,128]{3,2,1,0:T(8,128)(2,1)S(1)}, u32[]{:S(2)}, u32[]{:S(2)}) async-start(bf16[8,2,96,128]{3,2,1,0:T(8,128)(2,1)} %get-tuple-element.96), calls=%async_computation.7 | async-start | bytes 786432 | tf_op jit(solution)/shard_map/all_to_all | solution.py:350
  217.3 23.7 %all-to-all-start.10 = ((bf16[8,1,96,128]{3,2,1,0:T(8,128)(2,1)}), bf16[8,1,96,128]{3,2,1,0:T(8,128)(2,1)S(1)}, u32[]{:S(2)}, u32[]{:S(2)}) async-start(bf16[8,1,96,128]{3,2,1,0:T(8,128)(2,1)} %get-tuple-element.104), calls=%async_computation.10 | async-start | bytes 393216 | tf_op jit(solution)/shard_map/all_to_all | solution.py:350
  241.0 18.7 %all-to-all-start.9 = ((bf16[8,2,96,128]{3,2,1,0:T(8,128)(2,1)}), bf16[8,2,96,128]{3,2,1,0:T(8,128)(2,1)S(1)}, u32[]{:S(2)}, u32[]{:S(2)}) async-start(bf16[8,2,96,128]{3,2,1,0:T(8,128)(2,1)} %get-tuple-element.102), calls=%async_computation.9 | async-start | bytes 786432 | tf_op jit(solution)/shard_map/all_to_all | solution.py:350
  259.8 23.7 %all-to-all-start.12 = ((bf16[8,1,96,128]{3,2,1,0:T(8,128)(2,1)}), bf16[8,1,96,128]{3,2,1,0:T(8,128)(2,1)S(1)}, u32[]{:S(2)}, u32[]{:S(2)}) async-start(bf16[8,1,96,128]{3,2,1,0:T(8,128)(2,1)} %get-tuple-element.110), calls=%async_computation.12 | async-start | bytes 393216 | tf_op jit(solution)/shard_map/all_to_all | solution.py:350
  283.4 18.7 %all-to-all-start.11 = ((bf16[8,2,96,128]{3,2,1,0:T(8,128)(2,1)}), bf16[8,2,96,128]{3,2,1,0:T(8,128)(2,1)S(1)}, u32[]{:S(2)}, u32[]{:S(2)}) async-start(bf16[8,2,96,128]{3,2,1,0:T(8,128)(2,1)} %get-tuple-element.108), calls=%async_computation.11 | async-start | bytes 786432 | tf_op jit(solution)/shard_map/all_to_all | solution.py:350
  302.2 23.5 %all-to-all-start.14 = ((bf16[8,1,96,128]{3,2,1,0:T(8,128)(2,1)}), bf16[8,1,96,128]{3,2,1,0:T(8,128)(2,1)S(1)}, u32[]{:S(2)}, u32[]{:S(2)}) async-start(bf16[8,1,96,128]{3,2,1,0:T(8,128)(2,1)} %get-tuple-element.116), calls=%async_computation.14 | async-start | bytes 393216 | tf_op jit(solution)/shard_map/all_to_all | solution.py:350
  (9 other events, 16.9 us)

commit v9 on v8

--- a/solution.py
+++ b/solution.py
@@ -159,10 +159,11 @@
             )
         )
     start_all(copies)
+    tile_copy(0).start()
+    wait_all(copies)
     initial_copy.start()
-    for row in range(rows):
+    for row in range(1, rows):
         tile_copy(row).start()
-    wait_all(copies)
     initial_copy.wait()
 
     def one_row(row, carry):
@@ -205,8 +206,8 @@
             sources.append(("stale", blocks_dev + groups * part_count, distance))
             operands.append(pinned(stale_blocks))
             specs.append(hbm)
-    operands += after
-    specs += [anywhere] * len(after)
+    operands += [pinned(value) for value in after]
+    specs += [hbm] * len(after)
     table_size = blocks_dev + (2 * groups - 1) * part_count
     plan = (stream, group_blocks, fanout, sources, home, len(stale))
     flops = 2 * rows * fanout * block * block * part_width
@@ -287,7 +288,7 @@
         out_shape = [
             in_hbm(shapes[0]),
             jax.ShapeDtypeStruct(outgoing, jnp.bfloat16),
-            jax.ShapeDtypeStruct((16, 128), jnp.bfloat16),
+            in_hbm((16, 128)),
         ]
     return pl.pallas_call(
         functools.partial(finish_kernel, plan),
@@ -295,7 +296,7 @@
             num_scalar_prefetch=2,
             grid=(1,),
             in_specs=[whole(mixed.shape), whole(gathered.shape)]
-            + [hbm] * len(weights),
+            + [anywhere] * len(weights),
             out_specs=[whole(s) for s in shapes],
             scratch_shapes=[
                 pltpu.VMEM((part_width, width), jnp.bfloat16),
@@ -310,7 +311,7 @@
         ),
         compiler_params=params(),
         name="finish",
-    )(picks, section, mixed, gathered, *[pinned(w) for w in weights])
+    )(picks, section, mixed, gathered, *weights)
 
 
 def per_device(
@@ -363,7 +364,7 @@
     weights = spread(turn_blocks(section, layer_weights[None], (0,), section_count))
 
     pieces = []
-    after = []
+    after = [pieces[0] for pieces in turned[1:]]
     for layer in range(layers):
         last = layer == layers - 1
         own_next, imports_next = [], []
@@ -383,6 +384,8 @@
                 part_count,
                 after,
             )
+            if last:
+                after = [mixed[0]]
             gathered = lax.all_gather(mixed, "section", axis=0, tiled=False)
             result = finish(
                 picks, section, mixed, gathered, weights, layer, depth, stream, group_blocks,

time: 401 us -> 377 us (0.940)
  blocking collectives: 158 us -> 129 us
  starting transfers between devices: 88.1 us -> 99.8 us
    all_to_all x2 -> x0, blocking collectives: 28.8 us -> none  [exchange(): return lax.all_to_all(value, 'dom', split_axis=0, concat_axis=0, tiled=True)]
    pallas_call x16, Pallas kernels: 39.7 us -> 27.8 us  [finish(): pl.pallas_call(functools.partial(finish_kernel, plan), grid_spec=pltpu.Pr...]
    all_to_all x14 -> x16, starting transfers between devices: 82.5 us -> 94.2 us  [exchange(): return lax.all_to_all(value, 'dom', split_axis=0, concat_axis=0, tiled=True)]
    pallas_call x16, Pallas kernels: 87 us -> 96 us  [aggregate(): pl.pallas_call(functools.partial(aggregate_kernel, plan), grid_spec=pltpu...]
  transfers between devices with their start and end apart: 23 -> 25, of which waited for: 3 -> 3; matrix products, arithmetic and copies ran while one was open for 0% -> 0% of each run, Pallas kernels for 28% -> 33%
where the time goes in v9:
time: 377 us; the launch traced here: 375 us
  Pallas kernels  135 us (36%)
  blocking collectives  129 us (34%)
  starting transfers between devices  99.8 us (26%)
  waiting for transfers between devices  5.57 us (1%)
    all_gather x16, blocking collectives, per_device(): gathered = lax.all_gather(mixed, 'section', axis=0, tiled=False)  129 us
    pallas_call x16, Pallas kernels, aggregate(): pl.pallas_call(functools.partial(aggregate_kernel, plan), grid_spec=pltpu...  96 us
    all_to_all x16, starting transfers between devices, exchange(): return lax.all_to_all(value, 'dom', split_axis=0, concat_axis=0, tiled=True)  94.2 us
    pallas_call x16, Pallas kernels, finish(): pl.pallas_call(functools.partial(finish_kernel, plan), grid_spec=pltpu.Pr...  27.8 us
    pallas_call x3, Pallas kernels, turn_blocks(): pl.pallas_call(turn_kernel, grid_spec=pltpu.PrefetchScalarGridSpec(num_sc...  8.04 us
  transfers between devices with their start and end apart: 25, of which 3 were waited for; matrix products, arithmetic and copies ran while one was open for 0% of the time, Pallas kernels for 33%

profile of v9, /device:TPU:0, one launch (start us, length us, event | category | flops | bytes accessed | tf_op | source)
XLA Modules:
  0.0 374.6 jit_solution(16178726386937997125)
XLA Ops:
  7.1 7.3 %all-to-all-start = ((bf16[8,2,96,128]{3,2,1,0:T(8,128)(2,1)}), bf16[8,2,96,128]{3,2,1,0:T(8,128)(2,1)S(1)}, u32[]{:S(2)}, u32[]{:S(2)}) async-start(bf16[8,2,96,128]{3,2,1,0:T(8,128)(2,1)} %get-tuple-element.65), calls=%async_computation | async-start | bytes 786432 | tf_op jit(solution)/shard_map/all_to_all | solution.py:351
  34.9 7.4 %aggregate.16.mixed_ref = bf16[8,96,128]{2,1,0:T(8,128)(2,1)S(1)} custom-call(s32[288]{0:T(512)S(1)} %reshape.24.columns, s32[1]{0:T(128)} %bitcast.info, bf16[8,96,128]{2,1,0:T(8,128)(2,1)} %get-tuple-element.64.initial_ref.refs_0_, bf16[12,24,128,128]{3,2,1,0:T(8,128)(2,1)} %tiles_ref.31, bf16[8,96,128]{2,1,0:T(8,128)(2,1)} %get-tuple-element.64.initial_ref.refs_0_, ...), custom_call_target="tpu_custom_call" | custom-call | flops 603979776 | bytes 6291456 | tf_op jit(solution)/shard_map/aggregate/pallas_call | solution.py:214
  42.3 9.5 %all-gather = bf16[32,96,128]{2,1,0:T(8,128)(2,1)S(1)} all-gather(bf16[8,96,128]{2,1,0:T(8,128)(2,1)S(1)} %aggregate.16.mixed_ref), channel_id=2, replica_groups=mesh['section'=4,'dom'=8] {'section'}, dimensions={0}, use_global_device_ids=true | all-gather | bytes 983040 | tf_op jit(solution)/shard_map/all_gather | solution.py:389
  66.4 16.3 %all-gather.1 = bf16[16,96,128]{2,1,0:T(8,128)(2,1)S(1)} all-gather(bf16[4,96,128]{2,1,0:T(8,128)(2,1)S(1)} %aggregate.17.mixed_ref), channel_id=3, replica_groups=mesh['section'=4,'dom'=8] {'section'}, dimensions={0}, use_global_device_ids=true | all-gather | bytes 491520 | tf_op jit(solution)/shard_map/all_gather | solution.py:389
  91.5 7.4 %aggregate.18.mixed_ref = bf16[8,96,128]{2,1,0:T(8,128)(2,1)S(1)} custom-call(s32[288]{0:T(512)S(1)} %reshape.24.columns, s32[1]{0:T(128)} %bitcast.info, bf16[8,96,128]{2,1,0:T(8,128)(2,1)} %get-tuple-element.64.initial_ref.refs_0_, bf16[12,24,128,128]{3,2,1,0:T(8,128)(2,1)} %tiles_ref.31, bf16[8,96,128]{2,1,0:T(8,128)(2,1)} %get-tuple-element.74.refs_0_, ...), custom_call_target="tpu_custom_call" | custom-call | flops 603979776 | bytes 6291456 | tf_op jit(solution)/shard_map/aggregate/pallas_call | solution.py:214
  98.9 8.4 %all-gather.2 = bf16[32,96,128]{2,1,0:T(8,128)(2,1)S(1)} all-gather(bf16[8,96,128]{2,1,0:T(8,128)(2,1)S(1)} %aggregate.18.mixed_ref), channel_id=4, replica_groups=mesh['section'=4,'dom'=8] {'section'}, dimensions={0}, use_global_device_ids=true | all-gather | bytes 983040 | tf_op jit(solution)/shard_map/all_gather | solution.py:389
  119.7 6.3 %all-gather.3 = bf16[16,96,128]{2,1,0:T(8,128)(2,1)S(1)} all-gather(bf16[4,96,128]{2,1,0:T(8,128)(2,1)S(1)} %aggregate.19.mixed_ref), channel_id=5, replica_groups=mesh['section'=4,'dom'=8] {'section'}, dimensions={0}, use_global_device_ids=true | all-gather | bytes 491520 | tf_op jit(solution)/shard_map/all_gather | solution.py:389
  133.5 7.3 %aggregate.20.mixed_ref = bf16[8,96,128]{2,1,0:T(8,128)(2,1)S(1)} custom-call(s32[288]{0:T(512)S(1)} %reshape.24.columns, s32[1]{0:T(128)} %bitcast.info, bf16[8,96,128]{2,1,0:T(8,128)(2,1)} %get-tuple-element.64.initial_ref.refs_0_, bf16[12,24,128,128]{3,2,1,0:T(8,128)(2,1)} %tiles_ref.31, bf16[8,96,128]{2,1,0:T(8,128)(2,1)} %get-tuple-element.83.refs_0_, ...), custom_call_target="tpu_custom_call" | custom-call | flops 603979776 | bytes 6291456 | tf_op jit(solution)/shard_map/aggregate/pallas_call | solution.py:214
  140.9 8.4 %all-gather.4 = bf16[32,96,128]{2,1,0:T(8,128)(2,1)S(1)} all-gather(bf16[8,96,128]{2,1,0:T(8,128)(2,1)S(1)} %aggregate.20.mixed_ref), channel_id=6, replica_groups=mesh['section'=4,'dom'=8] {'section'}, dimensions={0}, use_global_device_ids=true | all-gather | bytes 983040 | tf_op jit(solution)/shard_map/all_gather | solution.py:389
  161.7 6.3 %all-gather.5 = bf16[16,96,128]{2,1,0:T(8,128)(2,1)S(1)} all-gather(bf16[4,96,128]{2,1,0:T(8,128)(2,1)S(1)} %aggregate.21.mixed_ref), channel_id=7, replica_groups=mesh['section'=4,'dom'=8] {'section'}, dimensions={0}, use_global_device_ids=true | all-gather | bytes 491520 | tf_op jit(solution)/shard_map/all_gather | solution.py:389
  175.6 7.4 %aggregate.22.mixed_ref = bf16[8,96,128]{2,1,0:T(8,128)(2,1)S(1)} custom-call(s32[288]{0:T(512)S(1)} %reshape.24.columns, s32[1]{0:T(128)} %bitcast.info, bf16[8,96,128]{2,1,0:T(8,128)(2,1)} %get-tuple-element.64.initial_ref.refs_0_, bf16[12,24,128,128]{3,2,1,0:T(8,128)(2,1)} %tiles_ref.31, bf16[8,96,128]{2,1,0:T(8,128)(2,1)} %get-tuple-element.89.refs_0_, ...), custom_call_target="tpu_custom_call" | custom-call | flops 603979776 | bytes 6291456 | tf_op jit(solution)/shard_map/aggregate/pallas_call | solution.py:214
  182.9 8.4 %all-gather.6 = bf16[32,96,128]{2,1,0:T(8,128)(2,1)S(1)} all-gather(bf16[8,96,128]{2,1,0:T(8,128)(2,1)S(1)} %aggregate.22.mixed_ref), channel_id=8, replica_groups=mesh['section'=4,'dom'=8] {'section'}, dimensions={0}, use_global_device_ids=true | all-gather | bytes 983040 | tf_op jit(solution)/shard_map/all_gather | solution.py:389
  203.7 6.3 %all-gather.7 = bf16[16,96,128]{2,1,0:T(8,128)(2,1)S(1)} all-gather(bf16[4,96,128]{2,1,0:T(8,128)(2,1)S(1)} %aggregate.23.mixed_ref), channel_id=9, replica_groups=mesh['section'=4,'dom'=8] {'section'}, dimensions={0}, use_global_device_ids=true | all-gather | bytes 491520 | tf_op jit(solution)/shard_map/all_gather | solution.py:389
  217.6 7.3 %aggregate.24.mixed_ref = bf16[8,96,128]{2,1,0:T(8,128)(2,1)S(1)} custom-call(s32[288]{0:T(512)S(1)} %reshape.24.columns, s32[1]{0:T(128)} %bitcast.info, bf16[8,96,128]{2,1,0:T(8,128)(2,1)} %get-tuple-element.64.initial_ref.refs_0_, bf16[12,24,128,128]{3,2,1,0:T(8,128)(2,1)} %tiles_ref.31, bf16[8,96,128]{2,1,0:T(8,128)(2,1)} %get-tuple-element.95.refs_0_, ...), custom_call_target="tpu_custom_call" | custom-call | flops 603979776 | bytes 6291456 | tf_op jit(solution)/shard_map/aggregate/pallas_call | solution.py:214
  225.0 8.4 %all-gather.8 = bf16[32,96,128]{2,1,0:T(8,128)(2,1)S(1)} all-gather(bf16[8,96,128]{2,1,0:T(8,128)(2,1)S(1)} %aggregate.24.mixed_ref), channel_id=10, replica_groups=mesh['section'=4,'dom'=8] {'section'}, dimensions={0}, use_global_device_ids=true | all-gather | bytes 983040 | tf_op jit(solution)/shard_map/all_gather | solution.py:389
  245.8 6.3 %all-gather.9 = bf16[16,96,128]{2,1,0:T(8,128)(2,1)S(1)} all-gather(bf16[4,96,128]{2,1,0:T(8,128)(2,1)S(1)} %aggregate.25.mixed_ref), channel_id=11, replica_groups=mesh['section'=4,'dom'=8] {'section'}, dimensions={0}, use_global_device_ids=true | all-gather | bytes 491520 | tf_op jit(solution)/shard_map/all_gather | solution.py:389
  259.8 7.3 %aggregate.26.mixed_ref = bf16[8,96,128]{2,1,0:T(8,128)(2,1)S(1)} custom-call(s32[288]{0:T(512)S(1)} %reshape.24.columns, s32[1]{0:T(128)} %bitcast.info, bf16[8,96,128]{2,1,0:T(8,128)(2,1)} %get-tuple-element.64.initial_ref.refs_0_, bf16[12,24,128,128]{3,2,1,0:T(8,128)(2,1)} %tiles_ref.31, bf16[8,96,128]{2,1,0:T(8,128)(2,1)} %get-tuple-element.101.refs_0_, ...), custom_call_target="tpu_custom_call" | custom-call | flops 603979776 | bytes 6291456 | tf_op jit(solution)/shard_map/aggregate/pallas_call | solution.py:214
  267.2 8.4 %all-gather.10 = bf16[32,96,128]{2,1,0:T(8,128)(2,1)S(1)} all-gather(bf16[8,96,128]{2,1,0:T(8,128)(2,1)S(1)} %aggregate.26.mixed_ref), channel_id=12, replica_groups=mesh['section'=4,'dom'=8] {'section'}, dimensions={0}, use_global_device_ids=true | all-gather | bytes 983040 | tf_op jit(solution)/shard_map/all_gather | solution.py:389
  288.0 6.3 %all-gather.11 = bf16[16,96,128]{2,1,0:T(8,128)(2,1)S(1)} all-gather(bf16[4,96,128]{2,1,0:T(8,128)(2,1)S(1)} %aggregate.27.mixed_ref), channel_id=13, replica_groups=mesh['section'=4,'dom'=8] {'section'}, dimensions={0}, use_global_device_ids=true | all-gather | bytes 491520 | tf_op jit(solution)/shard_map/all_gather | solution.py:389
  301.9 7.3 %aggregate.28.mixed_ref = bf16[8,96,128]{2,1,0:T(8,128)(2,1)S(1)} custom-call(s32[288]{0:T(512)S(1)} %reshape.24.columns, s32[1]{0:T(128)} %bitcast.info, bf16[8,96,128]{2,1,0:T(8,128)(2,1)} %get-tuple-element.64.initial_ref.refs_0_, bf16[12,24,128,128]{3,2,1,0:T(8,128)(2,1)} %tiles_ref.31, bf16[8,96,128]{2,1,0:T(8,128)(2,1)} %get-tuple-element.107.refs_0_, ...), custom_call_target="tpu_custom_call" | custom-call | flops 603979776 | bytes 6291456 | tf_op jit(solution)/shard_map/aggregate/pallas_call | solution.py:214
  309.2 8.4 %all-gather.12 = bf16[32,96,128]{2,1,0:T(8,128)(2,1)S(1)} all-gather(bf16[8,96,128]{2,1,0:T(8,128)(2,1)S(1)} %aggregate.28.mixed_ref), channel_id=14, replica_groups=mesh['section'=4,'dom'=8] {'section'}, dimensions={0}, use_global_device_ids=true | all-gather | bytes 983040 | tf_op jit(solution)/shard_map/all_gather | solution.py:389
  343.9 7.4 %aggregate.30.mixed_ref = bf16[8,96,128]{2,1,0:T(8,128)(2,1)S(1)} custom-call(s32[288]{0:T(512)S(1)} %reshape.24.columns, s32[1]{0:T(128)} %bitcast.info, bf16[8,96,128]{2,1,0:T(8,128)(2,1)} %get-tuple-element.64.initial_ref.refs_0_, bf16[12,24,128,128]{3,2,1,0:T(8,128)(2,1)} %tiles_ref.31, bf16[8,96,128]{2,1,0:T(8,128)(2,1)} %get-tuple-element.113.refs_0_, ...), custom_call_target="tpu_custom_call" | custom-call | flops 603979776 | bytes 6291456 | tf_op jit(solution)/shard_map/aggregate/pallas_call | solution.py:214
  351.9 8.4 %all-gather.14 = bf16[32,96,128]{2,1,0:T(8,128)(2,1)S(1)} all-gather(bf16[8,96,128]{2,1,0:T(8,128)(2,1)S(1)} %aggregate.30.mixed_ref), channel_id=16, replica_groups=mesh['section'=4,'dom'=8] {'section'}, dimensions={0}, use_global_device_ids=true | all-gather | bytes 983040 | tf_op jit(solution)/shard_map/all_gather | solution.py:389
  365.0 6.6 %all-gather.15 = bf16[16,96,128]{2,1,0:T(8,128)(2,1)S(1)} all-gather(bf16[4,96,128]{2,1,0:T(8,128)(2,1)S(1)} %aggregate.31.mixed_ref), channel_id=17, replica_groups=mesh['section'=4,'dom'=8] {'section'}, dimensions={0}, use_global_device_ids=true | all-gather | bytes 491520 | tf_op jit(solution)/shard_map/all_gather | solution.py:389
  (108 shorter events, 185.1 us)
Async XLA Ops:
  7.1 19.0 %all-to-all-start = ((bf16[8,2,96,128]{3,2,1,0:T(8,128)(2,1)}), bf16[8,2,96,128]{3,2,1,0:T(8,128)(2,1)S(1)}, u32[]{:S(2)}, u32[]{:S(2)}) async-start(bf16[8,2,96,128]{3,2,1,0:T(8,128)(2,1)} %get-tuple-element.65), calls=%async_computation | async-start | bytes 786432 | tf_op jit(solution)/shard_map/all_to_all | solution.py:351
  14.4 17.1 %collective-permute-start.1 = (bf16[16,96,128]{2,1,0:T(8,128)(2,1)}, bf16[16,96,128]{2,1,0:T(8,128)(2,1)S(1)}, u32[]{:S(2)}, u32[]{:S(2)}) collective-permute-start(bf16[16,96,128]{2,1,0:T(8,128)(2,1)} %get-tuple-element.67), channel_id=1, source_target_pairs={{0,16},{8,24},{16,0},{24,8},{1,17},{9,25},{17,1},{25,9},{2,18},{10... | collective-permute-start | bytes 1179656 | tf_op jit(solution)/shard_map/ppermute | solution.py:356
  15.9 18.2 %collective-permute-start.2 = (bf16[16,96,128]{2,1,0:T(8,128)(2,1)}, bf16[16,96,128]{2,1,0:T(8,128)(2,1)S(1)}, u32[]{:S(2)}, u32[]{:S(2)}) collective-permute-start(bf16[16,96,128]{2,1,0:T(8,128)(2,1)} %get-tuple-element.68), channel_id=1, source_target_pairs={{0,24},{8,0},{16,8},{24,16},{1,25},{9,1},{17,9},{25,17},{2,26},{10... | collective-permute-start | bytes 1179656 | tf_op jit(solution)/shard_map/ppermute | solution.py:356
  19.5 32.3 %collective-permute-start.3 = (bf16[2,96,384]{2,1,0:T(8,128)(2,1)}, bf16[2,96,384]{2,1,0:T(8,128)(2,1)S(1)}, u32[]{:S(2)}, u32[]{:S(2)}) collective-permute-start(bf16[2,96,384]{2,1,0:T(8,128)(2,1)} %get-tuple-element.71), channel_id=1, source_target_pairs={{0,8},{8,16},{16,24},{24,0},{1,9},{9,17},{17,25},{25,1},{2,10},{10... | collective-permute-start | bytes 442376 | tf_op jit(solution)/shard_map/ppermute | solution.py:356
  19.5 32.3 %collective-permute-start.4 = (bf16[2,96,384]{2,1,0:T(8,128)(2,1)}, bf16[2,96,384]{2,1,0:T(8,128)(2,1)S(1)}, u32[]{:S(2)}, u32[]{:S(2)}) collective-permute-start(bf16[2,96,384]{2,1,0:T(8,128)(2,1)} %get-tuple-element.72), channel_id=1, source_target_pairs={{0,16},{8,24},{16,0},{24,8},{1,17},{9,25},{17,1},{25,9},{2,18},{10... | collective-permute-start | bytes 442376 | tf_op jit(solution)/shard_map/ppermute | solution.py:356
  25.4 26.4 %collective-permute-start.5 = (bf16[2,96,384]{2,1,0:T(8,128)(2,1)S(1)}, bf16[2,96,384]{2,1,0:T(8,128)(2,1)S(1)}, u32[]{:S(2)}, u32[]{:S(2)}) collective-permute-start(bf16[2,96,384]{2,1,0:T(8,128)(2,1)S(1)} %copy-done.10), channel_id=1, source_target_pairs={{0,24},{8,0},{16,8},{24,16},{1,25},{9,1},{17,9},{25,17},{2,26},{10... | collective-permute-start | bytes 442376 | tf_op jit(solution)/shard_map/ppermute | solution.py:356
  26.0 27.7 %all-to-all-start.2 = ((bf16[8,1,96,128]{3,2,1,0:T(8,128)(2,1)}), bf16[8,1,96,128]{3,2,1,0:T(8,128)(2,1)S(1)}, u32[]{:S(2)}, u32[]{:S(2)}) async-start(bf16[8,1,96,128]{3,2,1,0:T(8,128)(2,1)} %get-tuple-element.80), calls=%async_computation.2 | async-start | bytes 393216 | tf_op jit(solution)/shard_map/all_to_all | solution.py:351
  53.7 30.7 %all-to-all-start.1 = ((bf16[8,2,96,128]{3,2,1,0:T(8,128)(2,1)}), bf16[8,2,96,128]{3,2,1,0:T(8,128)(2,1)S(1)}, u32[]{:S(2)}, u32[]{:S(2)}) async-start(bf16[8,2,96,128]{3,2,1,0:T(8,128)(2,1)} %get-tuple-element.75), calls=%async_computation.1 | async-start | bytes 786432 | tf_op jit(solution)/shard_map/all_to_all | solution.py:351
  59.7 30.8 %collective-permute-start.6 = (bf16[16,96,128]{2,1,0:T(8,128)(2,1)}, bf16[16,96,128]{2,1,0:T(8,128)(2,1)S(1)}, u32[]{:S(2)}, u32[]{:S(2)}) collective-permute-start(bf16[16,96,128]{2,1,0:T(8,128)(2,1)} %get-tuple-element.76), channel_id=1, source_target_pairs={{0,8},{8,16},{16,24},{24,0},{1,9},{9,17},{17,25},{25,1},{2,10},{10... | collective-permute-start | bytes 1179656 | tf_op jit(solution)/shard_map/ppermute | solution.py:356
  59.8 30.7 %collective-permute-start.7 = (bf16[16,96,128]{2,1,0:T(8,128)(2,1)S(1)}, bf16[16,96,128]{2,1,0:T(8,128)(2,1)S(1)}, u32[]{:S(2)}, u32[]{:S(2)}) collective-permute-start(bf16[16,96,128]{2,1,0:T(8,128)(2,1)S(1)} %copy-done.9), channel_id=1, source_target_pairs={{0,16},{8,24},{16,0},{24,8},{1,17},{9,25},{17,1},{25,9},{2,18},{10... | collective-permute-start | bytes 1179656 | tf_op jit(solution)/shard_map/ppermute | solution.py:356
  60.4 30.1 %collective-permute-start.8 = (bf16[16,96,128]{2,1,0:T(8,128)(2,1)S(1)}, bf16[16,96,128]{2,1,0:T(8,128)(2,1)S(1)}, u32[]{:S(2)}, u32[]{:S(2)}) collective-permute-start(bf16[16,96,128]{2,1,0:T(8,128)(2,1)S(1)} %copy-done.8), channel_id=1, source_target_pairs={{0,24},{8,0},{16,8},{24,16},{1,25},{9,1},{17,9},{25,17},{2,26},{10... | collective-permute-start | bytes 1179656 | tf_op jit(solution)/shard_map/ppermute | solution.py:356
  84.5 24.8 %all-to-all-start.4 = ((bf16[8,1,96,128]{3,2,1,0:T(8,128)(2,1)}), bf16[8,1,96,128]{3,2,1,0:T(8,128)(2,1)S(1)}, u32[]{:S(2)}, u32[]{:S(2)}) async-start(bf16[8,1,96,128]{3,2,1,0:T(8,128)(2,1)} %get-tuple-element.86), calls=%async_computation.4 | async-start | bytes 393216 | tf_op jit(solution)/shard_map/all_to_all | solution.py:351
  109.3 18.4 %all-to-all-start.3 = ((bf16[8,2,96,128]{3,2,1,0:T(8,128)(2,1)}), bf16[8,2,96,128]{3,2,1,0:T(8,128)(2,1)S(1)}, u32[]{:S(2)}, u32[]{:S(2)}) async-start(bf16[8,2,96,128]{3,2,1,0:T(8,128)(2,1)} %get-tuple-element.84), calls=%async_computation.3 | async-start | bytes 786432 | tf_op jit(solution)/shard_map/all_to_all | solution.py:351
  127.7 23.6 %all-to-all-start.6 = ((bf16[8,1,96,128]{3,2,1,0:T(8,128)(2,1)}), bf16[8,1,96,128]{3,2,1,0:T(8,128)(2,1)S(1)}, u32[]{:S(2)}, u32[]{:S(2)}) async-start(bf16[8,1,96,128]{3,2,1,0:T(8,128)(2,1)} %get-tuple-element.92), calls=%async_computation.6 | async-start | bytes 393216 | tf_op jit(solution)/shard_map/all_to_all | solution.py:351
  151.3 18.4 %all-to-all-start.5 = ((bf16[8,2,96,128]{3,2,1,0:T(8,128)(2,1)}), bf16[8,2,96,128]{3,2,1,0:T(8,128)(2,1)S(1)}, u32[]{:S(2)}, u32[]{:S(2)}) async-start(bf16[8,2,96,128]{3,2,1,0:T(8,128)(2,1)} %get-tuple-element.90), calls=%async_computation.5 | async-start | bytes 786432 | tf_op jit(solution)/shard_map/all_to_all | solution.py:351
  169.7 23.6 %all-to-all-start.8 = ((bf16[8,1,96,128]{3,2,1,0:T(8,128)(2,1)}), bf16[8,1,96,128]{3,2,1,0:T(8,128)(2,1)S(1)}, u32[]{:S(2)}, u32[]{:S(2)}) async-start(bf16[8,1,96,128]{3,2,1,0:T(8,128)(2,1)} %get-tuple-element.98), calls=%async_computation.8 | async-start | bytes 393216 | tf_op jit(solution)/shard_map/all_to_all | solution.py:351
  193.3 18.4 %all-to-all-start.7 = ((bf16[8,2,96,128]{3,2,1,0:T(8,128)(2,1)}), bf16[8,2,96,128]{3,2,1,0:T(8,128)(2,1)S(1)}, u32[]{:S(2)}, u32[]{:S(2)}) async-start(bf16[8,2,96,128]{3,2,1,0:T(8,128)(2,1)} %get-tuple-element.96), calls=%async_computation.7 | async-start | bytes 786432 | tf_op jit(solution)/shard_map/all_to_all | solution.py:351
  211.8 23.6 %all-to-all-start.10 = ((bf16[8,1,96,128]{3,2,1,0:T(8,128)(2,1)}), bf16[8,1,96,128]{3,2,1,0:T(8,128)(2,1)S(1)}, u32[]{:S(2)}, u32[]{:S(2)}) async-start(bf16[8,1,96,128]{3,2,1,0:T(8,128)(2,1)} %get-tuple-element.104), calls=%async_computation.10 | async-start | bytes 393216 | tf_op jit(solution)/shard_map/all_to_all | solution.py:351
  235.4 18.6 %all-to-all-start.9 = ((bf16[8,2,96,128]{3,2,1,0:T(8,128)(2,1)}), bf16[8,2,96,128]{3,2,1,0:T(8,128)(2,1)S(1)}, u32[]{:S(2)}, u32[]{:S(2)}) async-start(bf16[8,2,96,128]{3,2,1,0:T(8,128)(2,1)} %get-tuple-element.102), calls=%async_computation.9 | async-start | bytes 786432 | tf_op jit(solution)/shard_map/all_to_all | solution.py:351
  254.0 23.6 %all-to-all-start.12 = ((bf16[8,1,96,128]{3,2,1,0:T(8,128)(2,1)}), bf16[8,1,96,128]{3,2,1,0:T(8,128)(2,1)S(1)}, u32[]{:S(2)}, u32[]{:S(2)}) async-start(bf16[8,1,96,128]{3,2,1,0:T(8,128)(2,1)} %get-tuple-element.110), calls=%async_computation.12 | async-start | bytes 393216 | tf_op jit(solution)/shard_map/all_to_all | solution.py:351
  277.6 18.4 %all-to-all-start.11 = ((bf16[8,2,96,128]{3,2,1,0:T(8,128)(2,1)}), bf16[8,2,96,128]{3,2,1,0:T(8,128)(2,1)S(1)}, u32[]{:S(2)}, u32[]{:S(2)}) async-start(bf16[8,2,96,128]{3,2,1,0:T(8,128)(2,1)} %get-tuple-element.108), calls=%async_computation.11 | async-start | bytes 786432 | tf_op jit(solution)/shard_map/all_to_all | solution.py:351
  296.0 23.6 %all-to-all-start.14 = ((bf16[8,1,96,128]{3,2,1,0:T(8,128)(2,1)}), bf16[8,1,96,128]{3,2,1,0:T(8,128)(2,1)S(1)}, u32[]{:S(2)}, u32[]{:S(2)}) async-start(bf16[8,1,96,128]{3,2,1,0:T(8,128)(2,1)} %get-tuple-element.116), calls=%async_computation.14 | async-start | bytes 393216 | tf_op jit(solution)/shard_map/all_to_all | solution.py:351
  319.6 18.4 %all-to-all-start.13 = ((bf16[8,2,96,128]{3,2,1,0:T(8,128)(2,1)}), bf16[8,2,96,128]{3,2,1,0:T(8,128)(2,1)S(1)}, u32[]{:S(2)}, u32[]{:S(2)}) async-start(bf16[8,2,96,128]{3,2,1,0:T(8,128)(2,1)} %get-tuple-element.114), calls=%async_computation.13 | async-start | bytes 786432 | tf_op jit(solution)/shard_map/all_to_all | solution.py:351
  338.1 22.3 %all-to-all-start.15 = ((bf16[8,1,96,128]{3,2,1,0:T(8,128)(2,1)}), bf16[8,1,96,128]{3,2,1,0:T(8,128)(2,1)S(1)}, u32[]{:S(2)}, u32[]{:S(2)}) async-start(bf16[8,1,96,128]{3,2,1,0:T(8,128)(2,1)} %get-tuple-element.120), calls=%async_computation.15 | async-start | bytes 393216 | tf_op jit(solution)/shard_map/all_to_all | solution.py:351
  (12 other events, 103.6 us)

commit v10 on v9

--- a/solution.py
+++ b/solution.py
@@ -159,15 +159,20 @@
             )
         )
     start_all(copies)
-    tile_copy(0).start()
+    ahead = min(3, rows)
+    for row in range(ahead):
+        tile_copy(row).start()
+    initial_copy.start()
     wait_all(copies)
-    initial_copy.start()
-    for row in range(1, rows):
-        tile_copy(row).start()
     initial_copy.wait()
 
     def one_row(row, carry):
         tile_copy(row).wait()
+
+        @pl.when(row + ahead < rows)
+        def _():
+            tile_copy(row + ahead).start()
+
         base = (first_row + row) * fanout
         total = None
         for tile in range(0, fanout, 2):
@@ -364,7 +369,7 @@
     weights = spread(turn_blocks(section, layer_weights[None], (0,), section_count))
 
     pieces = []
-    after = [pieces[0] for pieces in turned[1:]]
+    after = [pieces[0] for pieces in turned[1:]] + weights[1:]
     for layer in range(layers):
         last = layer == layers - 1
         own_next, imports_next = [], []

time: 377 us -> 374 us (level)
  Pallas kernels: 135 us -> 119 us
  waiting for transfers between devices: 5.57 us -> 14 us
    pallas_call x16, Pallas kernels: 96 us -> 79.8 us  [aggregate(): pl.pallas_call(functools.partial(aggregate_kernel, plan), grid_spec=pltpu...]
    ppermute x9, waiting for transfers between devices: 4.87 us -> 14 us  [spread(): lax.ppermute(pieces[distance], 'section', [(s, (s + distance) % section_c...]
  transfers between devices with their start and end apart: 25 -> 25, of which waited for: 3 -> 1; matrix products, arithmetic and copies ran while one was open for 0% -> 0% of each run, Pallas kernels for 33% -> 29%
where the time goes in v10:
time: 374 us; the launch traced here: 371 us
  blocking collectives  128 us (34%)
  Pallas kernels  119 us (32%)
  starting transfers between devices  101 us (27%)
  waiting for transfers between devices  14 us (4%)
  local copies, waits for them, and re-layouts  6.45 us (2%)
    all_gather x16, blocking collectives, per_device(): gathered = lax.all_gather(mixed, 'section', axis=0, tiled=False)  128 us
    all_to_all x16, starting transfers between devices, exchange(): return lax.all_to_all(value, 'dom', split_axis=0, concat_axis=0, tiled=True)  95 us
    pallas_call x16, Pallas kernels, aggregate(): pl.pallas_call(functools.partial(aggregate_kernel, plan), grid_spec=pltpu...  79.8 us
    pallas_call x16, Pallas kernels, finish(): pl.pallas_call(functools.partial(finish_kernel, plan), grid_spec=pltpu.Pr...  28 us
    ppermute x9, waiting for transfers between devices, spread(): lax.ppermute(pieces[distance], 'section', [(s, (s + distance) % section_c...  14 us
    pallas_call x3, Pallas kernels, turn_blocks(): pl.pallas_call(turn_kernel, grid_spec=pltpu.PrefetchScalarGridSpec(num_sc...  8.05 us
  transfers between devices with their start and end apart: 25, of which 1 were waited for; matrix products, arithmetic and copies ran while one was open for 0% of the time, Pallas kernels for 29%

profile of v10, /device:TPU:0, one launch (start us, length us, event | category | flops | bytes accessed | tf_op | source)
XLA Modules:
  0.0 370.6 jit_solution(8176664307284984926)
XLA Ops:
  7.1 7.3 %all-to-all-start = ((bf16[8,2,96,128]{3,2,1,0:T(8,128)(2,1)}), bf16[8,2,96,128]{3,2,1,0:T(8,128)(2,1)S(1)}, u32[]{:S(2)}, u32[]{:S(2)}) async-start(bf16[8,2,96,128]{3,2,1,0:T(8,128)(2,1)} %get-tuple-element.65), calls=%async_computation | async-start | bytes 786432 | tf_op jit(solution)/shard_map/all_to_all | solution.py:356
  23.0 13.9 %collective-permute-done.3.refs_8_.refs_1_ = bf16[2,96,384]{2,1,0:T(8,128)(2,1)S(1)} collective-permute-done((bf16[2,96,384]{2,1,0:T(8,128)(2,1)}, bf16[2,96,384]{2,1,0:T(8,128)(2,1)S(1)}, u32[]{:S(2)}, u32[]{:S(2)}) %collective-permute-start.3) | collective-permute-done | bytes 147488 | tf_op jit(solution)/shard_map/ppermute | solution.py:361
  37.1 6.1 %all-to-all-start.2 = ((bf16[8,1,96,128]{3,2,1,0:T(8,128)(2,1)}), bf16[8,1,96,128]{3,2,1,0:T(8,128)(2,1)S(1)}, u32[]{:S(2)}, u32[]{:S(2)}) async-start(bf16[8,1,96,128]{3,2,1,0:T(8,128)(2,1)} %get-tuple-element.80), calls=%async_computation.2 | async-start | bytes 393216 | tf_op jit(solution)/shard_map/all_to_all | solution.py:356
  50.2 8.7 %all-gather = bf16[32,96,128]{2,1,0:T(8,128)(2,1)S(1)} all-gather(bf16[8,96,128]{2,1,0:T(8,128)(2,1)S(1)} %aggregate.16.mixed_ref), channel_id=2, replica_groups=mesh['section'=4,'dom'=8] {'section'}, dimensions={0}, use_global_device_ids=true | all-gather | bytes 983040 | tf_op jit(solution)/shard_map/all_gather | solution.py:394
  63.6 6.0 %all-to-all-start.1 = ((bf16[8,2,96,128]{3,2,1,0:T(8,128)(2,1)}), bf16[8,2,96,128]{3,2,1,0:T(8,128)(2,1)S(1)}, u32[]{:S(2)}, u32[]{:S(2)}) async-start(bf16[8,2,96,128]{3,2,1,0:T(8,128)(2,1)} %get-tuple-element.75), calls=%async_computation.1 | async-start | bytes 786432 | tf_op jit(solution)/shard_map/all_to_all | solution.py:356
  76.5 16.2 %all-gather.1 = bf16[16,96,128]{2,1,0:T(8,128)(2,1)S(1)} all-gather(bf16[4,96,128]{2,1,0:T(8,128)(2,1)S(1)} %aggregate.17.mixed_ref), channel_id=3, replica_groups=mesh['section'=4,'dom'=8] {'section'}, dimensions={0}, use_global_device_ids=true | all-gather | bytes 491520 | tf_op jit(solution)/shard_map/all_gather | solution.py:394
  94.4 6.0 %all-to-all-start.4 = ((bf16[8,1,96,128]{3,2,1,0:T(8,128)(2,1)}), bf16[8,1,96,128]{3,2,1,0:T(8,128)(2,1)S(1)}, u32[]{:S(2)}, u32[]{:S(2)}) async-start(bf16[8,1,96,128]{3,2,1,0:T(8,128)(2,1)} %get-tuple-element.86), calls=%async_computation.4 | async-start | bytes 393216 | tf_op jit(solution)/shard_map/all_to_all | solution.py:356
  107.2 8.4 %all-gather.2 = bf16[32,96,128]{2,1,0:T(8,128)(2,1)S(1)} all-gather(bf16[8,96,128]{2,1,0:T(8,128)(2,1)S(1)} %aggregate.18.mixed_ref), channel_id=4, replica_groups=mesh['section'=4,'dom'=8] {'section'}, dimensions={0}, use_global_device_ids=true | all-gather | bytes 983040 | tf_op jit(solution)/shard_map/all_gather | solution.py:394
  117.7 5.9 %all-to-all-start.3 = ((bf16[8,2,96,128]{3,2,1,0:T(8,128)(2,1)}), bf16[8,2,96,128]{3,2,1,0:T(8,128)(2,1)S(1)}, u32[]{:S(2)}, u32[]{:S(2)}) async-start(bf16[8,2,96,128]{3,2,1,0:T(8,128)(2,1)} %get-tuple-element.84), calls=%async_computation.3 | async-start | bytes 786432 | tf_op jit(solution)/shard_map/all_to_all | solution.py:356
  127.7 6.3 %all-gather.3 = bf16[16,96,128]{2,1,0:T(8,128)(2,1)S(1)} all-gather(bf16[4,96,128]{2,1,0:T(8,128)(2,1)S(1)} %aggregate.19.mixed_ref), channel_id=5, replica_groups=mesh['section'=4,'dom'=8] {'section'}, dimensions={0}, use_global_device_ids=true | all-gather | bytes 491520 | tf_op jit(solution)/shard_map/all_gather | solution.py:394
  135.8 5.9 %all-to-all-start.6 = ((bf16[8,1,96,128]{3,2,1,0:T(8,128)(2,1)}), bf16[8,1,96,128]{3,2,1,0:T(8,128)(2,1)S(1)}, u32[]{:S(2)}, u32[]{:S(2)}) async-start(bf16[8,1,96,128]{3,2,1,0:T(8,128)(2,1)} %get-tuple-element.92), calls=%async_computation.6 | async-start | bytes 393216 | tf_op jit(solution)/shard_map/all_to_all | solution.py:356
  147.4 8.4 %all-gather.4 = bf16[32,96,128]{2,1,0:T(8,128)(2,1)S(1)} all-gather(bf16[8,96,128]{2,1,0:T(8,128)(2,1)S(1)} %aggregate.20.mixed_ref), channel_id=6, replica_groups=mesh['section'=4,'dom'=8] {'section'}, dimensions={0}, use_global_device_ids=true | all-gather | bytes 983040 | tf_op jit(solution)/shard_map/all_gather | solution.py:394
  167.8 6.3 %all-gather.5 = bf16[16,96,128]{2,1,0:T(8,128)(2,1)S(1)} all-gather(bf16[4,96,128]{2,1,0:T(8,128)(2,1)S(1)} %aggregate.21.mixed_ref), channel_id=7, replica_groups=mesh['section'=4,'dom'=8] {'section'}, dimensions={0}, use_global_device_ids=true | all-gather | bytes 491520 | tf_op jit(solution)/shard_map/all_gather | solution.py:394
  187.5 8.4 %all-gather.6 = bf16[32,96,128]{2,1,0:T(8,128)(2,1)S(1)} all-gather(bf16[8,96,128]{2,1,0:T(8,128)(2,1)S(1)} %aggregate.22.mixed_ref), channel_id=8, replica_groups=mesh['section'=4,'dom'=8] {'section'}, dimensions={0}, use_global_device_ids=true | all-gather | bytes 983040 | tf_op jit(solution)/shard_map/all_gather | solution.py:394
  207.8 6.3 %all-gather.7 = bf16[16,96,128]{2,1,0:T(8,128)(2,1)S(1)} all-gather(bf16[4,96,128]{2,1,0:T(8,128)(2,1)S(1)} %aggregate.23.mixed_ref), channel_id=9, replica_groups=mesh['section'=4,'dom'=8] {'section'}, dimensions={0}, use_global_device_ids=true | all-gather | bytes 491520 | tf_op jit(solution)/shard_map/all_gather | solution.py:394
  215.8 5.9 %all-to-all-start.10 = ((bf16[8,1,96,128]{3,2,1,0:T(8,128)(2,1)}), bf16[8,1,96,128]{3,2,1,0:T(8,128)(2,1)S(1)}, u32[]{:S(2)}, u32[]{:S(2)}) async-start(bf16[8,1,96,128]{3,2,1,0:T(8,128)(2,1)} %get-tuple-element.104), calls=%async_computation.10 | async-start | bytes 393216 | tf_op jit(solution)/shard_map/all_to_all | solution.py:356
  227.5 8.4 %all-gather.8 = bf16[32,96,128]{2,1,0:T(8,128)(2,1)S(1)} all-gather(bf16[8,96,128]{2,1,0:T(8,128)(2,1)S(1)} %aggregate.24.mixed_ref), channel_id=10, replica_groups=mesh['section'=4,'dom'=8] {'section'}, dimensions={0}, use_global_device_ids=true | all-gather | bytes 983040 | tf_op jit(solution)/shard_map/all_gather | solution.py:394
  247.8 6.3 %all-gather.9 = bf16[16,96,128]{2,1,0:T(8,128)(2,1)S(1)} all-gather(bf16[4,96,128]{2,1,0:T(8,128)(2,1)S(1)} %aggregate.25.mixed_ref), channel_id=11, replica_groups=mesh['section'=4,'dom'=8] {'section'}, dimensions={0}, use_global_device_ids=true | all-gather | bytes 491520 | tf_op jit(solution)/shard_map/all_gather | solution.py:394
  267.7 8.4 %all-gather.10 = bf16[32,96,128]{2,1,0:T(8,128)(2,1)S(1)} all-gather(bf16[8,96,128]{2,1,0:T(8,128)(2,1)S(1)} %aggregate.26.mixed_ref), channel_id=12, replica_groups=mesh['section'=4,'dom'=8] {'section'}, dimensions={0}, use_global_device_ids=true | all-gather | bytes 983040 | tf_op jit(solution)/shard_map/all_gather | solution.py:394
  288.1 6.3 %all-gather.11 = bf16[16,96,128]{2,1,0:T(8,128)(2,1)S(1)} all-gather(bf16[4,96,128]{2,1,0:T(8,128)(2,1)S(1)} %aggregate.27.mixed_ref), channel_id=13, replica_groups=mesh['section'=4,'dom'=8] {'section'}, dimensions={0}, use_global_device_ids=true | all-gather | bytes 491520 | tf_op jit(solution)/shard_map/all_gather | solution.py:394
  307.8 8.4 %all-gather.12 = bf16[32,96,128]{2,1,0:T(8,128)(2,1)S(1)} all-gather(bf16[8,96,128]{2,1,0:T(8,128)(2,1)S(1)} %aggregate.28.mixed_ref), channel_id=14, replica_groups=mesh['section'=4,'dom'=8] {'section'}, dimensions={0}, use_global_device_ids=true | all-gather | bytes 983040 | tf_op jit(solution)/shard_map/all_gather | solution.py:394
  328.1 6.3 %all-gather.13 = bf16[16,96,128]{2,1,0:T(8,128)(2,1)S(1)} all-gather(bf16[4,96,128]{2,1,0:T(8,128)(2,1)S(1)} %aggregate.29.mixed_ref), channel_id=15, replica_groups=mesh['section'=4,'dom'=8] {'section'}, dimensions={0}, use_global_device_ids=true | all-gather | bytes 491520 | tf_op jit(solution)/shard_map/all_gather | solution.py:394
  348.4 8.4 %all-gather.14 = bf16[32,96,128]{2,1,0:T(8,128)(2,1)S(1)} all-gather(bf16[8,96,128]{2,1,0:T(8,128)(2,1)S(1)} %aggregate.30.mixed_ref), channel_id=16, replica_groups=mesh['section'=4,'dom'=8] {'section'}, dimensions={0}, use_global_device_ids=true | all-gather | bytes 983040 | tf_op jit(solution)/shard_map/all_gather | solution.py:394
  361.0 6.6 %all-gather.15 = bf16[16,96,128]{2,1,0:T(8,128)(2,1)S(1)} all-gather(bf16[4,96,128]{2,1,0:T(8,128)(2,1)S(1)} %aggregate.31.mixed_ref), channel_id=17, replica_groups=mesh['section'=4,'dom'=8] {'section'}, dimensions={0}, use_global_device_ids=true | all-gather | bytes 491520 | tf_op jit(solution)/shard_map/all_gather | solution.py:394
  (126 shorter events, 184.8 us)
Async XLA Ops:
  7.1 30.1 %all-to-all-start = ((bf16[8,2,96,128]{3,2,1,0:T(8,128)(2,1)}), bf16[8,2,96,128]{3,2,1,0:T(8,128)(2,1)S(1)}, u32[]{:S(2)}, u32[]{:S(2)}) async-start(bf16[8,2,96,128]{3,2,1,0:T(8,128)(2,1)} %get-tuple-element.65), calls=%async_computation | async-start | bytes 786432 | tf_op jit(solution)/shard_map/all_to_all | solution.py:356
  14.3 28.9 %collective-permute-start = (bf16[16,96,128]{2,1,0:T(8,128)(2,1)}, bf16[16,96,128]{2,1,0:T(8,128)(2,1)S(1)}, u32[]{:S(2)}, u32[]{:S(2)}) collective-permute-start(bf16[16,96,128]{2,1,0:T(8,128)(2,1)} %get-tuple-element.66), channel_id=1, source_target_pairs={{0,8},{8,16},{16,24},{24,0},{1,9},{9,17},{17,25},{25,1},{2,10},{10... | collective-permute-start | bytes 1179656 | tf_op jit(solution)/shard_map/ppermute | solution.py:361
  14.4 28.9 %collective-permute-start.1 = (bf16[16,96,128]{2,1,0:T(8,128)(2,1)}, bf16[16,96,128]{2,1,0:T(8,128)(2,1)S(1)}, u32[]{:S(2)}, u32[]{:S(2)}) collective-permute-start(bf16[16,96,128]{2,1,0:T(8,128)(2,1)} %get-tuple-element.67), channel_id=1, source_target_pairs={{0,16},{8,24},{16,0},{24,8},{1,17},{9,25},{17,1},{25,9},{2,18},{10... | collective-permute-start | bytes 1179656 | tf_op jit(solution)/shard_map/ppermute | solution.py:361
  15.9 27.4 %collective-permute-start.2 = (bf16[16,96,128]{2,1,0:T(8,128)(2,1)}, bf16[16,96,128]{2,1,0:T(8,128)(2,1)S(1)}, u32[]{:S(2)}, u32[]{:S(2)}) collective-permute-start(bf16[16,96,128]{2,1,0:T(8,128)(2,1)} %get-tuple-element.68), channel_id=1, source_target_pairs={{0,24},{8,0},{16,8},{24,16},{1,25},{9,1},{17,9},{25,17},{2,26},{10... | collective-permute-start | bytes 1179656 | tf_op jit(solution)/shard_map/ppermute | solution.py:361
  19.5 17.4 %collective-permute-start.3 = (bf16[2,96,384]{2,1,0:T(8,128)(2,1)}, bf16[2,96,384]{2,1,0:T(8,128)(2,1)S(1)}, u32[]{:S(2)}, u32[]{:S(2)}) collective-permute-start(bf16[2,96,384]{2,1,0:T(8,128)(2,1)} %get-tuple-element.70), channel_id=1, source_target_pairs={{0,8},{8,16},{16,24},{24,0},{1,9},{9,17},{17,25},{25,1},{2,10},{10... | collective-permute-start | bytes 442376 | tf_op jit(solution)/shard_map/ppermute | solution.py:361
  19.5 23.7 %collective-permute-start.4 = (bf16[2,96,384]{2,1,0:T(8,128)(2,1)}, bf16[2,96,384]{2,1,0:T(8,128)(2,1)S(1)}, u32[]{:S(2)}, u32[]{:S(2)}) collective-permute-start(bf16[2,96,384]{2,1,0:T(8,128)(2,1)} %get-tuple-element.71), channel_id=1, source_target_pairs={{0,16},{8,24},{16,0},{24,8},{1,17},{9,25},{17,1},{25,9},{2,18},{10... | collective-permute-start | bytes 442376 | tf_op jit(solution)/shard_map/ppermute | solution.py:361
  37.1 26.5 %all-to-all-start.2 = ((bf16[8,1,96,128]{3,2,1,0:T(8,128)(2,1)}), bf16[8,1,96,128]{3,2,1,0:T(8,128)(2,1)S(1)}, u32[]{:S(2)}, u32[]{:S(2)}) async-start(bf16[8,1,96,128]{3,2,1,0:T(8,128)(2,1)} %get-tuple-element.80), calls=%async_computation.2 | async-start | bytes 393216 | tf_op jit(solution)/shard_map/all_to_all | solution.py:356
  63.6 30.8 %all-to-all-start.1 = ((bf16[8,2,96,128]{3,2,1,0:T(8,128)(2,1)}), bf16[8,2,96,128]{3,2,1,0:T(8,128)(2,1)S(1)}, u32[]{:S(2)}, u32[]{:S(2)}) async-start(bf16[8,2,96,128]{3,2,1,0:T(8,128)(2,1)} %get-tuple-element.75), calls=%async_computation.1 | async-start | bytes 786432 | tf_op jit(solution)/shard_map/all_to_all | solution.py:356
  69.6 30.8 %collective-permute-start.6 = (bf16[16,96,128]{2,1,0:T(8,128)(2,1)}, bf16[16,96,128]{2,1,0:T(8,128)(2,1)S(1)}, u32[]{:S(2)}, u32[]{:S(2)}) collective-permute-start(bf16[16,96,128]{2,1,0:T(8,128)(2,1)} %get-tuple-element.76), channel_id=1, source_target_pairs={{0,8},{8,16},{16,24},{24,0},{1,9},{9,17},{17,25},{25,1},{2,10},{10... | collective-permute-start | bytes 1179656 | tf_op jit(solution)/shard_map/ppermute | solution.py:361
  69.7 30.7 %collective-permute-start.7 = (bf16[16,96,128]{2,1,0:T(8,128)(2,1)S(1)}, bf16[16,96,128]{2,1,0:T(8,128)(2,1)S(1)}, u32[]{:S(2)}, u32[]{:S(2)}) collective-permute-start(bf16[16,96,128]{2,1,0:T(8,128)(2,1)S(1)} %copy-done.18), channel_id=1, source_target_pairs={{0,16},{8,24},{16,0},{24,8},{1,17},{9,25},{17,1},{25,9},{2,18},{10... | collective-permute-start | bytes 1179656 | tf_op jit(solution)/shard_map/ppermute | solution.py:361
  70.9 29.5 %collective-permute-start.8 = (bf16[16,96,128]{2,1,0:T(8,128)(2,1)S(1)}, bf16[16,96,128]{2,1,0:T(8,128)(2,1)S(1)}, u32[]{:S(2)}, u32[]{:S(2)}) collective-permute-start(bf16[16,96,128]{2,1,0:T(8,128)(2,1)S(1)} %copy-done.17), channel_id=1, source_target_pairs={{0,24},{8,0},{16,8},{24,16},{1,25},{9,1},{17,9},{25,17},{2,26},{10... | collective-permute-start | bytes 1179656 | tf_op jit(solution)/shard_map/ppermute | solution.py:361
  94.4 23.3 %all-to-all-start.4 = ((bf16[8,1,96,128]{3,2,1,0:T(8,128)(2,1)}), bf16[8,1,96,128]{3,2,1,0:T(8,128)(2,1)S(1)}, u32[]{:S(2)}, u32[]{:S(2)}) async-start(bf16[8,1,96,128]{3,2,1,0:T(8,128)(2,1)} %get-tuple-element.86), calls=%async_computation.4 | async-start | bytes 393216 | tf_op jit(solution)/shard_map/all_to_all | solution.py:356
  117.7 18.1 %all-to-all-start.3 = ((bf16[8,2,96,128]{3,2,1,0:T(8,128)(2,1)}), bf16[8,2,96,128]{3,2,1,0:T(8,128)(2,1)S(1)}, u32[]{:S(2)}, u32[]{:S(2)}) async-start(bf16[8,2,96,128]{3,2,1,0:T(8,128)(2,1)} %get-tuple-element.84), calls=%async_computation.3 | async-start | bytes 786432 | tf_op jit(solution)/shard_map/all_to_all | solution.py:356
  135.8 22.1 %all-to-all-start.6 = ((bf16[8,1,96,128]{3,2,1,0:T(8,128)(2,1)}), bf16[8,1,96,128]{3,2,1,0:T(8,128)(2,1)S(1)}, u32[]{:S(2)}, u32[]{:S(2)}) async-start(bf16[8,1,96,128]{3,2,1,0:T(8,128)(2,1)} %get-tuple-element.92), calls=%async_computation.6 | async-start | bytes 393216 | tf_op jit(solution)/shard_map/all_to_all | solution.py:356
  157.8 18.0 %all-to-all-start.5 = ((bf16[8,2,96,128]{3,2,1,0:T(8,128)(2,1)}), bf16[8,2,96,128]{3,2,1,0:T(8,128)(2,1)S(1)}, u32[]{:S(2)}, u32[]{:S(2)}) async-start(bf16[8,2,96,128]{3,2,1,0:T(8,128)(2,1)} %get-tuple-element.90), calls=%async_computation.5 | async-start | bytes 786432 | tf_op jit(solution)/shard_map/all_to_all | solution.py:356
  175.8 22.1 %all-to-all-start.8 = ((bf16[8,1,96,128]{3,2,1,0:T(8,128)(2,1)}), bf16[8,1,96,128]{3,2,1,0:T(8,128)(2,1)S(1)}, u32[]{:S(2)}, u32[]{:S(2)}) async-start(bf16[8,1,96,128]{3,2,1,0:T(8,128)(2,1)} %get-tuple-element.98), calls=%async_computation.8 | async-start | bytes 393216 | tf_op jit(solution)/shard_map/all_to_all | solution.py:356
  197.9 17.9 %all-to-all-start.7 = ((bf16[8,2,96,128]{3,2,1,0:T(8,128)(2,1)}), bf16[8,2,96,128]{3,2,1,0:T(8,128)(2,1)S(1)}, u32[]{:S(2)}, u32[]{:S(2)}) async-start(bf16[8,2,96,128]{3,2,1,0:T(8,128)(2,1)} %get-tuple-element.96), calls=%async_computation.7 | async-start | bytes 786432 | tf_op jit(solution)/shard_map/all_to_all | solution.py:356
  215.8 22.1 %all-to-all-start.10 = ((bf16[8,1,96,128]{3,2,1,0:T(8,128)(2,1)}), bf16[8,1,96,128]{3,2,1,0:T(8,128)(2,1)S(1)}, u32[]{:S(2)}, u32[]{:S(2)}) async-start(bf16[8,1,96,128]{3,2,1,0:T(8,128)(2,1)} %get-tuple-element.104), calls=%async_computation.10 | async-start | bytes 393216 | tf_op jit(solution)/shard_map/all_to_all | solution.py:356
  237.9 18.1 %all-to-all-start.9 = ((bf16[8,2,96,128]{3,2,1,0:T(8,128)(2,1)}), bf16[8,2,96,128]{3,2,1,0:T(8,128)(2,1)S(1)}, u32[]{:S(2)}, u32[]{:S(2)}) async-start(bf16[8,2,96,128]{3,2,1,0:T(8,128)(2,1)} %get-tuple-element.102), calls=%async_computation.9 | async-start | bytes 786432 | tf_op jit(solution)/shard_map/all_to_all | solution.py:356
  256.1 22.1 %all-to-all-start.12 = ((bf16[8,1,96,128]{3,2,1,0:T(8,128)(2,1)}), bf16[8,1,96,128]{3,2,1,0:T(8,128)(2,1)S(1)}, u32[]{:S(2)}, u32[]{:S(2)}) async-start(bf16[8,1,96,128]{3,2,1,0:T(8,128)(2,1)} %get-tuple-element.110), calls=%async_computation.12 | async-start | bytes 393216 | tf_op jit(solution)/shard_map/all_to_all | solution.py:356
  278.1 18.0 %all-to-all-start.11 = ((bf16[8,2,96,128]{3,2,1,0:T(8,128)(2,1)}), bf16[8,2,96,128]{3,2,1,0:T(8,128)(2,1)S(1)}, u32[]{:S(2)}, u32[]{:S(2)}) async-start(bf16[8,2,96,128]{3,2,1,0:T(8,128)(2,1)} %get-tuple-element.108), calls=%async_computation.11 | async-start | bytes 786432 | tf_op jit(solution)/shard_map/all_to_all | solution.py:356
  296.1 22.1 %all-to-all-start.14 = ((bf16[8,1,96,128]{3,2,1,0:T(8,128)(2,1)}), bf16[8,1,96,128]{3,2,1,0:T(8,128)(2,1)S(1)}, u32[]{:S(2)}, u32[]{:S(2)}) async-start(bf16[8,1,96,128]{3,2,1,0:T(8,128)(2,1)} %get-tuple-element.116), calls=%async_computation.14 | async-start | bytes 393216 | tf_op jit(solution)/shard_map/all_to_all | solution.py:356
  318.2 17.9 %all-to-all-start.13 = ((bf16[8,2,96,128]{3,2,1,0:T(8,128)(2,1)}), bf16[8,2,96,128]{3,2,1,0:T(8,128)(2,1)S(1)}, u32[]{:S(2)}, u32[]{:S(2)}) async-start(bf16[8,2,96,128]{3,2,1,0:T(8,128)(2,1)} %get-tuple-element.114), calls=%async_computation.13 | async-start | bytes 786432 | tf_op jit(solution)/shard_map/all_to_all | solution.py:356
  336.1 20.7 %all-to-all-start.15 = ((bf16[8,1,96,128]{3,2,1,0:T(8,128)(2,1)}), bf16[8,1,96,128]{3,2,1,0:T(8,128)(2,1)S(1)}, u32[]{:S(2)}, u32[]{:S(2)}) async-start(bf16[8,1,96,128]{3,2,1,0:T(8,128)(2,1)} %get-tuple-element.120), calls=%async_computation.15 | async-start | bytes 393216 | tf_op jit(solution)/shard_map/all_to_all | solution.py:356
  (21 other events, 188.7 us)

commit v11 on v9

--- a/solution.py
+++ b/solution.py
@@ -132,61 +132,94 @@
     )(section, pinned(blocks))
 
 
+class Aggregate:
+    def __init__(self, plan, columns, info, initial_ref, tiles_ref, source_refs, mixed_ref, scratch):
+        self.stream, self.group_blocks, self.fanout, sources, home, sections = plan
+        self.columns, self.tiles_ref, self.mixed_ref = columns, tiles_ref, mixed_ref
+        self.table, self.tiles, self.initial, table_sem, self.tiles_sem, initial_sem = scratch
+        self.rows = len(self.stream) * self.group_blocks
+        self.first_row = self.stream[0] * self.group_blocks
+        self.ahead = min(3, self.rows)
+        self.initial_copy = pltpu.make_async_copy(initial_ref, self.initial, initial_sem)
+        self.copies = []
+        for index, (kind, target, detail) in enumerate(sources):
+            ref = source_refs[index]
+            source = ref.at[:, detail] if kind == "import" else ref
+            condition = None
+            if kind == "stale":
+                condition = lax.rem(info[0] - home + 2 * sections, sections) == detail
+            part = self.table.at[pl.ds(target, source.shape[0])]
+            copy = pltpu.make_async_copy(source, part, table_sem.at[index])
+            self.copies.append((condition, copy))
+
+    def tile_copy(self, row):
+        return pltpu.make_async_copy(
+            self.tiles_ref.at[self.first_row + row], self.tiles.at[row], self.tiles_sem.at[row]
+        )
+
+    def begin(self):
+        start_all(self.copies)
+        for row in range(self.ahead):
+            self.tile_copy(row).start()
+        self.initial_copy.start()
+
+    def run(self):
+        wait_all(self.copies)
+        self.initial_copy.wait()
+
+        def one_row(row, carry):
+            self.tile_copy(row).wait()
+
+            @pl.when(row + self.ahead < self.rows)
+            def _():
+                self.tile_copy(row + self.ahead).start()
+
+            base = (self.first_row + row) * self.fanout
+            total = None
+            for tile in range(0, self.fanout, 2):
+                span = range(tile, min(tile + 2, self.fanout))
+                left = jnp.concatenate([self.table[self.columns[base + t]] for t in span], 1)
+                right = jnp.concatenate([self.tiles[row, t] for t in span], 1)
+                term = lax.dot_general(
+                    left, right, (((1,), (1,)), ((), ())), preferred_element_type=jnp.float32
+                )
+                total = term if total is None else total + term
+            start = self.initial[row].astype(jnp.float32)
+            self.mixed_ref[row] = ((1.0 - alpha_mix) * total + alpha_mix * start).astype(
+                jnp.bfloat16
+            )
+            return carry
+
+        lax.fori_loop(0, self.rows, one_row, 0)
+
+
 def aggregate_kernel(plan, columns, info, initial_ref, tiles_ref, *refs):
-    stream, group_blocks, fanout, sources, home, sections = plan
-    source_refs = refs[: len(sources)]
-    mixed_ref, table, tiles, initial, table_sem, tiles_sem, initial_sem = refs[-7:]
-    rows = len(stream) * group_blocks
-    first_row = stream[0] * group_blocks
-
-    def tile_copy(row):
-        return pltpu.make_async_copy(tiles_ref.at[first_row + row], tiles.at[row], tiles_sem.at[row])
-
-    initial_copy = pltpu.make_async_copy(initial_ref, initial, initial_sem)
-    copies = []
-    for index, (kind, target, detail) in enumerate(sources):
-        ref = source_refs[index]
-        source = ref.at[:, detail] if kind == "import" else ref
-        condition = None
-        if kind == "stale":
-            condition = lax.rem(info[0] - home + 2 * sections, sections) == detail
-        copies.append(
-            (
-                condition,
-                pltpu.make_async_copy(
-                    source, table.at[pl.ds(target, source.shape[0])], table_sem.at[index]
-                ),
-            )
-        )
-    start_all(copies)
-    tile_copy(0).start()
-    wait_all(copies)
-    initial_copy.start()
-    for row in range(1, rows):
-        tile_copy(row).start()
-    initial_copy.wait()
-
-    def one_row(row, carry):
-        tile_copy(row).wait()
-        base = (first_row + row) * fanout
-        total = None
-        for tile in range(0, fanout, 2):
-            span = range(tile, min(tile + 2, fanout))
-            left = jnp.concatenate([table[columns[base + t]] for t in span], 1)
-            right = jnp.concatenate([tiles[row, t] for t in span], 1)
-            term = lax.dot_general(
-                left, right, (((1,), (1,)), ((), ())), preferred_element_type=jnp.float32
-            )
-            total = term if total is None else total + term
-        mixed_ref[row] = (
-            (1.0 - alpha_mix) * total + alpha_mix * initial[row].astype(jnp.float32)
-        ).astype(jnp.bfloat16)
-        return carry
-
-    lax.fori_loop(0, rows, one_row, 0)
-
-
-def aggregate(columns, section, initial_blocks, tiles, own, imports, stale, home, stream, streams, group_blocks, part_count, after):
+    count = len(plan[3])
+    work = Aggregate(plan, columns, info, initial_ref, tiles_ref, refs[:count], refs[-7], refs[-6:])
+    work.begin()
+    work.run()
+
+
+def both_kernel(finish_plan, aggregate_plan, columns, picks, info, mixed_ref, gathered_ref, *refs):
+    parts = gathered_ref.shape[0]
+    count = len(aggregate_plan[3])
+    weight_refs, refs = refs[:parts], refs[parts:]
+    initial_ref, tiles_ref = refs[:2]
+    source_refs, refs = refs[2 : 2 + count], refs[2 + count :]
+    own_ref, outgoing_ref, next_ref = refs[:3]
+    weight, weight_sem = refs[3:5]
+    work = Aggregate(
+        aggregate_plan, columns, info, initial_ref, tiles_ref, source_refs, next_ref, refs[5:]
+    )
+    work.begin()
+    finish_body(
+        finish_plan, picks, info, mixed_ref, gathered_ref, weight_refs, [own_ref, outgoing_ref],
+        weight, weight_sem,
+    )
+    work.run()
+
+
+def aggregate_parts(section, initial_blocks, tiles, own, imports, stale, home, stream, streams, group_blocks, part_count):
     rows, part_width, block = initial_blocks.shape
     blocks_dev, fanout = tiles.shape[:2]
     groups = blocks_dev // group_blocks
@@ -206,43 +239,92 @@
             sources.append(("stale", blocks_dev + groups * part_count, distance))
             operands.append(pinned(stale_blocks))
             specs.append(hbm)
-    operands += [pinned(value) for value in after]
-    specs += [hbm] * len(after)
     table_size = blocks_dev + (2 * groups - 1) * part_count
     plan = (stream, group_blocks, fanout, sources, home, len(stale))
-    flops = 2 * rows * fanout * block * block * part_width
+    scratch = [
+        pltpu.VMEM((table_size, part_width, block), jnp.bfloat16),
+        pltpu.VMEM((rows, fanout, block, block), jnp.bfloat16),
+        pltpu.VMEM(initial_blocks.shape, jnp.bfloat16),
+        pltpu.SemaphoreType.DMA((len(sources),)),
+        pltpu.SemaphoreType.DMA((rows,)),
+        pltpu.SemaphoreType.DMA,
+    ]
+    operands = [pinned(initial_blocks), pinned(tiles)] + operands
+    return plan, operands, [hbm, hbm] + specs, scratch
+
+
+def estimate(rows, fanout, block, part_width, width):
+    return pl.CostEstimate(
+        flops=2 * rows * block * part_width * (fanout * block + width),
+        bytes_accessed=rows * fanout * block * block * 2,
+        transcendentals=0,
+    )
+
+
+def aggregate(columns, section, parts, shape, after):
+    plan, operands, specs, scratch = parts
+    operands = operands + [pinned(value) for value in after]
     return pl.pallas_call(
         functools.partial(aggregate_kernel, plan),
         grid_spec=pltpu.PrefetchScalarGridSpec(
             num_scalar_prefetch=2,
             grid=(1,),
-            in_specs=[hbm, hbm] + specs,
-            out_specs=whole((rows, part_width, block)),
-            scratch_shapes=[
-                pltpu.VMEM((table_size, part_width, block), jnp.bfloat16),
-                pltpu.VMEM((rows, fanout, block, block), jnp.bfloat16),
-                pltpu.VMEM(initial_blocks.shape, jnp.bfloat16),
-                pltpu.SemaphoreType.DMA((len(sources),)),
-                pltpu.SemaphoreType.DMA((rows,)),
-                pltpu.SemaphoreType.DMA,
-            ],
-        ),
-        out_shape=jax.ShapeDtypeStruct((rows, part_width, block), jnp.bfloat16),
-        cost_estimate=pl.CostEstimate(
-            flops=flops, bytes_accessed=rows * fanout * block * block * 2, transcendentals=0
-        ),
+            in_specs=specs + [hbm] * len(after),
+            out_specs=whole(shape),
+            scratch_shapes=scratch,
+        ),
+        out_shape=jax.ShapeDtypeStruct(shape, jnp.bfloat16),
+        cost_estimate=estimate(shape[0], plan[2], shape[2], shape[1], 0),
         compiler_params=params(),
         name="aggregate",
-    )(columns, section, pinned(initial_blocks), pinned(tiles), *operands)
+    )(columns, section, *operands)
+
+
+def finish_and_aggregate(columns, picks, section, mixed, gathered, weights, layer, depth, stream, group_blocks, part_count, parts, shape):
+    aggregate_plan, operands, specs, scratch = parts
+    rows, part_width, block = mixed.shape
+    width = weights[0].shape[2]
+    beta_layer = math.log(lambda_decay / (layer + 1) + 1.0)
+    plan = (beta_layer, stream, group_blocks, part_count, layer % depth, layer // depth, False)
+    outgoing = (part_count, len(stream), part_width, block)
+    return pl.pallas_call(
+        functools.partial(both_kernel, plan, aggregate_plan),
+        grid_spec=pltpu.PrefetchScalarGridSpec(
+            num_scalar_prefetch=3,
+            grid=(1,),
+            in_specs=[whole(mixed.shape), whole(gathered.shape)] + [anywhere] * len(weights) + specs,
+            out_specs=[whole(mixed.shape), whole(outgoing), whole(shape)],
+            scratch_shapes=[
+                pltpu.VMEM((part_width, width), jnp.bfloat16),
+                pltpu.SemaphoreType.DMA((len(weights),)),
+            ]
+            + scratch,
+        ),
+        out_shape=[
+            in_hbm(mixed.shape),
+            jax.ShapeDtypeStruct(outgoing, jnp.bfloat16),
+            jax.ShapeDtypeStruct(shape, jnp.bfloat16),
+        ],
+        cost_estimate=estimate(shape[0], aggregate_plan[2], block, part_width, width),
+        compiler_params=params(),
+        name="finish_aggregate",
+    )(columns, picks, section, mixed, gathered, *weights, *operands)
 
 
 def finish_kernel(plan, picks, info, mixed_ref, gathered_ref, *refs):
+    parts = gathered_ref.shape[0]
+    out_refs = refs[parts:-2]
+    finish_body(
+        plan, picks, info, mixed_ref, gathered_ref, refs[:parts], out_refs, refs[-2], refs[-1]
+    )
+    if len(out_refs) > 2:
+        out_refs[2][...] = jnp.zeros_like(out_refs[2])
+
+
+def finish_body(plan, picks, info, mixed_ref, gathered_ref, weight_refs, refs, weight, weight_sem):
     beta_layer, stream, group_blocks, part_count, sub, home, last = plan
     rows, part_width, block = mixed_ref.shape
     parts = gathered_ref.shape[0]
-    weight_refs = refs[:parts]
-    weight, weight_sem = refs[-2:]
-    refs = refs[parts:-2]
     copies = [
         (
             lax.rem(info[0] - home + 2 * parts, parts) == distance,
@@ -269,7 +351,6 @@
                 refs[0][r] = value
     if not last:
         pick_outgoing(picks, refs[0], refs[1], stream, group_blocks, part_count)
-        refs[2][...] = jnp.zeros_like(refs[2])
 
 
 def finish(picks, section, mixed, gathered, weights, layer, depth, stream, group_blocks, part_count, last):
@@ -363,42 +444,40 @@
     stale = [spread(pieces) for pieces in turned]
     weights = spread(turn_blocks(section, layer_weights[None], (0,), section_count))
 
-    pieces = []
-    after = [pieces[0] for pieces in turned[1:]]
+    front, back = streams
+    turned_late = [pieces[0] for pieces in turned[1:]]
+
+    def parts_of(index, layer):
+        return aggregate_parts(
+            section, initial_blocks[index], adjacency_tiles, own, imports, stale[layer % depth],
+            layer // depth, streams[index], streams, group_blocks, part_count,
+        )
+
+    own, imports = list(own), list(imports)
+    shapes = [value.shape for value in initial_blocks]
+    mixed_front = aggregate(columns, section, parts_of(0, 0), shapes[0], turned_late)
     for layer in range(layers):
         last = layer == layers - 1
-        own_next, imports_next = [], []
-        for index, stream in enumerate(streams):
-            mixed = aggregate(
-                columns,
-                section,
-                initial_blocks[index],
-                adjacency_tiles,
-                own,
-                imports,
-                stale[layer % depth],
-                layer // depth,
-                stream,
-                streams,
-                group_blocks,
-                part_count,
-                after,
-            )
-            if last:
-                after = [mixed[0]]
-            gathered = lax.all_gather(mixed, "section", axis=0, tiled=False)
-            result = finish(
-                picks, section, mixed, gathered, weights, layer, depth, stream, group_blocks,
+        gathered = lax.all_gather(mixed_front, "section", axis=0, tiled=False)
+        front_result = finish(
+            picks, section, mixed_front, gathered, weights, layer, depth, front, group_blocks,
+            part_count, last,
+        )
+        after = [mixed_front[0]] if last else [front_result[2]]
+        mixed_back = aggregate(columns, section, parts_of(1, layer), shapes[1], after)
+        gathered = lax.all_gather(mixed_back, "section", axis=0, tiled=False)
+        if last:
+            back_result = finish(
+                picks, section, mixed_back, gathered, weights, layer, depth, back, group_blocks,
                 part_count, last,
             )
-            if last:
-                pieces.append(result[0])
-            else:
-                after = [result[2]]
-                own_next.append(result[0])
-                imports_next.append(exchange(result[1]))
-        own, imports = own_next, imports_next
-    return jnp.concatenate(pieces, 0) if len(pieces) > 1 else pieces[0]
+            return jnp.concatenate([front_result[0], back_result[0]], 0)
+        own[0], imports[0] = front_result[0], exchange(front_result[1])
+        own[1], outgoing, mixed_front = finish_and_aggregate(
+            columns, picks, section, mixed_back, gathered, weights, layer, depth, back,
+            group_blocks, part_count, parts_of(0, layer + 1), shapes[0],
+        )
+        imports[1] = exchange(outgoing)
 
 
 def solution(mesh):

time: 377 us -> 353 us (0.936)
  Pallas kernels: 135 us -> 111 us
  starting transfers between devices: 99.8 us -> 89.5 us
  waiting for transfers between devices: 5.57 us -> 15.8 us
    pallas_call x16 -> x9, Pallas kernels: 96 us -> 39.2 us  [aggregate(): pl.pallas_call(functools.partial(aggregate_kernel, plan), grid_spec=pltpu...]
    pallas_call x0 -> x7, Pallas kernels: none -> 44.6 us  [finish_and_aggregate(): pl.pallas_call(functools.partial(both_kernel, plan, aggregate_plan), grid...]
    pallas_call x16 -> x9, Pallas kernels: 27.8 us -> 15.7 us  [finish(): pl.pallas_call(functools.partial(finish_kernel, plan), grid_spec=pltpu.Pr...]
    all_to_all x16, starting transfers between devices: 94.2 us -> 83.9 us  [exchange(): return lax.all_to_all(value, 'dom', split_axis=0, concat_axis=0, tiled=True)]
    all_to_all x16, waiting for transfers between devices: 0.7 us -> 10.9 us  [exchange(): return lax.all_to_all(value, 'dom', split_axis=0, concat_axis=0, tiled=True)]
  transfers between devices with their start and end apart: 25 -> 25, of which waited for: 3 -> 9; matrix products, arithmetic and copies ran while one was open for 0% -> 0% of each run, Pallas kernels for 33% -> 16%
where the time goes in v11:
time: 353 us; the launch traced here: 350 us
  blocking collectives  130 us (37%)
  Pallas kernels  111 us (31%)
  starting transfers between devices  89.5 us (25%)
  waiting for transfers between devices  15.8 us (4%)
    all_to_all x16, starting transfers between devices, exchange(): return lax.all_to_all(value, 'dom', split_axis=0, concat_axis=0, tiled=True)  83.9 us
    all_gather x8, blocking collectives, per_device(): gathered = lax.all_gather(mixed_front, 'section', axis=0, tiled=False)  68.4 us
    all_gather x8, blocking collectives, per_device(): gathered = lax.all_gather(mixed_back, 'section', axis=0, tiled=False)  61.2 us
    pallas_call x7, Pallas kernels, finish_and_aggregate(): pl.pallas_call(functools.partial(both_kernel, plan, aggregate_plan), grid...  44.6 us
    pallas_call x9, Pallas kernels, aggregate(): pl.pallas_call(functools.partial(aggregate_kernel, plan), grid_spec=pltpu...  39.2 us
    pallas_call x9, Pallas kernels, finish(): pl.pallas_call(functools.partial(finish_kernel, plan), grid_spec=pltpu.Pr...  15.7 us
    all_to_all x16, waiting for transfers between devices, exchange(): return lax.all_to_all(value, 'dom', split_axis=0, concat_axis=0, tiled=True)  10.9 us
    pallas_call x3, Pallas kernels, turn_blocks(): pl.pallas_call(turn_kernel, grid_spec=pltpu.PrefetchScalarGridSpec(num_sc...  8.01 us
  transfers between devices with their start and end apart: 25, of which 9 were waited for; matrix products, arithmetic and copies ran while one was open for 0% of the time, Pallas kernels for 16%

profile of v11, /device:TPU:0, one launch (start us, length us, event | category | flops | bytes accessed | tf_op | source)
XLA Modules:
  0.0 350.5 jit_solution(11431694520011376293)
XLA Ops:
  7.1 7.3 %all-to-all-start = ((bf16[8,2,96,128]{3,2,1,0:T(8,128)(2,1)}), bf16[8,2,96,128]{3,2,1,0:T(8,128)(2,1)S(1)}, u32[]{:S(2)}, u32[]{:S(2)}) async-start(bf16[8,2,96,128]{3,2,1,0:T(8,128)(2,1)} %get-tuple-element.66), calls=%async_computation | async-start | bytes 786432 | tf_op jit(solution)/shard_map/all_to_all | solution.py:432
  40.7 9.5 %all-gather = bf16[32,96,128]{2,1,0:T(8,128)(2,1)S(1)} all-gather(bf16[8,96,128]{2,1,0:T(8,128)(2,1)S(1)} %aggregate.9.mixed_ref), channel_id=2, replica_groups=mesh['section'=4,'dom'=8] {'section'}, dimensions={0}, use_global_device_ids=true | all-gather | bytes 983040 | tf_op jit(solution)/shard_map/all_gather | solution.py:461
  64.4 16.8 %all-gather.1 = bf16[16,96,128]{2,1,0:T(8,128)(2,1)S(1)} all-gather(bf16[4,96,128]{2,1,0:T(8,128)(2,1)S(1)} %aggregate.10.mixed_ref), channel_id=3, replica_groups=mesh['section'=4,'dom'=8] {'section'}, dimensions={0}, use_global_device_ids=true | all-gather | bytes 491520 | tf_op jit(solution)/shard_map/all_gather | solution.py:468
  82.2 6.4 %finish_aggregate.7 = (bf16[4,96,128]{2,1,0:T(8,128)(2,1)}, bf16[8,1,96,128]{3,2,1,0:T(8,128)(2,1)}, bf16[8,96,128]{2,1,0:T(8,128)(2,1)S(1)}) custom-call(s32[288]{0:T(512)S(1)} %reshape.24.columns, s32[24]{0:T(128)S(1)} %reshape.22.picks, s32[1]{0:T(128)} %bitcast.info, bf16[4,96,128]{2,1,0:T(8,128)(2,1)S(1)} %aggregate.10.mixed_ref, ...), custom_call_target="tpu_custom_call" | custom-call | flops 679477248 | bytes 6291456 | tf_op jit(solution)/shard_map/finish_aggregate/pallas_call | solution.py:290
  94.6 8.4 %all-gather.2 = bf16[32,96,128]{2,1,0:T(8,128)(2,1)S(1)} all-gather(bf16[8,96,128]{2,1,0:T(8,128)(2,1)S(1)} %get-tuple-element.82.mixed_ref), channel_id=4, replica_groups=mesh['section'=4,'dom'=8] {'section'}, dimensions={0}, use_global_device_ids=true | all-gather | bytes 983040 | tf_op jit(solution)/shard_map/all_gather | solution.py:461
  114.9 6.3 %all-gather.3 = bf16[16,96,128]{2,1,0:T(8,128)(2,1)S(1)} all-gather(bf16[4,96,128]{2,1,0:T(8,128)(2,1)S(1)} %aggregate.11.mixed_ref), channel_id=5, replica_groups=mesh['section'=4,'dom'=8] {'section'}, dimensions={0}, use_global_device_ids=true | all-gather | bytes 491520 | tf_op jit(solution)/shard_map/all_gather | solution.py:468
  122.9 6.4 %finish_aggregate.8 = (bf16[4,96,128]{2,1,0:T(8,128)(2,1)}, bf16[8,1,96,128]{3,2,1,0:T(8,128)(2,1)}, bf16[8,96,128]{2,1,0:T(8,128)(2,1)S(1)}) custom-call(s32[288]{0:T(512)S(1)} %reshape.24.columns, s32[24]{0:T(128)S(1)} %reshape.22.picks, s32[1]{0:T(128)} %bitcast.info, bf16[4,96,128]{2,1,0:T(8,128)(2,1)S(1)} %aggregate.11.mixed_ref, ...), custom_call_target="tpu_custom_call" | custom-call | flops 679477248 | bytes 6291456 | tf_op jit(solution)/shard_map/finish_aggregate/pallas_call | solution.py:290
  133.4 8.4 %all-gather.4 = bf16[32,96,128]{2,1,0:T(8,128)(2,1)S(1)} all-gather(bf16[8,96,128]{2,1,0:T(8,128)(2,1)S(1)} %get-tuple-element.90.mixed_ref), channel_id=6, replica_groups=mesh['section'=4,'dom'=8] {'section'}, dimensions={0}, use_global_device_ids=true | all-gather | bytes 983040 | tf_op jit(solution)/shard_map/all_gather | solution.py:461
  153.7 6.3 %all-gather.5 = bf16[16,96,128]{2,1,0:T(8,128)(2,1)S(1)} all-gather(bf16[4,96,128]{2,1,0:T(8,128)(2,1)S(1)} %aggregate.12.mixed_ref), channel_id=7, replica_groups=mesh['section'=4,'dom'=8] {'section'}, dimensions={0}, use_global_device_ids=true | all-gather | bytes 491520 | tf_op jit(solution)/shard_map/all_gather | solution.py:468
  161.7 6.4 %finish_aggregate.9 = (bf16[4,96,128]{2,1,0:T(8,128)(2,1)}, bf16[8,1,96,128]{3,2,1,0:T(8,128)(2,1)}, bf16[8,96,128]{2,1,0:T(8,128)(2,1)S(1)}) custom-call(s32[288]{0:T(512)S(1)} %reshape.24.columns, s32[24]{0:T(128)S(1)} %reshape.22.picks, s32[1]{0:T(128)} %bitcast.info, bf16[4,96,128]{2,1,0:T(8,128)(2,1)S(1)} %aggregate.12.mixed_ref, ...), custom_call_target="tpu_custom_call" | custom-call | flops 679477248 | bytes 6291456 | tf_op jit(solution)/shard_map/finish_aggregate/pallas_call | solution.py:290
  172.3 8.4 %all-gather.6 = bf16[32,96,128]{2,1,0:T(8,128)(2,1)S(1)} all-gather(bf16[8,96,128]{2,1,0:T(8,128)(2,1)S(1)} %get-tuple-element.94.mixed_ref), channel_id=8, replica_groups=mesh['section'=4,'dom'=8] {'section'}, dimensions={0}, use_global_device_ids=true | all-gather | bytes 983040 | tf_op jit(solution)/shard_map/all_gather | solution.py:461
  192.6 6.3 %all-gather.7 = bf16[16,96,128]{2,1,0:T(8,128)(2,1)S(1)} all-gather(bf16[4,96,128]{2,1,0:T(8,128)(2,1)S(1)} %aggregate.13.mixed_ref), channel_id=9, replica_groups=mesh['section'=4,'dom'=8] {'section'}, dimensions={0}, use_global_device_ids=true | all-gather | bytes 491520 | tf_op jit(solution)/shard_map/all_gather | solution.py:468
  200.6 6.4 %finish_aggregate.10 = (bf16[4,96,128]{2,1,0:T(8,128)(2,1)}, bf16[8,1,96,128]{3,2,1,0:T(8,128)(2,1)}, bf16[8,96,128]{2,1,0:T(8,128)(2,1)S(1)}) custom-call(s32[288]{0:T(512)S(1)} %reshape.24.columns, s32[24]{0:T(128)S(1)} %reshape.22.picks, s32[1]{0:T(128)} %bitcast.info, bf16[4,96,128]{2,1,0:T(8,128)(2,1)S(1)} %aggregate.13.mixed_ref, ...), custom_call_target="tpu_custom_call" | custom-call | flops 679477248 | bytes 6291456 | tf_op jit(solution)/shard_map/finish_aggregate/pallas_call | solution.py:290
  211.1 8.4 %all-gather.8 = bf16[32,96,128]{2,1,0:T(8,128)(2,1)S(1)} all-gather(bf16[8,96,128]{2,1,0:T(8,128)(2,1)S(1)} %get-tuple-element.102.mixed_ref), channel_id=10, replica_groups=mesh['section'=4,'dom'=8] {'section'}, dimensions={0}, use_global_device_ids=true | all-gather | bytes 983040 | tf_op jit(solution)/shard_map/all_gather | solution.py:461
  231.4 6.3 %all-gather.9 = bf16[16,96,128]{2,1,0:T(8,128)(2,1)S(1)} all-gather(bf16[4,96,128]{2,1,0:T(8,128)(2,1)S(1)} %aggregate.14.mixed_ref), channel_id=11, replica_groups=mesh['section'=4,'dom'=8] {'section'}, dimensions={0}, use_global_device_ids=true | all-gather | bytes 491520 | tf_op jit(solution)/shard_map/all_gather | solution.py:468
  239.4 6.4 %finish_aggregate.11 = (bf16[4,96,128]{2,1,0:T(8,128)(2,1)}, bf16[8,1,96,128]{3,2,1,0:T(8,128)(2,1)}, bf16[8,96,128]{2,1,0:T(8,128)(2,1)S(1)}) custom-call(s32[288]{0:T(512)S(1)} %reshape.24.columns, s32[24]{0:T(128)S(1)} %reshape.22.picks, s32[1]{0:T(128)} %bitcast.info, bf16[4,96,128]{2,1,0:T(8,128)(2,1)S(1)} %aggregate.14.mixed_ref, ...), custom_call_target="tpu_custom_call" | custom-call | flops 679477248 | bytes 6291456 | tf_op jit(solution)/shard_map/finish_aggregate/pallas_call | solution.py:290
  249.9 8.4 %all-gather.10 = bf16[32,96,128]{2,1,0:T(8,128)(2,1)S(1)} all-gather(bf16[8,96,128]{2,1,0:T(8,128)(2,1)S(1)} %get-tuple-element.106.mixed_ref), channel_id=12, replica_groups=mesh['section'=4,'dom'=8] {'section'}, dimensions={0}, use_global_device_ids=true | all-gather | bytes 983040 | tf_op jit(solution)/shard_map/all_gather | solution.py:461
  270.2 6.3 %all-gather.11 = bf16[16,96,128]{2,1,0:T(8,128)(2,1)S(1)} all-gather(bf16[4,96,128]{2,1,0:T(8,128)(2,1)S(1)} %aggregate.15.mixed_ref), channel_id=13, replica_groups=mesh['section'=4,'dom'=8] {'section'}, dimensions={0}, use_global_device_ids=true | all-gather | bytes 491520 | tf_op jit(solution)/shard_map/all_gather | solution.py:468
  278.2 6.4 %finish_aggregate.12 = (bf16[4,96,128]{2,1,0:T(8,128)(2,1)}, bf16[8,1,96,128]{3,2,1,0:T(8,128)(2,1)}, bf16[8,96,128]{2,1,0:T(8,128)(2,1)S(1)}) custom-call(s32[288]{0:T(512)S(1)} %reshape.24.columns, s32[24]{0:T(128)S(1)} %reshape.22.picks, s32[1]{0:T(128)} %bitcast.info, bf16[4,96,128]{2,1,0:T(8,128)(2,1)S(1)} %aggregate.15.mixed_ref, ...), custom_call_target="tpu_custom_call" | custom-call | flops 679477248 | bytes 6291456 | tf_op jit(solution)/shard_map/finish_aggregate/pallas_call | solution.py:290
  288.7 8.4 %all-gather.12 = bf16[32,96,128]{2,1,0:T(8,128)(2,1)S(1)} all-gather(bf16[8,96,128]{2,1,0:T(8,128)(2,1)S(1)} %get-tuple-element.114.mixed_ref), channel_id=14, replica_groups=mesh['section'=4,'dom'=8] {'section'}, dimensions={0}, use_global_device_ids=true | all-gather | bytes 983040 | tf_op jit(solution)/shard_map/all_gather | solution.py:461
  309.1 6.3 %all-gather.13 = bf16[16,96,128]{2,1,0:T(8,128)(2,1)S(1)} all-gather(bf16[4,96,128]{2,1,0:T(8,128)(2,1)S(1)} %aggregate.16.mixed_ref), channel_id=15, replica_groups=mesh['section'=4,'dom'=8] {'section'}, dimensions={0}, use_global_device_ids=true | all-gather | bytes 491520 | tf_op jit(solution)/shard_map/all_gather | solution.py:468
  317.1 6.4 %finish_aggregate.13 = (bf16[4,96,128]{2,1,0:T(8,128)(2,1)}, bf16[8,1,96,128]{3,2,1,0:T(8,128)(2,1)}, bf16[8,96,128]{2,1,0:T(8,128)(2,1)S(1)}) custom-call(s32[288]{0:T(512)S(1)} %reshape.24.columns, s32[24]{0:T(128)S(1)} %reshape.22.picks, s32[1]{0:T(128)} %bitcast.info, bf16[4,96,128]{2,1,0:T(8,128)(2,1)S(1)} %aggregate.16.mixed_ref, ...), custom_call_target="tpu_custom_call" | custom-call | flops 679477248 | bytes 6291456 | tf_op jit(solution)/shard_map/finish_aggregate/pallas_call | solution.py:290
  327.6 8.4 %all-gather.14 = bf16[32,96,128]{2,1,0:T(8,128)(2,1)S(1)} all-gather(bf16[8,96,128]{2,1,0:T(8,128)(2,1)S(1)} %get-tuple-element.118.mixed_ref), channel_id=16, replica_groups=mesh['section'=4,'dom'=8] {'section'}, dimensions={0}, use_global_device_ids=true | all-gather | bytes 983040 | tf_op jit(solution)/shard_map/all_gather | solution.py:461
  341.9 6.6 %all-gather.15 = bf16[16,96,128]{2,1,0:T(8,128)(2,1)S(1)} all-gather(bf16[4,96,128]{2,1,0:T(8,128)(2,1)S(1)} %aggregate.17.mixed_ref), channel_id=17, replica_groups=mesh['section'=4,'dom'=8] {'section'}, dimensions={0}, use_global_device_ids=true | all-gather | bytes 491520 | tf_op jit(solution)/shard_map/all_gather | solution.py:468
  (99 shorter events, 168.6 us)
Async XLA Ops:
  7.1 19.0 %all-to-all-start = ((bf16[8,2,96,128]{3,2,1,0:T(8,128)(2,1)}), bf16[8,2,96,128]{3,2,1,0:T(8,128)(2,1)S(1)}, u32[]{:S(2)}, u32[]{:S(2)}) async-start(bf16[8,2,96,128]{3,2,1,0:T(8,128)(2,1)} %get-tuple-element.66), calls=%async_computation | async-start | bytes 786432 | tf_op jit(solution)/shard_map/all_to_all | solution.py:432
  14.4 17.1 %collective-permute-start.1 = (bf16[16,96,128]{2,1,0:T(8,128)(2,1)}, bf16[16,96,128]{2,1,0:T(8,128)(2,1)S(1)}, u32[]{:S(2)}, u32[]{:S(2)}) collective-permute-start(bf16[16,96,128]{2,1,0:T(8,128)(2,1)} %get-tuple-element.69), channel_id=1, source_target_pairs={{0,16},{8,24},{16,0},{24,8},{1,17},{9,25},{17,1},{25,9},{2,18},{10... | collective-permute-start | bytes 1179656 | tf_op jit(solution)/shard_map/ppermute | solution.py:437
  15.9 18.2 %collective-permute-start.2 = (bf16[16,96,128]{2,1,0:T(8,128)(2,1)}, bf16[16,96,128]{2,1,0:T(8,128)(2,1)S(1)}, u32[]{:S(2)}, u32[]{:S(2)}) collective-permute-start(bf16[16,96,128]{2,1,0:T(8,128)(2,1)} %get-tuple-element.70), channel_id=1, source_target_pairs={{0,24},{8,0},{16,8},{24,16},{1,25},{9,1},{17,9},{25,17},{2,26},{10... | collective-permute-start | bytes 1179656 | tf_op jit(solution)/shard_map/ppermute | solution.py:437
  19.5 30.7 %collective-permute-start.3 = (bf16[2,96,384]{2,1,0:T(8,128)(2,1)}, bf16[2,96,384]{2,1,0:T(8,128)(2,1)S(1)}, u32[]{:S(2)}, u32[]{:S(2)}) collective-permute-start(bf16[2,96,384]{2,1,0:T(8,128)(2,1)} %get-tuple-element.73), channel_id=1, source_target_pairs={{0,8},{8,16},{16,24},{24,0},{1,9},{9,17},{17,25},{25,1},{2,10},{10... | collective-permute-start | bytes 442376 | tf_op jit(solution)/shard_map/ppermute | solution.py:437
  19.5 30.7 %collective-permute-start.4 = (bf16[2,96,384]{2,1,0:T(8,128)(2,1)}, bf16[2,96,384]{2,1,0:T(8,128)(2,1)S(1)}, u32[]{:S(2)}, u32[]{:S(2)}) collective-permute-start(bf16[2,96,384]{2,1,0:T(8,128)(2,1)} %get-tuple-element.74), channel_id=1, source_target_pairs={{0,16},{8,24},{16,0},{24,8},{1,17},{9,25},{17,1},{25,9},{2,18},{10... | collective-permute-start | bytes 442376 | tf_op jit(solution)/shard_map/ppermute | solution.py:437
  25.4 24.8 %collective-permute-start.5 = (bf16[2,96,384]{2,1,0:T(8,128)(2,1)S(1)}, bf16[2,96,384]{2,1,0:T(8,128)(2,1)S(1)}, u32[]{:S(2)}, u32[]{:S(2)}) collective-permute-start(bf16[2,96,384]{2,1,0:T(8,128)(2,1)S(1)} %copy-done.9), channel_id=1, source_target_pairs={{0,24},{8,0},{16,8},{24,16},{1,25},{9,1},{17,9},{25,17},{2,26},{10... | collective-permute-start | bytes 442376 | tf_op jit(solution)/shard_map/ppermute | solution.py:437
  26.1 26.1 %all-to-all-start.1 = ((bf16[8,1,96,128]{3,2,1,0:T(8,128)(2,1)}), bf16[8,1,96,128]{3,2,1,0:T(8,128)(2,1)S(1)}, u32[]{:S(2)}, u32[]{:S(2)}) async-start(bf16[8,1,96,128]{3,2,1,0:T(8,128)(2,1)} %get-tuple-element.67), calls=%async_computation.1 | async-start | bytes 393216 | tf_op jit(solution)/shard_map/all_to_all | solution.py:432
  52.2 29.0 %all-to-all-start.2 = ((bf16[8,2,96,128]{3,2,1,0:T(8,128)(2,1)}), bf16[8,2,96,128]{3,2,1,0:T(8,128)(2,1)S(1)}, u32[]{:S(2)}, u32[]{:S(2)}) async-start(bf16[8,2,96,128]{3,2,1,0:T(8,128)(2,1)} %get-tuple-element.78), calls=%async_computation.2 | async-start | bytes 786432 | tf_op jit(solution)/shard_map/all_to_all | solution.py:432
  58.2 23.0 %collective-permute-start.6 = (bf16[16,96,128]{2,1,0:T(8,128)(2,1)}, bf16[16,96,128]{2,1,0:T(8,128)(2,1)S(1)}, u32[]{:S(2)}, u32[]{:S(2)}) collective-permute-start(bf16[16,96,128]{2,1,0:T(8,128)(2,1)} %get-tuple-element.79), channel_id=1, source_target_pairs={{0,8},{8,16},{16,24},{24,0},{1,9},{9,17},{17,25},{25,1},{2,10},{10... | collective-permute-start | bytes 1179656 | tf_op jit(solution)/shard_map/ppermute | solution.py:437
  58.2 22.9 %collective-permute-start.7 = (bf16[16,96,128]{2,1,0:T(8,128)(2,1)}, bf16[16,96,128]{2,1,0:T(8,128)(2,1)S(1)}, u32[]{:S(2)}, u32[]{:S(2)}) collective-permute-start(bf16[16,96,128]{2,1,0:T(8,128)(2,1)} %get-tuple-element.80), channel_id=1, source_target_pairs={{0,16},{8,24},{16,0},{24,8},{1,17},{9,25},{17,1},{25,9},{2,18},{10... | collective-permute-start | bytes 1179656 | tf_op jit(solution)/shard_map/ppermute | solution.py:437
  58.8 22.3 %collective-permute-start.8 = (bf16[16,96,128]{2,1,0:T(8,128)(2,1)S(1)}, bf16[16,96,128]{2,1,0:T(8,128)(2,1)S(1)}, u32[]{:S(2)}, u32[]{:S(2)}) collective-permute-start(bf16[16,96,128]{2,1,0:T(8,128)(2,1)S(1)} %copy-done.8), channel_id=1, source_target_pairs={{0,24},{8,0},{16,8},{24,16},{1,25},{9,1},{17,9},{25,17},{2,26},{10... | collective-permute-start | bytes 1179656 | tf_op jit(solution)/shard_map/ppermute | solution.py:437
  88.6 16.4 %all-to-all-start.4 = ((bf16[8,1,96,128]{3,2,1,0:T(8,128)(2,1)}), bf16[8,1,96,128]{3,2,1,0:T(8,128)(2,1)S(1)}, u32[]{:S(2)}, u32[]{:S(2)}) async-start(bf16[8,1,96,128]{3,2,1,0:T(8,128)(2,1)} %get-tuple-element.86), calls=%async_computation.4 | async-start | bytes 393216 | tf_op jit(solution)/shard_map/all_to_all | solution.py:432
  105.0 17.9 %all-to-all-start.3 = ((bf16[8,2,96,128]{3,2,1,0:T(8,128)(2,1)}), bf16[8,2,96,128]{3,2,1,0:T(8,128)(2,1)S(1)}, u32[]{:S(2)}, u32[]{:S(2)}) async-start(bf16[8,2,96,128]{3,2,1,0:T(8,128)(2,1)} %get-tuple-element.84), calls=%async_computation.3 | async-start | bytes 786432 | tf_op jit(solution)/shard_map/all_to_all | solution.py:432
  129.3 14.5 %all-to-all-start.5 = ((bf16[8,1,96,128]{3,2,1,0:T(8,128)(2,1)}), bf16[8,1,96,128]{3,2,1,0:T(8,128)(2,1)S(1)}, u32[]{:S(2)}, u32[]{:S(2)}) async-start(bf16[8,1,96,128]{3,2,1,0:T(8,128)(2,1)} %get-tuple-element.89), calls=%async_computation.5 | async-start | bytes 393216 | tf_op jit(solution)/shard_map/all_to_all | solution.py:432
  143.8 17.9 %all-to-all-start.6 = ((bf16[8,2,96,128]{3,2,1,0:T(8,128)(2,1)}), bf16[8,2,96,128]{3,2,1,0:T(8,128)(2,1)S(1)}, u32[]{:S(2)}, u32[]{:S(2)}) async-start(bf16[8,2,96,128]{3,2,1,0:T(8,128)(2,1)} %get-tuple-element.93), calls=%async_computation.6 | async-start | bytes 786432 | tf_op jit(solution)/shard_map/all_to_all | solution.py:432
  168.1 14.5 %all-to-all-start.8 = ((bf16[8,1,96,128]{3,2,1,0:T(8,128)(2,1)}), bf16[8,1,96,128]{3,2,1,0:T(8,128)(2,1)S(1)}, u32[]{:S(2)}, u32[]{:S(2)}) async-start(bf16[8,1,96,128]{3,2,1,0:T(8,128)(2,1)} %get-tuple-element.98), calls=%async_computation.8 | async-start | bytes 393216 | tf_op jit(solution)/shard_map/all_to_all | solution.py:432
  182.6 17.9 %all-to-all-start.7 = ((bf16[8,2,96,128]{3,2,1,0:T(8,128)(2,1)}), bf16[8,2,96,128]{3,2,1,0:T(8,128)(2,1)S(1)}, u32[]{:S(2)}, u32[]{:S(2)}) async-start(bf16[8,2,96,128]{3,2,1,0:T(8,128)(2,1)} %get-tuple-element.96), calls=%async_computation.7 | async-start | bytes 786432 | tf_op jit(solution)/shard_map/all_to_all | solution.py:432
  206.9 14.5 %all-to-all-start.9 = ((bf16[8,1,96,128]{3,2,1,0:T(8,128)(2,1)}), bf16[8,1,96,128]{3,2,1,0:T(8,128)(2,1)S(1)}, u32[]{:S(2)}, u32[]{:S(2)}) async-start(bf16[8,1,96,128]{3,2,1,0:T(8,128)(2,1)} %get-tuple-element.101), calls=%async_computation.9 | async-start | bytes 393216 | tf_op jit(solution)/shard_map/all_to_all | solution.py:432
  221.5 17.9 %all-to-all-start.10 = ((bf16[8,2,96,128]{3,2,1,0:T(8,128)(2,1)}), bf16[8,2,96,128]{3,2,1,0:T(8,128)(2,1)S(1)}, u32[]{:S(2)}, u32[]{:S(2)}) async-start(bf16[8,2,96,128]{3,2,1,0:T(8,128)(2,1)} %get-tuple-element.105), calls=%async_computation.10 | async-start | bytes 786432 | tf_op jit(solution)/shard_map/all_to_all | solution.py:432
  245.8 14.5 %all-to-all-start.12 = ((bf16[8,1,96,128]{3,2,1,0:T(8,128)(2,1)}), bf16[8,1,96,128]{3,2,1,0:T(8,128)(2,1)S(1)}, u32[]{:S(2)}, u32[]{:S(2)}) async-start(bf16[8,1,96,128]{3,2,1,0:T(8,128)(2,1)} %get-tuple-element.110), calls=%async_computation.12 | async-start | bytes 393216 | tf_op jit(solution)/shard_map/all_to_all | solution.py:432
  260.3 17.9 %all-to-all-start.11 = ((bf16[8,2,96,128]{3,2,1,0:T(8,128)(2,1)}), bf16[8,2,96,128]{3,2,1,0:T(8,128)(2,1)S(1)}, u32[]{:S(2)}, u32[]{:S(2)}) async-start(bf16[8,2,96,128]{3,2,1,0:T(8,128)(2,1)} %get-tuple-element.108), calls=%async_computation.11 | async-start | bytes 786432 | tf_op jit(solution)/shard_map/all_to_all | solution.py:432
  284.6 14.6 %all-to-all-start.13 = ((bf16[8,1,96,128]{3,2,1,0:T(8,128)(2,1)}), bf16[8,1,96,128]{3,2,1,0:T(8,128)(2,1)S(1)}, u32[]{:S(2)}, u32[]{:S(2)}) async-start(bf16[8,1,96,128]{3,2,1,0:T(8,128)(2,1)} %get-tuple-element.113), calls=%async_computation.13 | async-start | bytes 393216 | tf_op jit(solution)/shard_map/all_to_all | solution.py:432
  299.2 17.9 %all-to-all-start.14 = ((bf16[8,2,96,128]{3,2,1,0:T(8,128)(2,1)}), bf16[8,2,96,128]{3,2,1,0:T(8,128)(2,1)S(1)}, u32[]{:S(2)}, u32[]{:S(2)}) async-start(bf16[8,2,96,128]{3,2,1,0:T(8,128)(2,1)} %get-tuple-element.117), calls=%async_computation.14 | async-start | bytes 786432 | tf_op jit(solution)/shard_map/all_to_all | solution.py:432
  323.5 14.3 %all-to-all-start.15 = ((bf16[8,1,96,128]{3,2,1,0:T(8,128)(2,1)}), bf16[8,1,96,128]{3,2,1,0:T(8,128)(2,1)S(1)}, u32[]{:S(2)}, u32[]{:S(2)}) async-start(bf16[8,1,96,128]{3,2,1,0:T(8,128)(2,1)} %get-tuple-element.120), calls=%async_computation.15 | async-start | bytes 393216 | tf_op jit(solution)/shard_map/all_to_all | solution.py:432
  (11 other events, 84.5 us)

commit v12 on v11

--- a/solution.py
+++ b/solution.py
@@ -200,22 +200,20 @@
     work.run()
 
 
-def both_kernel(finish_plan, aggregate_plan, columns, picks, info, mixed_ref, gathered_ref, *refs):
+def both_kernel(plan, aggregate_plan, columns, picks, info, mixed_ref, gathered_ref, *refs):
     parts = gathered_ref.shape[0]
     count = len(aggregate_plan[3])
     weight_refs, refs = refs[:parts], refs[parts:]
     initial_ref, tiles_ref = refs[:2]
     source_refs, refs = refs[2 : 2 + count], refs[2 + count :]
     own_ref, outgoing_ref, next_ref = refs[:3]
-    weight, weight_sem = refs[3:5]
+    scratch = refs[3:7]
     work = Aggregate(
-        aggregate_plan, columns, info, initial_ref, tiles_ref, source_refs, next_ref, refs[5:]
+        aggregate_plan, columns, info, initial_ref, tiles_ref, source_refs, next_ref, refs[7:]
     )
+    copies = finish_begin(plan, info, mixed_ref, gathered_ref, weight_refs, scratch)
     work.begin()
-    finish_body(
-        finish_plan, picks, info, mixed_ref, gathered_ref, weight_refs, [own_ref, outgoing_ref],
-        weight, weight_sem,
-    )
+    finish_run(plan, copies, picks, [own_ref, outgoing_ref], scratch)
     work.run()
 
 
@@ -284,21 +282,16 @@
     aggregate_plan, operands, specs, scratch = parts
     rows, part_width, block = mixed.shape
     width = weights[0].shape[2]
-    beta_layer = math.log(lambda_decay / (layer + 1) + 1.0)
-    plan = (beta_layer, stream, group_blocks, part_count, layer % depth, layer // depth, False)
+    plan = finish_plan(layer, depth, stream, group_blocks, part_count, False)
     outgoing = (part_count, len(stream), part_width, block)
     return pl.pallas_call(
         functools.partial(both_kernel, plan, aggregate_plan),
         grid_spec=pltpu.PrefetchScalarGridSpec(
             num_scalar_prefetch=3,
             grid=(1,),
-            in_specs=[whole(mixed.shape), whole(gathered.shape)] + [anywhere] * len(weights) + specs,
+            in_specs=[anywhere] * (2 + len(weights)) + specs,
             out_specs=[whole(mixed.shape), whole(outgoing), whole(shape)],
-            scratch_shapes=[
-                pltpu.VMEM((part_width, width), jnp.bfloat16),
-                pltpu.SemaphoreType.DMA((len(weights),)),
-            ]
-            + scratch,
+            scratch_shapes=finish_scratch(mixed, gathered, weights) + scratch,
         ),
         out_shape=[
             in_hbm(mixed.shape),
@@ -311,28 +304,28 @@
     )(columns, picks, section, mixed, gathered, *weights, *operands)
 
 
-def finish_kernel(plan, picks, info, mixed_ref, gathered_ref, *refs):
-    parts = gathered_ref.shape[0]
-    out_refs = refs[parts:-2]
-    finish_body(
-        plan, picks, info, mixed_ref, gathered_ref, refs[:parts], out_refs, refs[-2], refs[-1]
-    )
-    if len(out_refs) > 2:
-        out_refs[2][...] = jnp.zeros_like(out_refs[2])
-
-
-def finish_body(plan, picks, info, mixed_ref, gathered_ref, weight_refs, refs, weight, weight_sem):
-    beta_layer, stream, group_blocks, part_count, sub, home, last = plan
-    rows, part_width, block = mixed_ref.shape
-    parts = gathered_ref.shape[0]
+def finish_begin(plan, info, mixed_ref, gathered_ref, weight_refs, scratch):
+    parts = len(weight_refs)
+    sub, home = plan[4:6]
+    mixed, gathered, weight, sem = scratch
     copies = [
         (
             lax.rem(info[0] - home + 2 * parts, parts) == distance,
-            pltpu.make_async_copy(weight_ref.at[sub], weight, weight_sem.at[distance]),
+            pltpu.make_async_copy(weight_ref.at[sub], weight, sem.at[distance]),
         )
         for distance, weight_ref in enumerate(weight_refs)
     ]
+    copies.append((None, pltpu.make_async_copy(gathered_ref, gathered, sem.at[parts])))
+    copies.append((None, pltpu.make_async_copy(mixed_ref, mixed, sem.at[parts + 1])))
     start_all(copies)
+    return copies
+
+
+def finish_run(plan, copies, picks, refs, scratch):
+    beta_layer, stream, group_blocks, part_count, sub, home, last = plan
+    mixed_ref, gathered_ref, weight, sem = scratch
+    rows, part_width, block = mixed_ref.shape
+    parts = gathered_ref.shape[0]
     wait_all(copies)
     for row in range(0, rows, 2):
         span = range(row, min(row + 2, rows))
@@ -346,45 +339,86 @@
             ]
             value = jnp.maximum(value, 0.0).astype(jnp.bfloat16)
             if last:
-                refs[0][r * block : (r + 1) * block, :] = value.T
+                low = (stream[0] * group_blocks + r) * block
+                refs[0][low : low + block, :] = value.T
             else:
                 refs[0][r] = value
     if not last:
         pick_outgoing(picks, refs[0], refs[1], stream, group_blocks, part_count)
 
 
-def finish(picks, section, mixed, gathered, weights, layer, depth, stream, group_blocks, part_count, last):
+def finish_kernel(plan, picks, info, mixed_ref, gathered_ref, *refs):
+    parts = gathered_ref.shape[0]
+    weight_refs, out_refs, scratch = refs[:parts], refs[parts:-4], refs[-4:]
+    copies = finish_begin(plan, info, mixed_ref, gathered_ref, weight_refs, scratch)
+    finish_run(plan, copies, picks, out_refs, scratch)
+    out_refs[2][...] = jnp.zeros_like(out_refs[2])
+
+
+def last_kernel(plans, picks, info, *refs):
+    parts = refs[1].shape[0]
+    weight_refs, out_ref = refs[4 : 4 + parts], refs[4 + parts]
+    scratches = [refs[5 + parts : 9 + parts], refs[9 + parts :]]
+    begun = [
+        finish_begin(plan, info, refs[2 * i], refs[2 * i + 1], weight_refs, scratches[i])
+        for i, plan in enumerate(plans)
+    ]
+    for plan, copies, scratch in zip(plans, begun, scratches):
+        finish_run(plan, copies, picks, [out_ref], scratch)
+
+
+def finish_plan(layer, depth, stream, group_blocks, part_count, last):
+    beta_layer = math.log(lambda_decay / (layer + 1) + 1.0)
+    return (beta_layer, stream, group_blocks, part_count, layer % depth, layer // depth, last)
+
+
+def finish_scratch(mixed, gathered, weights):
+    return [
+        pltpu.VMEM(mixed.shape, jnp.bfloat16),
+        pltpu.VMEM(gathered.shape, jnp.bfloat16),
+        pltpu.VMEM(weights[0].shape[1:], jnp.bfloat16),
+        pltpu.SemaphoreType.DMA((len(weights) + 2,)),
+    ]
+
+
+def finish_last(picks, section, pairs, weights, layer, depth, streams, group_blocks, part_count):
+    plans = [finish_plan(layer, depth, s, group_blocks, part_count, True) for s in streams]
+    rows = sum(mixed.shape[0] * mixed.shape[2] for mixed, gathered in pairs)
+    shape = (rows, pairs[0][0].shape[1])
+    return pl.pallas_call(
+        functools.partial(last_kernel, plans),
+        grid_spec=pltpu.PrefetchScalarGridSpec(
+            num_scalar_prefetch=2,
+            grid=(1,),
+            in_specs=[anywhere] * (2 * len(pairs) + len(weights)),
+            out_specs=whole(shape),
+            scratch_shapes=sum([finish_scratch(*pair, weights) for pair in pairs], []),
+        ),
+        out_shape=jax.ShapeDtypeStruct(shape, jnp.bfloat16),
+        compiler_params=params(),
+        name="finish_last",
+    )(picks, section, *[value for pair in pairs for value in pair], *weights)
+
+
+def finish(picks, section, mixed, gathered, weights, layer, depth, stream, group_blocks, part_count):
     rows, part_width, block = mixed.shape
     width = weights[0].shape[2]
-    beta_layer = math.log(lambda_decay / (layer + 1) + 1.0)
-    plan = (
-        beta_layer, stream, group_blocks, part_count, layer % depth, layer // depth, last,
-    )
-    if last:
-        shapes = [(rows * block, part_width)]
-        out_shape = [jax.ShapeDtypeStruct(shapes[0], jnp.bfloat16)]
-    else:
-        outgoing = (part_count, len(stream), part_width, block)
-        shapes = [(rows, part_width, block), outgoing, (16, 128)]
-        out_shape = [
-            in_hbm(shapes[0]),
-            jax.ShapeDtypeStruct(outgoing, jnp.bfloat16),
-            in_hbm((16, 128)),
-        ]
+    plan = finish_plan(layer, depth, stream, group_blocks, part_count, False)
+    outgoing = (part_count, len(stream), part_width, block)
     return pl.pallas_call(
         functools.partial(finish_kernel, plan),
         grid_spec=pltpu.PrefetchScalarGridSpec(
             num_scalar_prefetch=2,
             grid=(1,),
-            in_specs=[whole(mixed.shape), whole(gathered.shape)]
-            + [anywhere] * len(weights),
-            out_specs=[whole(s) for s in shapes],
-            scratch_shapes=[
-                pltpu.VMEM((part_width, width), jnp.bfloat16),
-                pltpu.SemaphoreType.DMA((len(weights),)),
-            ],
-        ),
-        out_shape=out_shape,
+            in_specs=[anywhere] * (2 + len(weights)),
+            out_specs=[whole(s) for s in [mixed.shape, outgoing, (16, 128)]],
+            scratch_shapes=finish_scratch(mixed, gathered, weights),
+        ),
+        out_shape=[
+            in_hbm(mixed.shape),
+            jax.ShapeDtypeStruct(outgoing, jnp.bfloat16),
+            in_hbm((16, 128)),
+        ],
         cost_estimate=pl.CostEstimate(
             flops=2 * rows * block * width * part_width,
             bytes_accessed=rows * block * width * 2,
@@ -458,20 +492,21 @@
     mixed_front = aggregate(columns, section, parts_of(0, 0), shapes[0], turned_late)
     for layer in range(layers):
         last = layer == layers - 1
-        gathered = lax.all_gather(mixed_front, "section", axis=0, tiled=False)
-        front_result = finish(
-            picks, section, mixed_front, gathered, weights, layer, depth, front, group_blocks,
-            part_count, last,
-        )
-        after = [mixed_front[0]] if last else [front_result[2]]
+        gathered_front = lax.all_gather(mixed_front, "section", axis=0, tiled=False)
+        after = []
+        if not last:
+            front_result = finish(
+                picks, section, mixed_front, gathered_front, weights, layer, depth, front,
+                group_blocks, part_count,
+            )
+            after = [front_result[2]]
         mixed_back = aggregate(columns, section, parts_of(1, layer), shapes[1], after)
         gathered = lax.all_gather(mixed_back, "section", axis=0, tiled=False)
         if last:
-            back_result = finish(
-                picks, section, mixed_back, gathered, weights, layer, depth, back, group_blocks,
-                part_count, last,
+            pairs = [(mixed_front, gathered_front), (mixed_back, gathered)]
+            return finish_last(
+                picks, section, pairs, weights, layer, depth, streams, group_blocks, part_count
             )
-            return jnp.concatenate([front_result[0], back_result[0]], 0)
         own[0], imports[0] = front_result[0], exchange(front_result[1])
         own[1], outgoing, mixed_front = finish_and_aggregate(
             columns, picks, section, mixed_back, gathered, weights, layer, depth, back,

time: 353 us -> 359 us (1.017)
  Pallas kernels: 111 us -> 117 us
    pallas_call x7, Pallas kernels: 44.6 us -> 48.2 us  [finish_and_aggregate(): pl.pallas_call(functools.partial(both_kernel, plan, aggregate_plan), grid...]
    pallas_call x9 -> x7, Pallas kernels: 15.7 us -> 15.9 us  [finish(): pl.pallas_call(functools.partial(finish_kernel, plan), grid_spec=pltpu.Pr...]
where the time goes in v12:
time: 359 us; the launch traced here: 356 us
  blocking collectives  130 us (36%)
  Pallas kernels  117 us (33%)
  starting transfers between devices  89.8 us (25%)
  waiting for transfers between devices  15.7 us (4%)
    all_to_all x16, starting transfers between devices, exchange(): return lax.all_to_all(value, 'dom', split_axis=0, concat_axis=0, tiled=True)  84.2 us
    all_gather x8, blocking collectives, per_device(): gathered_front = lax.all_gather(mixed_front, 'section', axis=0, tiled=False)  68.4 us
    all_gather x8, blocking collectives, per_device(): gathered = lax.all_gather(mixed_back, 'section', axis=0, tiled=False)  61.3 us
    pallas_call x7, Pallas kernels, finish_and_aggregate(): pl.pallas_call(functools.partial(both_kernel, plan, aggregate_plan), grid...  48.2 us
    pallas_call x9, Pallas kernels, aggregate(): pl.pallas_call(functools.partial(aggregate_kernel, plan), grid_spec=pltpu...  39.1 us
    pallas_call x7, Pallas kernels, finish(): pl.pallas_call(functools.partial(finish_kernel, plan), grid_spec=pltpu.Pr...  15.9 us
    all_to_all x16, waiting for transfers between devices, exchange(): return lax.all_to_all(value, 'dom', split_axis=0, concat_axis=0, tiled=True)  10.8 us
    pallas_call x3, Pallas kernels, turn_blocks(): pl.pallas_call(turn_kernel, grid_spec=pltpu.PrefetchScalarGridSpec(num_sc...  8.01 us
  transfers between devices with their start and end apart: 25, of which 9 were waited for; matrix products, arithmetic and copies ran while one was open for 0% of the time, Pallas kernels for 16%

profile of v12, /device:TPU:0, one launch (start us, length us, event | category | flops | bytes accessed | tf_op | source)
XLA Modules:
  0.0 356.0 jit_solution(741512581351861125)
XLA Ops:
  7.1 7.3 %all-to-all-start = ((bf16[8,2,96,128]{3,2,1,0:T(8,128)(2,1)}), bf16[8,2,96,128]{3,2,1,0:T(8,128)(2,1)S(1)}, u32[]{:S(2)}, u32[]{:S(2)}) async-start(bf16[8,2,96,128]{3,2,1,0:T(8,128)(2,1)} %get-tuple-element.66), calls=%async_computation | async-start | bytes 786432 | tf_op jit(solution)/shard_map/all_to_all | solution.py:466
  40.7 9.5 %all-gather = bf16[32,96,128]{2,1,0:T(8,128)(2,1)S(1)} all-gather(bf16[8,96,128]{2,1,0:T(8,128)(2,1)S(1)} %aggregate.9.mixed_ref), channel_id=2, replica_groups=mesh['section'=4,'dom'=8] {'section'}, dimensions={0}, use_global_device_ids=true | all-gather | bytes 983040 | tf_op jit(solution)/shard_map/all_gather | solution.py:495
  64.7 16.8 %all-gather.1 = bf16[16,96,128]{2,1,0:T(8,128)(2,1)S(1)} all-gather(bf16[4,96,128]{2,1,0:T(8,128)(2,1)S(1)} %aggregate.10.mixed_ref), channel_id=3, replica_groups=mesh['section'=4,'dom'=8] {'section'}, dimensions={0}, use_global_device_ids=true | all-gather | bytes 491520 | tf_op jit(solution)/shard_map/all_gather | solution.py:504
  82.5 6.9 %finish_aggregate.7 = (bf16[4,96,128]{2,1,0:T(8,128)(2,1)}, bf16[8,1,96,128]{3,2,1,0:T(8,128)(2,1)}, bf16[8,96,128]{2,1,0:T(8,128)(2,1)S(1)}) custom-call(s32[288]{0:T(512)S(1)} %reshape.24.columns, s32[24]{0:T(128)S(1)} %reshape.22.picks, s32[1]{0:T(128)} %bitcast.info, bf16[4,96,128]{2,1,0:T(8,128)(2,1)S(1)} %aggregate.10.mixed_ref, ...), custom_call_target="tpu_custom_call" | custom-call | flops 679477248 | bytes 6291456 | tf_op jit(solution)/shard_map/finish_aggregate/pallas_call | solution.py:287
  95.4 8.4 %all-gather.2 = bf16[32,96,128]{2,1,0:T(8,128)(2,1)S(1)} all-gather(bf16[8,96,128]{2,1,0:T(8,128)(2,1)S(1)} %get-tuple-element.82.mixed_ref), channel_id=4, replica_groups=mesh['section'=4,'dom'=8] {'section'}, dimensions={0}, use_global_device_ids=true | all-gather | bytes 983040 | tf_op jit(solution)/shard_map/all_gather | solution.py:495
  116.0 6.3 %all-gather.3 = bf16[16,96,128]{2,1,0:T(8,128)(2,1)S(1)} all-gather(bf16[4,96,128]{2,1,0:T(8,128)(2,1)S(1)} %aggregate.11.mixed_ref), channel_id=5, replica_groups=mesh['section'=4,'dom'=8] {'section'}, dimensions={0}, use_global_device_ids=true | all-gather | bytes 491520 | tf_op jit(solution)/shard_map/all_gather | solution.py:504
  124.1 6.9 %finish_aggregate.8 = (bf16[4,96,128]{2,1,0:T(8,128)(2,1)}, bf16[8,1,96,128]{3,2,1,0:T(8,128)(2,1)}, bf16[8,96,128]{2,1,0:T(8,128)(2,1)S(1)}) custom-call(s32[288]{0:T(512)S(1)} %reshape.24.columns, s32[24]{0:T(128)S(1)} %reshape.22.picks, s32[1]{0:T(128)} %bitcast.info, bf16[4,96,128]{2,1,0:T(8,128)(2,1)S(1)} %aggregate.11.mixed_ref, ...), custom_call_target="tpu_custom_call" | custom-call | flops 679477248 | bytes 6291456 | tf_op jit(solution)/shard_map/finish_aggregate/pallas_call | solution.py:287
  135.1 8.4 %all-gather.4 = bf16[32,96,128]{2,1,0:T(8,128)(2,1)S(1)} all-gather(bf16[8,96,128]{2,1,0:T(8,128)(2,1)S(1)} %get-tuple-element.90.mixed_ref), channel_id=6, replica_groups=mesh['section'=4,'dom'=8] {'section'}, dimensions={0}, use_global_device_ids=true | all-gather | bytes 983040 | tf_op jit(solution)/shard_map/all_gather | solution.py:495
  155.7 6.3 %all-gather.5 = bf16[16,96,128]{2,1,0:T(8,128)(2,1)S(1)} all-gather(bf16[4,96,128]{2,1,0:T(8,128)(2,1)S(1)} %aggregate.12.mixed_ref), channel_id=7, replica_groups=mesh['section'=4,'dom'=8] {'section'}, dimensions={0}, use_global_device_ids=true | all-gather | bytes 491520 | tf_op jit(solution)/shard_map/all_gather | solution.py:504
  163.7 6.9 %finish_aggregate.9 = (bf16[4,96,128]{2,1,0:T(8,128)(2,1)}, bf16[8,1,96,128]{3,2,1,0:T(8,128)(2,1)}, bf16[8,96,128]{2,1,0:T(8,128)(2,1)S(1)}) custom-call(s32[288]{0:T(512)S(1)} %reshape.24.columns, s32[24]{0:T(128)S(1)} %reshape.22.picks, s32[1]{0:T(128)} %bitcast.info, bf16[4,96,128]{2,1,0:T(8,128)(2,1)S(1)} %aggregate.12.mixed_ref, ...), custom_call_target="tpu_custom_call" | custom-call | flops 679477248 | bytes 6291456 | tf_op jit(solution)/shard_map/finish_aggregate/pallas_call | solution.py:287
  174.8 8.4 %all-gather.6 = bf16[32,96,128]{2,1,0:T(8,128)(2,1)S(1)} all-gather(bf16[8,96,128]{2,1,0:T(8,128)(2,1)S(1)} %get-tuple-element.94.mixed_ref), channel_id=8, replica_groups=mesh['section'=4,'dom'=8] {'section'}, dimensions={0}, use_global_device_ids=true | all-gather | bytes 983040 | tf_op jit(solution)/shard_map/all_gather | solution.py:495
  195.4 6.3 %all-gather.7 = bf16[16,96,128]{2,1,0:T(8,128)(2,1)S(1)} all-gather(bf16[4,96,128]{2,1,0:T(8,128)(2,1)S(1)} %aggregate.13.mixed_ref), channel_id=9, replica_groups=mesh['section'=4,'dom'=8] {'section'}, dimensions={0}, use_global_device_ids=true | all-gather | bytes 491520 | tf_op jit(solution)/shard_map/all_gather | solution.py:504
  203.4 6.9 %finish_aggregate.10 = (bf16[4,96,128]{2,1,0:T(8,128)(2,1)}, bf16[8,1,96,128]{3,2,1,0:T(8,128)(2,1)}, bf16[8,96,128]{2,1,0:T(8,128)(2,1)S(1)}) custom-call(s32[288]{0:T(512)S(1)} %reshape.24.columns, s32[24]{0:T(128)S(1)} %reshape.22.picks, s32[1]{0:T(128)} %bitcast.info, bf16[4,96,128]{2,1,0:T(8,128)(2,1)S(1)} %aggregate.13.mixed_ref, ...), custom_call_target="tpu_custom_call" | custom-call | flops 679477248 | bytes 6291456 | tf_op jit(solution)/shard_map/finish_aggregate/pallas_call | solution.py:287
  214.5 8.4 %all-gather.8 = bf16[32,96,128]{2,1,0:T(8,128)(2,1)S(1)} all-gather(bf16[8,96,128]{2,1,0:T(8,128)(2,1)S(1)} %get-tuple-element.102.mixed_ref), channel_id=10, replica_groups=mesh['section'=4,'dom'=8] {'section'}, dimensions={0}, use_global_device_ids=true | all-gather | bytes 983040 | tf_op jit(solution)/shard_map/all_gather | solution.py:495
  235.1 6.5 %all-gather.9 = bf16[16,96,128]{2,1,0:T(8,128)(2,1)S(1)} all-gather(bf16[4,96,128]{2,1,0:T(8,128)(2,1)S(1)} %aggregate.14.mixed_ref), channel_id=11, replica_groups=mesh['section'=4,'dom'=8] {'section'}, dimensions={0}, use_global_device_ids=true | all-gather | bytes 491520 | tf_op jit(solution)/shard_map/all_gather | solution.py:504
  243.1 6.9 %finish_aggregate.11 = (bf16[4,96,128]{2,1,0:T(8,128)(2,1)}, bf16[8,1,96,128]{3,2,1,0:T(8,128)(2,1)}, bf16[8,96,128]{2,1,0:T(8,128)(2,1)S(1)}) custom-call(s32[288]{0:T(512)S(1)} %reshape.24.columns, s32[24]{0:T(128)S(1)} %reshape.22.picks, s32[1]{0:T(128)} %bitcast.info, bf16[4,96,128]{2,1,0:T(8,128)(2,1)S(1)} %aggregate.14.mixed_ref, ...), custom_call_target="tpu_custom_call" | custom-call | flops 679477248 | bytes 6291456 | tf_op jit(solution)/shard_map/finish_aggregate/pallas_call | solution.py:287
  254.3 8.4 %all-gather.10 = bf16[32,96,128]{2,1,0:T(8,128)(2,1)S(1)} all-gather(bf16[8,96,128]{2,1,0:T(8,128)(2,1)S(1)} %get-tuple-element.106.mixed_ref), channel_id=12, replica_groups=mesh['section'=4,'dom'=8] {'section'}, dimensions={0}, use_global_device_ids=true | all-gather | bytes 983040 | tf_op jit(solution)/shard_map/all_gather | solution.py:495
  275.0 6.3 %all-gather.11 = bf16[16,96,128]{2,1,0:T(8,128)(2,1)S(1)} all-gather(bf16[4,96,128]{2,1,0:T(8,128)(2,1)S(1)} %aggregate.15.mixed_ref), channel_id=13, replica_groups=mesh['section'=4,'dom'=8] {'section'}, dimensions={0}, use_global_device_ids=true | all-gather | bytes 491520 | tf_op jit(solution)/shard_map/all_gather | solution.py:504
  283.0 6.9 %finish_aggregate.12 = (bf16[4,96,128]{2,1,0:T(8,128)(2,1)}, bf16[8,1,96,128]{3,2,1,0:T(8,128)(2,1)}, bf16[8,96,128]{2,1,0:T(8,128)(2,1)S(1)}) custom-call(s32[288]{0:T(512)S(1)} %reshape.24.columns, s32[24]{0:T(128)S(1)} %reshape.22.picks, s32[1]{0:T(128)} %bitcast.info, bf16[4,96,128]{2,1,0:T(8,128)(2,1)S(1)} %aggregate.15.mixed_ref, ...), custom_call_target="tpu_custom_call" | custom-call | flops 679477248 | bytes 6291456 | tf_op jit(solution)/shard_map/finish_aggregate/pallas_call | solution.py:287
  294.0 8.4 %all-gather.12 = bf16[32,96,128]{2,1,0:T(8,128)(2,1)S(1)} all-gather(bf16[8,96,128]{2,1,0:T(8,128)(2,1)S(1)} %get-tuple-element.114.mixed_ref), channel_id=14, replica_groups=mesh['section'=4,'dom'=8] {'section'}, dimensions={0}, use_global_device_ids=true | all-gather | bytes 983040 | tf_op jit(solution)/shard_map/all_gather | solution.py:495
  314.6 6.3 %all-gather.13 = bf16[16,96,128]{2,1,0:T(8,128)(2,1)S(1)} all-gather(bf16[4,96,128]{2,1,0:T(8,128)(2,1)S(1)} %aggregate.16.mixed_ref), channel_id=15, replica_groups=mesh['section'=4,'dom'=8] {'section'}, dimensions={0}, use_global_device_ids=true | all-gather | bytes 491520 | tf_op jit(solution)/shard_map/all_gather | solution.py:504
  322.7 6.9 %finish_aggregate.13 = (bf16[4,96,128]{2,1,0:T(8,128)(2,1)}, bf16[8,1,96,128]{3,2,1,0:T(8,128)(2,1)}, bf16[8,96,128]{2,1,0:T(8,128)(2,1)S(1)}) custom-call(s32[288]{0:T(512)S(1)} %reshape.24.columns, s32[24]{0:T(128)S(1)} %reshape.22.picks, s32[1]{0:T(128)} %bitcast.info, bf16[4,96,128]{2,1,0:T(8,128)(2,1)S(1)} %aggregate.16.mixed_ref, ...), custom_call_target="tpu_custom_call" | custom-call | flops 679477248 | bytes 6291456 | tf_op jit(solution)/shard_map/finish_aggregate/pallas_call | solution.py:287
  333.7 8.4 %all-gather.14 = bf16[32,96,128]{2,1,0:T(8,128)(2,1)S(1)} all-gather(bf16[8,96,128]{2,1,0:T(8,128)(2,1)S(1)} %get-tuple-element.118.refs_0_), channel_id=16, replica_groups=mesh['section'=4,'dom'=8] {'section'}, dimensions={0}, use_global_device_ids=true | all-gather | bytes 983040 | tf_op jit(solution)/shard_map/all_gather | solution.py:495
  346.3 6.5 %all-gather.15 = bf16[16,96,128]{2,1,0:T(8,128)(2,1)S(1)} all-gather(bf16[4,96,128]{2,1,0:T(8,128)(2,1)S(1)} %aggregate.17.refs_2_), channel_id=17, replica_groups=mesh['section'=4,'dom'=8] {'section'}, dimensions={0}, use_global_device_ids=true | all-gather | bytes 491520 | tf_op jit(solution)/shard_map/all_gather | solution.py:504
  (96 shorter events, 170.4 us)
Async XLA Ops:
  7.1 19.0 %all-to-all-start = ((bf16[8,2,96,128]{3,2,1,0:T(8,128)(2,1)}), bf16[8,2,96,128]{3,2,1,0:T(8,128)(2,1)S(1)}, u32[]{:S(2)}, u32[]{:S(2)}) async-start(bf16[8,2,96,128]{3,2,1,0:T(8,128)(2,1)} %get-tuple-element.66), calls=%async_computation | async-start | bytes 786432 | tf_op jit(solution)/shard_map/all_to_all | solution.py:466
  14.4 17.1 %collective-permute-start.1 = (bf16[16,96,128]{2,1,0:T(8,128)(2,1)}, bf16[16,96,128]{2,1,0:T(8,128)(2,1)S(1)}, u32[]{:S(2)}, u32[]{:S(2)}) collective-permute-start(bf16[16,96,128]{2,1,0:T(8,128)(2,1)} %get-tuple-element.69), channel_id=1, source_target_pairs={{0,16},{8,24},{16,0},{24,8},{1,17},{9,25},{17,1},{25,9},{2,18},{10... | collective-permute-start | bytes 1179656 | tf_op jit(solution)/shard_map/ppermute | solution.py:471
  15.9 18.2 %collective-permute-start.2 = (bf16[16,96,128]{2,1,0:T(8,128)(2,1)}, bf16[16,96,128]{2,1,0:T(8,128)(2,1)S(1)}, u32[]{:S(2)}, u32[]{:S(2)}) collective-permute-start(bf16[16,96,128]{2,1,0:T(8,128)(2,1)} %get-tuple-element.70), channel_id=1, source_target_pairs={{0,24},{8,0},{16,8},{24,16},{1,25},{9,1},{17,9},{25,17},{2,26},{10... | collective-permute-start | bytes 1179656 | tf_op jit(solution)/shard_map/ppermute | solution.py:471
  19.5 30.7 %collective-permute-start.3 = (bf16[2,96,384]{2,1,0:T(8,128)(2,1)}, bf16[2,96,384]{2,1,0:T(8,128)(2,1)S(1)}, u32[]{:S(2)}, u32[]{:S(2)}) collective-permute-start(bf16[2,96,384]{2,1,0:T(8,128)(2,1)} %get-tuple-element.73), channel_id=1, source_target_pairs={{0,8},{8,16},{16,24},{24,0},{1,9},{9,17},{17,25},{25,1},{2,10},{10... | collective-permute-start | bytes 442376 | tf_op jit(solution)/shard_map/ppermute | solution.py:471
  19.5 30.7 %collective-permute-start.4 = (bf16[2,96,384]{2,1,0:T(8,128)(2,1)}, bf16[2,96,384]{2,1,0:T(8,128)(2,1)S(1)}, u32[]{:S(2)}, u32[]{:S(2)}) collective-permute-start(bf16[2,96,384]{2,1,0:T(8,128)(2,1)} %get-tuple-element.74), channel_id=1, source_target_pairs={{0,16},{8,24},{16,0},{24,8},{1,17},{9,25},{17,1},{25,9},{2,18},{10... | collective-permute-start | bytes 442376 | tf_op jit(solution)/shard_map/ppermute | solution.py:471
  25.4 24.8 %collective-permute-start.5 = (bf16[2,96,384]{2,1,0:T(8,128)(2,1)S(1)}, bf16[2,96,384]{2,1,0:T(8,128)(2,1)S(1)}, u32[]{:S(2)}, u32[]{:S(2)}) collective-permute-start(bf16[2,96,384]{2,1,0:T(8,128)(2,1)S(1)} %copy-done.9), channel_id=1, source_target_pairs={{0,24},{8,0},{16,8},{24,16},{1,25},{9,1},{17,9},{25,17},{2,26},{10... | collective-permute-start | bytes 442376 | tf_op jit(solution)/shard_map/ppermute | solution.py:471
  26.1 26.5 %all-to-all-start.1 = ((bf16[8,1,96,128]{3,2,1,0:T(8,128)(2,1)}), bf16[8,1,96,128]{3,2,1,0:T(8,128)(2,1)S(1)}, u32[]{:S(2)}, u32[]{:S(2)}) async-start(bf16[8,1,96,128]{3,2,1,0:T(8,128)(2,1)} %get-tuple-element.67), calls=%async_computation.1 | async-start | bytes 393216 | tf_op jit(solution)/shard_map/all_to_all | solution.py:466
  52.5 29.0 %all-to-all-start.2 = ((bf16[8,2,96,128]{3,2,1,0:T(8,128)(2,1)}), bf16[8,2,96,128]{3,2,1,0:T(8,128)(2,1)S(1)}, u32[]{:S(2)}, u32[]{:S(2)}) async-start(bf16[8,2,96,128]{3,2,1,0:T(8,128)(2,1)} %get-tuple-element.78), calls=%async_computation.2 | async-start | bytes 786432 | tf_op jit(solution)/shard_map/all_to_all | solution.py:466
  58.5 23.0 %collective-permute-start.6 = (bf16[16,96,128]{2,1,0:T(8,128)(2,1)}, bf16[16,96,128]{2,1,0:T(8,128)(2,1)S(1)}, u32[]{:S(2)}, u32[]{:S(2)}) collective-permute-start(bf16[16,96,128]{2,1,0:T(8,128)(2,1)} %get-tuple-element.79), channel_id=1, source_target_pairs={{0,8},{8,16},{16,24},{24,0},{1,9},{9,17},{17,25},{25,1},{2,10},{10... | collective-permute-start | bytes 1179656 | tf_op jit(solution)/shard_map/ppermute | solution.py:471
  58.6 22.9 %collective-permute-start.7 = (bf16[16,96,128]{2,1,0:T(8,128)(2,1)}, bf16[16,96,128]{2,1,0:T(8,128)(2,1)S(1)}, u32[]{:S(2)}, u32[]{:S(2)}) collective-permute-start(bf16[16,96,128]{2,1,0:T(8,128)(2,1)} %get-tuple-element.80), channel_id=1, source_target_pairs={{0,16},{8,24},{16,0},{24,8},{1,17},{9,25},{17,1},{25,9},{2,18},{10... | collective-permute-start | bytes 1179656 | tf_op jit(solution)/shard_map/ppermute | solution.py:471
  59.2 22.3 %collective-permute-start.8 = (bf16[16,96,128]{2,1,0:T(8,128)(2,1)S(1)}, bf16[16,96,128]{2,1,0:T(8,128)(2,1)S(1)}, u32[]{:S(2)}, u32[]{:S(2)}) collective-permute-start(bf16[16,96,128]{2,1,0:T(8,128)(2,1)S(1)} %copy-done.8), channel_id=1, source_target_pairs={{0,24},{8,0},{16,8},{24,16},{1,25},{9,1},{17,9},{25,17},{2,26},{10... | collective-permute-start | bytes 1179656 | tf_op jit(solution)/shard_map/ppermute | solution.py:471
  89.4 16.7 %all-to-all-start.4 = ((bf16[8,1,96,128]{3,2,1,0:T(8,128)(2,1)}), bf16[8,1,96,128]{3,2,1,0:T(8,128)(2,1)S(1)}, u32[]{:S(2)}, u32[]{:S(2)}) async-start(bf16[8,1,96,128]{3,2,1,0:T(8,128)(2,1)} %get-tuple-element.86), calls=%async_computation.4 | async-start | bytes 393216 | tf_op jit(solution)/shard_map/all_to_all | solution.py:466
  106.1 17.9 %all-to-all-start.3 = ((bf16[8,2,96,128]{3,2,1,0:T(8,128)(2,1)}), bf16[8,2,96,128]{3,2,1,0:T(8,128)(2,1)S(1)}, u32[]{:S(2)}, u32[]{:S(2)}) async-start(bf16[8,2,96,128]{3,2,1,0:T(8,128)(2,1)} %get-tuple-element.84), calls=%async_computation.3 | async-start | bytes 786432 | tf_op jit(solution)/shard_map/all_to_all | solution.py:466
  131.0 14.8 %all-to-all-start.5 = ((bf16[8,1,96,128]{3,2,1,0:T(8,128)(2,1)}), bf16[8,1,96,128]{3,2,1,0:T(8,128)(2,1)S(1)}, u32[]{:S(2)}, u32[]{:S(2)}) async-start(bf16[8,1,96,128]{3,2,1,0:T(8,128)(2,1)} %get-tuple-element.89), calls=%async_computation.5 | async-start | bytes 393216 | tf_op jit(solution)/shard_map/all_to_all | solution.py:466
  145.8 17.9 %all-to-all-start.6 = ((bf16[8,2,96,128]{3,2,1,0:T(8,128)(2,1)}), bf16[8,2,96,128]{3,2,1,0:T(8,128)(2,1)S(1)}, u32[]{:S(2)}, u32[]{:S(2)}) async-start(bf16[8,2,96,128]{3,2,1,0:T(8,128)(2,1)} %get-tuple-element.93), calls=%async_computation.6 | async-start | bytes 786432 | tf_op jit(solution)/shard_map/all_to_all | solution.py:466
  170.6 14.9 %all-to-all-start.8 = ((bf16[8,1,96,128]{3,2,1,0:T(8,128)(2,1)}), bf16[8,1,96,128]{3,2,1,0:T(8,128)(2,1)S(1)}, u32[]{:S(2)}, u32[]{:S(2)}) async-start(bf16[8,1,96,128]{3,2,1,0:T(8,128)(2,1)} %get-tuple-element.98), calls=%async_computation.8 | async-start | bytes 393216 | tf_op jit(solution)/shard_map/all_to_all | solution.py:466
  185.5 17.9 %all-to-all-start.7 = ((bf16[8,2,96,128]{3,2,1,0:T(8,128)(2,1)}), bf16[8,2,96,128]{3,2,1,0:T(8,128)(2,1)S(1)}, u32[]{:S(2)}, u32[]{:S(2)}) async-start(bf16[8,2,96,128]{3,2,1,0:T(8,128)(2,1)} %get-tuple-element.96), calls=%async_computation.7 | async-start | bytes 786432 | tf_op jit(solution)/shard_map/all_to_all | solution.py:466
  210.3 14.9 %all-to-all-start.9 = ((bf16[8,1,96,128]{3,2,1,0:T(8,128)(2,1)}), bf16[8,1,96,128]{3,2,1,0:T(8,128)(2,1)S(1)}, u32[]{:S(2)}, u32[]{:S(2)}) async-start(bf16[8,1,96,128]{3,2,1,0:T(8,128)(2,1)} %get-tuple-element.101), calls=%async_computation.9 | async-start | bytes 393216 | tf_op jit(solution)/shard_map/all_to_all | solution.py:466
  225.2 17.9 %all-to-all-start.10 = ((bf16[8,2,96,128]{3,2,1,0:T(8,128)(2,1)}), bf16[8,2,96,128]{3,2,1,0:T(8,128)(2,1)S(1)}, u32[]{:S(2)}, u32[]{:S(2)}) async-start(bf16[8,2,96,128]{3,2,1,0:T(8,128)(2,1)} %get-tuple-element.105), calls=%async_computation.10 | async-start | bytes 786432 | tf_op jit(solution)/shard_map/all_to_all | solution.py:466
  250.0 15.0 %all-to-all-start.12 = ((bf16[8,1,96,128]{3,2,1,0:T(8,128)(2,1)}), bf16[8,1,96,128]{3,2,1,0:T(8,128)(2,1)S(1)}, u32[]{:S(2)}, u32[]{:S(2)}) async-start(bf16[8,1,96,128]{3,2,1,0:T(8,128)(2,1)} %get-tuple-element.110), calls=%async_computation.12 | async-start | bytes 393216 | tf_op jit(solution)/shard_map/all_to_all | solution.py:466
  265.1 17.9 %all-to-all-start.11 = ((bf16[8,2,96,128]{3,2,1,0:T(8,128)(2,1)}), bf16[8,2,96,128]{3,2,1,0:T(8,128)(2,1)S(1)}, u32[]{:S(2)}, u32[]{:S(2)}) async-start(bf16[8,2,96,128]{3,2,1,0:T(8,128)(2,1)} %get-tuple-element.108), calls=%async_computation.11 | async-start | bytes 786432 | tf_op jit(solution)/shard_map/all_to_all | solution.py:466
  289.8 14.9 %all-to-all-start.13 = ((bf16[8,1,96,128]{3,2,1,0:T(8,128)(2,1)}), bf16[8,1,96,128]{3,2,1,0:T(8,128)(2,1)S(1)}, u32[]{:S(2)}, u32[]{:S(2)}) async-start(bf16[8,1,96,128]{3,2,1,0:T(8,128)(2,1)} %get-tuple-element.113), calls=%async_computation.13 | async-start | bytes 393216 | tf_op jit(solution)/shard_map/all_to_all | solution.py:466
  304.7 17.9 %all-to-all-start.14 = ((bf16[8,2,96,128]{3,2,1,0:T(8,128)(2,1)}), bf16[8,2,96,128]{3,2,1,0:T(8,128)(2,1)S(1)}, u32[]{:S(2)}, u32[]{:S(2)}) async-start(bf16[8,2,96,128]{3,2,1,0:T(8,128)(2,1)} %get-tuple-element.117), calls=%async_computation.14 | async-start | bytes 786432 | tf_op jit(solution)/shard_map/all_to_all | solution.py:466
  329.6 12.6 %all-to-all-start.15 = ((bf16[8,1,96,128]{3,2,1,0:T(8,128)(2,1)}), bf16[8,1,96,128]{3,2,1,0:T(8,128)(2,1)S(1)}, u32[]{:S(2)}, u32[]{:S(2)}) async-start(bf16[8,1,96,128]{3,2,1,0:T(8,128)(2,1)} %get-tuple-element.120), calls=%async_computation.15 | async-start | bytes 393216 | tf_op jit(solution)/shard_map/all_to_all | solution.py:466
  (11 other events, 84.8 us)

commit v13 on v12

--- a/solution.py
+++ b/solution.py
@@ -207,13 +207,13 @@
     initial_ref, tiles_ref = refs[:2]
     source_refs, refs = refs[2 : 2 + count], refs[2 + count :]
     own_ref, outgoing_ref, next_ref = refs[:3]
-    scratch = refs[3:7]
+    scratch = refs[3:5]
     work = Aggregate(
-        aggregate_plan, columns, info, initial_ref, tiles_ref, source_refs, next_ref, refs[7:]
+        aggregate_plan, columns, info, initial_ref, tiles_ref, source_refs, next_ref, refs[5:]
     )
-    copies = finish_begin(plan, info, mixed_ref, gathered_ref, weight_refs, scratch)
+    copies = finish_begin(plan, info, weight_refs, scratch)
     work.begin()
-    finish_run(plan, copies, picks, [own_ref, outgoing_ref], scratch)
+    finish_run(plan, copies, picks, mixed_ref, gathered_ref, [own_ref, outgoing_ref], scratch)
     work.run()
 
 
@@ -289,9 +289,11 @@
         grid_spec=pltpu.PrefetchScalarGridSpec(
             num_scalar_prefetch=3,
             grid=(1,),
-            in_specs=[anywhere] * (2 + len(weights)) + specs,
+            in_specs=[whole(mixed.shape), whole(gathered.shape)]
+            + [anywhere] * len(weights)
+            + specs,
             out_specs=[whole(mixed.shape), whole(outgoing), whole(shape)],
-            scratch_shapes=finish_scratch(mixed, gathered, weights) + scratch,
+            scratch_shapes=finish_scratch(weights) + scratch,
         ),
         out_shape=[
             in_hbm(mixed.shape),
@@ -304,10 +306,10 @@
     )(columns, picks, section, mixed, gathered, *weights, *operands)
 
 
-def finish_begin(plan, info, mixed_ref, gathered_ref, weight_refs, scratch):
+def finish_begin(plan, info, weight_refs, scratch):
     parts = len(weight_refs)
     sub, home = plan[4:6]
-    mixed, gathered, weight, sem = scratch
+    weight, sem = scratch
     copies = [
         (
             lax.rem(info[0] - home + 2 * parts, parts) == distance,
@@ -315,15 +317,13 @@
         )
         for distance, weight_ref in enumerate(weight_refs)
     ]
-    copies.append((None, pltpu.make_async_copy(gathered_ref, gathered, sem.at[parts])))
-    copies.append((None, pltpu.make_async_copy(mixed_ref, mixed, sem.at[parts + 1])))
     start_all(copies)
     return copies
 
 
-def finish_run(plan, copies, picks, refs, scratch):
+def finish_run(plan, copies, picks, mixed_ref, gathered_ref, refs, scratch):
     beta_layer, stream, group_blocks, part_count, sub, home, last = plan
-    mixed_ref, gathered_ref, weight, sem = scratch
+    weight = scratch[0]
     rows, part_width, block = mixed_ref.shape
     parts = gathered_ref.shape[0]
     wait_all(copies)
@@ -349,22 +349,21 @@
 
 def finish_kernel(plan, picks, info, mixed_ref, gathered_ref, *refs):
     parts = gathered_ref.shape[0]
-    weight_refs, out_refs, scratch = refs[:parts], refs[parts:-4], refs[-4:]
-    copies = finish_begin(plan, info, mixed_ref, gathered_ref, weight_refs, scratch)
-    finish_run(plan, copies, picks, out_refs, scratch)
+    weight_refs, out_refs, scratch = refs[:parts], refs[parts:-2], refs[-2:]
+    copies = finish_begin(plan, info, weight_refs, scratch)
+    finish_run(plan, copies, picks, mixed_ref, gathered_ref, out_refs, scratch)
     out_refs[2][...] = jnp.zeros_like(out_refs[2])
 
 
 def last_kernel(plans, picks, info, *refs):
     parts = refs[1].shape[0]
     weight_refs, out_ref = refs[4 : 4 + parts], refs[4 + parts]
-    scratches = [refs[5 + parts : 9 + parts], refs[9 + parts :]]
-    begun = [
-        finish_begin(plan, info, refs[2 * i], refs[2 * i + 1], weight_refs, scratches[i])
-        for i, plan in enumerate(plans)
-    ]
-    for plan, copies, scratch in zip(plans, begun, scratches):
-        finish_run(plan, copies, picks, [out_ref], scratch)
+    scratch = refs[5 + parts :]
+    copies = finish_begin(plans[0], info, weight_refs, scratch)
+    for index, plan in enumerate(plans):
+        mixed_ref, gathered_ref = refs[2 * index : 2 * index + 2]
+        finish_run(plan, copies, picks, mixed_ref, gathered_ref, [out_ref], scratch)
+        copies = []
 
 
 def finish_plan(layer, depth, stream, group_blocks, part_count, last):
@@ -372,12 +371,10 @@
     return (beta_layer, stream, group_blocks, part_count, layer % depth, layer // depth, last)
 
 
-def finish_scratch(mixed, gathered, weights):
+def finish_scratch(weights):
     return [
-        pltpu.VMEM(mixed.shape, jnp.bfloat16),
-        pltpu.VMEM(gathered.shape, jnp.bfloat16),
         pltpu.VMEM(weights[0].shape[1:], jnp.bfloat16),
-        pltpu.SemaphoreType.DMA((len(weights) + 2,)),
+        pltpu.SemaphoreType.DMA((len(weights),)),
     ]
 
 
@@ -390,9 +387,10 @@
         grid_spec=pltpu.PrefetchScalarGridSpec(
             num_scalar_prefetch=2,
             grid=(1,),
-            in_specs=[anywhere] * (2 * len(pairs) + len(weights)),
+            in_specs=[whole(value.shape) for pair in pairs for value in pair]
+            + [anywhere] * len(weights),
             out_specs=whole(shape),
-            scratch_shapes=sum([finish_scratch(*pair, weights) for pair in pairs], []),
+            scratch_shapes=finish_scratch(weights),
         ),
         out_shape=jax.ShapeDtypeStruct(shape, jnp.bfloat16),
         compiler_params=params(),
@@ -410,9 +408,9 @@
         grid_spec=pltpu.PrefetchScalarGridSpec(
             num_scalar_prefetch=2,
             grid=(1,),
-            in_specs=[anywhere] * (2 + len(weights)),
+            in_specs=[whole(mixed.shape), whole(gathered.shape)] + [anywhere] * len(weights),
             out_specs=[whole(s) for s in [mixed.shape, outgoing, (16, 128)]],
-            scratch_shapes=finish_scratch(mixed, gathered, weights),
+            scratch_shapes=finish_scratch(weights),
         ),
         out_shape=[
             in_hbm(mixed.shape),

time: 359 us -> 353 us (0.983)
  Pallas kernels: 117 us -> 111 us
  transfers between devices with their start and end apart: 25 -> 25, of which waited for: 9 -> 9; matrix products, arithmetic and copies ran while one was open for 0% -> 0% of each run, Pallas kernels for 16% -> 15%
where the time goes in v13:
time: 353 us; the launch traced here: 350 us
  blocking collectives  130 us (37%)
  Pallas kernels  111 us (31%)
  starting transfers between devices  89.6 us (25%)
  waiting for transfers between devices  15.9 us (5%)
    all_to_all x16, starting transfers between devices, exchange(): return lax.all_to_all(value, 'dom', split_axis=0, concat_axis=0, tiled=True)  84 us
    all_gather x8, blocking collectives, per_device(): gathered_front = lax.all_gather(mixed_front, 'section', axis=0, tiled=False)  68.4 us
    all_gather x8, blocking collectives, per_device(): gathered = lax.all_gather(mixed_back, 'section', axis=0, tiled=False)  61.1 us
    pallas_call x7, Pallas kernels, finish_and_aggregate(): pl.pallas_call(functools.partial(both_kernel, plan, aggregate_plan), grid...  45.6 us
    pallas_call x9, Pallas kernels, aggregate(): pl.pallas_call(functools.partial(aggregate_kernel, plan), grid_spec=pltpu...  39.2 us
    pallas_call x7, Pallas kernels, finish(): pl.pallas_call(functools.partial(finish_kernel, plan), grid_spec=pltpu.Pr...  13.7 us
    all_to_all x16, waiting for transfers between devices, exchange(): return lax.all_to_all(value, 'dom', split_axis=0, concat_axis=0, tiled=True)  11 us
    pallas_call x3, Pallas kernels, turn_blocks(): pl.pallas_call(turn_kernel, grid_spec=pltpu.PrefetchScalarGridSpec(num_sc...  8.01 us
  transfers between devices with their start and end apart: 25, of which 9 were waited for; matrix products, arithmetic and copies ran while one was open for 0% of the time, Pallas kernels for 15%

profile of v13, /device:TPU:0, one launch (start us, length us, event | category | flops | bytes accessed | tf_op | source)
XLA Modules:
  0.0 349.9 jit_solution(1911643195350241482)
XLA Ops:
  7.1 7.3 %all-to-all-start = ((bf16[8,2,96,128]{3,2,1,0:T(8,128)(2,1)}), bf16[8,2,96,128]{3,2,1,0:T(8,128)(2,1)S(1)}, u32[]{:S(2)}, u32[]{:S(2)}) async-start(bf16[8,2,96,128]{3,2,1,0:T(8,128)(2,1)} %get-tuple-element.66), calls=%async_computation | async-start | bytes 786432 | tf_op jit(solution)/shard_map/all_to_all | solution.py:464
  40.7 9.5 %all-gather = bf16[32,96,128]{2,1,0:T(8,128)(2,1)S(1)} all-gather(bf16[8,96,128]{2,1,0:T(8,128)(2,1)S(1)} %aggregate.9.mixed_ref), channel_id=2, replica_groups=mesh['section'=4,'dom'=8] {'section'}, dimensions={0}, use_global_device_ids=true | all-gather | bytes 983040 | tf_op jit(solution)/shard_map/all_gather | solution.py:493
  64.4 16.8 %all-gather.1 = bf16[16,96,128]{2,1,0:T(8,128)(2,1)S(1)} all-gather(bf16[4,96,128]{2,1,0:T(8,128)(2,1)S(1)} %aggregate.10.mixed_ref), channel_id=3, replica_groups=mesh['section'=4,'dom'=8] {'section'}, dimensions={0}, use_global_device_ids=true | all-gather | bytes 491520 | tf_op jit(solution)/shard_map/all_gather | solution.py:502
  82.2 6.5 %finish_aggregate.7 = (bf16[4,96,128]{2,1,0:T(8,128)(2,1)}, bf16[8,1,96,128]{3,2,1,0:T(8,128)(2,1)}, bf16[8,96,128]{2,1,0:T(8,128)(2,1)S(1)}) custom-call(s32[288]{0:T(512)S(1)} %reshape.24.columns, s32[24]{0:T(128)S(1)} %reshape.22.picks, s32[1]{0:T(128)} %bitcast.info, bf16[4,96,128]{2,1,0:T(8,128)(2,1)S(1)} %aggregate.10.mixed_ref, ...), custom_call_target="tpu_custom_call" | custom-call | flops 679477248 | bytes 6291456 | tf_op jit(solution)/shard_map/finish_aggregate/pallas_call | solution.py:287
  94.7 8.4 %all-gather.2 = bf16[32,96,128]{2,1,0:T(8,128)(2,1)S(1)} all-gather(bf16[8,96,128]{2,1,0:T(8,128)(2,1)S(1)} %get-tuple-element.82.mixed_ref), channel_id=4, replica_groups=mesh['section'=4,'dom'=8] {'section'}, dimensions={0}, use_global_device_ids=true | all-gather | bytes 983040 | tf_op jit(solution)/shard_map/all_gather | solution.py:493
  115.0 6.3 %all-gather.3 = bf16[16,96,128]{2,1,0:T(8,128)(2,1)S(1)} all-gather(bf16[4,96,128]{2,1,0:T(8,128)(2,1)S(1)} %aggregate.11.mixed_ref), channel_id=5, replica_groups=mesh['section'=4,'dom'=8] {'section'}, dimensions={0}, use_global_device_ids=true | all-gather | bytes 491520 | tf_op jit(solution)/shard_map/all_gather | solution.py:502
  123.0 6.5 %finish_aggregate.8 = (bf16[4,96,128]{2,1,0:T(8,128)(2,1)}, bf16[8,1,96,128]{3,2,1,0:T(8,128)(2,1)}, bf16[8,96,128]{2,1,0:T(8,128)(2,1)S(1)}) custom-call(s32[288]{0:T(512)S(1)} %reshape.24.columns, s32[24]{0:T(128)S(1)} %reshape.22.picks, s32[1]{0:T(128)} %bitcast.info, bf16[4,96,128]{2,1,0:T(8,128)(2,1)S(1)} %aggregate.11.mixed_ref, ...), custom_call_target="tpu_custom_call" | custom-call | flops 679477248 | bytes 6291456 | tf_op jit(solution)/shard_map/finish_aggregate/pallas_call | solution.py:287
  133.7 8.4 %all-gather.4 = bf16[32,96,128]{2,1,0:T(8,128)(2,1)S(1)} all-gather(bf16[8,96,128]{2,1,0:T(8,128)(2,1)S(1)} %get-tuple-element.90.mixed_ref), channel_id=6, replica_groups=mesh['section'=4,'dom'=8] {'section'}, dimensions={0}, use_global_device_ids=true | all-gather | bytes 983040 | tf_op jit(solution)/shard_map/all_gather | solution.py:493
  153.9 6.3 %all-gather.5 = bf16[16,96,128]{2,1,0:T(8,128)(2,1)S(1)} all-gather(bf16[4,96,128]{2,1,0:T(8,128)(2,1)S(1)} %aggregate.12.mixed_ref), channel_id=7, replica_groups=mesh['section'=4,'dom'=8] {'section'}, dimensions={0}, use_global_device_ids=true | all-gather | bytes 491520 | tf_op jit(solution)/shard_map/all_gather | solution.py:502
  162.0 6.5 %finish_aggregate.9 = (bf16[4,96,128]{2,1,0:T(8,128)(2,1)}, bf16[8,1,96,128]{3,2,1,0:T(8,128)(2,1)}, bf16[8,96,128]{2,1,0:T(8,128)(2,1)S(1)}) custom-call(s32[288]{0:T(512)S(1)} %reshape.24.columns, s32[24]{0:T(128)S(1)} %reshape.22.picks, s32[1]{0:T(128)} %bitcast.info, bf16[4,96,128]{2,1,0:T(8,128)(2,1)S(1)} %aggregate.12.mixed_ref, ...), custom_call_target="tpu_custom_call" | custom-call | flops 679477248 | bytes 6291456 | tf_op jit(solution)/shard_map/finish_aggregate/pallas_call | solution.py:287
  172.6 8.4 %all-gather.6 = bf16[32,96,128]{2,1,0:T(8,128)(2,1)S(1)} all-gather(bf16[8,96,128]{2,1,0:T(8,128)(2,1)S(1)} %get-tuple-element.94.mixed_ref), channel_id=8, replica_groups=mesh['section'=4,'dom'=8] {'section'}, dimensions={0}, use_global_device_ids=true | all-gather | bytes 983040 | tf_op jit(solution)/shard_map/all_gather | solution.py:493
  192.9 6.3 %all-gather.7 = bf16[16,96,128]{2,1,0:T(8,128)(2,1)S(1)} all-gather(bf16[4,96,128]{2,1,0:T(8,128)(2,1)S(1)} %aggregate.13.mixed_ref), channel_id=9, replica_groups=mesh['section'=4,'dom'=8] {'section'}, dimensions={0}, use_global_device_ids=true | all-gather | bytes 491520 | tf_op jit(solution)/shard_map/all_gather | solution.py:502
  200.9 6.5 %finish_aggregate.10 = (bf16[4,96,128]{2,1,0:T(8,128)(2,1)}, bf16[8,1,96,128]{3,2,1,0:T(8,128)(2,1)}, bf16[8,96,128]{2,1,0:T(8,128)(2,1)S(1)}) custom-call(s32[288]{0:T(512)S(1)} %reshape.24.columns, s32[24]{0:T(128)S(1)} %reshape.22.picks, s32[1]{0:T(128)} %bitcast.info, bf16[4,96,128]{2,1,0:T(8,128)(2,1)S(1)} %aggregate.13.mixed_ref, ...), custom_call_target="tpu_custom_call" | custom-call | flops 679477248 | bytes 6291456 | tf_op jit(solution)/shard_map/finish_aggregate/pallas_call | solution.py:287
  211.6 8.4 %all-gather.8 = bf16[32,96,128]{2,1,0:T(8,128)(2,1)S(1)} all-gather(bf16[8,96,128]{2,1,0:T(8,128)(2,1)S(1)} %get-tuple-element.102.mixed_ref), channel_id=10, replica_groups=mesh['section'=4,'dom'=8] {'section'}, dimensions={0}, use_global_device_ids=true | all-gather | bytes 983040 | tf_op jit(solution)/shard_map/all_gather | solution.py:493
  231.9 6.3 %all-gather.9 = bf16[16,96,128]{2,1,0:T(8,128)(2,1)S(1)} all-gather(bf16[4,96,128]{2,1,0:T(8,128)(2,1)S(1)} %aggregate.14.mixed_ref), channel_id=11, replica_groups=mesh['section'=4,'dom'=8] {'section'}, dimensions={0}, use_global_device_ids=true | all-gather | bytes 491520 | tf_op jit(solution)/shard_map/all_gather | solution.py:502
  239.9 6.7 %finish_aggregate.11 = (bf16[4,96,128]{2,1,0:T(8,128)(2,1)}, bf16[8,1,96,128]{3,2,1,0:T(8,128)(2,1)}, bf16[8,96,128]{2,1,0:T(8,128)(2,1)S(1)}) custom-call(s32[288]{0:T(512)S(1)} %reshape.24.columns, s32[24]{0:T(128)S(1)} %reshape.22.picks, s32[1]{0:T(128)} %bitcast.info, bf16[4,96,128]{2,1,0:T(8,128)(2,1)S(1)} %aggregate.14.mixed_ref, ...), custom_call_target="tpu_custom_call" | custom-call | flops 679477248 | bytes 6291456 | tf_op jit(solution)/shard_map/finish_aggregate/pallas_call | solution.py:287
  250.7 8.4 %all-gather.10 = bf16[32,96,128]{2,1,0:T(8,128)(2,1)S(1)} all-gather(bf16[8,96,128]{2,1,0:T(8,128)(2,1)S(1)} %get-tuple-element.106.mixed_ref), channel_id=12, replica_groups=mesh['section'=4,'dom'=8] {'section'}, dimensions={0}, use_global_device_ids=true | all-gather | bytes 983040 | tf_op jit(solution)/shard_map/all_gather | solution.py:493
  271.0 6.3 %all-gather.11 = bf16[16,96,128]{2,1,0:T(8,128)(2,1)S(1)} all-gather(bf16[4,96,128]{2,1,0:T(8,128)(2,1)S(1)} %aggregate.15.mixed_ref), channel_id=13, replica_groups=mesh['section'=4,'dom'=8] {'section'}, dimensions={0}, use_global_device_ids=true | all-gather | bytes 491520 | tf_op jit(solution)/shard_map/all_gather | solution.py:502
  279.0 6.5 %finish_aggregate.12 = (bf16[4,96,128]{2,1,0:T(8,128)(2,1)}, bf16[8,1,96,128]{3,2,1,0:T(8,128)(2,1)}, bf16[8,96,128]{2,1,0:T(8,128)(2,1)S(1)}) custom-call(s32[288]{0:T(512)S(1)} %reshape.24.columns, s32[24]{0:T(128)S(1)} %reshape.22.picks, s32[1]{0:T(128)} %bitcast.info, bf16[4,96,128]{2,1,0:T(8,128)(2,1)S(1)} %aggregate.15.mixed_ref, ...), custom_call_target="tpu_custom_call" | custom-call | flops 679477248 | bytes 6291456 | tf_op jit(solution)/shard_map/finish_aggregate/pallas_call | solution.py:287
  289.7 8.4 %all-gather.12 = bf16[32,96,128]{2,1,0:T(8,128)(2,1)S(1)} all-gather(bf16[8,96,128]{2,1,0:T(8,128)(2,1)S(1)} %get-tuple-element.114.mixed_ref), channel_id=14, replica_groups=mesh['section'=4,'dom'=8] {'section'}, dimensions={0}, use_global_device_ids=true | all-gather | bytes 983040 | tf_op jit(solution)/shard_map/all_gather | solution.py:493
  310.0 6.3 %all-gather.13 = bf16[16,96,128]{2,1,0:T(8,128)(2,1)S(1)} all-gather(bf16[4,96,128]{2,1,0:T(8,128)(2,1)S(1)} %aggregate.16.mixed_ref), channel_id=15, replica_groups=mesh['section'=4,'dom'=8] {'section'}, dimensions={0}, use_global_device_ids=true | all-gather | bytes 491520 | tf_op jit(solution)/shard_map/all_gather | solution.py:502
  318.0 6.5 %finish_aggregate.13 = (bf16[4,96,128]{2,1,0:T(8,128)(2,1)}, bf16[8,1,96,128]{3,2,1,0:T(8,128)(2,1)}, bf16[8,96,128]{2,1,0:T(8,128)(2,1)S(1)}) custom-call(s32[288]{0:T(512)S(1)} %reshape.24.columns, s32[24]{0:T(128)S(1)} %reshape.22.picks, s32[1]{0:T(128)} %bitcast.info, bf16[4,96,128]{2,1,0:T(8,128)(2,1)S(1)} %aggregate.16.mixed_ref, ...), custom_call_target="tpu_custom_call" | custom-call | flops 679477248 | bytes 6291456 | tf_op jit(solution)/shard_map/finish_aggregate/pallas_call | solution.py:287
  328.6 8.4 %all-gather.14 = bf16[32,96,128]{2,1,0:T(8,128)(2,1)S(1)} all-gather(bf16[8,96,128]{2,1,0:T(8,128)(2,1)S(1)} %get-tuple-element.118.refs_0_), channel_id=16, replica_groups=mesh['section'=4,'dom'=8] {'section'}, dimensions={0}, use_global_device_ids=true | all-gather | bytes 983040 | tf_op jit(solution)/shard_map/all_gather | solution.py:493
  341.3 6.5 %all-gather.15 = bf16[16,96,128]{2,1,0:T(8,128)(2,1)S(1)} all-gather(bf16[4,96,128]{2,1,0:T(8,128)(2,1)S(1)} %aggregate.17.refs_2_), channel_id=17, replica_groups=mesh['section'=4,'dom'=8] {'section'}, dimensions={0}, use_global_device_ids=true | all-gather | bytes 491520 | tf_op jit(solution)/shard_map/all_gather | solution.py:502
  (96 shorter events, 167.1 us)
Async XLA Ops:
  7.1 19.0 %all-to-all-start = ((bf16[8,2,96,128]{3,2,1,0:T(8,128)(2,1)}), bf16[8,2,96,128]{3,2,1,0:T(8,128)(2,1)S(1)}, u32[]{:S(2)}, u32[]{:S(2)}) async-start(bf16[8,2,96,128]{3,2,1,0:T(8,128)(2,1)} %get-tuple-element.66), calls=%async_computation | async-start | bytes 786432 | tf_op jit(solution)/shard_map/all_to_all | solution.py:464
  14.4 17.1 %collective-permute-start.1 = (bf16[16,96,128]{2,1,0:T(8,128)(2,1)}, bf16[16,96,128]{2,1,0:T(8,128)(2,1)S(1)}, u32[]{:S(2)}, u32[]{:S(2)}) collective-permute-start(bf16[16,96,128]{2,1,0:T(8,128)(2,1)} %get-tuple-element.69), channel_id=1, source_target_pairs={{0,16},{8,24},{16,0},{24,8},{1,17},{9,25},{17,1},{25,9},{2,18},{10... | collective-permute-start | bytes 1179656 | tf_op jit(solution)/shard_map/ppermute | solution.py:469
  15.9 18.2 %collective-permute-start.2 = (bf16[16,96,128]{2,1,0:T(8,128)(2,1)}, bf16[16,96,128]{2,1,0:T(8,128)(2,1)S(1)}, u32[]{:S(2)}, u32[]{:S(2)}) collective-permute-start(bf16[16,96,128]{2,1,0:T(8,128)(2,1)} %get-tuple-element.70), channel_id=1, source_target_pairs={{0,24},{8,0},{16,8},{24,16},{1,25},{9,1},{17,9},{25,17},{2,26},{10... | collective-permute-start | bytes 1179656 | tf_op jit(solution)/shard_map/ppermute | solution.py:469
  19.5 30.7 %collective-permute-start.3 = (bf16[2,96,384]{2,1,0:T(8,128)(2,1)}, bf16[2,96,384]{2,1,0:T(8,128)(2,1)S(1)}, u32[]{:S(2)}, u32[]{:S(2)}) collective-permute-start(bf16[2,96,384]{2,1,0:T(8,128)(2,1)} %get-tuple-element.73), channel_id=1, source_target_pairs={{0,8},{8,16},{16,24},{24,0},{1,9},{9,17},{17,25},{25,1},{2,10},{10... | collective-permute-start | bytes 442376 | tf_op jit(solution)/shard_map/ppermute | solution.py:469
  19.5 30.7 %collective-permute-start.4 = (bf16[2,96,384]{2,1,0:T(8,128)(2,1)}, bf16[2,96,384]{2,1,0:T(8,128)(2,1)S(1)}, u32[]{:S(2)}, u32[]{:S(2)}) collective-permute-start(bf16[2,96,384]{2,1,0:T(8,128)(2,1)} %get-tuple-element.74), channel_id=1, source_target_pairs={{0,16},{8,24},{16,0},{24,8},{1,17},{9,25},{17,1},{25,9},{2,18},{10... | collective-permute-start | bytes 442376 | tf_op jit(solution)/shard_map/ppermute | solution.py:469
  25.4 24.8 %collective-permute-start.5 = (bf16[2,96,384]{2,1,0:T(8,128)(2,1)S(1)}, bf16[2,96,384]{2,1,0:T(8,128)(2,1)S(1)}, u32[]{:S(2)}, u32[]{:S(2)}) collective-permute-start(bf16[2,96,384]{2,1,0:T(8,128)(2,1)S(1)} %copy-done.9), channel_id=1, source_target_pairs={{0,24},{8,0},{16,8},{24,16},{1,25},{9,1},{17,9},{25,17},{2,26},{10... | collective-permute-start | bytes 442376 | tf_op jit(solution)/shard_map/ppermute | solution.py:469
  26.1 26.1 %all-to-all-start.1 = ((bf16[8,1,96,128]{3,2,1,0:T(8,128)(2,1)}), bf16[8,1,96,128]{3,2,1,0:T(8,128)(2,1)S(1)}, u32[]{:S(2)}, u32[]{:S(2)}) async-start(bf16[8,1,96,128]{3,2,1,0:T(8,128)(2,1)} %get-tuple-element.67), calls=%async_computation.1 | async-start | bytes 393216 | tf_op jit(solution)/shard_map/all_to_all | solution.py:464
  52.2 29.0 %all-to-all-start.2 = ((bf16[8,2,96,128]{3,2,1,0:T(8,128)(2,1)}), bf16[8,2,96,128]{3,2,1,0:T(8,128)(2,1)S(1)}, u32[]{:S(2)}, u32[]{:S(2)}) async-start(bf16[8,2,96,128]{3,2,1,0:T(8,128)(2,1)} %get-tuple-element.78), calls=%async_computation.2 | async-start | bytes 786432 | tf_op jit(solution)/shard_map/all_to_all | solution.py:464
  58.2 23.0 %collective-permute-start.6 = (bf16[16,96,128]{2,1,0:T(8,128)(2,1)}, bf16[16,96,128]{2,1,0:T(8,128)(2,1)S(1)}, u32[]{:S(2)}, u32[]{:S(2)}) collective-permute-start(bf16[16,96,128]{2,1,0:T(8,128)(2,1)} %get-tuple-element.79), channel_id=1, source_target_pairs={{0,8},{8,16},{16,24},{24,0},{1,9},{9,17},{17,25},{25,1},{2,10},{10... | collective-permute-start | bytes 1179656 | tf_op jit(solution)/shard_map/ppermute | solution.py:469
  58.2 22.9 %collective-permute-start.7 = (bf16[16,96,128]{2,1,0:T(8,128)(2,1)}, bf16[16,96,128]{2,1,0:T(8,128)(2,1)S(1)}, u32[]{:S(2)}, u32[]{:S(2)}) collective-permute-start(bf16[16,96,128]{2,1,0:T(8,128)(2,1)} %get-tuple-element.80), channel_id=1, source_target_pairs={{0,16},{8,24},{16,0},{24,8},{1,17},{9,25},{17,1},{25,9},{2,18},{10... | collective-permute-start | bytes 1179656 | tf_op jit(solution)/shard_map/ppermute | solution.py:469
  58.8 22.3 %collective-permute-start.8 = (bf16[16,96,128]{2,1,0:T(8,128)(2,1)S(1)}, bf16[16,96,128]{2,1,0:T(8,128)(2,1)S(1)}, u32[]{:S(2)}, u32[]{:S(2)}) collective-permute-start(bf16[16,96,128]{2,1,0:T(8,128)(2,1)S(1)} %copy-done.8), channel_id=1, source_target_pairs={{0,24},{8,0},{16,8},{24,16},{1,25},{9,1},{17,9},{25,17},{2,26},{10... | collective-permute-start | bytes 1179656 | tf_op jit(solution)/shard_map/ppermute | solution.py:469
  88.7 16.4 %all-to-all-start.4 = ((bf16[8,1,96,128]{3,2,1,0:T(8,128)(2,1)}), bf16[8,1,96,128]{3,2,1,0:T(8,128)(2,1)S(1)}, u32[]{:S(2)}, u32[]{:S(2)}) async-start(bf16[8,1,96,128]{3,2,1,0:T(8,128)(2,1)} %get-tuple-element.86), calls=%async_computation.4 | async-start | bytes 393216 | tf_op jit(solution)/shard_map/all_to_all | solution.py:464
  105.1 17.9 %all-to-all-start.3 = ((bf16[8,2,96,128]{3,2,1,0:T(8,128)(2,1)}), bf16[8,2,96,128]{3,2,1,0:T(8,128)(2,1)S(1)}, u32[]{:S(2)}, u32[]{:S(2)}) async-start(bf16[8,2,96,128]{3,2,1,0:T(8,128)(2,1)} %get-tuple-element.84), calls=%async_computation.3 | async-start | bytes 786432 | tf_op jit(solution)/shard_map/all_to_all | solution.py:464
  129.5 14.5 %all-to-all-start.5 = ((bf16[8,1,96,128]{3,2,1,0:T(8,128)(2,1)}), bf16[8,1,96,128]{3,2,1,0:T(8,128)(2,1)S(1)}, u32[]{:S(2)}, u32[]{:S(2)}) async-start(bf16[8,1,96,128]{3,2,1,0:T(8,128)(2,1)} %get-tuple-element.89), calls=%async_computation.5 | async-start | bytes 393216 | tf_op jit(solution)/shard_map/all_to_all | solution.py:464
  144.0 17.9 %all-to-all-start.6 = ((bf16[8,2,96,128]{3,2,1,0:T(8,128)(2,1)}), bf16[8,2,96,128]{3,2,1,0:T(8,128)(2,1)S(1)}, u32[]{:S(2)}, u32[]{:S(2)}) async-start(bf16[8,2,96,128]{3,2,1,0:T(8,128)(2,1)} %get-tuple-element.93), calls=%async_computation.6 | async-start | bytes 786432 | tf_op jit(solution)/shard_map/all_to_all | solution.py:464
  168.4 14.6 %all-to-all-start.8 = ((bf16[8,1,96,128]{3,2,1,0:T(8,128)(2,1)}), bf16[8,1,96,128]{3,2,1,0:T(8,128)(2,1)S(1)}, u32[]{:S(2)}, u32[]{:S(2)}) async-start(bf16[8,1,96,128]{3,2,1,0:T(8,128)(2,1)} %get-tuple-element.98), calls=%async_computation.8 | async-start | bytes 393216 | tf_op jit(solution)/shard_map/all_to_all | solution.py:464
  183.0 17.9 %all-to-all-start.7 = ((bf16[8,2,96,128]{3,2,1,0:T(8,128)(2,1)}), bf16[8,2,96,128]{3,2,1,0:T(8,128)(2,1)S(1)}, u32[]{:S(2)}, u32[]{:S(2)}) async-start(bf16[8,2,96,128]{3,2,1,0:T(8,128)(2,1)} %get-tuple-element.96), calls=%async_computation.7 | async-start | bytes 786432 | tf_op jit(solution)/shard_map/all_to_all | solution.py:464
  207.4 14.5 %all-to-all-start.9 = ((bf16[8,1,96,128]{3,2,1,0:T(8,128)(2,1)}), bf16[8,1,96,128]{3,2,1,0:T(8,128)(2,1)S(1)}, u32[]{:S(2)}, u32[]{:S(2)}) async-start(bf16[8,1,96,128]{3,2,1,0:T(8,128)(2,1)} %get-tuple-element.101), calls=%async_computation.9 | async-start | bytes 393216 | tf_op jit(solution)/shard_map/all_to_all | solution.py:464
  222.0 17.9 %all-to-all-start.10 = ((bf16[8,2,96,128]{3,2,1,0:T(8,128)(2,1)}), bf16[8,2,96,128]{3,2,1,0:T(8,128)(2,1)S(1)}, u32[]{:S(2)}, u32[]{:S(2)}) async-start(bf16[8,2,96,128]{3,2,1,0:T(8,128)(2,1)} %get-tuple-element.105), calls=%async_computation.10 | async-start | bytes 786432 | tf_op jit(solution)/shard_map/all_to_all | solution.py:464
  246.6 14.5 %all-to-all-start.12 = ((bf16[8,1,96,128]{3,2,1,0:T(8,128)(2,1)}), bf16[8,1,96,128]{3,2,1,0:T(8,128)(2,1)S(1)}, u32[]{:S(2)}, u32[]{:S(2)}) async-start(bf16[8,1,96,128]{3,2,1,0:T(8,128)(2,1)} %get-tuple-element.110), calls=%async_computation.12 | async-start | bytes 393216 | tf_op jit(solution)/shard_map/all_to_all | solution.py:464
  261.1 17.9 %all-to-all-start.11 = ((bf16[8,2,96,128]{3,2,1,0:T(8,128)(2,1)}), bf16[8,2,96,128]{3,2,1,0:T(8,128)(2,1)S(1)}, u32[]{:S(2)}, u32[]{:S(2)}) async-start(bf16[8,2,96,128]{3,2,1,0:T(8,128)(2,1)} %get-tuple-element.108), calls=%async_computation.11 | async-start | bytes 786432 | tf_op jit(solution)/shard_map/all_to_all | solution.py:464
  285.5 14.6 %all-to-all-start.13 = ((bf16[8,1,96,128]{3,2,1,0:T(8,128)(2,1)}), bf16[8,1,96,128]{3,2,1,0:T(8,128)(2,1)S(1)}, u32[]{:S(2)}, u32[]{:S(2)}) async-start(bf16[8,1,96,128]{3,2,1,0:T(8,128)(2,1)} %get-tuple-element.113), calls=%async_computation.13 | async-start | bytes 393216 | tf_op jit(solution)/shard_map/all_to_all | solution.py:464
  300.1 17.9 %all-to-all-start.14 = ((bf16[8,2,96,128]{3,2,1,0:T(8,128)(2,1)}), bf16[8,2,96,128]{3,2,1,0:T(8,128)(2,1)S(1)}, u32[]{:S(2)}, u32[]{:S(2)}) async-start(bf16[8,2,96,128]{3,2,1,0:T(8,128)(2,1)} %get-tuple-element.117), calls=%async_computation.14 | async-start | bytes 786432 | tf_op jit(solution)/shard_map/all_to_all | solution.py:464
  324.5 12.6 %all-to-all-start.15 = ((bf16[8,1,96,128]{3,2,1,0:T(8,128)(2,1)}), bf16[8,1,96,128]{3,2,1,0:T(8,128)(2,1)S(1)}, u32[]{:S(2)}, u32[]{:S(2)}) async-start(bf16[8,1,96,128]{3,2,1,0:T(8,128)(2,1)} %get-tuple-element.120), calls=%async_computation.15 | async-start | bytes 393216 | tf_op jit(solution)/shard_map/all_to_all | solution.py:464
  (11 other events, 84.5 us)

commit v14 on v13

--- a/solution.py
+++ b/solution.py
@@ -139,7 +139,7 @@
         self.table, self.tiles, self.initial, table_sem, self.tiles_sem, initial_sem = scratch
         self.rows = len(self.stream) * self.group_blocks
         self.first_row = self.stream[0] * self.group_blocks
-        self.ahead = min(3, self.rows)
+        self.ahead = min(4, self.rows)
         self.initial_copy = pltpu.make_async_copy(initial_ref, self.initial, initial_sem)
         self.copies = []
         for index, (kind, target, detail) in enumerate(sources):
@@ -190,7 +190,7 @@
             )
             return carry
 
-        lax.fori_loop(0, self.rows, one_row, 0)
+        lax.fori_loop(0, self.rows, one_row, 0, unroll=2 if self.rows % 2 == 0 else 1)
 
 
 def aggregate_kernel(plan, columns, info, initial_ref, tiles_ref, *refs):
@@ -211,8 +211,8 @@
     work = Aggregate(
         aggregate_plan, columns, info, initial_ref, tiles_ref, source_refs, next_ref, refs[5:]
     )
+    work.begin()
     copies = finish_begin(plan, info, weight_refs, scratch)
-    work.begin()
     finish_run(plan, copies, picks, mixed_ref, gathered_ref, [own_ref, outgoing_ref], scratch)
     work.run()
 

time: 353 us -> 368 us (1.042)
  Pallas kernels: 111 us -> 128 us
  starting transfers between devices: 89.6 us -> 94.7 us
  waiting for transfers between devices: 15.9 us -> 10.8 us
    pallas_call x7, Pallas kernels: 45.6 us -> 54.2 us  [finish_and_aggregate(): pl.pallas_call(functools.partial(both_kernel, plan, aggregate_plan), grid...]
    pallas_call x9, Pallas kernels: 39.2 us -> 47.4 us  [aggregate(): pl.pallas_call(functools.partial(aggregate_kernel, plan), grid_spec=pltpu...]
    all_to_all x16, waiting for transfers between devices: 11 us -> 5.83 us  [exchange(): return lax.all_to_all(value, 'dom', split_axis=0, concat_axis=0, tiled=True)]
    all_to_all x16, starting transfers between devices: 84 us -> 89.1 us  [exchange(): return lax.all_to_all(value, 'dom', split_axis=0, concat_axis=0, tiled=True)]
  transfers between devices with their start and end apart: 25 -> 25, of which waited for: 9 -> 9; matrix products, arithmetic and copies ran while one was open for 0% -> 0% of each run, Pallas kernels for 15% -> 17%
where the time goes in v14:
time: 368 us; the launch traced here: 366 us
  blocking collectives  129 us (35%)
  Pallas kernels  128 us (35%)
  starting transfers between devices  94.7 us (26%)
  waiting for transfers between devices  10.8 us (3%)
    all_to_all x16, starting transfers between devices, exchange(): return lax.all_to_all(value, 'dom', split_axis=0, concat_axis=0, tiled=True)  89.1 us
    all_gather x8, blocking collectives, per_device(): gathered_front = lax.all_gather(mixed_front, 'section', axis=0, tiled=False)  68.4 us
    all_gather x8, blocking collectives, per_device(): gathered = lax.all_gather(mixed_back, 'section', axis=0, tiled=False)  60.3 us
    pallas_call x7, Pallas kernels, finish_and_aggregate(): pl.pallas_call(functools.partial(both_kernel, plan, aggregate_plan), grid...  54.2 us
    pallas_call x9, Pallas kernels, aggregate(): pl.pallas_call(functools.partial(aggregate_kernel, plan), grid_spec=pltpu...  47.4 us
    pallas_call x7, Pallas kernels, finish(): pl.pallas_call(functools.partial(finish_kernel, plan), grid_spec=pltpu.Pr...  13.6 us
    pallas_call x3, Pallas kernels, turn_blocks(): pl.pallas_call(turn_kernel, grid_spec=pltpu.PrefetchScalarGridSpec(num_sc...  8.01 us
  transfers between devices with their start and end apart: 25, of which 9 were waited for; matrix products, arithmetic and copies ran while one was open for 0% of the time, Pallas kernels for 17%

profile of v14, /device:TPU:0, one launch (start us, length us, event | category | flops | bytes accessed | tf_op | source)
XLA Modules:
  0.0 365.9 jit_solution(11439517802848675567)
XLA Ops:
  7.1 7.3 %all-to-all-start = ((bf16[8,2,96,128]{3,2,1,0:T(8,128)(2,1)}), bf16[8,2,96,128]{3,2,1,0:T(8,128)(2,1)S(1)}, u32[]{:S(2)}, u32[]{:S(2)}) async-start(bf16[8,2,96,128]{3,2,1,0:T(8,128)(2,1)} %get-tuple-element.66), calls=%async_computation | async-start | bytes 786432 | tf_op jit(solution)/shard_map/all_to_all | solution.py:464
  34.9 7.2 %aggregate.9.mixed_ref = bf16[8,96,128]{2,1,0:T(8,128)(2,1)S(1)} custom-call(s32[288]{0:T(512)S(1)} %reshape.24.columns, s32[1]{0:T(128)} %bitcast.info, bf16[8,96,128]{2,1,0:T(8,128)(2,1)} %get-tuple-element.65.initial_ref.refs_0_.refs_4_, bf16[12,24,128,128]{3,2,1,0:T(8,128)(2,1)} %tiles_ref.17, ...), custom_call_target="tpu_custom_call" | custom-call | flops 603979776 | bytes 6291456 | tf_op jit(solution)/shard_map/aggregate/pallas_call | solution.py:265
  42.1 9.5 %all-gather = bf16[32,96,128]{2,1,0:T(8,128)(2,1)S(1)} all-gather(bf16[8,96,128]{2,1,0:T(8,128)(2,1)S(1)} %aggregate.9.mixed_ref), channel_id=2, replica_groups=mesh['section'=4,'dom'=8] {'section'}, dimensions={0}, use_global_device_ids=true | all-gather | bytes 983040 | tf_op jit(solution)/shard_map/all_gather | solution.py:493
  66.7 15.9 %all-gather.1 = bf16[16,96,128]{2,1,0:T(8,128)(2,1)S(1)} all-gather(bf16[4,96,128]{2,1,0:T(8,128)(2,1)S(1)} %aggregate.10.mixed_ref), channel_id=3, replica_groups=mesh['section'=4,'dom'=8] {'section'}, dimensions={0}, use_global_device_ids=true | all-gather | bytes 491520 | tf_op jit(solution)/shard_map/all_gather | solution.py:502
  83.6 7.7 %finish_aggregate.7 = (bf16[4,96,128]{2,1,0:T(8,128)(2,1)}, bf16[8,1,96,128]{3,2,1,0:T(8,128)(2,1)}, bf16[8,96,128]{2,1,0:T(8,128)(2,1)S(1)}) custom-call(s32[288]{0:T(512)S(1)} %reshape.24.columns, s32[24]{0:T(128)S(1)} %reshape.22.picks, s32[1]{0:T(128)} %bitcast.info, bf16[4,96,128]{2,1,0:T(8,128)(2,1)S(1)} %aggregate.10.mixed_ref, ...), custom_call_target="tpu_custom_call" | custom-call | flops 679477248 | bytes 6291456 | tf_op jit(solution)/shard_map/finish_aggregate/pallas_call | solution.py:287
  97.4 8.4 %all-gather.2 = bf16[32,96,128]{2,1,0:T(8,128)(2,1)S(1)} all-gather(bf16[8,96,128]{2,1,0:T(8,128)(2,1)S(1)} %get-tuple-element.82.mixed_ref), channel_id=4, replica_groups=mesh['section'=4,'dom'=8] {'section'}, dimensions={0}, use_global_device_ids=true | all-gather | bytes 983040 | tf_op jit(solution)/shard_map/all_gather | solution.py:493
  118.5 6.3 %all-gather.3 = bf16[16,96,128]{2,1,0:T(8,128)(2,1)S(1)} all-gather(bf16[4,96,128]{2,1,0:T(8,128)(2,1)S(1)} %aggregate.11.mixed_ref), channel_id=5, replica_groups=mesh['section'=4,'dom'=8] {'section'}, dimensions={0}, use_global_device_ids=true | all-gather | bytes 491520 | tf_op jit(solution)/shard_map/all_gather | solution.py:502
  125.7 7.8 %finish_aggregate.8 = (bf16[4,96,128]{2,1,0:T(8,128)(2,1)}, bf16[8,1,96,128]{3,2,1,0:T(8,128)(2,1)}, bf16[8,96,128]{2,1,0:T(8,128)(2,1)S(1)}) custom-call(s32[288]{0:T(512)S(1)} %reshape.24.columns, s32[24]{0:T(128)S(1)} %reshape.22.picks, s32[1]{0:T(128)} %bitcast.info, bf16[4,96,128]{2,1,0:T(8,128)(2,1)S(1)} %aggregate.11.mixed_ref, ...), custom_call_target="tpu_custom_call" | custom-call | flops 679477248 | bytes 6291456 | tf_op jit(solution)/shard_map/finish_aggregate/pallas_call | solution.py:287
  138.4 8.4 %all-gather.4 = bf16[32,96,128]{2,1,0:T(8,128)(2,1)S(1)} all-gather(bf16[8,96,128]{2,1,0:T(8,128)(2,1)S(1)} %get-tuple-element.90.mixed_ref), channel_id=6, replica_groups=mesh['section'=4,'dom'=8] {'section'}, dimensions={0}, use_global_device_ids=true | all-gather | bytes 983040 | tf_op jit(solution)/shard_map/all_gather | solution.py:493
  159.6 6.3 %all-gather.5 = bf16[16,96,128]{2,1,0:T(8,128)(2,1)S(1)} all-gather(bf16[4,96,128]{2,1,0:T(8,128)(2,1)S(1)} %aggregate.12.mixed_ref), channel_id=7, replica_groups=mesh['section'=4,'dom'=8] {'section'}, dimensions={0}, use_global_device_ids=true | all-gather | bytes 491520 | tf_op jit(solution)/shard_map/all_gather | solution.py:502
  166.7 7.8 %finish_aggregate.9 = (bf16[4,96,128]{2,1,0:T(8,128)(2,1)}, bf16[8,1,96,128]{3,2,1,0:T(8,128)(2,1)}, bf16[8,96,128]{2,1,0:T(8,128)(2,1)S(1)}) custom-call(s32[288]{0:T(512)S(1)} %reshape.24.columns, s32[24]{0:T(128)S(1)} %reshape.22.picks, s32[1]{0:T(128)} %bitcast.info, bf16[4,96,128]{2,1,0:T(8,128)(2,1)S(1)} %aggregate.12.mixed_ref, ...), custom_call_target="tpu_custom_call" | custom-call | flops 679477248 | bytes 6291456 | tf_op jit(solution)/shard_map/finish_aggregate/pallas_call | solution.py:287
  179.5 8.4 %all-gather.6 = bf16[32,96,128]{2,1,0:T(8,128)(2,1)S(1)} all-gather(bf16[8,96,128]{2,1,0:T(8,128)(2,1)S(1)} %get-tuple-element.94.mixed_ref), channel_id=8, replica_groups=mesh['section'=4,'dom'=8] {'section'}, dimensions={0}, use_global_device_ids=true | all-gather | bytes 983040 | tf_op jit(solution)/shard_map/all_gather | solution.py:493
  200.7 6.3 %all-gather.7 = bf16[16,96,128]{2,1,0:T(8,128)(2,1)S(1)} all-gather(bf16[4,96,128]{2,1,0:T(8,128)(2,1)S(1)} %aggregate.13.mixed_ref), channel_id=9, replica_groups=mesh['section'=4,'dom'=8] {'section'}, dimensions={0}, use_global_device_ids=true | all-gather | bytes 491520 | tf_op jit(solution)/shard_map/all_gather | solution.py:502
  207.8 7.8 %finish_aggregate.10 = (bf16[4,96,128]{2,1,0:T(8,128)(2,1)}, bf16[8,1,96,128]{3,2,1,0:T(8,128)(2,1)}, bf16[8,96,128]{2,1,0:T(8,128)(2,1)S(1)}) custom-call(s32[288]{0:T(512)S(1)} %reshape.24.columns, s32[24]{0:T(128)S(1)} %reshape.22.picks, s32[1]{0:T(128)} %bitcast.info, bf16[4,96,128]{2,1,0:T(8,128)(2,1)S(1)} %aggregate.13.mixed_ref, ...), custom_call_target="tpu_custom_call" | custom-call | flops 679477248 | bytes 6291456 | tf_op jit(solution)/shard_map/finish_aggregate/pallas_call | solution.py:287
  220.6 8.4 %all-gather.8 = bf16[32,96,128]{2,1,0:T(8,128)(2,1)S(1)} all-gather(bf16[8,96,128]{2,1,0:T(8,128)(2,1)S(1)} %get-tuple-element.102.mixed_ref), channel_id=10, replica_groups=mesh['section'=4,'dom'=8] {'section'}, dimensions={0}, use_global_device_ids=true | all-gather | bytes 983040 | tf_op jit(solution)/shard_map/all_gather | solution.py:493
  241.7 6.3 %all-gather.9 = bf16[16,96,128]{2,1,0:T(8,128)(2,1)S(1)} all-gather(bf16[4,96,128]{2,1,0:T(8,128)(2,1)S(1)} %aggregate.14.mixed_ref), channel_id=11, replica_groups=mesh['section'=4,'dom'=8] {'section'}, dimensions={0}, use_global_device_ids=true | all-gather | bytes 491520 | tf_op jit(solution)/shard_map/all_gather | solution.py:502
  248.9 7.8 %finish_aggregate.11 = (bf16[4,96,128]{2,1,0:T(8,128)(2,1)}, bf16[8,1,96,128]{3,2,1,0:T(8,128)(2,1)}, bf16[8,96,128]{2,1,0:T(8,128)(2,1)S(1)}) custom-call(s32[288]{0:T(512)S(1)} %reshape.24.columns, s32[24]{0:T(128)S(1)} %reshape.22.picks, s32[1]{0:T(128)} %bitcast.info, bf16[4,96,128]{2,1,0:T(8,128)(2,1)S(1)} %aggregate.14.mixed_ref, ...), custom_call_target="tpu_custom_call" | custom-call | flops 679477248 | bytes 6291456 | tf_op jit(solution)/shard_map/finish_aggregate/pallas_call | solution.py:287
  261.7 8.4 %all-gather.10 = bf16[32,96,128]{2,1,0:T(8,128)(2,1)S(1)} all-gather(bf16[8,96,128]{2,1,0:T(8,128)(2,1)S(1)} %get-tuple-element.106.mixed_ref), channel_id=12, replica_groups=mesh['section'=4,'dom'=8] {'section'}, dimensions={0}, use_global_device_ids=true | all-gather | bytes 983040 | tf_op jit(solution)/shard_map/all_gather | solution.py:493
  282.8 6.3 %all-gather.11 = bf16[16,96,128]{2,1,0:T(8,128)(2,1)S(1)} all-gather(bf16[4,96,128]{2,1,0:T(8,128)(2,1)S(1)} %aggregate.15.mixed_ref), channel_id=13, replica_groups=mesh['section'=4,'dom'=8] {'section'}, dimensions={0}, use_global_device_ids=true | all-gather | bytes 491520 | tf_op jit(solution)/shard_map/all_gather | solution.py:502
  290.0 7.7 %finish_aggregate.12 = (bf16[4,96,128]{2,1,0:T(8,128)(2,1)}, bf16[8,1,96,128]{3,2,1,0:T(8,128)(2,1)}, bf16[8,96,128]{2,1,0:T(8,128)(2,1)S(1)}) custom-call(s32[288]{0:T(512)S(1)} %reshape.24.columns, s32[24]{0:T(128)S(1)} %reshape.22.picks, s32[1]{0:T(128)} %bitcast.info, bf16[4,96,128]{2,1,0:T(8,128)(2,1)S(1)} %aggregate.15.mixed_ref, ...), custom_call_target="tpu_custom_call" | custom-call | flops 679477248 | bytes 6291456 | tf_op jit(solution)/shard_map/finish_aggregate/pallas_call | solution.py:287
  302.7 8.4 %all-gather.12 = bf16[32,96,128]{2,1,0:T(8,128)(2,1)S(1)} all-gather(bf16[8,96,128]{2,1,0:T(8,128)(2,1)S(1)} %get-tuple-element.114.mixed_ref), channel_id=14, replica_groups=mesh['section'=4,'dom'=8] {'section'}, dimensions={0}, use_global_device_ids=true | all-gather | bytes 983040 | tf_op jit(solution)/shard_map/all_gather | solution.py:493
  331.0 7.7 %finish_aggregate.13 = (bf16[4,96,128]{2,1,0:T(8,128)(2,1)}, bf16[8,1,96,128]{3,2,1,0:T(8,128)(2,1)}, bf16[8,96,128]{2,1,0:T(8,128)(2,1)S(1)}) custom-call(s32[288]{0:T(512)S(1)} %reshape.24.columns, s32[24]{0:T(128)S(1)} %reshape.22.picks, s32[1]{0:T(128)} %bitcast.info, bf16[4,96,128]{2,1,0:T(8,128)(2,1)S(1)} %aggregate.16.mixed_ref, ...), custom_call_target="tpu_custom_call" | custom-call | flops 679477248 | bytes 6291456 | tf_op jit(solution)/shard_map/finish_aggregate/pallas_call | solution.py:287
  343.8 8.4 %all-gather.14 = bf16[32,96,128]{2,1,0:T(8,128)(2,1)S(1)} all-gather(bf16[8,96,128]{2,1,0:T(8,128)(2,1)S(1)} %get-tuple-element.118.refs_0_), channel_id=16, replica_groups=mesh['section'=4,'dom'=8] {'section'}, dimensions={0}, use_global_device_ids=true | all-gather | bytes 983040 | tf_op jit(solution)/shard_map/all_gather | solution.py:493
  357.3 6.5 %all-gather.15 = bf16[16,96,128]{2,1,0:T(8,128)(2,1)S(1)} all-gather(bf16[4,96,128]{2,1,0:T(8,128)(2,1)S(1)} %aggregate.17.refs_2_), channel_id=17, replica_groups=mesh['section'=4,'dom'=8] {'section'}, dimensions={0}, use_global_device_ids=true | all-gather | bytes 491520 | tf_op jit(solution)/shard_map/all_gather | solution.py:502
  (96 shorter events, 174.4 us)
Async XLA Ops:
  7.1 19.0 %all-to-all-start = ((bf16[8,2,96,128]{3,2,1,0:T(8,128)(2,1)}), bf16[8,2,96,128]{3,2,1,0:T(8,128)(2,1)S(1)}, u32[]{:S(2)}, u32[]{:S(2)}) async-start(bf16[8,2,96,128]{3,2,1,0:T(8,128)(2,1)} %get-tuple-element.66), calls=%async_computation | async-start | bytes 786432 | tf_op jit(solution)/shard_map/all_to_all | solution.py:464
  14.4 17.1 %collective-permute-start.1 = (bf16[16,96,128]{2,1,0:T(8,128)(2,1)}, bf16[16,96,128]{2,1,0:T(8,128)(2,1)S(1)}, u32[]{:S(2)}, u32[]{:S(2)}) collective-permute-start(bf16[16,96,128]{2,1,0:T(8,128)(2,1)} %get-tuple-element.69), channel_id=1, source_target_pairs={{0,16},{8,24},{16,0},{24,8},{1,17},{9,25},{17,1},{25,9},{2,18},{10... | collective-permute-start | bytes 1179656 | tf_op jit(solution)/shard_map/ppermute | solution.py:469
  15.9 18.2 %collective-permute-start.2 = (bf16[16,96,128]{2,1,0:T(8,128)(2,1)}, bf16[16,96,128]{2,1,0:T(8,128)(2,1)S(1)}, u32[]{:S(2)}, u32[]{:S(2)}) collective-permute-start(bf16[16,96,128]{2,1,0:T(8,128)(2,1)} %get-tuple-element.70), channel_id=1, source_target_pairs={{0,24},{8,0},{16,8},{24,16},{1,25},{9,1},{17,9},{25,17},{2,26},{10... | collective-permute-start | bytes 1179656 | tf_op jit(solution)/shard_map/ppermute | solution.py:469
  19.5 32.1 %collective-permute-start.3 = (bf16[2,96,384]{2,1,0:T(8,128)(2,1)}, bf16[2,96,384]{2,1,0:T(8,128)(2,1)S(1)}, u32[]{:S(2)}, u32[]{:S(2)}) collective-permute-start(bf16[2,96,384]{2,1,0:T(8,128)(2,1)} %get-tuple-element.73), channel_id=1, source_target_pairs={{0,8},{8,16},{16,24},{24,0},{1,9},{9,17},{17,25},{25,1},{2,10},{10... | collective-permute-start | bytes 442376 | tf_op jit(solution)/shard_map/ppermute | solution.py:469
  19.5 32.1 %collective-permute-start.4 = (bf16[2,96,384]{2,1,0:T(8,128)(2,1)}, bf16[2,96,384]{2,1,0:T(8,128)(2,1)S(1)}, u32[]{:S(2)}, u32[]{:S(2)}) collective-permute-start(bf16[2,96,384]{2,1,0:T(8,128)(2,1)} %get-tuple-element.74), channel_id=1, source_target_pairs={{0,16},{8,24},{16,0},{24,8},{1,17},{9,25},{17,1},{25,9},{2,18},{10... | collective-permute-start | bytes 442376 | tf_op jit(solution)/shard_map/ppermute | solution.py:469
  25.4 26.2 %collective-permute-start.5 = (bf16[2,96,384]{2,1,0:T(8,128)(2,1)S(1)}, bf16[2,96,384]{2,1,0:T(8,128)(2,1)S(1)}, u32[]{:S(2)}, u32[]{:S(2)}) collective-permute-start(bf16[2,96,384]{2,1,0:T(8,128)(2,1)S(1)} %copy-done.9), channel_id=1, source_target_pairs={{0,24},{8,0},{16,8},{24,16},{1,25},{9,1},{17,9},{25,17},{2,26},{10... | collective-permute-start | bytes 442376 | tf_op jit(solution)/shard_map/ppermute | solution.py:469
  26.1 27.5 %all-to-all-start.1 = ((bf16[8,1,96,128]{3,2,1,0:T(8,128)(2,1)}), bf16[8,1,96,128]{3,2,1,0:T(8,128)(2,1)S(1)}, u32[]{:S(2)}, u32[]{:S(2)}) async-start(bf16[8,1,96,128]{3,2,1,0:T(8,128)(2,1)} %get-tuple-element.67), calls=%async_computation.1 | async-start | bytes 393216 | tf_op jit(solution)/shard_map/all_to_all | solution.py:464
  53.6 29.0 %all-to-all-start.2 = ((bf16[8,2,96,128]{3,2,1,0:T(8,128)(2,1)}), bf16[8,2,96,128]{3,2,1,0:T(8,128)(2,1)S(1)}, u32[]{:S(2)}, u32[]{:S(2)}) async-start(bf16[8,2,96,128]{3,2,1,0:T(8,128)(2,1)} %get-tuple-element.78), calls=%async_computation.2 | async-start | bytes 786432 | tf_op jit(solution)/shard_map/all_to_all | solution.py:464
  59.6 23.0 %collective-permute-start.6 = (bf16[16,96,128]{2,1,0:T(8,128)(2,1)}, bf16[16,96,128]{2,1,0:T(8,128)(2,1)S(1)}, u32[]{:S(2)}, u32[]{:S(2)}) collective-permute-start(bf16[16,96,128]{2,1,0:T(8,128)(2,1)} %get-tuple-element.79), channel_id=1, source_target_pairs={{0,8},{8,16},{16,24},{24,0},{1,9},{9,17},{17,25},{25,1},{2,10},{10... | collective-permute-start | bytes 1179656 | tf_op jit(solution)/shard_map/ppermute | solution.py:469
  59.6 22.9 %collective-permute-start.7 = (bf16[16,96,128]{2,1,0:T(8,128)(2,1)}, bf16[16,96,128]{2,1,0:T(8,128)(2,1)S(1)}, u32[]{:S(2)}, u32[]{:S(2)}) collective-permute-start(bf16[16,96,128]{2,1,0:T(8,128)(2,1)} %get-tuple-element.80), channel_id=1, source_target_pairs={{0,16},{8,24},{16,0},{24,8},{1,17},{9,25},{17,1},{25,9},{2,18},{10... | collective-permute-start | bytes 1179656 | tf_op jit(solution)/shard_map/ppermute | solution.py:469
  60.2 22.4 %collective-permute-start.8 = (bf16[16,96,128]{2,1,0:T(8,128)(2,1)S(1)}, bf16[16,96,128]{2,1,0:T(8,128)(2,1)S(1)}, u32[]{:S(2)}, u32[]{:S(2)}) collective-permute-start(bf16[16,96,128]{2,1,0:T(8,128)(2,1)S(1)} %copy-done.8), channel_id=1, source_target_pairs={{0,24},{8,0},{16,8},{24,16},{1,25},{9,1},{17,9},{25,17},{2,26},{10... | collective-permute-start | bytes 1179656 | tf_op jit(solution)/shard_map/ppermute | solution.py:469
  91.4 16.4 %all-to-all-start.4 = ((bf16[8,1,96,128]{3,2,1,0:T(8,128)(2,1)}), bf16[8,1,96,128]{3,2,1,0:T(8,128)(2,1)S(1)}, u32[]{:S(2)}, u32[]{:S(2)}) async-start(bf16[8,1,96,128]{3,2,1,0:T(8,128)(2,1)} %get-tuple-element.86), calls=%async_computation.4 | async-start | bytes 393216 | tf_op jit(solution)/shard_map/all_to_all | solution.py:464
  107.8 17.9 %all-to-all-start.3 = ((bf16[8,2,96,128]{3,2,1,0:T(8,128)(2,1)}), bf16[8,2,96,128]{3,2,1,0:T(8,128)(2,1)S(1)}, u32[]{:S(2)}, u32[]{:S(2)}) async-start(bf16[8,2,96,128]{3,2,1,0:T(8,128)(2,1)} %get-tuple-element.84), calls=%async_computation.3 | async-start | bytes 786432 | tf_op jit(solution)/shard_map/all_to_all | solution.py:464
  133.4 15.4 %all-to-all-start.5 = ((bf16[8,1,96,128]{3,2,1,0:T(8,128)(2,1)}), bf16[8,1,96,128]{3,2,1,0:T(8,128)(2,1)S(1)}, u32[]{:S(2)}, u32[]{:S(2)}) async-start(bf16[8,1,96,128]{3,2,1,0:T(8,128)(2,1)} %get-tuple-element.89), calls=%async_computation.5 | async-start | bytes 393216 | tf_op jit(solution)/shard_map/all_to_all | solution.py:464
  148.8 17.9 %all-to-all-start.6 = ((bf16[8,2,96,128]{3,2,1,0:T(8,128)(2,1)}), bf16[8,2,96,128]{3,2,1,0:T(8,128)(2,1)S(1)}, u32[]{:S(2)}, u32[]{:S(2)}) async-start(bf16[8,2,96,128]{3,2,1,0:T(8,128)(2,1)} %get-tuple-element.93), calls=%async_computation.6 | async-start | bytes 786432 | tf_op jit(solution)/shard_map/all_to_all | solution.py:464
  174.5 15.4 %all-to-all-start.8 = ((bf16[8,1,96,128]{3,2,1,0:T(8,128)(2,1)}), bf16[8,1,96,128]{3,2,1,0:T(8,128)(2,1)S(1)}, u32[]{:S(2)}, u32[]{:S(2)}) async-start(bf16[8,1,96,128]{3,2,1,0:T(8,128)(2,1)} %get-tuple-element.98), calls=%async_computation.8 | async-start | bytes 393216 | tf_op jit(solution)/shard_map/all_to_all | solution.py:464
  189.9 17.9 %all-to-all-start.7 = ((bf16[8,2,96,128]{3,2,1,0:T(8,128)(2,1)}), bf16[8,2,96,128]{3,2,1,0:T(8,128)(2,1)S(1)}, u32[]{:S(2)}, u32[]{:S(2)}) async-start(bf16[8,2,96,128]{3,2,1,0:T(8,128)(2,1)} %get-tuple-element.96), calls=%async_computation.7 | async-start | bytes 786432 | tf_op jit(solution)/shard_map/all_to_all | solution.py:464
  215.6 15.4 %all-to-all-start.9 = ((bf16[8,1,96,128]{3,2,1,0:T(8,128)(2,1)}), bf16[8,1,96,128]{3,2,1,0:T(8,128)(2,1)S(1)}, u32[]{:S(2)}, u32[]{:S(2)}) async-start(bf16[8,1,96,128]{3,2,1,0:T(8,128)(2,1)} %get-tuple-element.101), calls=%async_computation.9 | async-start | bytes 393216 | tf_op jit(solution)/shard_map/all_to_all | solution.py:464
  231.0 17.9 %all-to-all-start.10 = ((bf16[8,2,96,128]{3,2,1,0:T(8,128)(2,1)}), bf16[8,2,96,128]{3,2,1,0:T(8,128)(2,1)S(1)}, u32[]{:S(2)}, u32[]{:S(2)}) async-start(bf16[8,2,96,128]{3,2,1,0:T(8,128)(2,1)} %get-tuple-element.105), calls=%async_computation.10 | async-start | bytes 786432 | tf_op jit(solution)/shard_map/all_to_all | solution.py:464
  256.7 15.4 %all-to-all-start.12 = ((bf16[8,1,96,128]{3,2,1,0:T(8,128)(2,1)}), bf16[8,1,96,128]{3,2,1,0:T(8,128)(2,1)S(1)}, u32[]{:S(2)}, u32[]{:S(2)}) async-start(bf16[8,1,96,128]{3,2,1,0:T(8,128)(2,1)} %get-tuple-element.110), calls=%async_computation.12 | async-start | bytes 393216 | tf_op jit(solution)/shard_map/all_to_all | solution.py:464
  272.1 17.9 %all-to-all-start.11 = ((bf16[8,2,96,128]{3,2,1,0:T(8,128)(2,1)}), bf16[8,2,96,128]{3,2,1,0:T(8,128)(2,1)S(1)}, u32[]{:S(2)}, u32[]{:S(2)}) async-start(bf16[8,2,96,128]{3,2,1,0:T(8,128)(2,1)} %get-tuple-element.108), calls=%async_computation.11 | async-start | bytes 786432 | tf_op jit(solution)/shard_map/all_to_all | solution.py:464
  297.7 15.4 %all-to-all-start.13 = ((bf16[8,1,96,128]{3,2,1,0:T(8,128)(2,1)}), bf16[8,1,96,128]{3,2,1,0:T(8,128)(2,1)S(1)}, u32[]{:S(2)}, u32[]{:S(2)}) async-start(bf16[8,1,96,128]{3,2,1,0:T(8,128)(2,1)} %get-tuple-element.113), calls=%async_computation.13 | async-start | bytes 393216 | tf_op jit(solution)/shard_map/all_to_all | solution.py:464
  313.1 17.9 %all-to-all-start.14 = ((bf16[8,2,96,128]{3,2,1,0:T(8,128)(2,1)}), bf16[8,2,96,128]{3,2,1,0:T(8,128)(2,1)S(1)}, u32[]{:S(2)}, u32[]{:S(2)}) async-start(bf16[8,2,96,128]{3,2,1,0:T(8,128)(2,1)} %get-tuple-element.117), calls=%async_computation.14 | async-start | bytes 786432 | tf_op jit(solution)/shard_map/all_to_all | solution.py:464
  338.8 13.5 %all-to-all-start.15 = ((bf16[8,1,96,128]{3,2,1,0:T(8,128)(2,1)}), bf16[8,1,96,128]{3,2,1,0:T(8,128)(2,1)S(1)}, u32[]{:S(2)}, u32[]{:S(2)}) async-start(bf16[8,1,96,128]{3,2,1,0:T(8,128)(2,1)} %get-tuple-element.120), calls=%async_computation.15 | async-start | bytes 393216 | tf_op jit(solution)/shard_map/all_to_all | solution.py:464
  (11 other events, 85.9 us)

commit v15 on v13

--- a/solution.py
+++ b/solution.py
@@ -175,15 +175,12 @@
                 self.tile_copy(row + self.ahead).start()
 
             base = (self.first_row + row) * self.fanout
-            total = None
-            for tile in range(0, self.fanout, 2):
-                span = range(tile, min(tile + 2, self.fanout))
-                left = jnp.concatenate([self.table[self.columns[base + t]] for t in span], 1)
-                right = jnp.concatenate([self.tiles[row, t] for t in span], 1)
-                term = lax.dot_general(
-                    left, right, (((1,), (1,)), ((), ())), preferred_element_type=jnp.float32
-                )
-                total = term if total is None else total + term
+            span = range(self.fanout)
+            left = jnp.concatenate([self.table[self.columns[base + t]] for t in span], 1)
+            right = jnp.concatenate([self.tiles[row, t] for t in span], 1)
+            total = lax.dot_general(
+                left, right, (((1,), (1,)), ((), ())), preferred_element_type=jnp.float32
+            )
             start = self.initial[row].astype(jnp.float32)
             self.mixed_ref[row] = ((1.0 - alpha_mix) * total + alpha_mix * start).astype(
                 jnp.bfloat16

time: 353 us -> 353 us (level)
  no operation moved by 1% of the time
where the time goes in v15:
time: 353 us; the launch traced here: 350 us
  blocking collectives  130 us (37%)
  Pallas kernels  111 us (31%)
  starting transfers between devices  89.6 us (25%)
  waiting for transfers between devices  15.9 us (5%)
    all_to_all x16, starting transfers between devices, exchange(): return lax.all_to_all(value, 'dom', split_axis=0, concat_axis=0, tiled=True)  84 us
    all_gather x8, blocking collectives, per_device(): gathered_front = lax.all_gather(mixed_front, 'section', axis=0, tiled=False)  68.4 us
    all_gather x8, blocking collectives, per_device(): gathered = lax.all_gather(mixed_back, 'section', axis=0, tiled=False)  61.1 us
    pallas_call x7, Pallas kernels, finish_and_aggregate(): pl.pallas_call(functools.partial(both_kernel, plan, aggregate_plan), grid...  45.6 us
    pallas_call x9, Pallas kernels, aggregate(): pl.pallas_call(functools.partial(aggregate_kernel, plan), grid_spec=pltpu...  39.2 us
    pallas_call x7, Pallas kernels, finish(): pl.pallas_call(functools.partial(finish_kernel, plan), grid_spec=pltpu.Pr...  13.7 us
    all_to_all x16, waiting for transfers between devices, exchange(): return lax.all_to_all(value, 'dom', split_axis=0, concat_axis=0, tiled=True)  11 us
    pallas_call x3, Pallas kernels, turn_blocks(): pl.pallas_call(turn_kernel, grid_spec=pltpu.PrefetchScalarGridSpec(num_sc...  8.01 us
  transfers between devices with their start and end apart: 25, of which 9 were waited for; matrix products, arithmetic and copies ran while one was open for 0% of the time, Pallas kernels for 15%

profile of v15, /device:TPU:0, one launch (start us, length us, event | category | flops | bytes accessed | tf_op | source)
XLA Modules:
  0.0 349.9 jit_solution(2635258307423602771)
XLA Ops:
  7.1 7.3 %all-to-all-start = ((bf16[8,2,96,128]{3,2,1,0:T(8,128)(2,1)}), bf16[8,2,96,128]{3,2,1,0:T(8,128)(2,1)S(1)}, u32[]{:S(2)}, u32[]{:S(2)}) async-start(bf16[8,2,96,128]{3,2,1,0:T(8,128)(2,1)} %get-tuple-element.66), calls=%async_computation | async-start | bytes 786432 | tf_op jit(solution)/shard_map/all_to_all | solution.py:461
  40.7 9.5 %all-gather = bf16[32,96,128]{2,1,0:T(8,128)(2,1)S(1)} all-gather(bf16[8,96,128]{2,1,0:T(8,128)(2,1)S(1)} %aggregate.9.mixed_ref), channel_id=2, replica_groups=mesh['section'=4,'dom'=8] {'section'}, dimensions={0}, use_global_device_ids=true | all-gather | bytes 983040 | tf_op jit(solution)/shard_map/all_gather | solution.py:490
  64.4 16.8 %all-gather.1 = bf16[16,96,128]{2,1,0:T(8,128)(2,1)S(1)} all-gather(bf16[4,96,128]{2,1,0:T(8,128)(2,1)S(1)} %aggregate.10.mixed_ref), channel_id=3, replica_groups=mesh['section'=4,'dom'=8] {'section'}, dimensions={0}, use_global_device_ids=true | all-gather | bytes 491520 | tf_op jit(solution)/shard_map/all_gather | solution.py:499
  82.2 6.5 %finish_aggregate.7 = (bf16[4,96,128]{2,1,0:T(8,128)(2,1)}, bf16[8,1,96,128]{3,2,1,0:T(8,128)(2,1)}, bf16[8,96,128]{2,1,0:T(8,128)(2,1)S(1)}) custom-call(s32[288]{0:T(512)S(1)} %reshape.24.columns, s32[24]{0:T(128)S(1)} %reshape.22.picks, s32[1]{0:T(128)} %bitcast.info, bf16[4,96,128]{2,1,0:T(8,128)(2,1)S(1)} %aggregate.10.mixed_ref, ...), custom_call_target="tpu_custom_call" | custom-call | flops 679477248 | bytes 6291456 | tf_op jit(solution)/shard_map/finish_aggregate/pallas_call | solution.py:284
  94.7 8.4 %all-gather.2 = bf16[32,96,128]{2,1,0:T(8,128)(2,1)S(1)} all-gather(bf16[8,96,128]{2,1,0:T(8,128)(2,1)S(1)} %get-tuple-element.82.mixed_ref), channel_id=4, replica_groups=mesh['section'=4,'dom'=8] {'section'}, dimensions={0}, use_global_device_ids=true | all-gather | bytes 983040 | tf_op jit(solution)/shard_map/all_gather | solution.py:490
  115.0 6.3 %all-gather.3 = bf16[16,96,128]{2,1,0:T(8,128)(2,1)S(1)} all-gather(bf16[4,96,128]{2,1,0:T(8,128)(2,1)S(1)} %aggregate.11.mixed_ref), channel_id=5, replica_groups=mesh['section'=4,'dom'=8] {'section'}, dimensions={0}, use_global_device_ids=true | all-gather | bytes 491520 | tf_op jit(solution)/shard_map/all_gather | solution.py:499
  123.0 6.5 %finish_aggregate.8 = (bf16[4,96,128]{2,1,0:T(8,128)(2,1)}, bf16[8,1,96,128]{3,2,1,0:T(8,128)(2,1)}, bf16[8,96,128]{2,1,0:T(8,128)(2,1)S(1)}) custom-call(s32[288]{0:T(512)S(1)} %reshape.24.columns, s32[24]{0:T(128)S(1)} %reshape.22.picks, s32[1]{0:T(128)} %bitcast.info, bf16[4,96,128]{2,1,0:T(8,128)(2,1)S(1)} %aggregate.11.mixed_ref, ...), custom_call_target="tpu_custom_call" | custom-call | flops 679477248 | bytes 6291456 | tf_op jit(solution)/shard_map/finish_aggregate/pallas_call | solution.py:284
  133.7 8.4 %all-gather.4 = bf16[32,96,128]{2,1,0:T(8,128)(2,1)S(1)} all-gather(bf16[8,96,128]{2,1,0:T(8,128)(2,1)S(1)} %get-tuple-element.90.mixed_ref), channel_id=6, replica_groups=mesh['section'=4,'dom'=8] {'section'}, dimensions={0}, use_global_device_ids=true | all-gather | bytes 983040 | tf_op jit(solution)/shard_map/all_gather | solution.py:490
  154.0 6.3 %all-gather.5 = bf16[16,96,128]{2,1,0:T(8,128)(2,1)S(1)} all-gather(bf16[4,96,128]{2,1,0:T(8,128)(2,1)S(1)} %aggregate.12.mixed_ref), channel_id=7, replica_groups=mesh['section'=4,'dom'=8] {'section'}, dimensions={0}, use_global_device_ids=true | all-gather | bytes 491520 | tf_op jit(solution)/shard_map/all_gather | solution.py:499
  162.0 6.5 %finish_aggregate.9 = (bf16[4,96,128]{2,1,0:T(8,128)(2,1)}, bf16[8,1,96,128]{3,2,1,0:T(8,128)(2,1)}, bf16[8,96,128]{2,1,0:T(8,128)(2,1)S(1)}) custom-call(s32[288]{0:T(512)S(1)} %reshape.24.columns, s32[24]{0:T(128)S(1)} %reshape.22.picks, s32[1]{0:T(128)} %bitcast.info, bf16[4,96,128]{2,1,0:T(8,128)(2,1)S(1)} %aggregate.12.mixed_ref, ...), custom_call_target="tpu_custom_call" | custom-call | flops 679477248 | bytes 6291456 | tf_op jit(solution)/shard_map/finish_aggregate/pallas_call | solution.py:284
  172.6 8.4 %all-gather.6 = bf16[32,96,128]{2,1,0:T(8,128)(2,1)S(1)} all-gather(bf16[8,96,128]{2,1,0:T(8,128)(2,1)S(1)} %get-tuple-element.94.mixed_ref), channel_id=8, replica_groups=mesh['section'=4,'dom'=8] {'section'}, dimensions={0}, use_global_device_ids=true | all-gather | bytes 983040 | tf_op jit(solution)/shard_map/all_gather | solution.py:490
  193.0 6.3 %all-gather.7 = bf16[16,96,128]{2,1,0:T(8,128)(2,1)S(1)} all-gather(bf16[4,96,128]{2,1,0:T(8,128)(2,1)S(1)} %aggregate.13.mixed_ref), channel_id=9, replica_groups=mesh['section'=4,'dom'=8] {'section'}, dimensions={0}, use_global_device_ids=true | all-gather | bytes 491520 | tf_op jit(solution)/shard_map/all_gather | solution.py:499
  201.0 6.5 %finish_aggregate.10 = (bf16[4,96,128]{2,1,0:T(8,128)(2,1)}, bf16[8,1,96,128]{3,2,1,0:T(8,128)(2,1)}, bf16[8,96,128]{2,1,0:T(8,128)(2,1)S(1)}) custom-call(s32[288]{0:T(512)S(1)} %reshape.24.columns, s32[24]{0:T(128)S(1)} %reshape.22.picks, s32[1]{0:T(128)} %bitcast.info, bf16[4,96,128]{2,1,0:T(8,128)(2,1)S(1)} %aggregate.13.mixed_ref, ...), custom_call_target="tpu_custom_call" | custom-call | flops 679477248 | bytes 6291456 | tf_op jit(solution)/shard_map/finish_aggregate/pallas_call | solution.py:284
  211.6 8.4 %all-gather.8 = bf16[32,96,128]{2,1,0:T(8,128)(2,1)S(1)} all-gather(bf16[8,96,128]{2,1,0:T(8,128)(2,1)S(1)} %get-tuple-element.102.mixed_ref), channel_id=10, replica_groups=mesh['section'=4,'dom'=8] {'section'}, dimensions={0}, use_global_device_ids=true | all-gather | bytes 983040 | tf_op jit(solution)/shard_map/all_gather | solution.py:490
  231.9 6.3 %all-gather.9 = bf16[16,96,128]{2,1,0:T(8,128)(2,1)S(1)} all-gather(bf16[4,96,128]{2,1,0:T(8,128)(2,1)S(1)} %aggregate.14.mixed_ref), channel_id=11, replica_groups=mesh['section'=4,'dom'=8] {'section'}, dimensions={0}, use_global_device_ids=true | all-gather | bytes 491520 | tf_op jit(solution)/shard_map/all_gather | solution.py:499
  239.9 6.7 %finish_aggregate.11 = (bf16[4,96,128]{2,1,0:T(8,128)(2,1)}, bf16[8,1,96,128]{3,2,1,0:T(8,128)(2,1)}, bf16[8,96,128]{2,1,0:T(8,128)(2,1)S(1)}) custom-call(s32[288]{0:T(512)S(1)} %reshape.24.columns, s32[24]{0:T(128)S(1)} %reshape.22.picks, s32[1]{0:T(128)} %bitcast.info, bf16[4,96,128]{2,1,0:T(8,128)(2,1)S(1)} %aggregate.14.mixed_ref, ...), custom_call_target="tpu_custom_call" | custom-call | flops 679477248 | bytes 6291456 | tf_op jit(solution)/shard_map/finish_aggregate/pallas_call | solution.py:284
  250.8 8.4 %all-gather.10 = bf16[32,96,128]{2,1,0:T(8,128)(2,1)S(1)} all-gather(bf16[8,96,128]{2,1,0:T(8,128)(2,1)S(1)} %get-tuple-element.106.mixed_ref), channel_id=12, replica_groups=mesh['section'=4,'dom'=8] {'section'}, dimensions={0}, use_global_device_ids=true | all-gather | bytes 983040 | tf_op jit(solution)/shard_map/all_gather | solution.py:490
  271.1 6.3 %all-gather.11 = bf16[16,96,128]{2,1,0:T(8,128)(2,1)S(1)} all-gather(bf16[4,96,128]{2,1,0:T(8,128)(2,1)S(1)} %aggregate.15.mixed_ref), channel_id=13, replica_groups=mesh['section'=4,'dom'=8] {'section'}, dimensions={0}, use_global_device_ids=true | all-gather | bytes 491520 | tf_op jit(solution)/shard_map/all_gather | solution.py:499
  279.1 6.5 %finish_aggregate.12 = (bf16[4,96,128]{2,1,0:T(8,128)(2,1)}, bf16[8,1,96,128]{3,2,1,0:T(8,128)(2,1)}, bf16[8,96,128]{2,1,0:T(8,128)(2,1)S(1)}) custom-call(s32[288]{0:T(512)S(1)} %reshape.24.columns, s32[24]{0:T(128)S(1)} %reshape.22.picks, s32[1]{0:T(128)} %bitcast.info, bf16[4,96,128]{2,1,0:T(8,128)(2,1)S(1)} %aggregate.15.mixed_ref, ...), custom_call_target="tpu_custom_call" | custom-call | flops 679477248 | bytes 6291456 | tf_op jit(solution)/shard_map/finish_aggregate/pallas_call | solution.py:284
  289.7 8.4 %all-gather.12 = bf16[32,96,128]{2,1,0:T(8,128)(2,1)S(1)} all-gather(bf16[8,96,128]{2,1,0:T(8,128)(2,1)S(1)} %get-tuple-element.114.mixed_ref), channel_id=14, replica_groups=mesh['section'=4,'dom'=8] {'section'}, dimensions={0}, use_global_device_ids=true | all-gather | bytes 983040 | tf_op jit(solution)/shard_map/all_gather | solution.py:490
  310.0 6.3 %all-gather.13 = bf16[16,96,128]{2,1,0:T(8,128)(2,1)S(1)} all-gather(bf16[4,96,128]{2,1,0:T(8,128)(2,1)S(1)} %aggregate.16.mixed_ref), channel_id=15, replica_groups=mesh['section'=4,'dom'=8] {'section'}, dimensions={0}, use_global_device_ids=true | all-gather | bytes 491520 | tf_op jit(solution)/shard_map/all_gather | solution.py:499
  318.1 6.5 %finish_aggregate.13 = (bf16[4,96,128]{2,1,0:T(8,128)(2,1)}, bf16[8,1,96,128]{3,2,1,0:T(8,128)(2,1)}, bf16[8,96,128]{2,1,0:T(8,128)(2,1)S(1)}) custom-call(s32[288]{0:T(512)S(1)} %reshape.24.columns, s32[24]{0:T(128)S(1)} %reshape.22.picks, s32[1]{0:T(128)} %bitcast.info, bf16[4,96,128]{2,1,0:T(8,128)(2,1)S(1)} %aggregate.16.mixed_ref, ...), custom_call_target="tpu_custom_call" | custom-call | flops 679477248 | bytes 6291456 | tf_op jit(solution)/shard_map/finish_aggregate/pallas_call | solution.py:284
  328.7 8.4 %all-gather.14 = bf16[32,96,128]{2,1,0:T(8,128)(2,1)S(1)} all-gather(bf16[8,96,128]{2,1,0:T(8,128)(2,1)S(1)} %get-tuple-element.118.refs_0_), channel_id=16, replica_groups=mesh['section'=4,'dom'=8] {'section'}, dimensions={0}, use_global_device_ids=true | all-gather | bytes 983040 | tf_op jit(solution)/shard_map/all_gather | solution.py:490
  341.3 6.5 %all-gather.15 = bf16[16,96,128]{2,1,0:T(8,128)(2,1)S(1)} all-gather(bf16[4,96,128]{2,1,0:T(8,128)(2,1)S(1)} %aggregate.17.refs_2_), channel_id=17, replica_groups=mesh['section'=4,'dom'=8] {'section'}, dimensions={0}, use_global_device_ids=true | all-gather | bytes 491520 | tf_op jit(solution)/shard_map/all_gather | solution.py:499
  (96 shorter events, 167.2 us)
Async XLA Ops:
  7.1 19.0 %all-to-all-start = ((bf16[8,2,96,128]{3,2,1,0:T(8,128)(2,1)}), bf16[8,2,96,128]{3,2,1,0:T(8,128)(2,1)S(1)}, u32[]{:S(2)}, u32[]{:S(2)}) async-start(bf16[8,2,96,128]{3,2,1,0:T(8,128)(2,1)} %get-tuple-element.66), calls=%async_computation | async-start | bytes 786432 | tf_op jit(solution)/shard_map/all_to_all | solution.py:461
  14.4 17.1 %collective-permute-start.1 = (bf16[16,96,128]{2,1,0:T(8,128)(2,1)}, bf16[16,96,128]{2,1,0:T(8,128)(2,1)S(1)}, u32[]{:S(2)}, u32[]{:S(2)}) collective-permute-start(bf16[16,96,128]{2,1,0:T(8,128)(2,1)} %get-tuple-element.69), channel_id=1, source_target_pairs={{0,16},{8,24},{16,0},{24,8},{1,17},{9,25},{17,1},{25,9},{2,18},{10... | collective-permute-start | bytes 1179656 | tf_op jit(solution)/shard_map/ppermute | solution.py:466
  15.9 18.2 %collective-permute-start.2 = (bf16[16,96,128]{2,1,0:T(8,128)(2,1)}, bf16[16,96,128]{2,1,0:T(8,128)(2,1)S(1)}, u32[]{:S(2)}, u32[]{:S(2)}) collective-permute-start(bf16[16,96,128]{2,1,0:T(8,128)(2,1)} %get-tuple-element.70), channel_id=1, source_target_pairs={{0,24},{8,0},{16,8},{24,16},{1,25},{9,1},{17,9},{25,17},{2,26},{10... | collective-permute-start | bytes 1179656 | tf_op jit(solution)/shard_map/ppermute | solution.py:466
  19.5 30.7 %collective-permute-start.3 = (bf16[2,96,384]{2,1,0:T(8,128)(2,1)}, bf16[2,96,384]{2,1,0:T(8,128)(2,1)S(1)}, u32[]{:S(2)}, u32[]{:S(2)}) collective-permute-start(bf16[2,96,384]{2,1,0:T(8,128)(2,1)} %get-tuple-element.73), channel_id=1, source_target_pairs={{0,8},{8,16},{16,24},{24,0},{1,9},{9,17},{17,25},{25,1},{2,10},{10... | collective-permute-start | bytes 442376 | tf_op jit(solution)/shard_map/ppermute | solution.py:466
  19.5 30.7 %collective-permute-start.4 = (bf16[2,96,384]{2,1,0:T(8,128)(2,1)}, bf16[2,96,384]{2,1,0:T(8,128)(2,1)S(1)}, u32[]{:S(2)}, u32[]{:S(2)}) collective-permute-start(bf16[2,96,384]{2,1,0:T(8,128)(2,1)} %get-tuple-element.74), channel_id=1, source_target_pairs={{0,16},{8,24},{16,0},{24,8},{1,17},{9,25},{17,1},{25,9},{2,18},{10... | collective-permute-start | bytes 442376 | tf_op jit(solution)/shard_map/ppermute | solution.py:466
  25.4 24.8 %collective-permute-start.5 = (bf16[2,96,384]{2,1,0:T(8,128)(2,1)S(1)}, bf16[2,96,384]{2,1,0:T(8,128)(2,1)S(1)}, u32[]{:S(2)}, u32[]{:S(2)}) collective-permute-start(bf16[2,96,384]{2,1,0:T(8,128)(2,1)S(1)} %copy-done.9), channel_id=1, source_target_pairs={{0,24},{8,0},{16,8},{24,16},{1,25},{9,1},{17,9},{25,17},{2,26},{10... | collective-permute-start | bytes 442376 | tf_op jit(solution)/shard_map/ppermute | solution.py:466
  26.1 26.1 %all-to-all-start.1 = ((bf16[8,1,96,128]{3,2,1,0:T(8,128)(2,1)}), bf16[8,1,96,128]{3,2,1,0:T(8,128)(2,1)S(1)}, u32[]{:S(2)}, u32[]{:S(2)}) async-start(bf16[8,1,96,128]{3,2,1,0:T(8,128)(2,1)} %get-tuple-element.67), calls=%async_computation.1 | async-start | bytes 393216 | tf_op jit(solution)/shard_map/all_to_all | solution.py:461
  52.2 29.0 %all-to-all-start.2 = ((bf16[8,2,96,128]{3,2,1,0:T(8,128)(2,1)}), bf16[8,2,96,128]{3,2,1,0:T(8,128)(2,1)S(1)}, u32[]{:S(2)}, u32[]{:S(2)}) async-start(bf16[8,2,96,128]{3,2,1,0:T(8,128)(2,1)} %get-tuple-element.78), calls=%async_computation.2 | async-start | bytes 786432 | tf_op jit(solution)/shard_map/all_to_all | solution.py:461
  58.2 23.0 %collective-permute-start.6 = (bf16[16,96,128]{2,1,0:T(8,128)(2,1)}, bf16[16,96,128]{2,1,0:T(8,128)(2,1)S(1)}, u32[]{:S(2)}, u32[]{:S(2)}) collective-permute-start(bf16[16,96,128]{2,1,0:T(8,128)(2,1)} %get-tuple-element.79), channel_id=1, source_target_pairs={{0,8},{8,16},{16,24},{24,0},{1,9},{9,17},{17,25},{25,1},{2,10},{10... | collective-permute-start | bytes 1179656 | tf_op jit(solution)/shard_map/ppermute | solution.py:466
  58.2 22.9 %collective-permute-start.7 = (bf16[16,96,128]{2,1,0:T(8,128)(2,1)}, bf16[16,96,128]{2,1,0:T(8,128)(2,1)S(1)}, u32[]{:S(2)}, u32[]{:S(2)}) collective-permute-start(bf16[16,96,128]{2,1,0:T(8,128)(2,1)} %get-tuple-element.80), channel_id=1, source_target_pairs={{0,16},{8,24},{16,0},{24,8},{1,17},{9,25},{17,1},{25,9},{2,18},{10... | collective-permute-start | bytes 1179656 | tf_op jit(solution)/shard_map/ppermute | solution.py:466
  58.8 22.4 %collective-permute-start.8 = (bf16[16,96,128]{2,1,0:T(8,128)(2,1)S(1)}, bf16[16,96,128]{2,1,0:T(8,128)(2,1)S(1)}, u32[]{:S(2)}, u32[]{:S(2)}) collective-permute-start(bf16[16,96,128]{2,1,0:T(8,128)(2,1)S(1)} %copy-done.8), channel_id=1, source_target_pairs={{0,24},{8,0},{16,8},{24,16},{1,25},{9,1},{17,9},{25,17},{2,26},{10... | collective-permute-start | bytes 1179656 | tf_op jit(solution)/shard_map/ppermute | solution.py:466
  88.7 16.4 %all-to-all-start.4 = ((bf16[8,1,96,128]{3,2,1,0:T(8,128)(2,1)}), bf16[8,1,96,128]{3,2,1,0:T(8,128)(2,1)S(1)}, u32[]{:S(2)}, u32[]{:S(2)}) async-start(bf16[8,1,96,128]{3,2,1,0:T(8,128)(2,1)} %get-tuple-element.86), calls=%async_computation.4 | async-start | bytes 393216 | tf_op jit(solution)/shard_map/all_to_all | solution.py:461
  105.1 17.9 %all-to-all-start.3 = ((bf16[8,2,96,128]{3,2,1,0:T(8,128)(2,1)}), bf16[8,2,96,128]{3,2,1,0:T(8,128)(2,1)S(1)}, u32[]{:S(2)}, u32[]{:S(2)}) async-start(bf16[8,2,96,128]{3,2,1,0:T(8,128)(2,1)} %get-tuple-element.84), calls=%async_computation.3 | async-start | bytes 786432 | tf_op jit(solution)/shard_map/all_to_all | solution.py:461
  129.5 14.5 %all-to-all-start.5 = ((bf16[8,1,96,128]{3,2,1,0:T(8,128)(2,1)}), bf16[8,1,96,128]{3,2,1,0:T(8,128)(2,1)S(1)}, u32[]{:S(2)}, u32[]{:S(2)}) async-start(bf16[8,1,96,128]{3,2,1,0:T(8,128)(2,1)} %get-tuple-element.89), calls=%async_computation.5 | async-start | bytes 393216 | tf_op jit(solution)/shard_map/all_to_all | solution.py:461
  144.1 17.9 %all-to-all-start.6 = ((bf16[8,2,96,128]{3,2,1,0:T(8,128)(2,1)}), bf16[8,2,96,128]{3,2,1,0:T(8,128)(2,1)S(1)}, u32[]{:S(2)}, u32[]{:S(2)}) async-start(bf16[8,2,96,128]{3,2,1,0:T(8,128)(2,1)} %get-tuple-element.93), calls=%async_computation.6 | async-start | bytes 786432 | tf_op jit(solution)/shard_map/all_to_all | solution.py:461
  168.5 14.6 %all-to-all-start.8 = ((bf16[8,1,96,128]{3,2,1,0:T(8,128)(2,1)}), bf16[8,1,96,128]{3,2,1,0:T(8,128)(2,1)S(1)}, u32[]{:S(2)}, u32[]{:S(2)}) async-start(bf16[8,1,96,128]{3,2,1,0:T(8,128)(2,1)} %get-tuple-element.98), calls=%async_computation.8 | async-start | bytes 393216 | tf_op jit(solution)/shard_map/all_to_all | solution.py:461
  183.0 17.9 %all-to-all-start.7 = ((bf16[8,2,96,128]{3,2,1,0:T(8,128)(2,1)}), bf16[8,2,96,128]{3,2,1,0:T(8,128)(2,1)S(1)}, u32[]{:S(2)}, u32[]{:S(2)}) async-start(bf16[8,2,96,128]{3,2,1,0:T(8,128)(2,1)} %get-tuple-element.96), calls=%async_computation.7 | async-start | bytes 786432 | tf_op jit(solution)/shard_map/all_to_all | solution.py:461
  207.5 14.6 %all-to-all-start.9 = ((bf16[8,1,96,128]{3,2,1,0:T(8,128)(2,1)}), bf16[8,1,96,128]{3,2,1,0:T(8,128)(2,1)S(1)}, u32[]{:S(2)}, u32[]{:S(2)}) async-start(bf16[8,1,96,128]{3,2,1,0:T(8,128)(2,1)} %get-tuple-element.101), calls=%async_computation.9 | async-start | bytes 393216 | tf_op jit(solution)/shard_map/all_to_all | solution.py:461
  222.0 17.9 %all-to-all-start.10 = ((bf16[8,2,96,128]{3,2,1,0:T(8,128)(2,1)}), bf16[8,2,96,128]{3,2,1,0:T(8,128)(2,1)S(1)}, u32[]{:S(2)}, u32[]{:S(2)}) async-start(bf16[8,2,96,128]{3,2,1,0:T(8,128)(2,1)} %get-tuple-element.105), calls=%async_computation.10 | async-start | bytes 786432 | tf_op jit(solution)/shard_map/all_to_all | solution.py:461
  246.6 14.5 %all-to-all-start.12 = ((bf16[8,1,96,128]{3,2,1,0:T(8,128)(2,1)}), bf16[8,1,96,128]{3,2,1,0:T(8,128)(2,1)S(1)}, u32[]{:S(2)}, u32[]{:S(2)}) async-start(bf16[8,1,96,128]{3,2,1,0:T(8,128)(2,1)} %get-tuple-element.110), calls=%async_computation.12 | async-start | bytes 393216 | tf_op jit(solution)/shard_map/all_to_all | solution.py:461
  261.2 17.9 %all-to-all-start.11 = ((bf16[8,2,96,128]{3,2,1,0:T(8,128)(2,1)}), bf16[8,2,96,128]{3,2,1,0:T(8,128)(2,1)S(1)}, u32[]{:S(2)}, u32[]{:S(2)}) async-start(bf16[8,2,96,128]{3,2,1,0:T(8,128)(2,1)} %get-tuple-element.108), calls=%async_computation.11 | async-start | bytes 786432 | tf_op jit(solution)/shard_map/all_to_all | solution.py:461
  285.6 14.6 %all-to-all-start.13 = ((bf16[8,1,96,128]{3,2,1,0:T(8,128)(2,1)}), bf16[8,1,96,128]{3,2,1,0:T(8,128)(2,1)S(1)}, u32[]{:S(2)}, u32[]{:S(2)}) async-start(bf16[8,1,96,128]{3,2,1,0:T(8,128)(2,1)} %get-tuple-element.113), calls=%async_computation.13 | async-start | bytes 393216 | tf_op jit(solution)/shard_map/all_to_all | solution.py:461
  300.1 17.9 %all-to-all-start.14 = ((bf16[8,2,96,128]{3,2,1,0:T(8,128)(2,1)}), bf16[8,2,96,128]{3,2,1,0:T(8,128)(2,1)S(1)}, u32[]{:S(2)}, u32[]{:S(2)}) async-start(bf16[8,2,96,128]{3,2,1,0:T(8,128)(2,1)} %get-tuple-element.117), calls=%async_computation.14 | async-start | bytes 786432 | tf_op jit(solution)/shard_map/all_to_all | solution.py:461
  324.6 12.6 %all-to-all-start.15 = ((bf16[8,1,96,128]{3,2,1,0:T(8,128)(2,1)}), bf16[8,1,96,128]{3,2,1,0:T(8,128)(2,1)S(1)}, u32[]{:S(2)}, u32[]{:S(2)}) async-start(bf16[8,1,96,128]{3,2,1,0:T(8,128)(2,1)} %get-tuple-element.120), calls=%async_computation.15 | async-start | bytes 393216 | tf_op jit(solution)/shard_map/all_to_all | solution.py:461
  (11 other events, 84.5 us)

commit v16 on v14

--- a/solution.py
+++ b/solution.py
@@ -190,7 +190,7 @@
             )
             return carry
 
-        lax.fori_loop(0, self.rows, one_row, 0, unroll=2 if self.rows % 2 == 0 else 1)
+        lax.fori_loop(0, self.rows, one_row, 0)
 
 
 def aggregate_kernel(plan, columns, info, initial_ref, tiles_ref, *refs):

time: 368 us -> 354 us (0.962)
  Pallas kernels: 128 us -> 113 us
  starting transfers between devices: 94.7 us -> 90.9 us
  waiting for transfers between devices: 10.8 us -> 14.5 us
    pallas_call x7, Pallas kernels: 54.2 us -> 45.7 us  [finish_and_aggregate(): pl.pallas_call(functools.partial(both_kernel, plan, aggregate_plan), grid...]
    pallas_call x9, Pallas kernels: 47.4 us -> 41.2 us  [aggregate(): pl.pallas_call(functools.partial(aggregate_kernel, plan), grid_spec=pltpu...]
    all_to_all x16, starting transfers between devices: 89.1 us -> 85.3 us  [exchange(): return lax.all_to_all(value, 'dom', split_axis=0, concat_axis=0, tiled=True)]
    all_to_all x16, waiting for transfers between devices: 5.83 us -> 9.56 us  [exchange(): return lax.all_to_all(value, 'dom', split_axis=0, concat_axis=0, tiled=True)]
  transfers between devices with their start and end apart: 25 -> 25, of which waited for: 9 -> 9; matrix products, arithmetic and copies ran while one was open for 0% -> 0% of each run, Pallas kernels for 17% -> 16%
where the time goes in v16:
time: 354 us; the launch traced here: 352 us
  blocking collectives  129 us (36%)
  Pallas kernels  113 us (32%)
  starting transfers between devices  90.9 us (26%)
  waiting for transfers between devices  14.5 us (4%)
    all_to_all x16, starting transfers between devices, exchange(): return lax.all_to_all(value, 'dom', split_axis=0, concat_axis=0, tiled=True)  85.3 us
    all_gather x8, blocking collectives, per_device(): gathered_front = lax.all_gather(mixed_front, 'section', axis=0, tiled=False)  68.5 us
    all_gather x8, blocking collectives, per_device(): gathered = lax.all_gather(mixed_back, 'section', axis=0, tiled=False)  60.9 us
    pallas_call x7, Pallas kernels, finish_and_aggregate(): pl.pallas_call(functools.partial(both_kernel, plan, aggregate_plan), grid...  45.7 us
    pallas_call x9, Pallas kernels, aggregate(): pl.pallas_call(functools.partial(aggregate_kernel, plan), grid_spec=pltpu...  41.2 us
    pallas_call x7, Pallas kernels, finish(): pl.pallas_call(functools.partial(finish_kernel, plan), grid_spec=pltpu.Pr...  13.7 us
    all_to_all x16, waiting for transfers between devices, exchange(): return lax.all_to_all(value, 'dom', split_axis=0, concat_axis=0, tiled=True)  9.56 us
    pallas_call x3, Pallas kernels, turn_blocks(): pl.pallas_call(turn_kernel, grid_spec=pltpu.PrefetchScalarGridSpec(num_sc...  8.01 us
  transfers between devices with their start and end apart: 25, of which 9 were waited for; matrix products, arithmetic and copies ran while one was open for 0% of the time, Pallas kernels for 16%

profile of v16, /device:TPU:0, one launch (start us, length us, event | category | flops | bytes accessed | tf_op | source)
XLA Modules:
  0.0 351.7 jit_solution(10019971925379020979)
XLA Ops:
  7.1 7.3 %all-to-all-start = ((bf16[8,2,96,128]{3,2,1,0:T(8,128)(2,1)}), bf16[8,2,96,128]{3,2,1,0:T(8,128)(2,1)S(1)}, u32[]{:S(2)}, u32[]{:S(2)}) async-start(bf16[8,2,96,128]{3,2,1,0:T(8,128)(2,1)} %get-tuple-element.66), calls=%async_computation | async-start | bytes 786432 | tf_op jit(solution)/shard_map/all_to_all | solution.py:464
  40.9 9.5 %all-gather = bf16[32,96,128]{2,1,0:T(8,128)(2,1)S(1)} all-gather(bf16[8,96,128]{2,1,0:T(8,128)(2,1)S(1)} %aggregate.9.mixed_ref), channel_id=2, replica_groups=mesh['section'=4,'dom'=8] {'section'}, dimensions={0}, use_global_device_ids=true | all-gather | bytes 983040 | tf_op jit(solution)/shard_map/all_gather | solution.py:493
  64.8 16.5 %all-gather.1 = bf16[16,96,128]{2,1,0:T(8,128)(2,1)S(1)} all-gather(bf16[4,96,128]{2,1,0:T(8,128)(2,1)S(1)} %aggregate.10.mixed_ref), channel_id=3, replica_groups=mesh['section'=4,'dom'=8] {'section'}, dimensions={0}, use_global_device_ids=true | all-gather | bytes 491520 | tf_op jit(solution)/shard_map/all_gather | solution.py:502
  82.4 6.5 %finish_aggregate.7 = (bf16[4,96,128]{2,1,0:T(8,128)(2,1)}, bf16[8,1,96,128]{3,2,1,0:T(8,128)(2,1)}, bf16[8,96,128]{2,1,0:T(8,128)(2,1)S(1)}) custom-call(s32[288]{0:T(512)S(1)} %reshape.24.columns, s32[24]{0:T(128)S(1)} %reshape.22.picks, s32[1]{0:T(128)} %bitcast.info, bf16[4,96,128]{2,1,0:T(8,128)(2,1)S(1)} %aggregate.10.mixed_ref, ...), custom_call_target="tpu_custom_call" | custom-call | flops 679477248 | bytes 6291456 | tf_op jit(solution)/shard_map/finish_aggregate/pallas_call | solution.py:287
  94.9 8.4 %all-gather.2 = bf16[32,96,128]{2,1,0:T(8,128)(2,1)S(1)} all-gather(bf16[8,96,128]{2,1,0:T(8,128)(2,1)S(1)} %get-tuple-element.82.mixed_ref), channel_id=4, replica_groups=mesh['section'=4,'dom'=8] {'section'}, dimensions={0}, use_global_device_ids=true | all-gather | bytes 983040 | tf_op jit(solution)/shard_map/all_gather | solution.py:493
  115.4 6.3 %all-gather.3 = bf16[16,96,128]{2,1,0:T(8,128)(2,1)S(1)} all-gather(bf16[4,96,128]{2,1,0:T(8,128)(2,1)S(1)} %aggregate.11.mixed_ref), channel_id=5, replica_groups=mesh['section'=4,'dom'=8] {'section'}, dimensions={0}, use_global_device_ids=true | all-gather | bytes 491520 | tf_op jit(solution)/shard_map/all_gather | solution.py:502
  123.2 6.5 %finish_aggregate.8 = (bf16[4,96,128]{2,1,0:T(8,128)(2,1)}, bf16[8,1,96,128]{3,2,1,0:T(8,128)(2,1)}, bf16[8,96,128]{2,1,0:T(8,128)(2,1)S(1)}) custom-call(s32[288]{0:T(512)S(1)} %reshape.24.columns, s32[24]{0:T(128)S(1)} %reshape.22.picks, s32[1]{0:T(128)} %bitcast.info, bf16[4,96,128]{2,1,0:T(8,128)(2,1)S(1)} %aggregate.11.mixed_ref, ...), custom_call_target="tpu_custom_call" | custom-call | flops 679477248 | bytes 6291456 | tf_op jit(solution)/shard_map/finish_aggregate/pallas_call | solution.py:287
  134.1 8.4 %all-gather.4 = bf16[32,96,128]{2,1,0:T(8,128)(2,1)S(1)} all-gather(bf16[8,96,128]{2,1,0:T(8,128)(2,1)S(1)} %get-tuple-element.90.mixed_ref), channel_id=6, replica_groups=mesh['section'=4,'dom'=8] {'section'}, dimensions={0}, use_global_device_ids=true | all-gather | bytes 983040 | tf_op jit(solution)/shard_map/all_gather | solution.py:493
  154.6 6.3 %all-gather.5 = bf16[16,96,128]{2,1,0:T(8,128)(2,1)S(1)} all-gather(bf16[4,96,128]{2,1,0:T(8,128)(2,1)S(1)} %aggregate.12.mixed_ref), channel_id=7, replica_groups=mesh['section'=4,'dom'=8] {'section'}, dimensions={0}, use_global_device_ids=true | all-gather | bytes 491520 | tf_op jit(solution)/shard_map/all_gather | solution.py:502
  162.4 6.5 %finish_aggregate.9 = (bf16[4,96,128]{2,1,0:T(8,128)(2,1)}, bf16[8,1,96,128]{3,2,1,0:T(8,128)(2,1)}, bf16[8,96,128]{2,1,0:T(8,128)(2,1)S(1)}) custom-call(s32[288]{0:T(512)S(1)} %reshape.24.columns, s32[24]{0:T(128)S(1)} %reshape.22.picks, s32[1]{0:T(128)} %bitcast.info, bf16[4,96,128]{2,1,0:T(8,128)(2,1)S(1)} %aggregate.12.mixed_ref, ...), custom_call_target="tpu_custom_call" | custom-call | flops 679477248 | bytes 6291456 | tf_op jit(solution)/shard_map/finish_aggregate/pallas_call | solution.py:287
  173.3 8.4 %all-gather.6 = bf16[32,96,128]{2,1,0:T(8,128)(2,1)S(1)} all-gather(bf16[8,96,128]{2,1,0:T(8,128)(2,1)S(1)} %get-tuple-element.94.mixed_ref), channel_id=8, replica_groups=mesh['section'=4,'dom'=8] {'section'}, dimensions={0}, use_global_device_ids=true | all-gather | bytes 983040 | tf_op jit(solution)/shard_map/all_gather | solution.py:493
  193.9 6.3 %all-gather.7 = bf16[16,96,128]{2,1,0:T(8,128)(2,1)S(1)} all-gather(bf16[4,96,128]{2,1,0:T(8,128)(2,1)S(1)} %aggregate.13.mixed_ref), channel_id=9, replica_groups=mesh['section'=4,'dom'=8] {'section'}, dimensions={0}, use_global_device_ids=true | all-gather | bytes 491520 | tf_op jit(solution)/shard_map/all_gather | solution.py:502
  201.6 6.5 %finish_aggregate.10 = (bf16[4,96,128]{2,1,0:T(8,128)(2,1)}, bf16[8,1,96,128]{3,2,1,0:T(8,128)(2,1)}, bf16[8,96,128]{2,1,0:T(8,128)(2,1)S(1)}) custom-call(s32[288]{0:T(512)S(1)} %reshape.24.columns, s32[24]{0:T(128)S(1)} %reshape.22.picks, s32[1]{0:T(128)} %bitcast.info, bf16[4,96,128]{2,1,0:T(8,128)(2,1)S(1)} %aggregate.13.mixed_ref, ...), custom_call_target="tpu_custom_call" | custom-call | flops 679477248 | bytes 6291456 | tf_op jit(solution)/shard_map/finish_aggregate/pallas_call | solution.py:287
  212.5 8.4 %all-gather.8 = bf16[32,96,128]{2,1,0:T(8,128)(2,1)S(1)} all-gather(bf16[8,96,128]{2,1,0:T(8,128)(2,1)S(1)} %get-tuple-element.102.mixed_ref), channel_id=10, replica_groups=mesh['section'=4,'dom'=8] {'section'}, dimensions={0}, use_global_device_ids=true | all-gather | bytes 983040 | tf_op jit(solution)/shard_map/all_gather | solution.py:493
  233.1 6.3 %all-gather.9 = bf16[16,96,128]{2,1,0:T(8,128)(2,1)S(1)} all-gather(bf16[4,96,128]{2,1,0:T(8,128)(2,1)S(1)} %aggregate.14.mixed_ref), channel_id=11, replica_groups=mesh['section'=4,'dom'=8] {'section'}, dimensions={0}, use_global_device_ids=true | all-gather | bytes 491520 | tf_op jit(solution)/shard_map/all_gather | solution.py:502
  240.9 6.5 %finish_aggregate.11 = (bf16[4,96,128]{2,1,0:T(8,128)(2,1)}, bf16[8,1,96,128]{3,2,1,0:T(8,128)(2,1)}, bf16[8,96,128]{2,1,0:T(8,128)(2,1)S(1)}) custom-call(s32[288]{0:T(512)S(1)} %reshape.24.columns, s32[24]{0:T(128)S(1)} %reshape.22.picks, s32[1]{0:T(128)} %bitcast.info, bf16[4,96,128]{2,1,0:T(8,128)(2,1)S(1)} %aggregate.14.mixed_ref, ...), custom_call_target="tpu_custom_call" | custom-call | flops 679477248 | bytes 6291456 | tf_op jit(solution)/shard_map/finish_aggregate/pallas_call | solution.py:287
  251.8 8.4 %all-gather.10 = bf16[32,96,128]{2,1,0:T(8,128)(2,1)S(1)} all-gather(bf16[8,96,128]{2,1,0:T(8,128)(2,1)S(1)} %get-tuple-element.106.mixed_ref), channel_id=12, replica_groups=mesh['section'=4,'dom'=8] {'section'}, dimensions={0}, use_global_device_ids=true | all-gather | bytes 983040 | tf_op jit(solution)/shard_map/all_gather | solution.py:493
  272.3 6.3 %all-gather.11 = bf16[16,96,128]{2,1,0:T(8,128)(2,1)S(1)} all-gather(bf16[4,96,128]{2,1,0:T(8,128)(2,1)S(1)} %aggregate.15.mixed_ref), channel_id=13, replica_groups=mesh['section'=4,'dom'=8] {'section'}, dimensions={0}, use_global_device_ids=true | all-gather | bytes 491520 | tf_op jit(solution)/shard_map/all_gather | solution.py:502
  280.1 6.5 %finish_aggregate.12 = (bf16[4,96,128]{2,1,0:T(8,128)(2,1)}, bf16[8,1,96,128]{3,2,1,0:T(8,128)(2,1)}, bf16[8,96,128]{2,1,0:T(8,128)(2,1)S(1)}) custom-call(s32[288]{0:T(512)S(1)} %reshape.24.columns, s32[24]{0:T(128)S(1)} %reshape.22.picks, s32[1]{0:T(128)} %bitcast.info, bf16[4,96,128]{2,1,0:T(8,128)(2,1)S(1)} %aggregate.15.mixed_ref, ...), custom_call_target="tpu_custom_call" | custom-call | flops 679477248 | bytes 6291456 | tf_op jit(solution)/shard_map/finish_aggregate/pallas_call | solution.py:287
  291.0 8.4 %all-gather.12 = bf16[32,96,128]{2,1,0:T(8,128)(2,1)S(1)} all-gather(bf16[8,96,128]{2,1,0:T(8,128)(2,1)S(1)} %get-tuple-element.114.mixed_ref), channel_id=14, replica_groups=mesh['section'=4,'dom'=8] {'section'}, dimensions={0}, use_global_device_ids=true | all-gather | bytes 983040 | tf_op jit(solution)/shard_map/all_gather | solution.py:493
  311.5 6.3 %all-gather.13 = bf16[16,96,128]{2,1,0:T(8,128)(2,1)S(1)} all-gather(bf16[4,96,128]{2,1,0:T(8,128)(2,1)S(1)} %aggregate.16.mixed_ref), channel_id=15, replica_groups=mesh['section'=4,'dom'=8] {'section'}, dimensions={0}, use_global_device_ids=true | all-gather | bytes 491520 | tf_op jit(solution)/shard_map/all_gather | solution.py:502
  319.3 6.5 %finish_aggregate.13 = (bf16[4,96,128]{2,1,0:T(8,128)(2,1)}, bf16[8,1,96,128]{3,2,1,0:T(8,128)(2,1)}, bf16[8,96,128]{2,1,0:T(8,128)(2,1)S(1)}) custom-call(s32[288]{0:T(512)S(1)} %reshape.24.columns, s32[24]{0:T(128)S(1)} %reshape.22.picks, s32[1]{0:T(128)} %bitcast.info, bf16[4,96,128]{2,1,0:T(8,128)(2,1)S(1)} %aggregate.16.mixed_ref, ...), custom_call_target="tpu_custom_call" | custom-call | flops 679477248 | bytes 6291456 | tf_op jit(solution)/shard_map/finish_aggregate/pallas_call | solution.py:287
  330.2 8.4 %all-gather.14 = bf16[32,96,128]{2,1,0:T(8,128)(2,1)S(1)} all-gather(bf16[8,96,128]{2,1,0:T(8,128)(2,1)S(1)} %get-tuple-element.118.refs_0_), channel_id=16, replica_groups=mesh['section'=4,'dom'=8] {'section'}, dimensions={0}, use_global_device_ids=true | all-gather | bytes 983040 | tf_op jit(solution)/shard_map/all_gather | solution.py:493
  343.1 6.5 %all-gather.15 = bf16[16,96,128]{2,1,0:T(8,128)(2,1)S(1)} all-gather(bf16[4,96,128]{2,1,0:T(8,128)(2,1)S(1)} %aggregate.17.refs_2_), channel_id=17, replica_groups=mesh['section'=4,'dom'=8] {'section'}, dimensions={0}, use_global_device_ids=true | all-gather | bytes 491520 | tf_op jit(solution)/shard_map/all_gather | solution.py:502
  (96 shorter events, 169.1 us)
Async XLA Ops:
  7.1 19.0 %all-to-all-start = ((bf16[8,2,96,128]{3,2,1,0:T(8,128)(2,1)}), bf16[8,2,96,128]{3,2,1,0:T(8,128)(2,1)S(1)}, u32[]{:S(2)}, u32[]{:S(2)}) async-start(bf16[8,2,96,128]{3,2,1,0:T(8,128)(2,1)} %get-tuple-element.66), calls=%async_computation | async-start | bytes 786432 | tf_op jit(solution)/shard_map/all_to_all | solution.py:464
  14.4 17.1 %collective-permute-start.1 = (bf16[16,96,128]{2,1,0:T(8,128)(2,1)}, bf16[16,96,128]{2,1,0:T(8,128)(2,1)S(1)}, u32[]{:S(2)}, u32[]{:S(2)}) collective-permute-start(bf16[16,96,128]{2,1,0:T(8,128)(2,1)} %get-tuple-element.69), channel_id=1, source_target_pairs={{0,16},{8,24},{16,0},{24,8},{1,17},{9,25},{17,1},{25,9},{2,18},{10... | collective-permute-start | bytes 1179656 | tf_op jit(solution)/shard_map/ppermute | solution.py:469
  15.9 18.2 %collective-permute-start.2 = (bf16[16,96,128]{2,1,0:T(8,128)(2,1)}, bf16[16,96,128]{2,1,0:T(8,128)(2,1)S(1)}, u32[]{:S(2)}, u32[]{:S(2)}) collective-permute-start(bf16[16,96,128]{2,1,0:T(8,128)(2,1)} %get-tuple-element.70), channel_id=1, source_target_pairs={{0,24},{8,0},{16,8},{24,16},{1,25},{9,1},{17,9},{25,17},{2,26},{10... | collective-permute-start | bytes 1179656 | tf_op jit(solution)/shard_map/ppermute | solution.py:469
  19.5 30.9 %collective-permute-start.3 = (bf16[2,96,384]{2,1,0:T(8,128)(2,1)}, bf16[2,96,384]{2,1,0:T(8,128)(2,1)S(1)}, u32[]{:S(2)}, u32[]{:S(2)}) collective-permute-start(bf16[2,96,384]{2,1,0:T(8,128)(2,1)} %get-tuple-element.73), channel_id=1, source_target_pairs={{0,8},{8,16},{16,24},{24,0},{1,9},{9,17},{17,25},{25,1},{2,10},{10... | collective-permute-start | bytes 442376 | tf_op jit(solution)/shard_map/ppermute | solution.py:469
  19.5 30.9 %collective-permute-start.4 = (bf16[2,96,384]{2,1,0:T(8,128)(2,1)}, bf16[2,96,384]{2,1,0:T(8,128)(2,1)S(1)}, u32[]{:S(2)}, u32[]{:S(2)}) collective-permute-start(bf16[2,96,384]{2,1,0:T(8,128)(2,1)} %get-tuple-element.74), channel_id=1, source_target_pairs={{0,16},{8,24},{16,0},{24,8},{1,17},{9,25},{17,1},{25,9},{2,18},{10... | collective-permute-start | bytes 442376 | tf_op jit(solution)/shard_map/ppermute | solution.py:469
  25.4 25.0 %collective-permute-start.5 = (bf16[2,96,384]{2,1,0:T(8,128)(2,1)S(1)}, bf16[2,96,384]{2,1,0:T(8,128)(2,1)S(1)}, u32[]{:S(2)}, u32[]{:S(2)}) collective-permute-start(bf16[2,96,384]{2,1,0:T(8,128)(2,1)S(1)} %copy-done.9), channel_id=1, source_target_pairs={{0,24},{8,0},{16,8},{24,16},{1,25},{9,1},{17,9},{25,17},{2,26},{10... | collective-permute-start | bytes 442376 | tf_op jit(solution)/shard_map/ppermute | solution.py:469
  26.1 26.3 %all-to-all-start.1 = ((bf16[8,1,96,128]{3,2,1,0:T(8,128)(2,1)}), bf16[8,1,96,128]{3,2,1,0:T(8,128)(2,1)S(1)}, u32[]{:S(2)}, u32[]{:S(2)}) async-start(bf16[8,1,96,128]{3,2,1,0:T(8,128)(2,1)} %get-tuple-element.67), calls=%async_computation.1 | async-start | bytes 393216 | tf_op jit(solution)/shard_map/all_to_all | solution.py:464
  52.4 29.0 %all-to-all-start.2 = ((bf16[8,2,96,128]{3,2,1,0:T(8,128)(2,1)}), bf16[8,2,96,128]{3,2,1,0:T(8,128)(2,1)S(1)}, u32[]{:S(2)}, u32[]{:S(2)}) async-start(bf16[8,2,96,128]{3,2,1,0:T(8,128)(2,1)} %get-tuple-element.78), calls=%async_computation.2 | async-start | bytes 786432 | tf_op jit(solution)/shard_map/all_to_all | solution.py:464
  58.3 23.0 %collective-permute-start.6 = (bf16[16,96,128]{2,1,0:T(8,128)(2,1)}, bf16[16,96,128]{2,1,0:T(8,128)(2,1)S(1)}, u32[]{:S(2)}, u32[]{:S(2)}) collective-permute-start(bf16[16,96,128]{2,1,0:T(8,128)(2,1)} %get-tuple-element.79), channel_id=1, source_target_pairs={{0,8},{8,16},{16,24},{24,0},{1,9},{9,17},{17,25},{25,1},{2,10},{10... | collective-permute-start | bytes 1179656 | tf_op jit(solution)/shard_map/ppermute | solution.py:469
  58.4 22.9 %collective-permute-start.7 = (bf16[16,96,128]{2,1,0:T(8,128)(2,1)}, bf16[16,96,128]{2,1,0:T(8,128)(2,1)S(1)}, u32[]{:S(2)}, u32[]{:S(2)}) collective-permute-start(bf16[16,96,128]{2,1,0:T(8,128)(2,1)} %get-tuple-element.80), channel_id=1, source_target_pairs={{0,16},{8,24},{16,0},{24,8},{1,17},{9,25},{17,1},{25,9},{2,18},{10... | collective-permute-start | bytes 1179656 | tf_op jit(solution)/shard_map/ppermute | solution.py:469
  59.0 22.3 %collective-permute-start.8 = (bf16[16,96,128]{2,1,0:T(8,128)(2,1)S(1)}, bf16[16,96,128]{2,1,0:T(8,128)(2,1)S(1)}, u32[]{:S(2)}, u32[]{:S(2)}) collective-permute-start(bf16[16,96,128]{2,1,0:T(8,128)(2,1)S(1)} %copy-done.8), channel_id=1, source_target_pairs={{0,24},{8,0},{16,8},{24,16},{1,25},{9,1},{17,9},{25,17},{2,26},{10... | collective-permute-start | bytes 1179656 | tf_op jit(solution)/shard_map/ppermute | solution.py:469
  88.9 16.4 %all-to-all-start.4 = ((bf16[8,1,96,128]{3,2,1,0:T(8,128)(2,1)}), bf16[8,1,96,128]{3,2,1,0:T(8,128)(2,1)S(1)}, u32[]{:S(2)}, u32[]{:S(2)}) async-start(bf16[8,1,96,128]{3,2,1,0:T(8,128)(2,1)} %get-tuple-element.86), calls=%async_computation.4 | async-start | bytes 393216 | tf_op jit(solution)/shard_map/all_to_all | solution.py:464
  105.3 17.9 %all-to-all-start.3 = ((bf16[8,2,96,128]{3,2,1,0:T(8,128)(2,1)}), bf16[8,2,96,128]{3,2,1,0:T(8,128)(2,1)S(1)}, u32[]{:S(2)}, u32[]{:S(2)}) async-start(bf16[8,2,96,128]{3,2,1,0:T(8,128)(2,1)} %get-tuple-element.84), calls=%async_computation.3 | async-start | bytes 786432 | tf_op jit(solution)/shard_map/all_to_all | solution.py:464
  129.7 14.8 %all-to-all-start.5 = ((bf16[8,1,96,128]{3,2,1,0:T(8,128)(2,1)}), bf16[8,1,96,128]{3,2,1,0:T(8,128)(2,1)S(1)}, u32[]{:S(2)}, u32[]{:S(2)}) async-start(bf16[8,1,96,128]{3,2,1,0:T(8,128)(2,1)} %get-tuple-element.89), calls=%async_computation.5 | async-start | bytes 393216 | tf_op jit(solution)/shard_map/all_to_all | solution.py:464
  144.5 17.9 %all-to-all-start.6 = ((bf16[8,2,96,128]{3,2,1,0:T(8,128)(2,1)}), bf16[8,2,96,128]{3,2,1,0:T(8,128)(2,1)S(1)}, u32[]{:S(2)}, u32[]{:S(2)}) async-start(bf16[8,2,96,128]{3,2,1,0:T(8,128)(2,1)} %get-tuple-element.93), calls=%async_computation.6 | async-start | bytes 786432 | tf_op jit(solution)/shard_map/all_to_all | solution.py:464
  169.0 14.8 %all-to-all-start.8 = ((bf16[8,1,96,128]{3,2,1,0:T(8,128)(2,1)}), bf16[8,1,96,128]{3,2,1,0:T(8,128)(2,1)S(1)}, u32[]{:S(2)}, u32[]{:S(2)}) async-start(bf16[8,1,96,128]{3,2,1,0:T(8,128)(2,1)} %get-tuple-element.98), calls=%async_computation.8 | async-start | bytes 393216 | tf_op jit(solution)/shard_map/all_to_all | solution.py:464
  183.7 17.9 %all-to-all-start.7 = ((bf16[8,2,96,128]{3,2,1,0:T(8,128)(2,1)}), bf16[8,2,96,128]{3,2,1,0:T(8,128)(2,1)S(1)}, u32[]{:S(2)}, u32[]{:S(2)}) async-start(bf16[8,2,96,128]{3,2,1,0:T(8,128)(2,1)} %get-tuple-element.96), calls=%async_computation.7 | async-start | bytes 786432 | tf_op jit(solution)/shard_map/all_to_all | solution.py:464
  208.2 14.8 %all-to-all-start.9 = ((bf16[8,1,96,128]{3,2,1,0:T(8,128)(2,1)}), bf16[8,1,96,128]{3,2,1,0:T(8,128)(2,1)S(1)}, u32[]{:S(2)}, u32[]{:S(2)}) async-start(bf16[8,1,96,128]{3,2,1,0:T(8,128)(2,1)} %get-tuple-element.101), calls=%async_computation.9 | async-start | bytes 393216 | tf_op jit(solution)/shard_map/all_to_all | solution.py:464
  222.9 17.9 %all-to-all-start.10 = ((bf16[8,2,96,128]{3,2,1,0:T(8,128)(2,1)}), bf16[8,2,96,128]{3,2,1,0:T(8,128)(2,1)S(1)}, u32[]{:S(2)}, u32[]{:S(2)}) async-start(bf16[8,2,96,128]{3,2,1,0:T(8,128)(2,1)} %get-tuple-element.105), calls=%async_computation.10 | async-start | bytes 786432 | tf_op jit(solution)/shard_map/all_to_all | solution.py:464
  247.4 14.8 %all-to-all-start.12 = ((bf16[8,1,96,128]{3,2,1,0:T(8,128)(2,1)}), bf16[8,1,96,128]{3,2,1,0:T(8,128)(2,1)S(1)}, u32[]{:S(2)}, u32[]{:S(2)}) async-start(bf16[8,1,96,128]{3,2,1,0:T(8,128)(2,1)} %get-tuple-element.110), calls=%async_computation.12 | async-start | bytes 393216 | tf_op jit(solution)/shard_map/all_to_all | solution.py:464
  262.2 17.9 %all-to-all-start.11 = ((bf16[8,2,96,128]{3,2,1,0:T(8,128)(2,1)}), bf16[8,2,96,128]{3,2,1,0:T(8,128)(2,1)S(1)}, u32[]{:S(2)}, u32[]{:S(2)}) async-start(bf16[8,2,96,128]{3,2,1,0:T(8,128)(2,1)} %get-tuple-element.108), calls=%async_computation.11 | async-start | bytes 786432 | tf_op jit(solution)/shard_map/all_to_all | solution.py:464
  286.6 14.8 %all-to-all-start.13 = ((bf16[8,1,96,128]{3,2,1,0:T(8,128)(2,1)}), bf16[8,1,96,128]{3,2,1,0:T(8,128)(2,1)S(1)}, u32[]{:S(2)}, u32[]{:S(2)}) async-start(bf16[8,1,96,128]{3,2,1,0:T(8,128)(2,1)} %get-tuple-element.113), calls=%async_computation.13 | async-start | bytes 393216 | tf_op jit(solution)/shard_map/all_to_all | solution.py:464
  301.4 17.9 %all-to-all-start.14 = ((bf16[8,2,96,128]{3,2,1,0:T(8,128)(2,1)}), bf16[8,2,96,128]{3,2,1,0:T(8,128)(2,1)S(1)}, u32[]{:S(2)}, u32[]{:S(2)}) async-start(bf16[8,2,96,128]{3,2,1,0:T(8,128)(2,1)} %get-tuple-element.117), calls=%async_computation.14 | async-start | bytes 786432 | tf_op jit(solution)/shard_map/all_to_all | solution.py:464
  325.9 12.8 %all-to-all-start.15 = ((bf16[8,1,96,128]{3,2,1,0:T(8,128)(2,1)}), bf16[8,1,96,128]{3,2,1,0:T(8,128)(2,1)S(1)}, u32[]{:S(2)}, u32[]{:S(2)}) async-start(bf16[8,1,96,128]{3,2,1,0:T(8,128)(2,1)} %get-tuple-element.120), calls=%async_computation.15 | async-start | bytes 393216 | tf_op jit(solution)/shard_map/all_to_all | solution.py:464
  (11 other events, 84.7 us)
